TPU v7x, 32 devices: a whole 2x2x4 slice. The times are simulated.
32 devices in a mesh: dp: 2 (over y), ctx: 16 (over z, x, core).
Axes of the slice: x: 2, y: 2, z: 4, core: 2. Of those that a mesh axis runs over, the one named last changes fastest.
Arguments:
- layer_input: bfloat16 [2, 2048, 3072], P('dp', 'ctx'), may hold values from -6 to 6
- query_rows: bfloat16 [2, 2048, 3072], P('dp', 'ctx'), may hold values from -6 to 6
- key_rows: bfloat16 [2, 2048, 3072], P('dp', 'ctx'), may hold values from -6 to 6
- value_rows: bfloat16 [2, 2048, 3072], P('dp', 'ctx'), may hold values from -6 to 6
- out_grad: bfloat16 [2, 2048, 3072], P('dp', 'ctx'), may hold values from -6 to 6
Outputs:
- query_grad: bfloat16 [2, 2048, 3072], P('dp', 'ctx')
- key_grad: bfloat16 [2, 2048, 3072], P('dp', 'ctx')
- value_grad: bfloat16 [2, 2048, 3072], P('dp', 'ctx')
- key_weight_grad: float32 [3072, 3072], P('ctx', 'dp')
All inputs are finite; a program needn't handle non-finite values.
Results may differ from a plain program's by a relative error of at most 0.028.
Values may be sent and summed in bfloat16 or wider, within the bound.
No kernel may reach another device: no remote copies, remote signals or barrier semaphores. Data moves between devices by JAX's collectives and lax.ppermute only.
A program may use at most 192 MiB of HBM per device.

v0:
```python
import jax
import jax.numpy as jnp
from jax import lax
from jax.sharding import PartitionSpec as P

HEADS = 24
HEAD_DIM = 128


epsilon = 1e-05


def prefix(array, axis, join, neutral, backward):
    count = lax.axis_size(axis)
    place = lax.axis_index(axis)
    ahead = count - 1 - place if backward else place
    gathered = lax.all_gather(array.astype(jnp.bfloat16), axis)
    state = jnp.zeros_like(array) + jnp.asarray(neutral, array.dtype)

    def one(turn, state):
        source = count - 1 - turn if backward else turn
        return join(state, lax.dynamic_index_in_dim(gathered, source, 0, False).astype(array.dtype))

    return lax.fori_loop(0, ahead, one, state)


def feature(values):
    wide = values.astype(jnp.float32)
    return jax.nn.elu(wide) + 1.0


def slope(values):
    wide = values.astype(jnp.float32)
    return jnp.where(wide > 0, 1.0, jnp.exp(jnp.minimum(wide, 0.0)))


def accumulate(earlier, later):
    return earlier + later


def shards(layer_input, query_rows, key_rows, value_rows, out_grad):
    tokens = query_rows.shape[1]
    shaped = (tokens, HEADS, HEAD_DIM)
    query = query_rows[0].reshape(shaped)
    keyed = key_rows[0].reshape(shaped)
    values = value_rows[0].reshape(shaped)
    upstream = out_grad[0].reshape(shaped).astype(jnp.float32)
    query_feature = feature(query).astype(jnp.bfloat16)
    key_feature = feature(keyed).astype(jnp.bfloat16)
    block_state = jnp.einsum(
        "thd,the->hde", key_feature, values, preferred_element_type=jnp.float32
    )
    zero_state = jnp.zeros_like(block_state)
    state_in = prefix(block_state, "ctx", accumulate, zero_state, False).astype(jnp.bfloat16)
    rows_index = lax.broadcasted_iota(jnp.int32, (tokens, tokens), 0)
    cols_index = lax.broadcasted_iota(jnp.int32, (tokens, tokens), 1)
    causal = (cols_index <= rows_index)[None]
    scores = jnp.einsum(
        "thd,shd->hts", query_feature, key_feature, preferred_element_type=jnp.float32
    )
    scores = jnp.where(causal, scores, 0.0).astype(jnp.bfloat16)
    output = jnp.einsum("hts,she->the", scores, values, preferred_element_type=jnp.float32)
    output = output + jnp.einsum(
        "thd,hde->the", query_feature, state_in, preferred_element_type=jnp.float32
    )
    inverse_rms = lax.rsqrt(jnp.mean(output * output, axis=-1, keepdims=True) + epsilon)
    normed = output * inverse_rms
    projection = jnp.mean(upstream * normed, axis=-1, keepdims=True)
    grad_output = (inverse_rms * (upstream - normed * projection)).astype(jnp.bfloat16)
    block_grad = jnp.einsum(
        "thd,the->hde", query_feature, grad_output, preferred_element_type=jnp.float32
    )
    grad_in = prefix(block_grad, "ctx", accumulate, zero_state, True).astype(jnp.bfloat16)
    grad_scores = jnp.einsum(
        "the,she->hts", grad_output, values, preferred_element_type=jnp.float32
    )
    grad_scores = jnp.where(causal, grad_scores, 0.0).astype(jnp.bfloat16)
    query_total = jnp.einsum(
        "hts,shd->thd", grad_scores, key_feature, preferred_element_type=jnp.float32
    )
    query_total = query_total + jnp.einsum(
        "the,hde->thd", grad_output, state_in, preferred_element_type=jnp.float32
    )
    key_total = jnp.einsum(
        "hts,thd->shd", grad_scores, query_feature, preferred_element_type=jnp.float32
    )
    key_total = key_total + jnp.einsum(
        "she,hde->shd", values, grad_in, preferred_element_type=jnp.float32
    )
    value_total = jnp.einsum(
        "hts,the->she", scores, grad_output, preferred_element_type=jnp.float32
    )
    value_total = value_total + jnp.einsum(
        "shd,hde->she", key_feature, grad_in, preferred_element_type=jnp.float32
    )
    key_flat = (key_total * slope(keyed)).astype(jnp.bfloat16).reshape(tokens, -1)
    query_grad = (query_total * slope(query)).astype(jnp.bfloat16).reshape(1, tokens, -1)
    value_grad = value_total.astype(jnp.bfloat16).reshape(1, tokens, -1)
    key_grad = key_flat.reshape(1, tokens, -1)
    input_flat = layer_input[0]
    scale = (lax.axis_size("dp") * lax.axis_size("ctx") * tokens) ** (-0.5)
    contract = (((0,), (0,)), ((), ()))
    by_context = lax.psum_scatter(
        lax.dot_general(key_flat, input_flat, contract, preferred_element_type=jnp.float32).astype(
            jnp.bfloat16
        ),
        "ctx",
        scatter_dimension=0,
        tiled=True,
    )
    summed = lax.psum_scatter(by_context, "dp", scatter_dimension=1, tiled=True).astype(jnp.float32)
    weight_grad = summed * scale
    return (query_grad, key_grad, value_grad, weight_grad)


def solution(mesh):
    placed = (
        P("dp", "ctx", None),
        P("dp", "ctx", None),
        P("dp", "ctx", None),
        P("dp", "ctx", None),
        P("dp", "ctx", None),
    )
    return jax.shard_map(
        shards,
        mesh=mesh,
        in_specs=placed,
        out_specs=(
            P("dp", "ctx", None),
            P("dp", "ctx", None),
            P("dp", "ctx", None),
            P("ctx", "dp"),
        ),
        check_vma=False,
    )
```

profile of v0, /device:TPU:0, one launch (start us, length us, event | category | flops | bytes accessed | tf_op | source)
XLA Modules:
  0.0 508.8 jit_solution(944658450925000637)
XLA Ops:
  7.2 2.7 copy.29
  9.9 1.5 copy.28
  11.5 1.5 copy-done.7
  13.1 2.7 fusion.2
  15.8 1.2 convolution_convert_fusion.2
  17.1 2.6 copy.36
  19.7 0.4 select_convert_fusion.1
  20.2 0.9 copy-done.14
  21.1 1.9 fusion.11
  22.9 97.8 %all-gather.5.cloned.1.call-done = bf16[384,128,128]{2,1,0:T(8,128)(2,1)} async-done(((bf16[24,128,128]{2,1,0:T(8,128)(2,1)}), bf16[384,128,128]{2,1,0:T(8,128)(2,1)}) %all-gather.5.cloned.1.call-update) | async-done | bytes 12582928 | tf_op jit(solution)/shard_map/all_gather | solution.py:17
  120.9 2.7 multiply_reduce_fusion.1
  124.0 0.4 multiply_convert_fusion
  124.4 0.9 copy-done.11
  125.3 1.6 convolution_convert_fusion.1
  126.9 1.8 select_convert_fusion
  128.8 0.9 copy-done.15
  129.6 1.5 fusion.21
  131.1 117.6 %all-gather.7.cloned.1.call-done = bf16[384,128,128]{2,1,0:T(8,128)(2,1)} async-done(((bf16[24,128,128]{2,1,0:T(8,128)(2,1)}), bf16[384,128,128]{2,1,0:T(8,128)(2,1)}) %all-gather.7.cloned.1.call-update) | async-done | bytes 12582928 | tf_op jit(solution)/shard_map/all_gather | solution.py:17
  248.9 23.0 %while.23 = (s32[]{:T(128)}, f32[24,128,128]{2,1,0:T(8,128)S(1)}, s32[]{:T(128)}, bf16[16,24,128,128]{3,2,1,0:T(8,128)(2,1)}, s32[]{:T(128)}, /*index=5*/s32[]{:T(128)}, s32[]{:T(128)}, s32[]{:T(128)}) while((s32[]{:T(128)}, f32[24,128,128]{2,1,0:T(8,128)S(1)}, s32[]{:T(128)}, bf16[16,24,128,128]{3,2,1,0:T(8,128)(2,1)}, s32[]{:T(128)}, ...), condition=%wide.region_5.6_spmd, body=%wide.region_4.5_spmd.sunk | while | flops 786438 | bytes 3932303 | solution.py:24
  248.9 1.5 convert_add_fusion.5
  250.4 1.5 convert_add_fusion.5
  252.0 1.5 convert_add_fusion.5
  253.5 1.5 convert_add_fusion.5
  255.0 1.5 convert_add_fusion.5
  256.6 1.5 convert_add_fusion.5
  258.1 1.5 convert_add_fusion.5
  259.6 1.5 convert_add_fusion.5
  261.2 1.5 convert_add_fusion.5
  262.7 1.5 convert_add_fusion.5
  264.2 1.5 convert_add_fusion.5
  265.7 1.5 convert_add_fusion.5
  267.3 1.5 convert_add_fusion.5
  268.8 1.5 convert_add_fusion.5
  270.3 1.5 convert_add_fusion.5
  271.9 2.8 fusion.4
  274.7 0.9 copy-done.13
  275.6 9.1 %convolution_convert_fusion = bf16[3072,3072]{1,0:T(8,128)(2,1)} fusion(bf16[128,3072]{0,1:T(8,128)(2,1)S(1)} %bitcast.62, bf16[1,128,3072]{2,1,0:T(8,128)(2,1)S(1)} %copy-done), kind=kOutput, calls=%fused_computation.2 | convolution fusion | flops 2425356288 | bytes 20447232 | tf_op jit(solution)/shard_map/dot_general | solution.py:104
  284.9 192.1 %reduce-scatter.3.cloned.1.call-done = bf16[192,3072]{1,0:T(8,128)(2,1)} async-done(((bf16[3072,3072]{1,0:T(8,128)(2,1)}), bf16[192,3072]{1,0:T(8,128)(2,1)}) %reduce-scatter.3.cloned.1.call-update) | async-done | bytes 1179664 | tf_op jit(solution)/shard_map/reduce_scatter | solution.py:103
  477.1 1.9 fusion.20
  479.0 0.4 copy-done.8
  479.4 1.5 fusion.9
  480.9 2.3 copy.44
  483.2 2.8 fusion.22
  485.9 2.3 copy.45
  488.2 2.7 add_convert_fusion
  490.9 2.4 copy.46
  493.3 6.7 %reduce-scatter.5.cloned.1.call-done = bf16[192,1536]{1,0:T(8,128)(2,1)} async-done(((bf16[192,3072]{1,0:T(8,128)(2,1)}), bf16[192,1536]{1,0:T(8,128)(2,1)}) %reduce-scatter.5.cloned.1.call-update) | async-done | bytes 589840 | tf_op jit(solution)/shard_map/reduce_scatter | solution.py:111
  500.0 2.2 convert_multiply_fusion
  (46 shorter events, 1.3 us)
Async XLA Ops:
  7.2 268.4 %copy-start = (bf16[1,128,3072]{2,1,0:T(8,128)(2,1)S(1)}, bf16[1,128,3072]{2,1,0:T(8,128)(2,1)}, u32[]{:S(2)}) copy-start(bf16[1,128,3072]{2,1,0:T(8,128)(2,1)} %param.9) | copy-start | bytes 2359300
  7.2 2.7 copy-start.17
  7.2 113.5 %all-gather.5.cloned.1.call-start = ((), (), s32[]{:S(2)}) async-start(), calls=%async_computation.4 | async-start | bytes 13369344 | tf_op jit(solution)/shard_map/all_gather | solution.py:17
  9.9 1.5 copy-start.16
  11.4 1.7 copy-start.7
  11.5 8.6 %copy-start.9 = (bf16[16,8,24,128]{3,2,1,0:T(8,128)(2,1)}, bf16[16,8,24,128]{3,2,1,0:T(8,128)(2,1)S(1)}, u32[]{:S(2)}) copy-start(bf16[16,8,24,128]{3,2,1,0:T(8,128)(2,1)S(1)} %copy.56) | copy-start | bytes 2359300
  15.8 3.9 copy-start.4
  17.1 231.7 %all-gather.7.cloned.1.call-start = ((), (), s32[]{:S(2)}) async-start(), calls=%async_computation.5 | async-start | bytes 13369344 | tf_op jit(solution)/shard_map/all_gather | solution.py:17
  20.2 0.9 copy-start.14
  120.9 2.7 copy-start.2
  120.9 2.7 copy-start.6
  124.0 1.3 copy-start.5
  124.4 0.9 copy-start.11
  125.3 1.6 copy-start.10
  126.9 350.2 %reduce-scatter.3.cloned.1.call-start = ((), (), s32[]{:S(2)}) async-start(), calls=%async_computation.2 | async-start | bytes 20054016 | tf_op jit(solution)/shard_map/reduce_scatter | solution.py:103
  128.8 0.9 copy-start.15
  274.7 0.9 copy-start.13
  284.7 215.3 %reduce-scatter.5.cloned.1.call-start = ((), (), s32[]{:S(2)}) async-start(), calls=%async_computation.3 | async-start | bytes 1769472 | tf_op jit(solution)/shard_map/reduce_scatter | solution.py:111
  477.0 2.0 copy-start.12
  477.0 2.0 copy-start.3
  477.0 2.3 copy-start.8
  490.9 11.3 %copy-start.1 = (bf16[1,128,3072]{2,1,0:T(8,128)(2,1)S(1)}, bf16[1,128,3072]{2,1,0:T(8,128)(2,1)}, u32[]{:S(2)}) copy-start(bf16[1,128,3072]{2,1,0:T(8,128)(2,1)} %param.9) | copy-start | bytes 2359300
Sparse Core Ops, SparseCore 0:
  17.2 103.4 all-gather.4
  127.0 121.7 all-gather.6
  284.8 192.1 reduce-scatter.2
  479.1 20.8 reduce-scatter.4
where the time goes:
time: 510 us; the launch traced here: 509 us
  waiting for transfers between devices  414 us (81%)
  matrix products  31.9 us (6%)
  other arithmetic  28.2 us (6%)
  local copies, waits for them, and re-layouts  19.5 us (4%)
  between operations  14 us (3%)
    all_gather x2, waiting for transfers between devices, prefix(): gathered = lax.all_gather(array.astype(jnp.bfloat16), axis)  215 us
    reduce_scatter x1, waiting for transfers between devices, shards(): lax.psum_scatter(lax.dot_general(key_flat, input_flat, contract, preferre...  192 us
    add x15, other arithmetic, accumulate(): return earlier + later  22.5 us
    unnamed x40, local copies, waits for them, and re-layouts  12.5 us
  transfers between devices with their start and end apart: 4, of which 4 were waited for; matrix products, arithmetic and copies ran while one was open for 5% of the time, Pallas kernels for 0%

commit v1 on v0

v1 whole, which is shorter than its diff:
```python
import functools

import jax
import jax.numpy as jnp
from jax import lax
from jax.experimental import pallas as pl
from jax.experimental.pallas import tpu as pltpu
from jax.sharding import PartitionSpec as P

HEAD_DIM = 128
EPSILON = 1e-05
F32 = jnp.float32
BF16 = jnp.bfloat16

NN = (((1,), (0,)), ((), ()))
NT = (((1,), (1,)), ((), ()))
TN = (((0,), (0,)), ((), ()))


def dot(a, b, dims):
    return lax.dot_general(a, b, dims, preferred_element_type=F32)


def slope(values):
    wide = values.astype(F32)
    return jnp.where(wide > 0, 1.0, jnp.exp(jnp.minimum(wide, 0.0)))


def feature(values):
    wide = values.astype(F32)
    return jnp.where(wide > 0, wide + 1.0, jnp.exp(jnp.minimum(wide, 0.0))).astype(BF16)


def causal(rows):
    t = lax.broadcasted_iota(jnp.int32, (rows, rows), 0)
    s = lax.broadcasted_iota(jnp.int32, (rows, rows), 1)
    return s <= t


def heads_of(ref):
    for head in range(ref.shape[1] // HEAD_DIM):
        yield slice(head * HEAD_DIM, (head + 1) * HEAD_DIM)


def block_state_kernel(k_ref, v_ref, state_ref):
    for at in heads_of(k_ref):
        state_ref[at, :] = dot(feature(k_ref[:, at]), v_ref[:, at], TN).astype(BF16)


def local_output_kernel(q_ref, k_ref, v_ref, scores_ref, local_ref):
    keep = causal(q_ref.shape[0])
    for at in heads_of(q_ref):
        scores = dot(feature(q_ref[:, at]), feature(k_ref[:, at]), NT)
        scores = jnp.where(keep, scores, 0.0).astype(BF16)
        scores_ref[:, at] = scores
        local_ref[:, at] = dot(scores, v_ref[:, at], NN)


def grad_output_kernel(q_ref, local_ref, upstream_ref, state_ref, grad_ref, block_ref):
    for at in heads_of(q_ref):
        query = feature(q_ref[:, at])
        output = local_ref[:, at] + dot(query, state_ref[at, :], NN)
        inverse_rms = lax.rsqrt(jnp.mean(output * output, axis=-1, keepdims=True) + EPSILON)
        normed = output * inverse_rms
        upstream = upstream_ref[:, at].astype(F32)
        projection = jnp.mean(upstream * normed, axis=-1, keepdims=True)
        grad = (inverse_rms * (upstream - normed * projection)).astype(BF16)
        grad_ref[:, at] = grad
        block_ref[at, :] = dot(query, grad, TN).astype(BF16)


def local_grads_kernel(
    q_ref, k_ref, v_ref, scores_ref, grad_ref, state_ref, query_out, key_out, value_out
):
    keep = causal(q_ref.shape[0])
    for at in heads_of(q_ref):
        grad = grad_ref[:, at]
        grad_scores = jnp.where(keep, dot(grad, v_ref[:, at], NT), 0.0).astype(BF16)
        query = dot(grad_scores, feature(k_ref[:, at]), NN) + dot(grad, state_ref[at, :], NT)
        query_out[:, at] = (query * slope(q_ref[:, at])).astype(BF16)
        key_out[:, at] = dot(grad_scores, feature(q_ref[:, at]), TN)
        value_out[:, at] = dot(scores_ref[:, at], grad, TN)


def key_grad_kernel(k_ref, v_ref, local_ref, state_ref, key_out, turned_out):
    for at in heads_of(k_ref):
        key = local_ref[:, at] + dot(v_ref[:, at], state_ref[at, :], NT)
        key = key * slope(k_ref[:, at])
        key_out[:, at] = key.astype(BF16)
        turned_out[at, :] = key.T.astype(BF16)


def value_grad_kernel(k_ref, local_ref, state_ref, value_out):
    for at in heads_of(k_ref):
        value_out[:, at] = (local_ref[:, at] + dot(feature(k_ref[:, at]), state_ref[at, :], NN)).astype(
            BF16
        )


def by_heads(kernel, operands, outs, matmuls):
    tokens, features = operands[0][1].shape
    group = 4 * HEAD_DIM
    while features % group:
        group -= HEAD_DIM
    specs = {
        "row": pl.BlockSpec((tokens, group), lambda i: (0, i)),
        "state": pl.BlockSpec((group, HEAD_DIM), lambda i: (i, 0)),
    }
    shapes = {"row": (tokens, features), "state": (features, HEAD_DIM)}
    moved = sum(a.size * a.dtype.itemsize for _, a in operands)
    moved += sum(shapes[kind][0] * shapes[kind][1] * jnp.dtype(dtype).itemsize for kind, dtype in outs)
    return pl.pallas_call(
        kernel,
        grid=(features // group,),
        in_specs=[specs[kind] for kind, _ in operands],
        out_specs=[specs[kind] for kind, _ in outs],
        out_shape=[jax.ShapeDtypeStruct(shapes[kind], dtype) for kind, dtype in outs],
        compiler_params=pltpu.CompilerParams(vmem_limit_bytes=32 * 1024 * 1024),
        cost_estimate=pl.CostEstimate(
            flops=2 * matmuls * tokens * features * HEAD_DIM, bytes_accessed=moved, transcendentals=0
        ),
    )(*[a for _, a in operands])


def swap(array, axis, bit):
    size = lax.axis_size(axis)
    return lax.ppermute(array, axis, [(i, i ^ bit) for i in range(size)])


def shift(array, axis, step):
    size = lax.axis_size(axis)
    return lax.ppermute(array, axis, [(i, i + step) for i in range(size) if 0 <= i + step < size])


def half_of(array, which):
    rows = array.shape[0] // 2
    return lax.dynamic_slice_in_dim(array, which * rows, rows, 0)


def joined(own, other, which):
    return jnp.where(which == 0, jnp.concatenate([own, other]), jnp.concatenate([other, own]))


def add(a, b):
    return (a.astype(F32) + b.astype(F32)).astype(BF16)


def scan_blocks(state, axis, backward):
    place = lax.axis_index(axis)
    core, side = place % 2, (place // 2) % 2
    second = 0 if backward else 1
    sign = -1 if backward else 1
    zero = jnp.zeros((), BF16)

    other = swap(state, axis, 1)
    pair = add(half_of(state, core), half_of(other, core))
    pair_other = swap(pair, axis, 2)
    total = add(half_of(pair, side), half_of(pair_other, side))
    before = None
    running = total
    step = 4
    while step < lax.axis_size(axis):
        arrived = shift(running, axis, sign * step)
        running = add(running, arrived)
        before = arrived if before is None else add(before, arrived)
        step *= 2
    half = joined(before, swap(before, axis, 2), side)
    half = add(half, jnp.where(side == second, pair_other, zero))
    whole = joined(half, swap(half, axis, 1), core)
    return add(whole, jnp.where(core == second, other, zero))


def weight_kernel(which_ref, turned_ref, input_ref, out_ref):
    sources, rows, tokens = turned_ref.shape
    total = jnp.zeros(out_ref.shape, F32)
    for at in range(0, sources, 2):
        pair = jnp.concatenate([turned_ref[at], turned_ref[at + 1]], axis=1)
        total += dot(pair, input_ref[at * tokens : (at + 2) * tokens, :], NN)
    out_ref[...] = total.astype(out_ref.dtype)


def weight_part(turned, inputs, which, parts, dtype):
    sources, rows, tokens = turned.shape
    columns = inputs.shape[1] // parts
    tile = columns
    while tile > 512:
        tile //= 2
    steps = columns // tile
    return pl.pallas_call(
        weight_kernel,
        grid_spec=pltpu.PrefetchScalarGridSpec(
            num_scalar_prefetch=1,
            grid=(steps,),
            in_specs=[
                pl.BlockSpec((sources, rows, tokens), lambda i, which: (0, 0, 0)),
                pl.BlockSpec((sources * tokens, tile), lambda i, which: (0, which[0] * steps + i)),
            ],
            out_specs=pl.BlockSpec((rows, tile), lambda i, which: (0, i)),
        ),
        out_shape=jax.ShapeDtypeStruct((rows, columns), dtype),
        compiler_params=pltpu.CompilerParams(vmem_limit_bytes=40 * 1024 * 1024),
        cost_estimate=pl.CostEstimate(
            flops=2 * sources * tokens * rows * columns,
            bytes_accessed=sources * tokens * columns * 2 + rows * columns * 4,
            transcendentals=0,
        ),
    )(jnp.reshape(which, (1,)).astype(jnp.int32), turned, inputs)


def shards(layer_input, query_rows, key_rows, value_rows, out_grad):
    tokens = query_rows.shape[1]
    query, key, value, upstream = query_rows[0], key_rows[0], value_rows[0], out_grad[0]
    gathered = lax.all_gather(layer_input[0], "ctx", axis=0, tiled=True)

    (block_state,) = by_heads(
        block_state_kernel, [("row", key), ("row", value)], [("state", BF16)], 1
    )
    scores, local_output = by_heads(
        local_output_kernel,
        [("row", query), ("row", key), ("row", value)],
        [("row", BF16), ("row", F32)],
        2,
    )
    state_in = scan_blocks(block_state, "ctx", False)
    grad_output, block_grad = by_heads(
        grad_output_kernel,
        [("row", query), ("row", local_output), ("row", upstream), ("state", state_in)],
        [("row", BF16), ("state", BF16)],
        2,
    )
    query_grad, key_local, value_local = by_heads(
        local_grads_kernel,
        [
            ("row", query),
            ("row", key),
            ("row", value),
            ("row", scores),
            ("row", grad_output),
            ("state", state_in),
        ],
        [("row", BF16), ("row", F32), ("row", F32)],
        5,
    )
    grad_in = scan_blocks(block_grad, "ctx", True)
    key_grad, turned = by_heads(
        key_grad_kernel,
        [("row", key), ("row", value), ("row", key_local), ("state", grad_in)],
        [("row", BF16), ("state", BF16)],
        1,
    )
    (value_grad,) = by_heads(
        value_grad_kernel,
        [("row", key), ("row", value_local), ("state", grad_in)],
        [("row", BF16)],
        1,
    )

    places, parts = lax.axis_size("ctx"), lax.axis_size("dp")
    turned = turned.reshape(places, -1, tokens)
    turned = lax.all_to_all(turned, "ctx", 0, 0)
    scale = (parts * places * tokens) ** (-0.5)
    if parts == 2:
        mine = lax.axis_index("dp")
        sent = weight_part(turned, gathered, 1 - mine, 2, BF16)
        arrived = swap(sent, "dp", 1)
        kept = weight_part(turned, gathered, mine, 2, F32)
        weight_grad = (kept + arrived.astype(F32)) * scale
    else:
        whole = weight_part(turned, gathered, jnp.zeros((), jnp.int32), 1, BF16)
        weight_grad = lax.psum_scatter(whole, "dp", scatter_dimension=1, tiled=True).astype(F32) * scale
    return (query_grad[None], key_grad[None], value_grad[None], weight_grad)


def solution(mesh):
    rows = P("dp", "ctx", None)
    return jax.shard_map(
        shards,
        mesh=mesh,
        in_specs=(rows,) * 5,
        out_specs=(rows, rows, rows, P("ctx", "dp")),
        check_vma=False,
    )
```

time: 510 us -> 208 us (0.41)
  waiting for transfers between devices: 414 us -> 112 us
  matrix products: 31.9 us -> 0 us
  starting transfers between devices: 0.34 us -> 31.6 us
  Pallas kernels: 0 us -> 29.1 us
  other arithmetic: 28.2 us -> 7.68 us
  local copies, waits for them, and re-layouts: 19.5 us -> 12.6 us
    all_gather x2 -> x1, waiting for transfers between devices: 215 us -> 0.01 us  [shards(): gathered = lax.all_gather(layer_input[0], 'ctx', axis=0, tiled=True)]
    reduce_scatter x2 -> x0, waiting for transfers between devices: 199 us -> none  [the longest x1 192 us: shards(): lax.psum_scatter(lax.dot_general(key_flat, input_flat, contract, preferre...]
    ppermute x0 -> x13, waiting for transfers between devices: none -> 92.7 us  [the longest x9 53.3 us: swap(): return lax.ppermute(array, axis, [(i, i ^ bit) for i in range(size)])]
    dot_general x13 -> x0, matrix products: 31.9 us -> none  [the longest x1 9.06 us: shards(): lax.dot_general(key_flat, input_flat, contract, preferred_element_type=jn...]
    pallas_call x0 -> x8, Pallas kernels: none -> 29.1 us  [the longest x6 22.4 us: by_heads(): pl.pallas_call(kernel, grid=(features // group,), in_specs=[specs[kind] f...]
    ppermute x0 -> x13, starting transfers between devices: none -> 27.9 us  [the longest x4 16.6 us: shift(): lax.ppermute(array, axis, [(i, i + step) for i in range(size) if 0 <= i +...]
    add x15 -> x0, other arithmetic: 22.5 us -> none  [accumulate(): return earlier + later]
    all_to_all x0 -> x1, waiting for transfers between devices: none -> 18.7 us  [shards(): turned = lax.all_to_all(turned, 'ctx', 0, 0)]
  transfers between devices with their start and end apart: 4 -> 15, of which waited for: 4 -> 12; matrix products, arithmetic and copies ran while one was open for 5% -> 3% of each run, Pallas kernels for 0% -> 12%
where the time goes in v1:
time: 208 us; the launch traced here: 207 us
  waiting for transfers between devices  112 us (54%)
  starting transfers between devices  31.6 us (15%)
  Pallas kernels  29.1 us (14%)
  between operations  14.2 us (7%)
  local copies, waits for them, and re-layouts  12.6 us (6%)
  other arithmetic  7.68 us (4%)
    ppermute x9, waiting for transfers between devices, swap(): return lax.ppermute(array, axis, [(i, i ^ bit) for i in range(size)])  53.3 us
    ppermute x4, waiting for transfers between devices, shift(): lax.ppermute(array, axis, [(i, i + step) for i in range(size) if 0 <= i +...  39.4 us
    pallas_call x6, Pallas kernels, by_heads(): pl.pallas_call(kernel, grid=(features // group,), in_specs=[specs[kind] f...  22.4 us
    all_to_all x1, waiting for transfers between devices, shards(): turned = lax.all_to_all(turned, 'ctx', 0, 0)  18.7 us
    ppermute x4, starting transfers between devices, shift(): lax.ppermute(array, axis, [(i, i + step) for i in range(size) if 0 <= i +...  16.6 us
    unnamed x22, local copies, waits for them, and re-layouts  12.6 us
    ppermute x9, starting transfers between devices, swap(): return lax.ppermute(array, axis, [(i, i ^ bit) for i in range(size)])  11.3 us
    pallas_call x2, Pallas kernels, weight_part(): pl.pallas_call(weight_kernel, grid_spec=pltpu.PrefetchScalarGridSpec(num_...  6.73 us
  transfers between devices with their start and end apart: 15, of which 12 were waited for; matrix products, arithmetic and copies ran while one was open for 3% of the time, Pallas kernels for 12%

profile of v1, /device:TPU:0, one launch (start us, length us, event | category | flops | bytes accessed | tf_op | source)
XLA Modules:
  0.0 207.2 jit_solution(12565759827709960182)
XLA Ops:
  7.2 0.7 all-gather.3.cloned.1.call-update
  7.9 1.1 copy-done.2
  9.0 1.1 copy-done.4
  10.2 1.6 shard_map.85
  11.8 0.5 collective-permute-start
  12.3 1.9 collective-permute-done
  14.2 0.8 add_convert_fusion.5
  15.1 2.9 %collective-permute-start.1 = (bf16[1536,128]{1,0:T(8,128)(2,1)}, bf16[1536,128]{1,0:T(8,128)(2,1)S(1)}, u32[]{:S(2)}, u32[]{:S(2)}) collective-permute-start(bf16[1536,128]{1,0:T(8,128)(2,1)} %add_convert_fusion.5), channel_id=1, source_target_pairs={{0,2},{1,3},{2,0},{3,1},{4,6},{5,7},{6,4},{7,5},{8,10},{9,11},{10,... | collective-permute-start | bytes 1179656 | tf_op jit(solution)/shard_map/ppermute | solution.py:127
  18.0 14.8 %collective-permute-done.1 = bf16[1536,128]{1,0:T(8,128)(2,1)S(1)} collective-permute-done((bf16[1536,128]{1,0:T(8,128)(2,1)}, bf16[1536,128]{1,0:T(8,128)(2,1)S(1)}, u32[]{:S(2)}, u32[]{:S(2)}) %collective-permute-start.1) | collective-permute-done | bytes 393248 | tf_op jit(solution)/shard_map/ppermute | solution.py:127
  32.7 1.1 add_convert_fusion.7
  33.9 3.4 %collective-permute-start.2 = (bf16[768,128]{1,0:T(8,128)(2,1)S(1)}, bf16[768,128]{1,0:T(8,128)(2,1)S(1)}, u32[]{:S(2)}, u32[]{:S(2)}) collective-permute-start(bf16[768,128]{1,0:T(8,128)(2,1)S(1)} %add_convert_fusion.7), channel_id=1, source_target_pairs={{0,4},{1,5},{2,6},{3,7},{4,8},{5,9},{6,10},{7,11},{8,12},{9,13},{1... | collective-permute-start | bytes 589832 | tf_op jit(solution)/shard_map/ppermute | solution.py:132
  37.2 8.3 %collective-permute-done.2 = bf16[768,128]{1,0:T(8,128)(2,1)S(1)} collective-permute-done((bf16[768,128]{1,0:T(8,128)(2,1)S(1)}, bf16[768,128]{1,0:T(8,128)(2,1)S(1)}, u32[]{:S(2)}, u32[]{:S(2)}) %collective-permute-start.2) | collective-permute-done | bytes 196640 | tf_op jit(solution)/shard_map/ppermute | solution.py:132
  45.6 10.7 %collective-permute-start.3 = (bf16[768,128]{1,0:T(8,128)(2,1)S(1)}, bf16[768,128]{1,0:T(8,128)(2,1)S(1)}, u32[]{:S(2)}, u32[]{:S(2)}) collective-permute-start(bf16[768,128]{1,0:T(8,128)(2,1)S(1)} %fusion), channel_id=1, source_target_pairs={{0,8},{1,9},{2,10},{3,11},{4,12},{5,13},{6,14},{7,15},{16,24},{17,... | collective-permute-start | bytes 589832 | tf_op jit(solution)/shard_map/ppermute | solution.py:132
  56.2 3.2 %collective-permute-done.3 = bf16[768,128]{1,0:T(8,128)(2,1)S(1)} collective-permute-done((bf16[768,128]{1,0:T(8,128)(2,1)S(1)}, bf16[768,128]{1,0:T(8,128)(2,1)S(1)}, u32[]{:S(2)}, u32[]{:S(2)}) %collective-permute-start.3) | collective-permute-done | bytes 196640 | tf_op jit(solution)/shard_map/ppermute | solution.py:132
  59.4 0.7 fusion.1
  60.2 2.0 collective-permute-start.4
  62.2 8.2 %collective-permute-done.4 = bf16[768,128]{1,0:T(8,128)(2,1)} collective-permute-done((bf16[768,128]{1,0:T(8,128)(2,1)}, bf16[768,128]{1,0:T(8,128)(2,1)}, u32[]{:S(2)}, u32[]{:S(2)}) %collective-permute-start.4) | collective-permute-done | bytes 196640 | tf_op jit(solution)/shard_map/ppermute | solution.py:127
  70.3 1.4 add_convert_fusion.4
  71.7 0.1 collective-permute-start.5
  71.9 4.9 %shard_map.84 = (bf16[128,3072]{1,0:T(8,128)(2,1)S(1)}, f32[128,3072]{1,0:T(8,128)S(1)}) custom-call(bf16[128,3072]{1,0:T(8,128)(2,1)S(1)} %bitcast.22, bf16[128,3072]{1,0:T(8,128)(2,1)S(1)} %bitcast.14, bf16[128,3072]{1,0:T(8,128)(2,1)S(1)} %bitcast.19), custom_call_target="tpu_custom_call" | custom-call | flops 201326592 | bytes 4718592 | tf_op jit(solution)/shard_map/pallas_call | solution.py:112
  76.8 1.5 add_convert_fusion.1.state_ref
  78.4 3.5 %shard_map.86 = (bf16[128,3072]{1,0:T(8,128)(2,1)S(1)}, bf16[3072,128]{1,0:T(8,128)(2,1)S(1)}) custom-call(bf16[128,3072]{1,0:T(8,128)(2,1)S(1)} %bitcast.23, f32[128,3072]{1,0:T(8,128)S(1)} %get-tuple-element.14.local_ref, bf16[128,3072]{1,0:T(8,128)(2,1)S(1)} %bitcast.25, bf16[3072,128]{1,0:T(8,128)(2,1)S(1)} %add_convert_fusion.1.state_ref), custom_call_target="tpu_custom_call" | custom-call | flops 201326592 | bytes 5505024 | tf_op jit(solution)/shard_map/pallas_call | solution.py:112
  81.9 0.5 collective-permute-start.6
  82.4 1.9 collective-permute-done.6
  84.3 0.1 add_convert_fusion.3
  84.4 2.2 %collective-permute-start.7 = (bf16[1536,128]{1,0:T(8,128)(2,1)S(1)}, bf16[1536,128]{1,0:T(8,128)(2,1)S(1)}, u32[]{:S(2)}, u32[]{:S(2)}) collective-permute-start(bf16[1536,128]{1,0:T(8,128)(2,1)S(1)} %add_convert_fusion.3), channel_id=1, source_target_pairs={{0,2},{1,3},{2,0},{3,1},{4,6},{5,7},{6,4},{7,5},{8,10},{9,11},{10,... | collective-permute-start | bytes 1179656 | tf_op jit(solution)/shard_map/ppermute | solution.py:127
  86.7 18.2 %collective-permute-done.7 = bf16[1536,128]{1,0:T(8,128)(2,1)S(1)} collective-permute-done((bf16[1536,128]{1,0:T(8,128)(2,1)S(1)}, bf16[1536,128]{1,0:T(8,128)(2,1)S(1)}, u32[]{:S(2)}, u32[]{:S(2)}) %collective-permute-start.7) | collective-permute-done | bytes 393248 | tf_op jit(solution)/shard_map/ppermute | solution.py:127
  104.9 1.3 collective-permute-start.8
  106.2 12.6 %collective-permute-done.8 = bf16[768,128]{1,0:T(8,128)(2,1)S(1)} collective-permute-done((bf16[768,128]{1,0:T(8,128)(2,1)S(1)}, bf16[768,128]{1,0:T(8,128)(2,1)S(1)}, u32[]{:S(2)}, u32[]{:S(2)}) %collective-permute-start.8) | collective-permute-done | bytes 196640 | tf_op jit(solution)/shard_map/ppermute | solution.py:132
  118.9 1.3 collective-permute-start.9
  120.2 15.3 %collective-permute-done.9 = bf16[768,128]{1,0:T(8,128)(2,1)S(1)} collective-permute-done((bf16[768,128]{1,0:T(8,128)(2,1)S(1)}, bf16[768,128]{1,0:T(8,128)(2,1)S(1)}, u32[]{:S(2)}, u32[]{:S(2)}) %collective-permute-start.9) | collective-permute-done | bytes 196640 | tf_op jit(solution)/shard_map/ppermute | solution.py:132
  135.6 1.1 collective-permute-start.10
  136.7 5.4 %collective-permute-done.10 = bf16[768,128]{1,0:T(8,128)(2,1)S(1)} collective-permute-done((bf16[768,128]{1,0:T(8,128)(2,1)S(1)}, bf16[768,128]{1,0:T(8,128)(2,1)S(1)}, u32[]{:S(2)}, u32[]{:S(2)}) %collective-permute-start.10) | collective-permute-done | bytes 196640 | tf_op jit(solution)/shard_map/ppermute | solution.py:127
  142.1 0.2 add_convert_fusion.2
  142.4 6.0 %shard_map.87 = (bf16[128,3072]{1,0:T(8,128)(2,1)}, f32[128,3072]{1,0:T(8,128)S(1)}, f32[128,3072]{1,0:T(8,128)S(1)}) custom-call(bf16[128,3072]{1,0:T(8,128)(2,1)S(1)} %bitcast.24, bf16[128,3072]{1,0:T(8,128)(2,1)S(1)} %bitcast.15, bf16[128,3072]{1,0:T(8,128)(2,1)S(1)} %bitcast.20, bf16[128,3072]{1,0:T(8,128)(2,1)S(1)} %get-tuple-element.13.scores_ref, ...), custom_call_target="tpu_custom_call" | custom-call | flops 503316480 | bytes 8650752 | tf_op jit(solution)/shard_map/pallas_call | solution.py:112
  148.4 1.1 copy-done.7
  149.5 0.4 add_convert_fusion.state_ref
  149.9 3.4 %shard_map.88 = (bf16[128,3072]{1,0:T(8,128)(2,1)}, bf16[3072,128]{1,0:T(8,128)(2,1)}) custom-call(bf16[128,3072]{1,0:T(8,128)(2,1)S(1)} %bitcast.16, bf16[128,3072]{1,0:T(8,128)(2,1)S(1)} %bitcast.21, f32[128,3072]{1,0:T(8,128)S(1)} %get-tuple-element.17.local_ref, bf16[3072,128]{1,0:T(8,128)(2,1)S(1)} %add_convert_fusion.state_ref), custom_call_target="tpu_custom_call" | custom-call | flops 100663296 | bytes 5505024 | tf_op jit(solution)/shard_map/pallas_call | solution.py:112
  153.3 3.6 %all-to-all-start = ((bf16[16,192,128]{2,1,0:T(8,128)(2,1)}), bf16[16,192,128]{2,1,0:T(8,128)(2,1)S(1)}, u32[]{:S(2)}, u32[]{:S(2)}) async-start(bf16[16,192,128]{2,1,0:T(8,128)(2,1)} %bitcast.8), calls=%async_computation | async-start | bytes 1572864 | tf_op jit(solution)/shard_map/all_to_all | solution.py:260
  156.9 18.7 %all-to-all-done.turned_ref = bf16[16,192,128]{2,1,0:T(8,128)(2,1)S(1)} async-done(((bf16[16,192,128]{2,1,0:T(8,128)(2,1)}), bf16[16,192,128]{2,1,0:T(8,128)(2,1)S(1)}, u32[]{:S(2)}, u32[]{:S(2)}) %all-to-all-start) | async-done | bytes 786464 | tf_op jit(solution)/shard_map/all_to_all | solution.py:260
  175.6 4.6 %copy-done = bf16[1,2048,3072]{2,1,0:T(8,128)(2,1)S(1)} copy-done((bf16[1,2048,3072]{2,1,0:T(8,128)(2,1)S(1)}, bf16[1,2048,3072]{2,1,0:T(8,128)(2,1)}, u32[]{:S(2)}) %copy-start) | copy-done | bytes 12582936
  180.2 3.4 %shard_map.91 = bf16[192,1536]{1,0:T(8,128)(2,1)S(1)} custom-call(s32[1]{0:T(128)} %bitcast.10.which_ref, bf16[16,192,128]{2,1,0:T(8,128)(2,1)S(1)} %all-to-all-done.turned_ref, bf16[2048,3072]{1,0:T(8,128)(2,1)S(1)} %bitcast.11), custom_call_target="tpu_custom_call" | custom-call | flops 1207959552 | bytes 7471104 | tf_op jit(solution)/shard_map/pallas_call | solution.py:189
  183.6 1.9 collective-permute-start.12
  185.5 2.9 %shard_map.89 = bf16[128,3072]{1,0:T(8,128)(2,1)} custom-call(bf16[128,3072]{1,0:T(8,128)(2,1)S(1)} %bitcast.17, f32[128,3072]{1,0:T(8,128)S(1)} %copy-done.8, bf16[3072,128]{1,0:T(8,128)(2,1)S(1)} %add_convert_fusion.state_ref), custom_call_target="tpu_custom_call" | custom-call | flops 100663296 | bytes 3932160 | tf_op jit(solution)/shard_map/pallas_call | solution.py:112
  188.4 4.6 %copy-done.1 = bf16[1,2048,3072]{2,1,0:T(8,128)(2,1)S(1)} copy-done((bf16[1,2048,3072]{2,1,0:T(8,128)(2,1)S(1)}, bf16[1,2048,3072]{2,1,0:T(8,128)(2,1)}, u32[]{:S(2)}) %copy-start.1) | copy-done | bytes 12582936
  193.0 3.4 %shard_map.90 = f32[192,1536]{1,0:T(8,128)S(1)} custom-call(s32[1]{0:T(128)} %bitcast.7.which_ref, bf16[16,192,128]{2,1,0:T(8,128)(2,1)S(1)} %all-to-all-done.turned_ref, bf16[2048,3072]{1,0:T(8,128)(2,1)S(1)} %bitcast.12), custom_call_target="tpu_custom_call" | custom-call | flops 1207959552 | bytes 7471104 | tf_op jit(solution)/shard_map/pallas_call | solution.py:189
  196.3 2.9 %collective-permute-done.12 = bf16[192,1536]{1,0:T(8,128)(2,1)S(1)} collective-permute-done((bf16[192,1536]{1,0:T(8,128)(2,1)S(1)}, bf16[192,1536]{1,0:T(8,128)(2,1)S(1)}, u32[]{:S(2)}, u32[]{:S(2)}) %collective-permute-start.12) | collective-permute-done | bytes 589856 | tf_op jit(solution)/shard_map/ppermute | solution.py:127
  199.2 1.2 add_multiply_fusion
  (26 shorter events, 0.4 us)
Async XLA Ops:
  7.2 168.4 %all-gather.3.cloned.1.call-start = ((), (), s32[]{:S(2)}) async-start(), calls=%async_computation.1 | async-start | bytes 13369344 | tf_op jit(solution)/shard_map/all_gather | solution.py:213
  7.9 1.1 copy-start.2
  9.0 1.1 copy-start.4
  11.8 2.4 %collective-permute-start = (bf16[3072,128]{1,0:T(8,128)(2,1)S(1)}, bf16[3072,128]{1,0:T(8,128)(2,1)S(1)}, u32[]{:S(2)}, u32[]{:S(2)}) collective-permute-start(bf16[3072,128]{1,0:T(8,128)(2,1)S(1)} %shard_map.85), channel_id=1, source_target_pairs={{0,1},{1,0},{2,3},{3,2},{4,5},{5,4},{6,7},{7,6},{8,9},{9,8},{10,11... | collective-permute-start | bytes 2359304 | tf_op jit(solution)/shard_map/ppermute | solution.py:127
  15.1 56.7 %copy-start.3 = (bf16[1,128,3072]{2,1,0:T(8,128)(2,1)S(1)}, bf16[1,128,3072]{2,1,0:T(8,128)(2,1)}, u32[]{:S(2)}) copy-start(bf16[1,128,3072]{2,1,0:T(8,128)(2,1)} %param.7) | copy-start | bytes 2359300
  15.1 56.7 %copy-start.5 = (bf16[1,128,3072]{2,1,0:T(8,128)(2,1)S(1)}, bf16[1,128,3072]{2,1,0:T(8,128)(2,1)}, u32[]{:S(2)}) copy-start(bf16[1,128,3072]{2,1,0:T(8,128)(2,1)} %param.8) | copy-start | bytes 2359300
  15.1 56.8 %copy-start.6 = (bf16[1,128,3072]{2,1,0:T(8,128)(2,1)S(1)}, bf16[1,128,3072]{2,1,0:T(8,128)(2,1)}, u32[]{:S(2)}) copy-start(bf16[1,128,3072]{2,1,0:T(8,128)(2,1)} %param.6) | copy-start | bytes 2359300
  15.1 17.6 %collective-permute-start.1 = (bf16[1536,128]{1,0:T(8,128)(2,1)}, bf16[1536,128]{1,0:T(8,128)(2,1)S(1)}, u32[]{:S(2)}, u32[]{:S(2)}) collective-permute-start(bf16[1536,128]{1,0:T(8,128)(2,1)} %add_convert_fusion.5), channel_id=1, source_target_pairs={{0,2},{1,3},{2,0},{3,1},{4,6},{5,7},{6,4},{7,5},{8,10},{9,11},{10,... | collective-permute-start | bytes 1179656 | tf_op jit(solution)/shard_map/ppermute | solution.py:127
  32.7 29.4 %copy-start.10 = (bf16[1536,128]{1,0:T(8,128)(2,1)}, bf16[1536,128]{1,0:T(8,128)(2,1)S(1)}, u32[]{:S(2)}) copy-start(bf16[1536,128]{1,0:T(8,128)(2,1)S(1)} %collective-permute-done.1) | copy-start | bytes 1179652
  33.9 11.6 %collective-permute-start.2 = (bf16[768,128]{1,0:T(8,128)(2,1)S(1)}, bf16[768,128]{1,0:T(8,128)(2,1)S(1)}, u32[]{:S(2)}, u32[]{:S(2)}) collective-permute-start(bf16[768,128]{1,0:T(8,128)(2,1)S(1)} %add_convert_fusion.7), channel_id=1, source_target_pairs={{0,4},{1,5},{2,6},{3,7},{4,8},{5,9},{6,10},{7,11},{8,12},{9,13},{1... | collective-permute-start | bytes 589832 | tf_op jit(solution)/shard_map/ppermute | solution.py:132
  45.6 13.9 %collective-permute-start.3 = (bf16[768,128]{1,0:T(8,128)(2,1)S(1)}, bf16[768,128]{1,0:T(8,128)(2,1)S(1)}, u32[]{:S(2)}, u32[]{:S(2)}) collective-permute-start(bf16[768,128]{1,0:T(8,128)(2,1)S(1)} %fusion), channel_id=1, source_target_pairs={{0,8},{1,9},{2,10},{3,11},{4,12},{5,13},{6,14},{7,15},{16,24},{17,... | collective-permute-start | bytes 589832 | tf_op jit(solution)/shard_map/ppermute | solution.py:132
  60.2 10.2 %collective-permute-start.4 = (bf16[768,128]{1,0:T(8,128)(2,1)}, bf16[768,128]{1,0:T(8,128)(2,1)}, u32[]{:S(2)}, u32[]{:S(2)}) collective-permute-start(bf16[768,128]{1,0:T(8,128)(2,1)} %fusion.1), channel_id=1, source_target_pairs={{0,2},{1,3},{2,0},{3,1},{4,6},{5,7},{6,4},{7,5},{8,10},{9,11},{10,... | collective-permute-start | bytes 589832 | tf_op jit(solution)/shard_map/ppermute | solution.py:127
  71.7 5.1 %collective-permute-start.5 = (bf16[1536,128]{1,0:T(8,128)(2,1)S(1)}, bf16[1536,128]{1,0:T(8,128)(2,1)}, u32[]{:S(2)}, u32[]{:S(2)}) collective-permute-start(bf16[1536,128]{1,0:T(8,128)(2,1)S(1)} %add_convert_fusion.4), channel_id=1, source_target_pairs={{0,1},{1,0},{2,3},{3,2},{4,5},{5,4},{6,7},{7,6},{8,9},{9,8},{10,11... | collective-permute-start | bytes 1179656 | tf_op jit(solution)/shard_map/ppermute | solution.py:127
  76.8 1.6 copy-start.9
  81.9 2.4 %collective-permute-start.6 = (bf16[3072,128]{1,0:T(8,128)(2,1)S(1)}, bf16[3072,128]{1,0:T(8,128)(2,1)S(1)}, u32[]{:S(2)}, u32[]{:S(2)}) collective-permute-start(bf16[3072,128]{1,0:T(8,128)(2,1)S(1)} %get-tuple-element.18), channel_id=1, source_target_pairs={{0,1},{1,0},{2,3},{3,2},{4,5},{5,4},{6,7},{7,6},{8,9},{9,8},{10,11... | collective-permute-start | bytes 2359304 | tf_op jit(solution)/shard_map/ppermute | solution.py:127
  84.4 20.4 %collective-permute-start.7 = (bf16[1536,128]{1,0:T(8,128)(2,1)S(1)}, bf16[1536,128]{1,0:T(8,128)(2,1)S(1)}, u32[]{:S(2)}, u32[]{:S(2)}) collective-permute-start(bf16[1536,128]{1,0:T(8,128)(2,1)S(1)} %add_convert_fusion.3), channel_id=1, source_target_pairs={{0,2},{1,3},{2,0},{3,1},{4,6},{5,7},{6,4},{7,5},{8,10},{9,11},{10,... | collective-permute-start | bytes 1179656 | tf_op jit(solution)/shard_map/ppermute | solution.py:127
  104.9 13.9 %collective-permute-start.8 = (bf16[768,128]{1,0:T(8,128)(2,1)S(1)}, bf16[768,128]{1,0:T(8,128)(2,1)S(1)}, u32[]{:S(2)}, u32[]{:S(2)}) collective-permute-start(bf16[768,128]{1,0:T(8,128)(2,1)S(1)} %add_convert_fusion.6), channel_id=1, source_target_pairs={{4,0},{5,1},{6,2},{7,3},{8,4},{9,5},{10,6},{11,7},{12,8},{13,9},{1... | collective-permute-start | bytes 589832 | tf_op jit(solution)/shard_map/ppermute | solution.py:132
  118.9 16.6 %collective-permute-start.9 = (bf16[768,128]{1,0:T(8,128)(2,1)S(1)}, bf16[768,128]{1,0:T(8,128)(2,1)S(1)}, u32[]{:S(2)}, u32[]{:S(2)}) collective-permute-start(bf16[768,128]{1,0:T(8,128)(2,1)S(1)} %fusion.2), channel_id=1, source_target_pairs={{8,0},{9,1},{10,2},{11,3},{12,4},{13,5},{14,6},{15,7},{24,16},{25,... | collective-permute-start | bytes 589832 | tf_op jit(solution)/shard_map/ppermute | solution.py:132
  135.6 6.5 %collective-permute-start.10 = (bf16[768,128]{1,0:T(8,128)(2,1)S(1)}, bf16[768,128]{1,0:T(8,128)(2,1)S(1)}, u32[]{:S(2)}, u32[]{:S(2)}) collective-permute-start(bf16[768,128]{1,0:T(8,128)(2,1)S(1)} %fusion.3), channel_id=1, source_target_pairs={{0,2},{1,3},{2,0},{3,1},{4,6},{5,7},{6,4},{7,5},{8,10},{9,11},{10,... | collective-permute-start | bytes 589832 | tf_op jit(solution)/shard_map/ppermute | solution.py:127
  142.3 7.2 %collective-permute-start.11 = (bf16[1536,128]{1,0:T(8,128)(2,1)S(1)}, bf16[1536,128]{1,0:T(8,128)(2,1)S(1)}, u32[]{:S(2)}, u32[]{:S(2)}) collective-permute-start(bf16[1536,128]{1,0:T(8,128)(2,1)S(1)} %add_convert_fusion.2), channel_id=1, source_target_pairs={{0,1},{1,0},{2,3},{3,2},{4,5},{5,4},{6,7},{7,6},{8,9},{9,8},{10,11... | collective-permute-start | bytes 1179656 | tf_op jit(solution)/shard_map/ppermute | solution.py:127
  148.4 1.1 copy-start.7
  153.3 22.3 %all-to-all-start = ((bf16[16,192,128]{2,1,0:T(8,128)(2,1)}), bf16[16,192,128]{2,1,0:T(8,128)(2,1)S(1)}, u32[]{:S(2)}, u32[]{:S(2)}) async-start(bf16[16,192,128]{2,1,0:T(8,128)(2,1)} %bitcast.8), calls=%async_computation | async-start | bytes 1572864 | tf_op jit(solution)/shard_map/all_to_all | solution.py:260
  175.6 4.6 %copy-start = (bf16[1,2048,3072]{2,1,0:T(8,128)(2,1)S(1)}, bf16[1,2048,3072]{2,1,0:T(8,128)(2,1)}, u32[]{:S(2)}) copy-start(bf16[1,2048,3072]{2,1,0:T(8,128)(2,1)} %all-gather.3.cloned.1.call-done) | copy-start | bytes 37748740
  180.2 5.3 %copy-start.8 = (f32[128,3072]{1,0:T(8,128)S(1)}, f32[128,3072]{1,0:T(8,128)}, u32[]{:S(2)}) copy-start(f32[128,3072]{1,0:T(8,128)} %copy-done.7) | copy-start | bytes 4718596
  183.6 15.7 %collective-permute-start.12 = (bf16[192,1536]{1,0:T(8,128)(2,1)S(1)}, bf16[192,1536]{1,0:T(8,128)(2,1)S(1)}, u32[]{:S(2)}, u32[]{:S(2)}) collective-permute-start(bf16[192,1536]{1,0:T(8,128)(2,1)S(1)} %shard_map.91), channel_id=1, source_target_pairs={{0,16},{16,0},{1,17},{17,1},{2,18},{18,2},{3,19},{19,3},{4,20},{20... | collective-permute-start | bytes 1769480 | tf_op jit(solution)/shard_map/ppermute | solution.py:127
  188.4 4.6 %copy-start.1 = (bf16[1,2048,3072]{2,1,0:T(8,128)(2,1)S(1)}, bf16[1,2048,3072]{2,1,0:T(8,128)(2,1)}, u32[]{:S(2)}) copy-start(bf16[1,2048,3072]{2,1,0:T(8,128)(2,1)} %all-gather.3.cloned.1.call-done) | copy-start | bytes 37748740
Sparse Core Ops, SparseCore 0:
  10.3 119.2 all-gather.2

commit v2 on v1

v2 whole, which is shorter than its diff:
```python
import functools

import jax
import jax.numpy as jnp
from jax import lax
from jax.experimental import pallas as pl
from jax.experimental.pallas import tpu as pltpu
from jax.sharding import PartitionSpec as P

HEAD_DIM = 128
EPSILON = 1e-05
F32 = jnp.float32
BF16 = jnp.bfloat16

NN = (((1,), (0,)), ((), ()))
NT = (((1,), (1,)), ((), ()))
TN = (((0,), (0,)), ((), ()))


def dot(a, b, dims):
    return lax.dot_general(a, b, dims, preferred_element_type=F32)


def slope(values):
    wide = values.astype(F32)
    return jnp.where(wide > 0, 1.0, jnp.exp(jnp.minimum(wide, 0.0)))


def feature(values):
    wide = values.astype(F32)
    return jnp.where(wide > 0, wide + 1.0, jnp.exp(jnp.minimum(wide, 0.0))).astype(BF16)


def causal(rows):
    t = lax.broadcasted_iota(jnp.int32, (rows, rows), 0)
    s = lax.broadcasted_iota(jnp.int32, (rows, rows), 1)
    return s <= t


def heads_of(ref):
    for head in range(ref.shape[1] // HEAD_DIM):
        yield slice(head * HEAD_DIM, (head + 1) * HEAD_DIM)


def block_state_kernel(k_ref, v_ref, state_ref):
    for at in heads_of(k_ref):
        state_ref[at, :] = dot(feature(k_ref[:, at]), v_ref[:, at], TN).astype(BF16)


def masked_scores(rows, columns):
    return jnp.where(causal(rows.shape[0]), dot(rows, columns, NT), 0.0).astype(BF16)


def local_output_kernel(q_ref, k_ref, v_ref, local_ref):
    for at in heads_of(q_ref):
        scores = masked_scores(feature(q_ref[:, at]), feature(k_ref[:, at]))
        local_ref[:, at] = dot(scores, v_ref[:, at], NN)


def grad_output_kernel(q_ref, local_ref, upstream_ref, state_ref, grad_ref, block_ref):
    for at in heads_of(q_ref):
        query = feature(q_ref[:, at])
        output = local_ref[:, at] + dot(query, state_ref[at, :], NN)
        inverse_rms = lax.rsqrt(jnp.mean(output * output, axis=-1, keepdims=True) + EPSILON)
        normed = output * inverse_rms
        upstream = upstream_ref[:, at].astype(F32)
        projection = jnp.mean(upstream * normed, axis=-1, keepdims=True)
        grad = (inverse_rms * (upstream - normed * projection)).astype(BF16)
        grad_ref[:, at] = grad
        block_ref[at, :] = dot(query, grad, TN).astype(BF16)


def key_local_kernel(q_ref, v_ref, grad_ref, key_out):
    for at in heads_of(q_ref):
        grad_scores = masked_scores(grad_ref[:, at], v_ref[:, at])
        key_out[:, at] = dot(grad_scores, feature(q_ref[:, at]), TN)


def key_grad_kernel(k_ref, v_ref, local_ref, state_ref, key_out, turned_out):
    for at in heads_of(k_ref):
        key = local_ref[:, at] + dot(v_ref[:, at], state_ref[at, :], NT)
        key = key * slope(k_ref[:, at])
        key_out[:, at] = key.astype(BF16)
        turned = key.T.astype(BF16)
        for copy in range(turned_out.shape[0]):
            turned_out[copy, at, :] = turned


def other_grads_kernel(q_ref, k_ref, v_ref, grad_ref, state_ref, later_ref, query_out, value_out):
    for at in heads_of(k_ref):
        grad = grad_ref[:, at]
        key = feature(k_ref[:, at])
        grad_scores = masked_scores(grad, v_ref[:, at])
        query = dot(grad_scores, key, NN) + dot(grad, state_ref[at, :], NT)
        query_out[:, at] = (query * slope(q_ref[:, at])).astype(BF16)
        scores = masked_scores(feature(q_ref[:, at]), key)
        value = dot(scores, grad, TN) + dot(key, later_ref[at, :], NN)
        value_out[:, at] = value.astype(BF16)


def by_heads(kernel, shape, split, operands, outs, matmuls, into=(), vmem=6):
    tokens, features = shape
    parts, part = split
    width = features // parts
    groups = max(g for g in (1, 2, 3, 4) if width % (g * HEAD_DIM) == 0)
    group = width // groups
    copies = lax.axis_size("dp")
    specs = {
        "row": pl.BlockSpec((tokens, group), lambda i: (0, part * groups + i)),
        "part": pl.BlockSpec((tokens, group), lambda i: (0, i)),
        "state": pl.BlockSpec((group, HEAD_DIM), lambda i: (i, 0)),
        "copies": pl.BlockSpec((copies, group, HEAD_DIM), lambda i: (0, i, 0)),
    }
    shapes = {
        "row": (tokens, features),
        "part": (tokens, width),
        "state": (width, HEAD_DIM),
        "copies": (copies, width, HEAD_DIM),
    }
    moved = tokens * width * 4 * (len(operands) + len(outs))
    held = len(operands)

    def body(*refs):
        kernel(*refs[:held], *refs[held + len(into) :])

    return pl.pallas_call(
        body,
        grid=(groups,),
        in_specs=[specs[kind] for kind, _ in operands] + [pl.BlockSpec(memory_space=pl.ANY)] * len(into),
        out_specs=[specs[kind] for kind, _ in outs],
        out_shape=[jax.ShapeDtypeStruct(shapes[kind], dtype) for kind, dtype in outs],
        input_output_aliases={held + i: i for i in range(len(into))},
        compiler_params=pltpu.CompilerParams(vmem_limit_bytes=vmem * 1024 * 1024),
        cost_estimate=pl.CostEstimate(
            flops=2 * matmuls * tokens * width * HEAD_DIM, bytes_accessed=moved, transcendentals=0
        ),
    )(*[a for _, a in operands], *into)


def swap(array, axis):
    return lax.ppermute(array, axis, [(0, 1), (1, 0)])


def add(a, b):
    return (a.astype(F32) + b.astype(F32)).astype(BF16)


def added_if(flag, a, b):
    return add(a, jnp.where(flag, b, jnp.zeros((), BF16)))


def pick(array, place):
    return jnp.where(place == 0, array[0], array[1])


def both(own, other, place):
    return jnp.where(place == 0, jnp.stack([own, other]), jnp.stack([other, own]))


def after(array, *others):
    if not others:
        return array
    return lax.optimization_barrier((array,) + others)[0]


class Scan:
    def __init__(self, state, bits, backward):
        self.first, self.second, *self.rest = bits
        self.after = 0 if backward else 1
        self.place = {bit: lax.axis_index(bit) for bit in bits}
        self.width = state.shape[0]
        first, second = self.first, self.second
        state = state.reshape(2, 2, self.width // 4, HEAD_DIM)
        self.other = swap(state, first)
        self.pair = add(pick(state, self.place[first]), pick(self.other, self.place[first]))
        self.pair_other = swap(self.pair, second)

    def spread(self, *others):
        place = self.place
        self.pair_other = after(self.pair_other, *others)
        self.total = add(pick(self.pair, place[self.second]), pick(self.pair_other, place[self.second]))
        total, before = self.total, None
        for bit in self.rest:
            arrived = swap(total, bit)
            flag = place[bit] == self.after
            if before is None:
                before = jnp.where(flag, arrived, jnp.zeros((), BF16))
            else:
                before = added_if(flag, before, arrived)
            total = add(total, arrived)
        self.before = before

    def collect(self, *others):
        second, place = self.second, self.place
        before = after(self.before, *others)
        half = both(before, swap(before, second), place[second])
        self.half = added_if(place[second] == self.after, half, self.pair_other)

    def finish(self):
        first, place = self.first, self.place
        whole = both(self.half, swap(self.half, first), place[first])
        whole = added_if(place[first] == self.after, whole, self.other)
        return whole.reshape(self.width, HEAD_DIM)


def sides_kernel(which_ref, in_ref, own_ref, gone_ref):
    columns = own_ref.shape[1]

    @pl.when(which_ref[0] == 0)
    def _():
        own_ref[...] = in_ref[:, :columns]
        gone_ref[...] = in_ref[:, columns:]

    @pl.when(which_ref[0] == 1)
    def _():
        own_ref[...] = in_ref[:, columns:]
        gone_ref[...] = in_ref[:, :columns]


def sides(array, which):
    rows, columns = array.shape
    tile = rows // 4
    out = jax.ShapeDtypeStruct((rows, columns // 2), array.dtype)
    return pl.pallas_call(
        sides_kernel,
        grid_spec=pltpu.PrefetchScalarGridSpec(
            num_scalar_prefetch=1,
            grid=(rows // tile,),
            in_specs=[pl.BlockSpec((tile, columns), lambda i, which: (i, 0))],
            out_specs=[pl.BlockSpec((tile, columns // 2), lambda i, which: (i, 0))] * 2,
        ),
        out_shape=[out, out],
        compiler_params=pltpu.CompilerParams(vmem_limit_bytes=6 * 1024 * 1024),
        cost_estimate=pl.CostEstimate(flops=0, bytes_accessed=4 * array.size, transcendentals=0),
    )(jnp.reshape(which, (1,)).astype(jnp.int32), array)


def weight_kernel(order_ref, turned_ref, *refs):
    *held, kept_ref, sent_ref, lhs_ref = refs
    sources, rows, tokens = turned_ref.shape

    @pl.when(pl.program_id(0) == 0)
    def _():
        for source in range(sources):
            lhs_ref[:, source * tokens : (source + 1) * tokens] = turned_ref[order_ref[source]]

    blocks = [ref[at] for ref in held for at in range(ref.shape[0])]
    total = jnp.zeros(kept_ref.shape, F32)
    for at in range(0, sources, 2):
        lhs = lhs_ref[:, at * tokens : (at + 2) * tokens]
        total += dot(lhs, jnp.concatenate(blocks[at : at + 2], axis=0), NN)
    kept_ref[...] = total
    sent_ref[...] = total.astype(BF16)


def weight_part(order, turned, inputs):
    sources, rows, tokens = turned.shape
    columns = inputs[0].shape[-1]
    tile = 512 if columns % 512 == 0 else columns
    out = pl.BlockSpec((rows, tile), lambda i, order: (0, i))
    return pl.pallas_call(
        weight_kernel,
        grid_spec=pltpu.PrefetchScalarGridSpec(
            num_scalar_prefetch=1,
            grid=(columns // tile,),
            in_specs=[pl.BlockSpec((sources, rows, tokens), lambda i, order: (0, 0, 0))]
            + [pl.BlockSpec((array.shape[0], tokens, tile), lambda i, order: (0, 0, i)) for array in inputs],
            out_specs=[out, out],
            scratch_shapes=[pltpu.VMEM((rows, sources * tokens), BF16)],
        ),
        out_shape=[jax.ShapeDtypeStruct((rows, columns), F32), jax.ShapeDtypeStruct((rows, columns), BF16)],
        compiler_params=pltpu.CompilerParams(vmem_limit_bytes=56 * 1024 * 1024),
        cost_estimate=pl.CostEstimate(
            flops=2 * sources * tokens * rows * columns,
            bytes_accessed=sources * tokens * columns * 2 + rows * columns * 6,
            transcendentals=0,
        ),
    )(order, turned, *inputs)


def shards(layer_input, query_rows, key_rows, value_rows, out_grad, bits):
    query, key, value, upstream = query_rows[0], key_rows[0], value_rows[0], out_grad[0]
    shape = tokens, features = query.shape
    sequences = lax.axis_size("dp")
    places = 2 ** len(bits)
    core, side, layer, *high = bits
    spans = tuple(reversed(high))
    halves = places // 8
    rows = features // places

    def run(kernel, part, operands, outs, matmuls, into=()):
        return by_heads(kernel, shape, (halves, part), operands, outs, matmuls, into)

    mine = lax.axis_index("dp")
    if sequences == 2:
        own, gone = sides(layer_input[0], mine)
        held = [own[None], swap(gone, "dp")[None]]
        order = jnp.arange(2, dtype=jnp.int32) ^ mine
    else:
        held = [lax.all_to_all(layer_input[0].reshape(tokens, sequences, -1), "dp", 1, 0)]
        order = jnp.arange(sequences, dtype=jnp.int32)
    order = order * 8

    parts = range(halves)
    forward, backward, outputs, states, grads, key_locals, turns = [], [], [], [], [], [], []
    for part in parts:
        (block_state,) = run(block_state_kernel, part, [("row", key), ("row", value)], [("state", BF16)], 1)
        forward.append(Scan(block_state, bits, False))
    pairs = [scan.pair for scan in forward]

    def spread_inputs(held, order, bit, weight, *others):
        at = lax.axis_index(bit) * weight
        held = held + [swap(after(array, *others), bit) for array in held]
        return held, jnp.concatenate([order + at, order + weight - at])

    near, order = spread_inputs(held, order, side, 2, *pairs)

    for part in parts:
        outputs += run(
            local_output_kernel,
            part,
            [("row", after(query, *pairs)), ("row", key), ("row", value)],
            [("part", F32)],
            2,
        )
    for part in parts:
        forward[part].spread(*outputs, *held)
    arrived = [scan.before for scan in forward]
    for part in parts:
        forward[part].collect(*near)
    held, order = spread_inputs(near, order, layer, 4, *arrived)
    for part in parts:
        states.append(forward[part].finish())
        grad_output, block_grad = run(
            grad_output_kernel,
            part,
            [("row", query), ("part", outputs[part]), ("row", upstream), ("state", states[part])],
            [("part", BF16), ("state", BF16)],
            2,
        )
        grads.append(grad_output)
        backward.append(Scan(block_grad, bits, True))
    pairs = [scan.pair for scan in backward]
    for part in parts:
        key_locals += run(
            key_local_kernel,
            part,
            [("row", query), ("row", value), ("part", after(grads[part], *pairs))],
            [("part", F32)],
            2,
        )
    for part in parts:
        backward[part].spread(*key_locals)
    for part in parts:
        backward[part].collect(*held)
    halves_in = [scan.half for scan in backward]
    held, order = spread_inputs(held, order, core, 1)

    key_grad, other_grads = [], []
    for part in parts:
        later = backward[part].finish()
        *key_grad, turned = run(
            key_grad_kernel,
            part,
            [("row", key), ("row", value), ("part", key_locals[part]), ("state", later)],
            [("row", BF16), ("copies", BF16)],
            1,
            key_grad,
        )
        turns.append(after(turned, *halves_in))
        other_grads = run(
            other_grads_kernel,
            part,
            [
                ("row", query),
                ("row", key),
                ("row", value),
                ("part", after(grads[part], *turns)),
                ("state", states[part]),
                ("state", later),
            ],
            [("row", BF16), ("row", BF16)],
            6,
            other_grads,
        )
    query_grad, value_grad = other_grads

    span = lax.axis_index(spans)
    weight_grad = None
    for target, turned in enumerate(turns):
        turned = turned.reshape(sequences * 8, rows, tokens)
        turned = lax.all_to_all(turned, ("dp", layer, side, core), 0, 0, tiled=True)
        kept, sent = weight_part(order, turned, held)
        for turn in range(1, halves):
            kept += lax.ppermute(sent, spans, [((target + turn) % halves, target)]).astype(F32)
        weight_grad = kept if weight_grad is None else jnp.where(span == target, kept, weight_grad)
    weight_grad = weight_grad * (sequences * places * tokens) ** (-0.5)
    return (query_grad[None], key_grad[0][None], value_grad[None], weight_grad)


def solution(mesh):
    sequences, places = mesh.shape["dp"], mesh.shape["ctx"]
    bits = tuple(f"bit{i}" for i in range(places.bit_length() - 1))
    ctx = tuple(reversed(bits))
    devices = mesh.devices.reshape((sequences,) + (2,) * len(bits))
    rows = P("dp", ctx, None)
    return jax.shard_map(
        functools.partial(shards, bits=bits),
        mesh=jax.sharding.Mesh(devices, ("dp",) + ctx),
        in_specs=(rows,) * 5,
        out_specs=(rows, rows, rows, P(ctx, "dp")),
        check_vma=False,
    )
```

time: 208 us -> 187 us (0.90)
  the two profiles are of different devices: /device:TPU:0 before, /device:TPU:29 now
where the time goes in v2:
time: 187 us; the launch traced here: 186 us
  waiting for transfers between devices  71.6 us (38%)
  starting transfers between devices  51.4 us (27%)
  Pallas kernels  45.4 us (24%)
  other arithmetic  10.4 us (6%)
  local copies, waits for them, and re-layouts  5.96 us (3%)
    ppermute x39, waiting for transfers between devices, swap(): return lax.ppermute(array, axis, [(0, 1), (1, 0)])  43.7 us
    ppermute x39, starting transfers between devices, swap(): return lax.ppermute(array, axis, [(0, 1), (1, 0)])  32 us
    pallas_call x12, Pallas kernels, by_heads(): pl.pallas_call(body, grid=(groups,), in_specs=[specs[kind] for kind, _ in...  30.1 us
    ppermute x2, waiting for transfers between devices, shards(): lax.ppermute(sent, spans, [((target + turn) % halves, target)]).astype(F32)  22.2 us
    all_to_all x2, starting transfers between devices, shards(): turned = lax.all_to_all(turned, ('dp', layer, side, core), 0, 0, tiled=True)  14.5 us
    pallas_call x2, Pallas kernels, weight_part(): pl.pallas_call(weight_kernel, grid_spec=pltpu.PrefetchScalarGridSpec(num_...  13.9 us
    convert_element_type x24, other arithmetic, add(): return (a.astype(F32) + b.astype(F32)).astype(BF16)  6.73 us
    unnamed x76, local copies, waits for them, and re-layouts  5.96 us
  transfers between devices with their start and end apart: 43, of which 21 were waited for; matrix products, arithmetic and copies ran while one was open for 4% of the time, Pallas kernels for 23%

profile of v2, /device:TPU:29, one launch (start us, length us, event | category | flops | bytes accessed | tf_op | source)
XLA Modules:
  0.0 186.0 jit_solution(6038166916917014753)
XLA Ops:
  0.6 1.1 copy-done
  1.8 1.1 copy-done.3
  5.9 1.4 shard_map.88
  7.6 1.3 fusion.2
  8.8 1.3 collective-permute-start.2
  11.6 1.2 collective-permute-start.6
  12.8 5.1 %collective-permute-done.3 = bf16[128,1536]{1,0:T(8,128)(2,1)} collective-permute-done((bf16[128,1536]{1,0:T(8,128)(2,1)}, bf16[128,1536]{1,0:T(8,128)(2,1)}, u32[]{:S(2)}, u32[]{:S(2)}) %collective-permute-start.3) | collective-permute-done | bytes 393248 | tf_op jit(solution)/shard_map/ppermute | solution.py:141
  17.9 1.2 collective-permute-start.7
  19.1 2.6 %shard_map.86.refs_1_ = f32[128,1536]{1,0:T(8,128)S(1)} custom-call(bf16[128,3072]{1,0:T(8,128)(2,1)S(1)} %bitcast.87, bf16[128,3072]{1,0:T(8,128)(2,1)S(1)} %bitcast.97, bf16[128,3072]{1,0:T(8,128)(2,1)S(1)} %bitcast.79), custom_call_target="tpu_custom_call" | custom-call | flops 100663296 | bytes 3145728 | tf_op jit(solution)/shard_map/pallas_call | solution.py:126
  21.7 2.6 %shard_map.87.refs_1_ = f32[128,1536]{1,0:T(8,128)S(1)} custom-call(bf16[128,3072]{1,0:T(8,128)(2,1)S(1)} %bitcast.88, bf16[128,3072]{1,0:T(8,128)(2,1)S(1)} %bitcast.98, bf16[128,3072]{1,0:T(8,128)(2,1)S(1)} %bitcast.80), custom_call_target="tpu_custom_call" | custom-call | flops 100663296 | bytes 3145728 | tf_op jit(solution)/shard_map/pallas_call | solution.py:126
  24.7 1.4 collective-permute-start.11
  26.0 2.2 %collective-permute-done.4 = bf16[384,128]{1,0:T(8,128)(2,1)S(1)} collective-permute-done((bf16[384,128]{1,0:T(8,128)(2,1)S(1)}, bf16[384,128]{1,0:T(8,128)(2,1)S(1)}, u32[]{:S(2)}, u32[]{:S(2)}) %collective-permute-start.4) | collective-permute-done | bytes 98336 | tf_op jit(solution)/shard_map/ppermute | solution.py:141
  29.3 1.5 collective-permute-start.12
  30.8 4.2 %collective-permute-done.5 = bf16[384,128]{1,0:T(8,128)(2,1)S(1)} collective-permute-done((bf16[384,128]{1,0:T(8,128)(2,1)S(1)}, bf16[384,128]{1,0:T(8,128)(2,1)S(1)}, u32[]{:S(2)}, u32[]{:S(2)}) %collective-permute-start.5) | collective-permute-done | bytes 98336 | tf_op jit(solution)/shard_map/ppermute | solution.py:141
  35.7 1.2 collective-permute-start.8
  36.9 2.3 %collective-permute-done.12 = bf16[384,128]{1,0:T(8,128)(2,1)S(1)} collective-permute-done((bf16[384,128]{1,0:T(8,128)(2,1)S(1)}, bf16[384,128]{1,0:T(8,128)(2,1)S(1)}, u32[]{:S(2)}, u32[]{:S(2)}) %collective-permute-start.12) | collective-permute-done | bytes 98336 | tf_op jit(solution)/shard_map/ppermute | solution.py:141
  39.6 1.5 collective-permute-start.21
  41.2 3.5 %collective-permute-start.9 = (bf16[2,384,128]{2,1,0:T(8,128)(2,1)S(1)}, bf16[2,384,128]{2,1,0:T(8,128)(2,1)S(1)}, u32[]{:S(2)}, u32[]{:S(2)}) collective-permute-start(bf16[2,384,128]{2,1,0:T(8,128)(2,1)S(1)} %add_convert_fusion.7), channel_id=1, source_target_pairs={{0,1},{1,0},{2,3},{3,2},{4,5},{5,4},{6,7},{7,6},{8,9},{9,8},{10,11... | collective-permute-start | bytes 589832 | tf_op jit(solution)/shard_map/ppermute | solution.py:141
  45.8 1.1 add_convert_fusion.3
  47.0 2.3 %shard_map.89 = (bf16[128,1536]{1,0:T(8,128)(2,1)S(1)}, bf16[1536,128]{1,0:T(8,128)(2,1)S(1)}) custom-call(bf16[128,3072]{1,0:T(8,128)(2,1)S(1)} %bitcast.89, f32[128,1536]{1,0:T(8,128)S(1)} %shard_map.86.refs_1_, bf16[128,3072]{1,0:T(8,128)(2,1)S(1)} %bitcast.111, bf16[1536,128]{1,0:T(8,128)(2,1)S(1)} %bitcast.105), custom_call_target="tpu_custom_call" | custom-call | flops 100663296 | bytes 4718592 | tf_op jit(solution)/shard_map/pallas_call | solution.py:126
  49.3 1.3 add_convert_fusion.2
  50.6 2.3 %shard_map.90 = (bf16[128,1536]{1,0:T(8,128)(2,1)S(1)}, bf16[1536,128]{1,0:T(8,128)(2,1)S(1)}) custom-call(bf16[128,3072]{1,0:T(8,128)(2,1)S(1)} %bitcast.90, f32[128,1536]{1,0:T(8,128)S(1)} %shard_map.87.refs_1_, bf16[128,3072]{1,0:T(8,128)(2,1)S(1)} %bitcast.112, bf16[1536,128]{1,0:T(8,128)(2,1)S(1)} %bitcast.107), custom_call_target="tpu_custom_call" | custom-call | flops 100663296 | bytes 4718592 | tf_op jit(solution)/shard_map/pallas_call | solution.py:126
  53.5 1.2 collective-permute-done.15
  54.7 1.1 collective-permute-start.23
  56.7 3.2 %shard_map.91.refs_2_ = f32[128,1536]{1,0:T(8,128)S(1)} custom-call(bf16[128,3072]{1,0:T(8,128)(2,1)S(1)} %bitcast.91, bf16[128,3072]{1,0:T(8,128)(2,1)S(1)} %bitcast.81, bf16[128,1536]{1,0:T(8,128)(2,1)S(1)} %get-tuple-element.72.refs_2_.refs_3_), custom_call_target="tpu_custom_call" | custom-call | flops 100663296 | bytes 3145728 | tf_op jit(solution)/shard_map/pallas_call | solution.py:126
  59.9 3.2 %shard_map.92.refs_2_ = f32[128,1536]{1,0:T(8,128)S(1)} custom-call(bf16[128,3072]{1,0:T(8,128)(2,1)S(1)} %bitcast.92, bf16[128,3072]{1,0:T(8,128)(2,1)S(1)} %bitcast.82, bf16[128,1536]{1,0:T(8,128)(2,1)S(1)} %get-tuple-element.71.refs_2_.refs_3_), custom_call_target="tpu_custom_call" | custom-call | flops 100663296 | bytes 3145728 | tf_op jit(solution)/shard_map/pallas_call | solution.py:126
  65.0 4.8 %collective-permute-done.26 = bf16[2,384,128]{2,1,0:T(8,128)(2,1)S(1)} collective-permute-done((bf16[2,384,128]{2,1,0:T(8,128)(2,1)S(1)}, bf16[2,384,128]{2,1,0:T(8,128)(2,1)S(1)}, u32[]{:S(2)}, u32[]{:S(2)}) %collective-permute-start.26) | collective-permute-done | bytes 196640 | tf_op jit(solution)/shard_map/ppermute | solution.py:141
  70.3 4.9 %collective-permute-done.18 = bf16[384,128]{1,0:T(8,128)(2,1)S(1)} collective-permute-done((bf16[384,128]{1,0:T(8,128)(2,1)S(1)}, bf16[384,128]{1,0:T(8,128)(2,1)S(1)}, u32[]{:S(2)}, u32[]{:S(2)}) %collective-permute-start.18) | collective-permute-done | bytes 98336 | tf_op jit(solution)/shard_map/ppermute | solution.py:141
  75.6 3.3 %collective-permute-done.27 = bf16[384,128]{1,0:T(8,128)(2,1)S(1)} collective-permute-done((bf16[384,128]{1,0:T(8,128)(2,1)S(1)}, bf16[384,128]{1,0:T(8,128)(2,1)S(1)}, u32[]{:S(2)}, u32[]{:S(2)}) %collective-permute-start.27) | collective-permute-done | bytes 98336 | tf_op jit(solution)/shard_map/ppermute | solution.py:141
  78.9 5.3 %collective-permute-done.19 = bf16[384,128]{1,0:T(8,128)(2,1)S(1)} collective-permute-done((bf16[384,128]{1,0:T(8,128)(2,1)S(1)}, bf16[384,128]{1,0:T(8,128)(2,1)S(1)}, u32[]{:S(2)}, u32[]{:S(2)}) %collective-permute-start.19) | collective-permute-done | bytes 98336 | tf_op jit(solution)/shard_map/ppermute | solution.py:141
  84.3 1.8 collective-permute-start.24
  86.1 4.8 %collective-permute-done.28 = bf16[384,128]{1,0:T(8,128)(2,1)S(1)} collective-permute-done((bf16[384,128]{1,0:T(8,128)(2,1)S(1)}, bf16[384,128]{1,0:T(8,128)(2,1)S(1)}, u32[]{:S(2)}, u32[]{:S(2)}) %collective-permute-start.28) | collective-permute-done | bytes 98336 | tf_op jit(solution)/shard_map/ppermute | solution.py:141
  91.0 1.4 collective-permute-start.29
  92.6 6.2 %collective-permute-start.25 = (bf16[2,384,128]{2,1,0:T(8,128)(2,1)S(1)}, bf16[2,384,128]{2,1,0:T(8,128)(2,1)S(1)}, u32[]{:S(2)}, u32[]{:S(2)}) collective-permute-start(bf16[2,384,128]{2,1,0:T(8,128)(2,1)S(1)} %add_convert_fusion.5), channel_id=1, source_target_pairs={{0,1},{1,0},{2,3},{3,2},{4,5},{5,4},{6,7},{7,6},{8,9},{9,8},{10,11... | collective-permute-start | bytes 589832 | tf_op jit(solution)/shard_map/ppermute | solution.py:141
  100.1 2.2 %shard_map.93 = (bf16[128,3072]{1,0:T(8,128)(2,1)}, bf16[2,1536,128]{2,1,0:T(8,128)(2,1)S(1)}) custom-call(bf16[128,3072]{1,0:T(8,128)(2,1)S(1)} %bitcast.99, bf16[128,3072]{1,0:T(8,128)(2,1)S(1)} %bitcast.83, f32[128,1536]{1,0:T(8,128)S(1)} %shard_map.91.refs_2_, bf16[1536,128]{1,0:T(8,128)(2,1)S(1)} %bitcast.109), custom_call_target="tpu_custom_call" | custom-call | flops 50331648 | bytes 4718592 | tf_op jit(solution)/shard_map/pallas_call | solution.py:126
  103.1 7.5 %all-to-all-start.1 = ((bf16[16,192,128]{2,1,0:T(8,128)(2,1)}), bf16[16,192,128]{2,1,0:T(8,128)(2,1)}, u32[]{:S(2)}, u32[]{:S(2)}) async-start(bf16[16,192,128]{2,1,0:T(8,128)(2,1)} %bitcast.121), calls=%async_computation.1 | async-start | bytes 1572864 | tf_op jit(solution)/shard_map/all_to_all | solution.py:392
  111.2 1.2 collective-permute-done.30
  112.5 2.2 %shard_map.94 = (bf16[128,3072]{1,0:T(8,128)(2,1)}, bf16[2,1536,128]{2,1,0:T(8,128)(2,1)S(1)}) custom-call(bf16[128,3072]{1,0:T(8,128)(2,1)S(1)} %bitcast.100, bf16[128,3072]{1,0:T(8,128)(2,1)S(1)} %bitcast.84, f32[128,1536]{1,0:T(8,128)S(1)} %copy-done.8, bf16[1536,128]{1,0:T(8,128)(2,1)S(1)} %bitcast.103, ...), custom_call_target="tpu_custom_call", output_to_operand_aliasing={{0}: (4, {})} | custom-call | flops 50331648 | bytes 4718592 | tf_op jit(solution)/shard_map/pallas_call | solution.py:126
  115.6 5.7 %all-to-all-done.1.turned_ref = bf16[16,192,128]{2,1,0:T(8,128)(2,1)} async-done(((bf16[16,192,128]{2,1,0:T(8,128)(2,1)}), bf16[16,192,128]{2,1,0:T(8,128)(2,1)}, u32[]{:S(2)}, u32[]{:S(2)}) %all-to-all-start.1) | async-done | bytes 786464 | tf_op jit(solution)/shard_map/all_to_all | solution.py:392
  121.3 7.0 %all-to-all-start = ((bf16[16,192,128]{2,1,0:T(8,128)(2,1)}), bf16[16,192,128]{2,1,0:T(8,128)(2,1)}, u32[]{:S(2)}, u32[]{:S(2)}) async-start(bf16[16,192,128]{2,1,0:T(8,128)(2,1)} %bitcast.120), calls=%async_computation | async-start | bytes 1572864 | tf_op jit(solution)/shard_map/all_to_all | solution.py:392
  135.1 6.9 %shard_map.98 = (f32[192,1536]{1,0:T(8,128)}, bf16[192,1536]{1,0:T(8,128)(2,1)}) custom-call(s32[16]{0:T(128)} %pad_add_fusion.2.order_ref, bf16[16,192,128]{2,1,0:T(8,128)(2,1)} %all-to-all-done.1.turned_ref, bf16[1,128,1536]{2,1,0:T(8,128)(2,1)} %bitcast.116, bf16[1,128,1536]{2,1,0:T(8,128)(2,1)} %bitcast.13.refs_1_, bf16[1,128,1536]{2,1,0:T(8,128)(2,1)} %copy-done.20, ...), custom_call_target="tpu_custom_call" | custom-call | flops 1207959552 | bytes 8060928 | tf_op jit(solution)/shard_map/pallas_call | solution.py:261
  142.0 3.5 %collective-permute-start.40 = (bf16[192,1536]{1,0:T(8,128)(2,1)}, bf16[192,1536]{1,0:T(8,128)(2,1)}, u32[]{:S(2)}, u32[]{:S(2)}) collective-permute-start(bf16[192,1536]{1,0:T(8,128)(2,1)} %get-tuple-element.81), channel_id=1, source_target_pairs={{8,0},{9,1},{10,2},{11,3},{12,4},{13,5},{14,6},{15,7},{24,16},{25,... | collective-permute-start | bytes 1769480 | tf_op jit(solution)/shard_map/ppermute | solution.py:395
  145.5 7.0 %shard_map.97 = (f32[192,1536]{1,0:T(8,128)}, bf16[192,1536]{1,0:T(8,128)(2,1)}) custom-call(s32[16]{0:T(128)} %pad_add_fusion.2.order_ref, bf16[16,192,128]{2,1,0:T(8,128)(2,1)} %all-to-all-done.turned_ref, bf16[1,128,1536]{2,1,0:T(8,128)(2,1)} %bitcast.117, bf16[1,128,1536]{2,1,0:T(8,128)(2,1)} %bitcast.13.refs_1_, bf16[1,128,1536]{2,1,0:T(8,128)(2,1)} %copy-done.20, ...), custom_call_target="tpu_custom_call" | custom-call | flops 1207959552 | bytes 8060928 | tf_op jit(solution)/shard_map/pallas_call | solution.py:261
  152.5 1.4 collective-permute-start.39
  154.0 3.7 %shard_map.95 = (bf16[128,3072]{1,0:T(8,128)(2,1)}, bf16[128,3072]{1,0:T(8,128)(2,1)}) custom-call(bf16[128,3072]{1,0:T(8,128)(2,1)S(1)} %bitcast.93, bf16[128,3072]{1,0:T(8,128)(2,1)S(1)} %bitcast.101, bf16[128,3072]{1,0:T(8,128)(2,1)S(1)} %bitcast.85, bf16[128,1536]{1,0:T(8,128)(2,1)S(1)} %copy-done.14, bf16[1536,128]{1,0:T(8,128)(2,1)S(1)} %bitcast.108, ...), custom_call_target="tpu_custom_call" | custom-call | flops 301989888 | bytes 6291456 | tf_op jit(solution)/shard_map/pallas_call | solution.py:126
  157.7 3.7 %shard_map.96 = (bf16[128,3072]{1,0:T(8,128)(2,1)}, bf16[128,3072]{1,0:T(8,128)(2,1)}) custom-call(bf16[128,3072]{1,0:T(8,128)(2,1)S(1)} %bitcast.94, bf16[128,3072]{1,0:T(8,128)(2,1)S(1)} %bitcast.102, bf16[128,3072]{1,0:T(8,128)(2,1)S(1)} %bitcast.86, bf16[128,1536]{1,0:T(8,128)(2,1)S(1)} %copy-done.12, ...), custom_call_target="tpu_custom_call", output_to_operand_aliasing={{0}: (6, {}), {1}: (7, {})} | custom-call | flops 301989888 | bytes 6291456 | tf_op jit(solution)/shard_map/pallas_call | solution.py:126
  161.4 22.2 %collective-permute-done.39 = bf16[192,1536]{1,0:T(8,128)(2,1)S(1)} collective-permute-done((bf16[192,1536]{1,0:T(8,128)(2,1)}, bf16[192,1536]{1,0:T(8,128)(2,1)S(1)}, u32[]{:S(2)}, u32[]{:S(2)}) %collective-permute-start.39) | collective-permute-done | bytes 589856 | tf_op jit(solution)/shard_map/ppermute | solution.py:395
  183.5 2.4 %select_multiply_fusion = f32[192,1536]{1,0:T(8,128)} fusion(f32[192,1536]{1,0:T(8,128)S(1)} %copy-done.32, bf16[192,1536]{1,0:T(8,128)(2,1)} %collective-permute-done.40, f32[192,1536]{1,0:T(8,128)S(1)} %copy-done.33, bf16[192,1536]{1,0:T(8,128)(2,1)S(1)} %collective-permute-done.39, pred[]{:T(512)S(6)} %eq.19), kind=kLoop, calls=%fused_computation | loop fusion | flops 1769472 | bytes 4718593 | tf_op jit(solution)/shard_map/mul | solution.py:397
  (165 shorter events, 23.3 us)
Async XLA Ops:
  4.0 3.6 %collective-permute-start.1 = (bf16[2,2,384,128]{3,2,1,0:T(8,128)(2,1)S(1)}, bf16[2,2,384,128]{3,2,1,0:T(8,128)(2,1)}, u32[]{:S(2)}, u32[]{:S(2)}) collective-permute-start(bf16[2,2,384,128]{3,2,1,0:T(8,128)(2,1)S(1)} %bitcast.119), channel_id=1, source_target_pairs={{0,1},{1,0},{2,3},{3,2},{4,5},{5,4},{6,7},{7,6},{8,9},{9,8},{10,11... | collective-permute-start | bytes 1179656 | tf_op jit(solution)/shard_map/ppermute | solution.py:141
  5.8 4.3 %collective-permute-start = (bf16[2,2,384,128]{3,2,1,0:T(8,128)(2,1)S(1)}, bf16[2,2,384,128]{3,2,1,0:T(8,128)(2,1)}, u32[]{:S(2)}, u32[]{:S(2)}) collective-permute-start(bf16[2,2,384,128]{3,2,1,0:T(8,128)(2,1)S(1)} %bitcast.118), channel_id=1, source_target_pairs={{0,1},{1,0},{2,3},{3,2},{4,5},{5,4},{6,7},{7,6},{8,9},{9,8},{10,11... | collective-permute-start | bytes 1179656 | tf_op jit(solution)/shard_map/ppermute | solution.py:141
  7.3 32.3 %copy-start.10 = (bf16[128,1536]{1,0:T(8,128)(2,1)}, bf16[128,1536]{1,0:T(8,128)(2,1)S(1)}, u32[]{:S(2)}) copy-start(bf16[128,1536]{1,0:T(8,128)(2,1)S(1)} %get-tuple-element.44) | copy-start | bytes 1179652
  7.3 10.6 %collective-permute-start.3 = (bf16[128,1536]{1,0:T(8,128)(2,1)}, bf16[128,1536]{1,0:T(8,128)(2,1)}, u32[]{:S(2)}, u32[]{:S(2)}) collective-permute-start(bf16[128,1536]{1,0:T(8,128)(2,1)} %get-tuple-element.45), channel_id=1, source_target_pairs={{0,16},{16,0},{1,17},{17,1},{2,18},{18,2},{3,19},{19,3},{4,20},{20... | collective-permute-start | bytes 1179656 | tf_op jit(solution)/shard_map/ppermute | solution.py:141
  8.8 15.5 %collective-permute-start.2 = (bf16[2,384,128]{2,1,0:T(8,128)(2,1)S(1)}, bf16[2,384,128]{2,1,0:T(8,128)(2,1)S(1)}, u32[]{:S(2)}, u32[]{:S(2)}) collective-permute-start(bf16[2,384,128]{2,1,0:T(8,128)(2,1)S(1)} %fusion.2), channel_id=1, source_target_pairs={{0,2},{2,0},{1,3},{3,1},{4,6},{6,4},{5,7},{7,5},{8,10},{10,8},{9,1... | collective-permute-start | bytes 589832 | tf_op jit(solution)/shard_map/ppermute | solution.py:141
  11.2 13.4 %collective-permute-start.10 = (bf16[2,384,128]{2,1,0:T(8,128)(2,1)S(1)}, bf16[2,384,128]{2,1,0:T(8,128)(2,1)S(1)}, u32[]{:S(2)}, u32[]{:S(2)}) collective-permute-start(bf16[2,384,128]{2,1,0:T(8,128)(2,1)S(1)} %fusion.3), channel_id=1, source_target_pairs={{0,2},{2,0},{1,3},{3,1},{4,6},{6,4},{5,7},{7,5},{8,10},{10,8},{9,1... | collective-permute-start | bytes 589832 | tf_op jit(solution)/shard_map/ppermute | solution.py:141
  11.6 23.5 %collective-permute-start.6 = (bf16[1,128,1536]{2,1,0:T(8,128)(2,1)S(1)}, bf16[1,128,1536]{2,1,0:T(8,128)(2,1)S(1)}, u32[]{:S(2)}, u32[]{:S(2)}) collective-permute-start(bf16[1,128,1536]{2,1,0:T(8,128)(2,1)S(1)} %bitcast.113), channel_id=1, source_target_pairs={{0,2},{2,0},{1,3},{3,1},{4,6},{6,4},{5,7},{7,5},{8,10},{10,8},{9,1... | collective-permute-start | bytes 1179656 | tf_op jit(solution)/shard_map/ppermute | solution.py:141
  17.9 17.8 %collective-permute-start.7 = (bf16[1,128,1536]{2,1,0:T(8,128)(2,1)}, bf16[1,128,1536]{2,1,0:T(8,128)(2,1)S(1)}, u32[]{:S(2)}, u32[]{:S(2)}) collective-permute-start(bf16[1,128,1536]{2,1,0:T(8,128)(2,1)} %bitcast.13.refs_1_), channel_id=1, source_target_pairs={{0,2},{2,0},{1,3},{3,1},{4,6},{6,4},{5,7},{7,5},{8,10},{10,8},{9,1... | collective-permute-start | bytes 1179656 | tf_op jit(solution)/shard_map/ppermute | solution.py:141
  24.4 3.8 %collective-permute-start.4 = (bf16[384,128]{1,0:T(8,128)(2,1)S(1)}, bf16[384,128]{1,0:T(8,128)(2,1)S(1)}, u32[]{:S(2)}, u32[]{:S(2)}) collective-permute-start(bf16[384,128]{1,0:T(8,128)(2,1)S(1)} %fusion.8), channel_id=1, source_target_pairs={{0,4},{4,0},{1,5},{5,1},{2,6},{6,2},{3,7},{7,3},{8,12},{12,8},{9,1... | collective-permute-start | bytes 294920 | tf_op jit(solution)/shard_map/ppermute | solution.py:141
  24.7 4.6 %collective-permute-start.11 = (bf16[384,128]{1,0:T(8,128)(2,1)S(1)}, bf16[384,128]{1,0:T(8,128)(2,1)S(1)}, u32[]{:S(2)}, u32[]{:S(2)}) collective-permute-start(bf16[384,128]{1,0:T(8,128)(2,1)S(1)} %fusion.9), channel_id=1, source_target_pairs={{0,4},{4,0},{1,5},{5,1},{2,6},{6,2},{3,7},{7,3},{8,12},{12,8},{9,1... | collective-permute-start | bytes 294920 | tf_op jit(solution)/shard_map/ppermute | solution.py:141
  28.2 6.7 %collective-permute-start.5 = (bf16[384,128]{1,0:T(8,128)(2,1)S(1)}, bf16[384,128]{1,0:T(8,128)(2,1)S(1)}, u32[]{:S(2)}, u32[]{:S(2)}) collective-permute-start(bf16[384,128]{1,0:T(8,128)(2,1)S(1)} %add_convert_fusion.18), channel_id=1, source_target_pairs={{0,8},{8,0},{1,9},{9,1},{2,10},{10,2},{3,11},{11,3},{4,12},{12,4},... | collective-permute-start | bytes 294920 | tf_op jit(solution)/shard_map/ppermute | solution.py:141
  29.3 9.9 %collective-permute-start.12 = (bf16[384,128]{1,0:T(8,128)(2,1)S(1)}, bf16[384,128]{1,0:T(8,128)(2,1)S(1)}, u32[]{:S(2)}, u32[]{:S(2)}) collective-permute-start(bf16[384,128]{1,0:T(8,128)(2,1)S(1)} %add_convert_fusion.15), channel_id=1, source_target_pairs={{0,8},{8,0},{1,9},{9,1},{2,10},{10,2},{3,11},{11,3},{4,12},{12,4},... | collective-permute-start | bytes 294920 | tf_op jit(solution)/shard_map/ppermute | solution.py:141
  35.7 19.0 %copy-start.21 = (bf16[1,128,1536]{2,1,0:T(8,128)(2,1)}, bf16[1,128,1536]{2,1,0:T(8,128)(2,1)S(1)}, u32[]{:S(2)}) copy-start(bf16[1,128,1536]{2,1,0:T(8,128)(2,1)S(1)} %collective-permute-done.7.refs_3_) | copy-start | bytes 1179652
  35.7 5.4 %collective-permute-start.8 = (bf16[384,128]{1,0:T(8,128)(2,1)S(1)}, bf16[384,128]{1,0:T(8,128)(2,1)S(1)}, u32[]{:S(2)}, u32[]{:S(2)}) collective-permute-start(bf16[384,128]{1,0:T(8,128)(2,1)S(1)} %add_convert_fusion.17), channel_id=1, source_target_pairs={{0,2},{2,0},{1,3},{3,1},{4,6},{6,4},{5,7},{7,5},{8,10},{10,8},{9,1... | collective-permute-start | bytes 294920 | tf_op jit(solution)/shard_map/ppermute | solution.py:141
  39.2 5.5 %collective-permute-start.13 = (bf16[384,128]{1,0:T(8,128)(2,1)S(1)}, bf16[384,128]{1,0:T(8,128)(2,1)S(1)}, u32[]{:S(2)}, u32[]{:S(2)}) collective-permute-start(bf16[384,128]{1,0:T(8,128)(2,1)S(1)} %add_convert_fusion.14), channel_id=1, source_target_pairs={{0,2},{2,0},{1,3},{3,1},{4,6},{6,4},{5,7},{7,5},{8,10},{10,8},{9,1... | collective-permute-start | bytes 294920 | tf_op jit(solution)/shard_map/ppermute | solution.py:141
  39.6 44.7 %collective-permute-start.20 = (bf16[1,128,1536]{2,1,0:T(8,128)(2,1)S(1)}, bf16[1,128,1536]{2,1,0:T(8,128)(2,1)S(1)}, u32[]{:S(2)}, u32[]{:S(2)}) collective-permute-start(bf16[1,128,1536]{2,1,0:T(8,128)(2,1)S(1)} %bitcast.114), channel_id=1, source_target_pairs={{0,4},{4,0},{1,5},{5,1},{2,6},{6,2},{3,7},{7,3},{8,12},{12,8},{9,1... | collective-permute-start | bytes 1179656 | tf_op jit(solution)/shard_map/ppermute | solution.py:141
  39.6 44.7 %collective-permute-start.21 = (bf16[1,128,1536]{2,1,0:T(8,128)(2,1)}, bf16[1,128,1536]{2,1,0:T(8,128)(2,1)S(1)}, u32[]{:S(2)}, u32[]{:S(2)}) collective-permute-start(bf16[1,128,1536]{2,1,0:T(8,128)(2,1)} %bitcast.13.refs_1_), channel_id=1, source_target_pairs={{0,4},{4,0},{1,5},{5,1},{2,6},{6,2},{3,7},{7,3},{8,12},{12,8},{9,1... | collective-permute-start | bytes 1179656 | tf_op jit(solution)/shard_map/ppermute | solution.py:141
  41.0 43.2 %collective-permute-start.22 = (bf16[1,128,1536]{2,1,0:T(8,128)(2,1)S(1)}, bf16[1,128,1536]{2,1,0:T(8,128)(2,1)S(1)}, u32[]{:S(2)}, u32[]{:S(2)}) collective-permute-start(bf16[1,128,1536]{2,1,0:T(8,128)(2,1)S(1)} %collective-permute-done.6.refs_2_), channel_id=1, source_target_pairs={{0,4},{4,0},{1,5},{5,1},{2,6},{6,2},{3,7},{7,3},{8,12},{12,8},{9,1... | collective-permute-start | bytes 1179656 | tf_op jit(solution)/shard_map/ppermute | solution.py:141
  41.2 4.6 %collective-permute-start.9 = (bf16[2,384,128]{2,1,0:T(8,128)(2,1)S(1)}, bf16[2,384,128]{2,1,0:T(8,128)(2,1)S(1)}, u32[]{:S(2)}, u32[]{:S(2)}) collective-permute-start(bf16[2,384,128]{2,1,0:T(8,128)(2,1)S(1)} %add_convert_fusion.7), channel_id=1, source_target_pairs={{0,1},{1,0},{2,3},{3,2},{4,5},{5,4},{6,7},{7,6},{8,9},{9,8},{10,11... | collective-permute-start | bytes 589832 | tf_op jit(solution)/shard_map/ppermute | solution.py:141
  44.8 4.5 %collective-permute-start.14 = (bf16[2,384,128]{2,1,0:T(8,128)(2,1)S(1)}, bf16[2,384,128]{2,1,0:T(8,128)(2,1)S(1)}, u32[]{:S(2)}, u32[]{:S(2)}) collective-permute-start(bf16[2,384,128]{2,1,0:T(8,128)(2,1)S(1)} %add_convert_fusion.6), channel_id=1, source_target_pairs={{0,1},{1,0},{2,3},{3,2},{4,5},{5,4},{6,7},{7,6},{8,9},{9,8},{10,11... | collective-permute-start | bytes 589832 | tf_op jit(solution)/shard_map/ppermute | solution.py:141
  52.9 1.8 collective-permute-start.15
  53.0 2.9 %collective-permute-start.16 = (bf16[2,2,384,128]{3,2,1,0:T(8,128)(2,1)S(1)}, bf16[2,2,384,128]{3,2,1,0:T(8,128)(2,1)S(1)}, u32[]{:S(2)}, u32[]{:S(2)}) collective-permute-start(bf16[2,2,384,128]{3,2,1,0:T(8,128)(2,1)S(1)} %bitcast.123), channel_id=1, source_target_pairs={{0,1},{1,0},{2,3},{3,2},{4,5},{5,4},{6,7},{7,6},{8,9},{9,8},{10,11... | collective-permute-start | bytes 1179656 | tf_op jit(solution)/shard_map/ppermute | solution.py:141
  54.7 29.6 %collective-permute-start.23 = (bf16[1,128,1536]{2,1,0:T(8,128)(2,1)S(1)}, bf16[1,128,1536]{2,1,0:T(8,128)(2,1)S(1)}, u32[]{:S(2)}, u32[]{:S(2)}) collective-permute-start(bf16[1,128,1536]{2,1,0:T(8,128)(2,1)S(1)} %collective-permute-done.7.refs_3_), channel_id=1, source_target_pairs={{0,4},{4,0},{1,5},{5,1},{2,6},{6,2},{3,7},{7,3},{8,12},{12,8},{9,1... | collective-permute-start | bytes 1179656 | tf_op jit(solution)/shard_map/ppermute | solution.py:141
  55.9 8.2 %collective-permute-start.17 = (bf16[2,384,128]{2,1,0:T(8,128)(2,1)S(1)}, bf16[2,384,128]{2,1,0:T(8,128)(2,1)S(1)}, u32[]{:S(2)}, u32[]{:S(2)}) collective-permute-start(bf16[2,384,128]{2,1,0:T(8,128)(2,1)S(1)} %fusion.1), channel_id=1, source_target_pairs={{0,2},{2,0},{1,3},{3,1},{4,6},{6,4},{5,7},{7,5},{8,10},{10,8},{9,1... | collective-permute-start | bytes 589832 | tf_op jit(solution)/shard_map/ppermute | solution.py:141
  64.1 5.7 %collective-permute-start.26 = (bf16[2,384,128]{2,1,0:T(8,128)(2,1)S(1)}, bf16[2,384,128]{2,1,0:T(8,128)(2,1)S(1)}, u32[]{:S(2)}, u32[]{:S(2)}) collective-permute-start(bf16[2,384,128]{2,1,0:T(8,128)(2,1)S(1)} %fusion), channel_id=1, source_target_pairs={{0,2},{2,0},{1,3},{3,1},{4,6},{6,4},{5,7},{7,5},{8,10},{10,8},{9,1... | collective-permute-start | bytes 589832 | tf_op jit(solution)/shard_map/ppermute | solution.py:141
  69.8 29.0 %copy-start.18 = (bf16[2,384,128]{2,1,0:T(8,128)(2,1)}, bf16[2,384,128]{2,1,0:T(8,128)(2,1)S(1)}, u32[]{:S(2)}) copy-start(bf16[2,384,128]{2,1,0:T(8,128)(2,1)S(1)} %collective-permute-done.26) | copy-start | bytes 589828
  69.8 5.5 %collective-permute-start.18 = (bf16[384,128]{1,0:T(8,128)(2,1)S(1)}, bf16[384,128]{1,0:T(8,128)(2,1)S(1)}, u32[]{:S(2)}, u32[]{:S(2)}) collective-permute-start(bf16[384,128]{1,0:T(8,128)(2,1)S(1)} %fusion.10), channel_id=1, source_target_pairs={{0,4},{4,0},{1,5},{5,1},{2,6},{6,2},{3,7},{7,3},{8,12},{12,8},{9,1... | collective-permute-start | bytes 294920 | tf_op jit(solution)/shard_map/ppermute | solution.py:141
  75.3 3.6 %collective-permute-start.27 = (bf16[384,128]{1,0:T(8,128)(2,1)S(1)}, bf16[384,128]{1,0:T(8,128)(2,1)S(1)}, u32[]{:S(2)}, u32[]{:S(2)}) collective-permute-start(bf16[384,128]{1,0:T(8,128)(2,1)S(1)} %fusion.11), channel_id=1, source_target_pairs={{0,4},{4,0},{1,5},{5,1},{2,6},{6,2},{3,7},{7,3},{8,12},{12,8},{9,1... | collective-permute-start | bytes 294920 | tf_op jit(solution)/shard_map/ppermute | solution.py:141
  78.8 5.3 %collective-permute-start.19 = (bf16[384,128]{1,0:T(8,128)(2,1)S(1)}, bf16[384,128]{1,0:T(8,128)(2,1)S(1)}, u32[]{:S(2)}, u32[]{:S(2)}) collective-permute-start(bf16[384,128]{1,0:T(8,128)(2,1)S(1)} %add_convert_fusion.12), channel_id=1, source_target_pairs={{0,8},{8,0},{1,9},{9,1},{2,10},{10,2},{3,11},{11,3},{4,12},{12,4},... | collective-permute-start | bytes 294920 | tf_op jit(solution)/shard_map/ppermute | solution.py:141
  84.2 6.8 %collective-permute-start.28 = (bf16[384,128]{1,0:T(8,128)(2,1)S(1)}, bf16[384,128]{1,0:T(8,128)(2,1)S(1)}, u32[]{:S(2)}, u32[]{:S(2)}) collective-permute-start(bf16[384,128]{1,0:T(8,128)(2,1)S(1)} %add_convert_fusion.9), channel_id=1, source_target_pairs={{0,8},{8,0},{1,9},{9,1},{2,10},{10,2},{3,11},{11,3},{4,12},{12,4},... | collective-permute-start | bytes 294920 | tf_op jit(solution)/shard_map/ppermute | solution.py:141
  84.3 8.1 %collective-permute-start.24 = (bf16[384,128]{1,0:T(8,128)(2,1)S(1)}, bf16[384,128]{1,0:T(8,128)(2,1)S(1)}, u32[]{:S(2)}, u32[]{:S(2)}) collective-permute-start(bf16[384,128]{1,0:T(8,128)(2,1)S(1)} %add_convert_fusion.11), channel_id=1, source_target_pairs={{0,2},{2,0},{1,3},{3,1},{4,6},{6,4},{5,7},{7,5},{8,10},{10,8},{9,1... | collective-permute-start | bytes 294920 | tf_op jit(solution)/shard_map/ppermute | solution.py:141
  91.0 7.8 %collective-permute-start.29 = (bf16[384,128]{1,0:T(8,128)(2,1)S(1)}, bf16[384,128]{1,0:T(8,128)(2,1)S(1)}, u32[]{:S(2)}, u32[]{:S(2)}) collective-permute-start(bf16[384,128]{1,0:T(8,128)(2,1)S(1)} %add_convert_fusion.8), channel_id=1, source_target_pairs={{0,2},{2,0},{1,3},{3,1},{4,6},{6,4},{5,7},{7,5},{8,10},{10,8},{9,1... | collective-permute-start | bytes 294920 | tf_op jit(solution)/shard_map/ppermute | solution.py:141
  92.6 7.3 %collective-permute-start.25 = (bf16[2,384,128]{2,1,0:T(8,128)(2,1)S(1)}, bf16[2,384,128]{2,1,0:T(8,128)(2,1)S(1)}, u32[]{:S(2)}, u32[]{:S(2)}) collective-permute-start(bf16[2,384,128]{2,1,0:T(8,128)(2,1)S(1)} %add_convert_fusion.5), channel_id=1, source_target_pairs={{0,1},{1,0},{2,3},{3,2},{4,5},{5,4},{6,7},{7,6},{8,9},{9,8},{10,11... | collective-permute-start | bytes 589832 | tf_op jit(solution)/shard_map/ppermute | solution.py:141
  103.1 18.2 %all-to-all-start.1 = ((bf16[16,192,128]{2,1,0:T(8,128)(2,1)}), bf16[16,192,128]{2,1,0:T(8,128)(2,1)}, u32[]{:S(2)}, u32[]{:S(2)}) async-start(bf16[16,192,128]{2,1,0:T(8,128)(2,1)} %bitcast.121), calls=%async_computation.1 | async-start | bytes 1572864 | tf_op jit(solution)/shard_map/all_to_all | solution.py:392
  110.6 1.7 collective-permute-start.30
  121.3 24.2 %all-to-all-start = ((bf16[16,192,128]{2,1,0:T(8,128)(2,1)}), bf16[16,192,128]{2,1,0:T(8,128)(2,1)}, u32[]{:S(2)}, u32[]{:S(2)}) async-start(bf16[16,192,128]{2,1,0:T(8,128)(2,1)} %bitcast.120), calls=%async_computation | async-start | bytes 1572864 | tf_op jit(solution)/shard_map/all_to_all | solution.py:392
  128.3 2.1 %collective-permute-start.31 = (bf16[1,128,1536]{2,1,0:T(8,128)(2,1)}, bf16[1,128,1536]{2,1,0:T(8,128)(2,1)}, u32[]{:S(2)}, u32[]{:S(2)}) collective-permute-start(bf16[1,128,1536]{2,1,0:T(8,128)(2,1)} %bitcast.115), channel_id=1, source_target_pairs={{0,1},{1,0},{2,3},{3,2},{4,5},{5,4},{6,7},{7,6},{8,9},{9,8},{10,11... | collective-permute-start | bytes 1179656 | tf_op jit(solution)/shard_map/ppermute | solution.py:141
  128.6 2.3 %collective-permute-start.32 = (bf16[1,128,1536]{2,1,0:T(8,128)(2,1)}, bf16[1,128,1536]{2,1,0:T(8,128)(2,1)}, u32[]{:S(2)}, u32[]{:S(2)}) collective-permute-start(bf16[1,128,1536]{2,1,0:T(8,128)(2,1)} %bitcast.13.refs_1_), channel_id=1, source_target_pairs={{0,1},{1,0},{2,3},{3,2},{4,5},{5,4},{6,7},{7,6},{8,9},{9,8},{10,11... | collective-permute-start | bytes 1179656 | tf_op jit(solution)/shard_map/ppermute | solution.py:141
  128.8 3.2 %collective-permute-start.33 = (bf16[1,128,1536]{2,1,0:T(8,128)(2,1)}, bf16[1,128,1536]{2,1,0:T(8,128)(2,1)}, u32[]{:S(2)}, u32[]{:S(2)}) collective-permute-start(bf16[1,128,1536]{2,1,0:T(8,128)(2,1)} %copy-done.20), channel_id=1, source_target_pairs={{0,1},{1,0},{2,3},{3,2},{4,5},{5,4},{6,7},{7,6},{8,9},{9,8},{10,11... | collective-permute-start | bytes 1179656 | tf_op jit(solution)/shard_map/ppermute | solution.py:141
  129.2 4.1 %collective-permute-start.34 = (bf16[1,128,1536]{2,1,0:T(8,128)(2,1)}, bf16[1,128,1536]{2,1,0:T(8,128)(2,1)S(1)}, u32[]{:S(2)}, u32[]{:S(2)}) collective-permute-start(bf16[1,128,1536]{2,1,0:T(8,128)(2,1)} %copy-done.21), channel_id=1, source_target_pairs={{0,1},{1,0},{2,3},{3,2},{4,5},{5,4},{6,7},{7,6},{8,9},{9,8},{10,11... | collective-permute-start | bytes 1179656 | tf_op jit(solution)/shard_map/ppermute | solution.py:141
  129.3 3.9 %collective-permute-start.35 = (bf16[1,128,1536]{2,1,0:T(8,128)(2,1)}, bf16[1,128,1536]{2,1,0:T(8,128)(2,1)S(1)}, u32[]{:S(2)}, u32[]{:S(2)}) collective-permute-start(bf16[1,128,1536]{2,1,0:T(8,128)(2,1)} %copy-done.22), channel_id=1, source_target_pairs={{0,1},{1,0},{2,3},{3,2},{4,5},{5,4},{6,7},{7,6},{8,9},{9,8},{10,11... | collective-permute-start | bytes 1179656 | tf_op jit(solution)/shard_map/ppermute | solution.py:141
  130.4 2.9 %collective-permute-start.36 = (bf16[1,128,1536]{2,1,0:T(8,128)(2,1)}, bf16[1,128,1536]{2,1,0:T(8,128)(2,1)S(1)}, u32[]{:S(2)}, u32[]{:S(2)}) collective-permute-start(bf16[1,128,1536]{2,1,0:T(8,128)(2,1)} %copy-done.23), channel_id=1, source_target_pairs={{0,1},{1,0},{2,3},{3,2},{4,5},{5,4},{6,7},{7,6},{8,9},{9,8},{10,11... | collective-permute-start | bytes 1179656 | tf_op jit(solution)/shard_map/ppermute | solution.py:141
  130.9 2.7 %collective-permute-start.37 = (bf16[1,128,1536]{2,1,0:T(8,128)(2,1)}, bf16[1,128,1536]{2,1,0:T(8,128)(2,1)S(1)}, u32[]{:S(2)}, u32[]{:S(2)}) collective-permute-start(bf16[1,128,1536]{2,1,0:T(8,128)(2,1)} %copy-done.24), channel_id=1, source_target_pairs={{0,1},{1,0},{2,3},{3,2},{4,5},{5,4},{6,7},{7,6},{8,9},{9,8},{10,11... | collective-permute-start | bytes 1179656 | tf_op jit(solution)/shard_map/ppermute | solution.py:141
  132.0 2.1 %collective-permute-start.38 = (bf16[1,128,1536]{2,1,0:T(8,128)(2,1)}, bf16[1,128,1536]{2,1,0:T(8,128)(2,1)S(1)}, u32[]{:S(2)}, u32[]{:S(2)}) collective-permute-start(bf16[1,128,1536]{2,1,0:T(8,128)(2,1)} %copy-done.25), channel_id=1, source_target_pairs={{0,1},{1,0},{2,3},{3,2},{4,5},{5,4},{6,7},{7,6},{8,9},{9,8},{10,11... | collective-permute-start | bytes 1179656 | tf_op jit(solution)/shard_map/ppermute | solution.py:141
  142.0 19.4 %collective-permute-start.40 = (bf16[192,1536]{1,0:T(8,128)(2,1)}, bf16[192,1536]{1,0:T(8,128)(2,1)}, u32[]{:S(2)}, u32[]{:S(2)}) collective-permute-start(bf16[192,1536]{1,0:T(8,128)(2,1)} %get-tuple-element.81), channel_id=1, source_target_pairs={{8,0},{9,1},{10,2},{11,3},{12,4},{13,5},{14,6},{15,7},{24,16},{25,... | collective-permute-start | bytes 1769480 | tf_op jit(solution)/shard_map/ppermute | solution.py:395
  152.5 31.0 %collective-permute-start.39 = (bf16[192,1536]{1,0:T(8,128)(2,1)}, bf16[192,1536]{1,0:T(8,128)(2,1)S(1)}, u32[]{:S(2)}, u32[]{:S(2)}) collective-permute-start(bf16[192,1536]{1,0:T(8,128)(2,1)} %get-tuple-element.79), channel_id=1, source_target_pairs={{0,8},{1,9},{2,10},{3,11},{4,12},{5,13},{6,14},{7,15},{16,24},{17,... | collective-permute-start | bytes 1769480 | tf_op jit(solution)/shard_map/ppermute | solution.py:395
  157.7 25.9 %copy-start.32 = (f32[192,1536]{1,0:T(8,128)S(1)}, f32[192,1536]{1,0:T(8,128)}, u32[]{:S(2)}) copy-start(f32[192,1536]{1,0:T(8,128)} %get-tuple-element.80) | copy-start | bytes 3538948
  157.7 25.9 %copy-start.33 = (f32[192,1536]{1,0:T(8,128)S(1)}, f32[192,1536]{1,0:T(8,128)}, u32[]{:S(2)}) copy-start(f32[192,1536]{1,0:T(8,128)} %get-tuple-element.78) | copy-start | bytes 3538948
  (33 other events, 200.4 us)

commit v3 on v0

v3 whole, which is shorter than its diff:
```python
import functools

import jax
import jax.numpy as jnp
from jax import lax
from jax.experimental import pallas as pl
from jax.experimental.pallas import tpu as pltpu
from jax.sharding import PartitionSpec as P

HEAD_DIM = 128
EPSILON = 1e-05
VMEM_MIB = 56
F32 = jnp.float32
BF16 = jnp.bfloat16

NN = (((1,), (0,)), ((), ()))
NT = (((1,), (1,)), ((), ()))
TN = (((0,), (0,)), ((), ()))


def dot(a, b, dims):
    return lax.dot_general(a, b, dims, preferred_element_type=F32)


def slope(values):
    wide = values.astype(F32)
    return jnp.where(wide > 0, 1.0, jnp.exp(jnp.minimum(wide, 0.0)))


def feature(values):
    wide = values.astype(F32)
    return jnp.where(wide > 0, wide + 1.0, jnp.exp(jnp.minimum(wide, 0.0))).astype(BF16)


def causal_scores(rows, columns):
    scores = dot(rows, columns, NT)
    t = lax.broadcasted_iota(jnp.int32, scores.shape, 0)
    s = lax.broadcasted_iota(jnp.int32, scores.shape, 1)
    return jnp.where(s <= t, scores, 0.0).astype(BF16)


def causal_scores_turned(rows, columns):
    scores = dot(columns, rows, NT)
    s = lax.broadcasted_iota(jnp.int32, scores.shape, 0)
    t = lax.broadcasted_iota(jnp.int32, scores.shape, 1)
    return jnp.where(s <= t, scores, 0.0).astype(BF16)


def block_state_head(at, k_ref, v_ref, state_ref):
    state_ref[at, :] = dot(feature(k_ref[:, at]), v_ref[:, at], TN).astype(BF16)


def local_output_head(at, q_ref, k_ref, v_ref, local_ref):
    scores = causal_scores(feature(q_ref[:, at]), feature(k_ref[:, at]))
    local_ref[:, at] = dot(scores, v_ref[:, at], NN)


def assemble(at, flags_ref, other_ref, quarter_refs, state_ref):
    size = quarter_refs[0].shape[0]
    quarter, start = divmod(at.start, size)
    near = flags_ref[0] == quarter // 2
    same = flags_ref[1] == quarter % 2
    own, other, swapped_own, swapped_other = [ref[start : start + HEAD_DIM, :] for ref in quarter_refs]
    total = jnp.where(same, jnp.where(near, own, swapped_own), jnp.where(near, other, swapped_other))
    total = added_if(flags_ref[2] == 1, total, other_ref[at, :])
    state_ref[at, :] = total
    return total


def grad_output_head(at, flags_ref, q_ref, local_ref, upstream_ref, other_ref, *refs):
    *quarter_refs, grad_ref, block_ref, state_ref = refs
    state = assemble(at, flags_ref, other_ref, quarter_refs, state_ref)
    query = feature(q_ref[:, at])
    output = local_ref[:, at] + dot(query, state, NN)
    inverse_rms = lax.rsqrt(jnp.mean(output * output, axis=-1, keepdims=True) + EPSILON)
    normed = output * inverse_rms
    upstream = upstream_ref[:, at].astype(F32)
    projection = jnp.mean(upstream * normed, axis=-1, keepdims=True)
    grad = (inverse_rms * (upstream - normed * projection)).astype(BF16)
    grad_ref[:, at] = grad
    block_ref[at, :] = dot(query, grad, TN).astype(BF16)


def key_local_head(at, q_ref, v_ref, grad_ref, key_out):
    grad_scores = causal_scores_turned(grad_ref[:, at], v_ref[:, at])
    key_out[:, at] = dot(grad_scores, feature(q_ref[:, at]), NN)


def key_grad_head(at, flags_ref, k_ref, v_ref, local_ref, other_ref, *refs):
    *quarter_refs, key_out, turned_out, state_ref = refs
    cuts, copies, devices, halves, rows, tokens = turned_out.shape
    state = assemble(at, flags_ref, other_ref, quarter_refs, state_ref)
    key = local_ref[:, at] + dot(v_ref[:, at], state, NT)
    key = (key * slope(k_ref[:, at])).astype(BF16)
    key_out[:, at] = key
    turned = key.T
    start = at.start
    while start < at.stop:
        block, row = divmod(start, rows)
        size = min(rows - row, at.stop - start)
        owner, cut = divmod(block, cuts)
        half, device = divmod(owner, devices)
        for copy in range(copies):
            turned_out[cut, copy, device, half, row : row + size] = turned[start - at.start : start - at.start + size]
        start += size


def other_grads_head(at, q_ref, k_ref, v_ref, grad_ref, state_ref, later_ref, query_out, value_out):
    grad = grad_ref[:, at]
    key = feature(k_ref[:, at])
    grad_scores = causal_scores(grad, v_ref[:, at])
    query = dot(grad_scores, key, NN) + dot(grad, state_ref[at, :], NT)
    query_out[:, at] = (query * slope(q_ref[:, at])).astype(BF16)
    scores = causal_scores_turned(feature(q_ref[:, at]), key)
    value = dot(scores, grad, NN) + dot(key, later_ref[at, :], NN)
    value_out[:, at] = value.astype(BF16)


def by_heads(head, operands, outs, matmuls, flags=None, vmem=12):
    tokens, features = operands[0][1].shape
    groups = 2 if features % (2 * HEAD_DIM) == 0 else 1
    group = features // groups
    shapes = {"row": (tokens, features), "state": (features, HEAD_DIM)}
    shapes_held = {"held row": shapes["row"], "held state": shapes["state"]}
    kinds = [kind for kind, _ in operands] + [kind for kind, _ in outs]
    results = [
        jax.ShapeDtypeStruct(shapes.get(kind) or shapes_held.get(kind, kind), dtype) for kind, dtype in outs
    ]
    held = [kind == "held" or kind in shapes_held for kind in kinds]
    arrays = [array for _, array in operands] + results
    count = len(operands)

    def part(kind, ref, index):
        cut = pl.ds(index * group, group)
        return ref.at[:, cut] if kind == "row" else ref.at[cut, :]

    def body(*refs):
        numbers = [] if flags is None else [refs[0]]
        refs = refs[len(numbers) :]
        there, moved = refs[: len(kinds)], refs[-1]
        scratch = iter(refs[len(kinds) : -1])
        here = [ref if stays else next(scratch) for stays, ref in zip(held, there)]

        def copy(index, step):
            source, target = (there, here) if index < count else (here, there)
            source, target = source[index], target[index]
            if kinds[index] in shapes:
                source, target = part(kinds[index], source, step), part(kinds[index], target, step)
            return pltpu.make_async_copy(source, target, moved.at[index, step])

        def at_once(index, step):
            return step == (0 if index < count else groups - 1)

        def due(step, indices):
            moving = [index for index in indices if not held[index]]
            return [index for index in moving if kinds[index] in shapes or at_once(index, step)]

        ins, outputs = range(count), range(count, len(kinds))
        for step in range(groups):
            for index in due(step, ins):
                copy(index, step).start()
        for step in range(groups):
            for index in due(step, ins):
                copy(index, step).wait()
            for start in range(step * group, (step + 1) * group, HEAD_DIM):
                head(slice(start, start + HEAD_DIM), *numbers, *here)
            for index in due(step, outputs):
                copy(index, step).start()
        for step in range(groups):
            for index in due(step, outputs):
                copy(index, step).wait()

    anywhere = pl.BlockSpec(memory_space=pl.ANY)
    places = [pl.BlockSpec(memory_space=pltpu.VMEM) if stays else anywhere for stays in held]
    return pl.pallas_call(
        body,
        in_specs=([] if flags is None else [pl.BlockSpec(memory_space=pltpu.SMEM)]) + places[:count],
        out_specs=places[count:],
        out_shape=results,
        scratch_shapes=[
            pltpu.VMEM(array.shape, array.dtype) for stays, array in zip(held, arrays) if not stays
        ]
        + [pltpu.SemaphoreType.DMA((len(kinds), groups))],
        compiler_params=pltpu.CompilerParams(vmem_limit_bytes=vmem * 1024 * 1024),
        cost_estimate=pl.CostEstimate(
            flops=2 * matmuls * tokens * features * HEAD_DIM,
            bytes_accessed=tokens * features * 2 * len(kinds),
            transcendentals=0,
        ),
    )(*([] if flags is None else [flags]), *[array for _, array in operands])


def swap(array, axis):
    return lax.ppermute(array, axis, [(0, 1), (1, 0)])


def added_if(flag, a, b):
    return (a.astype(F32) + jnp.where(flag, b.astype(F32), 0.0)).astype(BF16)


def small(body, flags, arrays, outs):
    vmem = pl.BlockSpec(memory_space=pltpu.VMEM)
    result = jax.ShapeDtypeStruct(arrays[-1].shape[-2:], BF16)

    def kernel(*refs):
        values = body(*refs[: 1 + len(arrays)])
        for ref, value in zip(refs[1 + len(arrays) :], values):
            ref[...] = value

    return pl.pallas_call(
        kernel,
        in_specs=[pl.BlockSpec(memory_space=pltpu.SMEM)] + [vmem] * len(arrays),
        out_specs=[vmem] * outs,
        out_shape=[result] * outs,
        compiler_params=pltpu.CompilerParams(vmem_limit_bytes=4 * 1024 * 1024),
        cost_estimate=pl.CostEstimate(flops=0, bytes_accessed=1024, transcendentals=0),
    )(flags, *arrays)


def after(array, *others):
    if not others:
        return array
    return lax.optimization_barrier((array,) + others)[0]


class Scan:
    def __init__(self, state, bits, backward):
        first, second, *self.rest = bits
        self.first, self.second = first, second
        after = 0 if backward else 1
        place = [lax.axis_index(bit) for bit in bits]
        self.flags = jnp.stack([*place, *[(at == after).astype(jnp.int32) for at in place]])
        self.counts = len(bits)
        state = state.reshape(2, 2, -1, HEAD_DIM)
        self.other = swap(state, first)

        def quarters(flags, state, other):
            core, side = flags[0], flags[1]
            return [added_if(True, state[core, at], other[core, at]) for at in (1 - side, side)]

        self.theirs, self.mine = small(quarters, self.flags, [state, self.other], 2)
        self.arrived = swap(self.theirs, second)

    def spread(self, due, meanwhile):
        counts = self.counts
        self.arrived = after(self.arrived, *due)

        def start(flags, mine, arrived):
            return [added_if(True, mine[...], arrived[...])]

        (total,) = small(start, self.flags, [self.mine, self.arrived], 1)
        self.rest_arrived = swap(after(self.mine, self.arrived), self.second)
        before = None
        for index, bit in enumerate(self.rest, 2):
            last = bit == self.rest[-1]
            pieces = meanwhile(total) if last else [self.rest_arrived]
            arrived = after(swap(total, bit), *pieces)

            def first(flags, total, arrived):
                values = arrived[...], total[...]
                return [jnp.where(flags[counts + 2] == 1, values[0], 0.0), added_if(True, *values)]

            def middle(flags, total, arrived, before):
                value = added_if(flags[counts + index] == 1, before[...], arrived[...])
                return [value, added_if(True, total[...], arrived[...])]

            def final(flags, side, arrived, before):
                value = added_if(flags[counts + index] == 1, before[...], arrived[...])
                return [value, added_if(flags[counts + 1] == 1, value, side[...])]

            if before is None:
                before, total = small(first, self.flags, [total, arrived], 2)
            elif not last:
                before, total = small(middle, self.flags, [total, arrived, before], 2)
            else:
                self.before, self.own = small(final, self.flags, [self.arrived, arrived, before], 2)

    def collect(self):
        counts = self.counts

        def finish(flags, swapped, rest):
            return [added_if(flags[counts + 1] == 1, swapped[...], rest[...])]

        arrays = [swap(self.before, self.second), self.rest_arrived]
        (other,) = small(finish, self.flags, arrays, 1)
        quarters = [self.own, other, swap(self.own, self.first), swap(other, self.first)]
        self.kinds = jnp.stack([self.flags[0], self.flags[1], self.flags[counts]])
        self.operands = [("whole", self.other.reshape(-1, HEAD_DIM))]
        self.operands += [("held", quarter) for quarter in quarters]


def sides_kernel(which_ref, in_ref, own_ref, gone_ref):
    columns = own_ref.shape[1]

    @pl.when(which_ref[0] == 0)
    def _():
        own_ref[...] = in_ref[:, :columns]
        gone_ref[...] = in_ref[:, columns:]

    @pl.when(which_ref[0] == 1)
    def _():
        own_ref[...] = in_ref[:, columns:]
        gone_ref[...] = in_ref[:, :columns]


def sides(array, which):
    rows, columns = array.shape
    tile = rows // 4
    out = jax.ShapeDtypeStruct((rows, columns // 2), array.dtype)
    return pl.pallas_call(
        sides_kernel,
        grid_spec=pltpu.PrefetchScalarGridSpec(
            num_scalar_prefetch=1,
            grid=(rows // tile,),
            in_specs=[pl.BlockSpec((tile, columns), lambda i, which: (i, 0))],
            out_specs=[pl.BlockSpec((tile, columns // 2), lambda i, which: (i, 0))] * 2,
        ),
        out_shape=[out, out],
        compiler_params=pltpu.CompilerParams(vmem_limit_bytes=6 * 1024 * 1024),
        cost_estimate=pl.CostEstimate(flops=0, bytes_accessed=4 * array.size, transcendentals=0),
    )(jnp.reshape(which, (1,)).astype(jnp.int32), array)


def weight_kernel(order_ref, turned_ref, *refs):
    *held, kept_ref, sent_ref, total_ref, buffer_ref, arrival = refs
    sources, _, tokens = turned_ref.shape
    others, rows, columns = sent_ref.shape
    copies, at = [], 0
    for index, ref in enumerate(held):
        count = ref.shape[0]
        copies.append(pltpu.make_async_copy(ref, buffer_ref.at[at : at + count], arrival.at[index]))
        copies[-1].start()
        at += count
    per_step, tile = 4, 512 if columns % 512 == 0 else columns
    steps = sources // per_step
    for step in range(steps):
        for copy in copies[step * len(copies) // steps : (step + 1) * len(copies) // steps]:
            copy.wait()
        first = step * per_step
        lhs = jnp.concatenate([turned_ref[order_ref[first + i]] for i in range(per_step)], axis=1)
        for start in range(0, columns, tile):
            cut = slice(start, start + tile)
            rhs = buffer_ref[first : first + per_step, :, cut].reshape(per_step * tokens, tile)
            product = dot(lhs, rhs, NN)
            total_ref[:, cut] = product if step == 0 else total_ref[:, cut] + product
    span = order_ref[sources]
    kept_ref[...] = total_ref[pl.ds(pl.multiple_of(span * rows, 16), rows), :]
    for turn in range(others):
        target = lax.rem(span + turn + 1, others + 1)
        sent_ref[turn] = total_ref[pl.ds(pl.multiple_of(target * rows, 16), rows), :].astype(BF16)


def weight_part(order, turned, inputs, halves):
    sources, rows, tokens = turned.shape
    columns = inputs[0].shape[-1]
    vmem = pl.BlockSpec(memory_space=pltpu.VMEM)
    return pl.pallas_call(
        weight_kernel,
        in_specs=[pl.BlockSpec(memory_space=pltpu.SMEM), vmem]
        + [pl.BlockSpec(memory_space=pl.ANY)] * len(inputs),
        out_specs=[vmem, vmem],
        out_shape=[
            jax.ShapeDtypeStruct((rows // halves, columns), F32),
            jax.ShapeDtypeStruct((halves - 1, rows // halves, columns), BF16),
        ],
        scratch_shapes=[
            pltpu.VMEM((rows, columns), F32),
            pltpu.VMEM((sources, tokens, columns), BF16),
            pltpu.SemaphoreType.DMA((len(inputs),)),
        ],
        compiler_params=pltpu.CompilerParams(vmem_limit_bytes=VMEM_MIB * 1024 * 1024),
        cost_estimate=pl.CostEstimate(
            flops=2 * sources * tokens * rows * columns,
            bytes_accessed=sources * tokens * columns * 2 + rows * columns * 6,
            transcendentals=0,
        ),
    )(order, turned, *inputs)


def shards(layer_input, query_rows, key_rows, value_rows, out_grad, bits):
    query, key, value, upstream = query_rows[0], key_rows[0], value_rows[0], out_grad[0]
    tokens, features = query.shape
    sequences = lax.axis_size("dp")
    places = 2 ** len(bits)
    core, side, layer, *high = bits
    spans = tuple(reversed(high))
    halves = places // 8
    cuts = 2
    rows = features // places // cuts

    mine = lax.axis_index("dp")
    if sequences == 2:
        own, gone = sides(layer_input[0], mine)
        own, far = own[None], swap(gone, "dp")[None]
        own_id, far_id = mine[None], 1 - mine[None]
    else:
        wide = lax.all_to_all(layer_input[0].reshape(tokens, sequences, -1), "dp", 1, 0)
        own, far = wide[: sequences // 2], wide[sequences // 2 :]
        own_id, far_id = jnp.split(jnp.arange(sequences), 2)
    own_layer = swap(own, layer)

    (block_state,) = by_heads(block_state_head, [("row", key), ("row", value)], [("held state", BF16)], 1)
    forward = Scan(block_state, bits, False)
    (output,) = by_heads(
        local_output_head,
        [("held", after(query, forward.mine)), ("held", key), ("held", value)],
        [("held row", F32)],
        2,
    )
    far_side = []

    def along_side(token):
        far_side.append(swap(after(far, token), side))
        return far_side

    forward.spread([output, far, own_layer], along_side)
    forward.collect()
    far_layer = swap(after(far, forward.before), layer)
    grad_output, block_grad, state_in = by_heads(
        grad_output_head,
        [("held", query), ("held", output), ("held", upstream), *forward.operands],
        [("held row", BF16), ("held state", BF16), ("state", BF16)],
        2,
        after(forward.kinds, far_layer),
    )
    backward = Scan(block_grad, bits, True)
    (key_local,) = by_heads(
        key_local_head,
        [("held", query), ("held", value), ("held", after(grad_output, backward.mine))],
        [("held row", F32)],
        2,
    )
    far_both = swap(after(far_side[0], backward.mine), layer)
    own_side = []

    def along_side_again(token):
        own_side.append(swap(after(own, token), side))
        return own_side

    backward.spread([key_local, far_both], along_side_again)
    backward.collect()
    own_both = swap(after(own_side[0], backward.before), layer)
    key_grad, turned, grad_in = by_heads(
        key_grad_head,
        [("held", key), ("held", value), ("held", key_local), *backward.operands],
        [("row", BF16), ((cuts, sequences, 8, halves, rows, tokens), BF16), ("state", BF16)],
        1,
        backward.kinds,
    )
    turned = after(turned, own_both)
    held, order = [], []
    for array, ids, layered, sided in (
        (own, own_id, 0, 0),
        (far, far_id, 0, 0),
        (own_layer, own_id, 1, 0),
        (far_layer, far_id, 1, 0),
        (far_side[0], far_id, 0, 1),
        (far_both, far_id, 1, 1),
        (own_side[0], own_id, 0, 1),
        (own_both, own_id, 1, 1),
    ):
        held.append(array)
        order.append(8 * ids + 4 * (lax.axis_index(layer) ^ layered) + 2 * (lax.axis_index(side) ^ sided))
    held += [swap(array, core) for array in held]
    at = lax.axis_index(core)
    span = lax.axis_index(spans)
    order = jnp.concatenate([ids + at for ids in order] + [ids + 1 - at for ids in order] + [span[None]])
    order = order.astype(jnp.int32)

    sums, done = [], turned
    for cut in range(cuts):
        part = turned[cut].reshape(sequences * 8, halves * rows, tokens)
        part = lax.all_to_all(part, ("dp", layer, side, core), 0, 0, tiled=True)
        total, sent = weight_part(order, after(part, done), held, halves)
        for turn in range(1, halves):
            moved = lax.ppermute(sent[turn - 1], spans, [(i, (i + turn) % halves) for i in range(halves)])
            total += moved.astype(F32)
        done = sent
        sums.append(total)
    weight_grad = jnp.concatenate(sums) * (sequences * places * tokens) ** (-0.5)
    query_grad, value_grad = by_heads(
        other_grads_head,
        [
            ("held", query),
            ("held", key),
            ("held", value),
            ("held", after(grad_output, done)),
            ("state", state_in),
            ("state", grad_in),
        ],
        [("row", BF16), ("row", BF16)],
        6,
    )
    return (query_grad[None], key_grad[None], value_grad[None], weight_grad)


def solution(mesh):
    sequences, places = mesh.shape["dp"], mesh.shape["ctx"]
    bits = tuple(f"bit{i}" for i in range(places.bit_length() - 1))
    ctx = tuple(reversed(bits))
    devices = mesh.devices.reshape((sequences,) + (2,) * len(bits))
    rows = P("dp", ctx, None)
    return jax.shard_map(
        functools.partial(shards, bits=bits),
        mesh=jax.sharding.Mesh(devices, ("dp",) + ctx),
        in_specs=(rows,) * 5,
        out_specs=(rows, rows, rows, P(ctx, "dp")),
        check_vma=False,
    )
```

time: 510 us -> 170 us (0.33)
  waiting for transfers between devices: 414 us -> 68.9 us
  Pallas kernels: 0 us -> 42.8 us
  matrix products: 31.9 us -> 0 us
  starting transfers between devices: 0.34 us -> 29.7 us
  other arithmetic: 28.2 us -> 1.36 us
  blocking collectives: 0 us -> 16.7 us
  between operations: 14 us -> 0.97 us
  local copies, waits for them, and re-layouts: 19.5 us -> 8.64 us
    all_gather x2 -> x0, waiting for transfers between devices: 215 us -> none  [prefix(): gathered = lax.all_gather(array.astype(jnp.bfloat16), axis)]
    reduce_scatter x2 -> x0, waiting for transfers between devices: 199 us -> none  [the longest x1 192 us: shards(): lax.psum_scatter(lax.dot_general(key_flat, input_flat, contract, preferre...]
    ppermute x0 -> x33, waiting for transfers between devices: none -> 68.9 us  [the longest x31 55.2 us: swap(): return lax.ppermute(array, axis, [(0, 1), (1, 0)])]
    pallas_call x0 -> x19, Pallas kernels: none -> 42.8 us  [the longest x6 22.6 us: by_heads(): pl.pallas_call(body, in_specs=([] if flags is None else [pl.BlockSpec(mem...]
    dot_general x13 -> x0, matrix products: 31.9 us -> none  [the longest x1 9.06 us: shards(): lax.dot_general(key_flat, input_flat, contract, preferred_element_type=jn...]
    ppermute x0 -> x33, starting transfers between devices: none -> 25.1 us  [the longest x31 21.4 us: swap(): return lax.ppermute(array, axis, [(0, 1), (1, 0)])]
    add x15 -> x2, other arithmetic: 22.5 us -> 0.1 us  [shards(): total += moved.astype(F32)]
    all_to_all x0 -> x1, blocking collectives: none -> 16.7 us  [shards(): part = lax.all_to_all(part, ('dp', layer, side, core), 0, 0, tiled=True)]
  transfers between devices with their start and end apart: 4 -> 34, of which waited for: 4 -> 23; matrix products, arithmetic and copies ran while one was open for 5% -> 1% of each run, Pallas kernels for 0% -> 19%
where the time goes in v3:
time: 170 us; the launch traced here: 169 us
  waiting for transfers between devices  68.9 us (41%)
  Pallas kernels  42.8 us (25%)
  starting transfers between devices  29.7 us (17%)
  blocking collectives  16.7 us (10%)
  local copies, waits for them, and re-layouts  8.64 us (5%)
    ppermute x31, waiting for transfers between devices, swap(): return lax.ppermute(array, axis, [(0, 1), (1, 0)])  55.2 us
    pallas_call x6, Pallas kernels, by_heads(): pl.pallas_call(body, in_specs=([] if flags is None else [pl.BlockSpec(mem...  22.6 us
    ppermute x31, starting transfers between devices, swap(): return lax.ppermute(array, axis, [(0, 1), (1, 0)])  21.4 us
    all_to_all x1, blocking collectives, shards(): part = lax.all_to_all(part, ('dp', layer, side, core), 0, 0, tiled=True)  16.7 us
    ppermute x2, waiting for transfers between devices, shards(): lax.ppermute(sent[turn - 1], spans, [(i, (i + turn) % halves) for i in ra...  13.7 us
    pallas_call x2, Pallas kernels, weight_part(): pl.pallas_call(weight_kernel, in_specs=[pl.BlockSpec(memory_space=pltpu.S...  11.3 us
    pallas_call x10, Pallas kernels, small(): pl.pallas_call(kernel, in_specs=[pl.BlockSpec(memory_space=pltpu.SMEM)] +...  7.44 us
    unnamed x54, local copies, waits for them, and re-layouts  6.8 us
  transfers between devices with their start and end apart: 34, of which 23 were waited for; matrix products, arithmetic and copies ran while one was open for 1% of the time, Pallas kernels for 19%

profile of v3, /device:TPU:0, one launch (start us, length us, event | category | flops | bytes accessed | tf_op | source)
XLA Modules:
  0.0 169.0 jit_solution(6252999681260973573)
XLA Ops:
  0.6 1.1 copy-done
  1.8 1.1 copy-done.2
  2.9 1.9 %shard_map.85 = bf16[3072,128]{1,0:T(8,128)(2,1)} custom-call(bf16[128,3072]{1,0:T(8,128)(2,1)S(1)} %bitcast.40, bf16[128,3072]{1,0:T(8,128)(2,1)S(1)} %bitcast.35), custom_call_target="tpu_custom_call" | custom-call | flops 100663296 | bytes 2359296 | tf_op jit(solution)/shard_map/pallas_call | solution.py:175
  5.3 1.1 copy-done.14
  6.5 1.4 shard_map.84
  7.8 2.6 %collective-permute-start.3 = (bf16[1,128,1536]{2,1,0:T(8,128)(2,1)S(1)}, bf16[1,128,1536]{2,1,0:T(8,128)(2,1)}, u32[]{:S(2)}, u32[]{:S(2)}) collective-permute-start(bf16[1,128,1536]{2,1,0:T(8,128)(2,1)S(1)} %bitcast.50), channel_id=1, source_target_pairs={{0,4},{4,0},{1,5},{5,1},{2,6},{6,2},{3,7},{7,3},{8,12},{12,8},{9,1... | collective-permute-start | bytes 1179656 | tf_op jit(solution)/shard_map/ppermute | solution.py:194
  10.4 1.5 collective-permute-start
  12.0 1.2 shard_map.86
  13.3 1.6 collective-permute-start.2
  14.8 3.9 %shard_map.87.refs_2_ = f32[128,3072]{1,0:T(8,128)S(1)} custom-call(bf16[128,3072]{1,0:T(8,128)(2,1)S(1)} %bitcast.44, bf16[128,3072]{1,0:T(8,128)(2,1)S(1)} %bitcast.41, bf16[128,3072]{1,0:T(8,128)(2,1)S(1)} %bitcast.36), custom_call_target="tpu_custom_call" | custom-call | flops 201326592 | bytes 3145728 | tf_op jit(solution)/shard_map/pallas_call | solution.py:175
  18.7 1.6 collective-permute-done.3.refs_2_
  20.3 1.7 collective-permute-done
  22.6 1.6 collective-permute-start.5
  24.6 4.3 %collective-permute-done.5.refs_2_ = bf16[768,128]{1,0:T(8,128)(2,1)S(1)} collective-permute-done((bf16[768,128]{1,0:T(8,128)(2,1)S(1)}, bf16[768,128]{1,0:T(8,128)(2,1)S(1)}, u32[]{:S(2)}, u32[]{:S(2)}) %collective-permute-start.5) | collective-permute-done | bytes 196640 | tf_op jit(solution)/shard_map/ppermute | solution.py:194
  28.8 1.2 collective-permute-done.4.refs_2_
  31.3 2.6 %collective-permute-start.6 = (bf16[768,128]{1,0:T(8,128)(2,1)S(1)}, bf16[768,128]{1,0:T(8,128)(2,1)S(1)}, u32[]{:S(2)}, u32[]{:S(2)}) collective-permute-start(bf16[768,128]{1,0:T(8,128)(2,1)S(1)} %get-tuple-element.58), channel_id=1, source_target_pairs={{0,8},{8,0},{1,9},{9,1},{2,10},{10,2},{3,11},{11,3},{4,12},{12,4},... | collective-permute-start | bytes 589832 | tf_op jit(solution)/shard_map/ppermute | solution.py:194
  33.9 7.3 %collective-permute-done.6.refs_2_ = bf16[768,128]{1,0:T(8,128)(2,1)S(1)} collective-permute-done((bf16[768,128]{1,0:T(8,128)(2,1)S(1)}, bf16[768,128]{1,0:T(8,128)(2,1)S(1)}, u32[]{:S(2)}, u32[]{:S(2)}) %collective-permute-start.6) | collective-permute-done | bytes 196640 | tf_op jit(solution)/shard_map/ppermute | solution.py:194
  41.9 1.4 collective-permute-start.9
  43.3 4.6 %collective-permute-done.9.refs_1_ = bf16[768,128]{1,0:T(8,128)(2,1)S(1)} collective-permute-done((bf16[768,128]{1,0:T(8,128)(2,1)S(1)}, bf16[768,128]{1,0:T(8,128)(2,1)S(1)}, u32[]{:S(2)}, u32[]{:S(2)}) %collective-permute-start.9) | collective-permute-done | bytes 196640 | tf_op jit(solution)/shard_map/ppermute | solution.py:194
  48.7 3.6 %collective-permute-done.8.refs_3_ = bf16[1,128,1536]{2,1,0:T(8,128)(2,1)S(1)} collective-permute-done((bf16[1,128,1536]{2,1,0:T(8,128)(2,1)}, bf16[1,128,1536]{2,1,0:T(8,128)(2,1)S(1)}, u32[]{:S(2)}, u32[]{:S(2)}) %collective-permute-start.8) | collective-permute-done | bytes 393248 | tf_op jit(solution)/shard_map/ppermute | solution.py:194
  52.3 4.2 %shard_map.92 = (bf16[128,3072]{1,0:T(8,128)(2,1)S(1)}, bf16[3072,128]{1,0:T(8,128)(2,1)}, bf16[3072,128]{1,0:T(8,128)(2,1)S(1)}) custom-call(s32[3]{0:T(128)S(1)} %pad_add_fusion.refs_0_, bf16[128,3072]{1,0:T(8,128)(2,1)S(1)} %bitcast.45, f32[128,3072]{1,0:T(8,128)S(1)} %shard_map.87.refs_2_, bf16[128,3072]{1,0:T(8,128)(2,1)S(1)} %bitcast.55, ...), custom_call_target="tpu_custom_call" | custom-call | flops 201326592 | bytes 8650752 | tf_op jit(solution)/shard_map/pallas_call | solution.py:175
  57.4 0.9 copy-done.10
  58.4 2.4 %collective-permute-done.12.refs_2_ = bf16[2,2,768,128]{3,2,1,0:T(8,128)(2,1)S(1)} collective-permute-done((bf16[2,2,768,128]{3,2,1,0:T(8,128)(2,1)}, bf16[2,2,768,128]{3,2,1,0:T(8,128)(2,1)S(1)}, u32[]{:S(2)}, u32[]{:S(2)}) %collective-permute-start.12) | collective-permute-done | bytes 786464 | tf_op jit(solution)/shard_map/ppermute | solution.py:194
  60.8 1.2 shard_map.93
  62.4 1.2 collective-permute-start.13
  63.6 3.9 %shard_map.94.refs_3_ = f32[128,3072]{1,0:T(8,128)S(1)} custom-call(bf16[128,3072]{1,0:T(8,128)(2,1)S(1)} %bitcast.46, bf16[128,3072]{1,0:T(8,128)(2,1)S(1)} %bitcast.37, bf16[128,3072]{1,0:T(8,128)(2,1)S(1)} %copy-done.6), custom_call_target="tpu_custom_call" | custom-call | flops 201326592 | bytes 3145728 | tf_op jit(solution)/shard_map/pallas_call | solution.py:175
  67.5 1.6 collective-permute-done.13.refs_2_.refs_1_
  69.1 4.1 %collective-permute-done.14.refs_5_ = bf16[1,128,1536]{2,1,0:T(8,128)(2,1)S(1)} collective-permute-done((bf16[1,128,1536]{2,1,0:T(8,128)(2,1)S(1)}, bf16[1,128,1536]{2,1,0:T(8,128)(2,1)S(1)}, u32[]{:S(2)}, u32[]{:S(2)}) %collective-permute-start.14) | collective-permute-done | bytes 393248 | tf_op jit(solution)/shard_map/ppermute | solution.py:194
  73.8 1.3 collective-permute-start.16
  75.4 4.6 %collective-permute-done.16.refs_2_ = bf16[768,128]{1,0:T(8,128)(2,1)S(1)} collective-permute-done((bf16[768,128]{1,0:T(8,128)(2,1)S(1)}, bf16[768,128]{1,0:T(8,128)(2,1)S(1)}, u32[]{:S(2)}, u32[]{:S(2)}) %collective-permute-start.16) | collective-permute-done | bytes 196640 | tf_op jit(solution)/shard_map/ppermute | solution.py:194
  80.0 0.9 collective-permute-done.15.refs_2_
  82.5 1.1 collective-permute-start.17
  83.6 8.3 %collective-permute-done.17.refs_2_ = bf16[768,128]{1,0:T(8,128)(2,1)S(1)} collective-permute-done((bf16[768,128]{1,0:T(8,128)(2,1)S(1)}, bf16[768,128]{1,0:T(8,128)(2,1)S(1)}, u32[]{:S(2)}, u32[]{:S(2)}) %collective-permute-start.17) | collective-permute-done | bytes 196640 | tf_op jit(solution)/shard_map/ppermute | solution.py:194
  92.6 1.5 collective-permute-start.19
  94.1 4.3 %collective-permute-done.19.refs_1_ = bf16[768,128]{1,0:T(8,128)(2,1)S(1)} collective-permute-done((bf16[768,128]{1,0:T(8,128)(2,1)S(1)}, bf16[768,128]{1,0:T(8,128)(2,1)S(1)}, u32[]{:S(2)}, u32[]{:S(2)}) %collective-permute-start.19) | collective-permute-done | bytes 196640 | tf_op jit(solution)/shard_map/ppermute | solution.py:194
  99.2 1.3 collective-permute-done.21.refs_8_
  100.5 2.9 %shard_map.99 = (bf16[128,3072]{1,0:T(8,128)(2,1)}, bf16[2,2,8,2,96,128]{5,4,3,2,1,0:T(8,128)(2,1)S(1)}, bf16[3072,128]{1,0:T(8,128)(2,1)S(1)}) custom-call(s32[3]{0:T(128)S(1)} %pad_add_fusion.2.refs_0_, bf16[128,3072]{1,0:T(8,128)(2,1)S(1)} %bitcast.42, bf16[128,3072]{1,0:T(8,128)(2,1)S(1)} %bitcast.38, f32[128,3072]{1,0:T(8,128)S(1)} %shard_map.94.refs_3_, ...), custom_call_target="tpu_custom_call" | custom-call | flops 100663296 | bytes 8650752 | tf_op jit(solution)/shard_map/pallas_call | solution.py:175
  104.7 1.0 fusion
  105.6 16.7 %all_to_all.10.turned_ref = bf16[16,192,128]{2,1,0:T(8,128)(2,1)} all-to-all(bf16[16,192,128]{2,1,0:T(8,128)(2,1)S(1)} %bitcast.57), channel_id=1, replica_groups=mesh['dp'=2,'bit3'=2,'bit2'=2,'bit1'=2,'bit0'=2] {'dp','bit2','bit1','bi..., dimensions={0} | all-to-all | bytes 1572864 | tf_op jit(solution)/shard_map/all_to_all | solution.py:473
  122.3 4.6 %all-to-all-start = ((bf16[16,192,128]{2,1,0:T(8,128)(2,1)}), bf16[16,192,128]{2,1,0:T(8,128)(2,1)}, u32[]{:S(2)}, u32[]{:S(2)}) async-start(bf16[16,192,128]{2,1,0:T(8,128)(2,1)} %bitcast.28), calls=%async_computation | async-start | bytes 1572864 | tf_op jit(solution)/shard_map/all_to_all | solution.py:473
  133.1 5.6 %shard_map.100 = (f32[96,1536]{1,0:T(8,128)}, bf16[1,96,1536]{2,1,0:T(8,128)(2,1)}) custom-call(s32[17]{0:T(128)} %concatenate.6.order_ref, bf16[16,192,128]{2,1,0:T(8,128)(2,1)} %all_to_all.10.turned_ref, bf16[1,128,1536]{2,1,0:T(8,128)(2,1)} %bitcast.53, bf16[1,128,1536]{2,1,0:T(8,128)(2,1)} %bitcast.8.refs_1_, ...), custom_call_target="tpu_custom_call" | custom-call | flops 1207959552 | bytes 8060928 | tf_op jit(solution)/shard_map/pallas_call | solution.py:357
  138.7 2.3 %collective-permute-start.31 = (bf16[96,1536]{1,0:T(8,128)(2,1)}, bf16[96,1536]{1,0:T(8,128)(2,1)S(1)}, u32[]{:S(2)}, u32[]{:S(2)}) collective-permute-start(bf16[96,1536]{1,0:T(8,128)(2,1)} %bitcast.61), channel_id=1, source_target_pairs={{0,8},{8,0},{1,9},{9,1},{2,10},{10,2},{3,11},{11,3},{4,12},{12,4},... | collective-permute-start | bytes 884744 | tf_op jit(solution)/shard_map/ppermute | solution.py:476
  141.0 5.7 %shard_map.101 = (f32[96,1536]{1,0:T(8,128)}, bf16[1,96,1536]{2,1,0:T(8,128)(2,1)}) custom-call(s32[17]{0:T(128)} %concatenate.6.order_ref, bf16[16,192,128]{2,1,0:T(8,128)(2,1)} %all-to-all-done.turned_ref, bf16[1,128,1536]{2,1,0:T(8,128)(2,1)} %bitcast.54, bf16[1,128,1536]{2,1,0:T(8,128)(2,1)} %bitcast.8.refs_1_, ...), custom_call_target="tpu_custom_call" | custom-call | flops 1207959552 | bytes 8060928 | tf_op jit(solution)/shard_map/pallas_call | solution.py:357
  146.7 1.4 collective-permute-start.32
  148.1 5.9 %shard_map.102 = (bf16[128,3072]{1,0:T(8,128)(2,1)}, bf16[128,3072]{1,0:T(8,128)(2,1)}) custom-call(bf16[128,3072]{1,0:T(8,128)(2,1)S(1)} %bitcast.47, bf16[128,3072]{1,0:T(8,128)(2,1)S(1)} %bitcast.43, bf16[128,3072]{1,0:T(8,128)(2,1)S(1)} %bitcast.39, bf16[128,3072]{1,0:T(8,128)(2,1)S(1)} %copy-done.7, bf16[3072,128]{1,0:T(8,128)(2,1)S(1)} %copy-done.11, ...), custom_call_target="tpu_custom_call" | custom-call | flops 603979776 | bytes 6291456 | tf_op jit(solution)/shard_map/pallas_call | solution.py:175
  154.1 8.3 %collective-permute-done.31 = bf16[96,1536]{1,0:T(8,128)(2,1)S(1)} collective-permute-done((bf16[96,1536]{1,0:T(8,128)(2,1)}, bf16[96,1536]{1,0:T(8,128)(2,1)S(1)}, u32[]{:S(2)}, u32[]{:S(2)}) %collective-permute-start.31) | collective-permute-done | bytes 294944 | tf_op jit(solution)/shard_map/ppermute | solution.py:476
  162.4 5.4 %collective-permute-done.32 = bf16[96,1536]{1,0:T(8,128)(2,1)S(1)} collective-permute-done((bf16[96,1536]{1,0:T(8,128)(2,1)}, bf16[96,1536]{1,0:T(8,128)(2,1)S(1)}, u32[]{:S(2)}, u32[]{:S(2)}) %collective-permute-start.32) | collective-permute-done | bytes 294944 | tf_op jit(solution)/shard_map/ppermute | solution.py:476
  167.9 1.1 maximum_multiply_fusion
  (103 shorter events, 17.0 us)
Async XLA Ops:
  4.8 7.2 %collective-permute-start.1 = (bf16[2,2,768,128]{3,2,1,0:T(8,128)(2,1)}, bf16[2,2,768,128]{3,2,1,0:T(8,128)(2,1)S(1)}, u32[]{:S(2)}, u32[]{:S(2)}) collective-permute-start(bf16[2,2,768,128]{3,2,1,0:T(8,128)(2,1)} %bitcast.14.refs_1_), channel_id=1, source_target_pairs={{0,1},{1,0},{2,3},{3,2},{4,5},{5,4},{6,7},{7,6},{8,9},{9,8},{10,11... | collective-permute-start | bytes 2359304 | tf_op jit(solution)/shard_map/ppermute | solution.py:194
  6.5 8.4 %copy-start.1 = (bf16[1,128,3072]{2,1,0:T(8,128)(2,1)S(1)}, bf16[1,128,3072]{2,1,0:T(8,128)(2,1)}, u32[]{:S(2)}) copy-start(bf16[1,128,3072]{2,1,0:T(8,128)(2,1)} %param.8) | copy-start | bytes 2359300
  6.5 8.4 %copy-start.3 = (bf16[1,128,3072]{2,1,0:T(8,128)(2,1)S(1)}, bf16[1,128,3072]{2,1,0:T(8,128)(2,1)}, u32[]{:S(2)}) copy-start(bf16[1,128,3072]{2,1,0:T(8,128)(2,1)} %param.7) | copy-start | bytes 2359300
  6.5 8.4 %copy-start.4 = (bf16[1,128,3072]{2,1,0:T(8,128)(2,1)S(1)}, bf16[1,128,3072]{2,1,0:T(8,128)(2,1)}, u32[]{:S(2)}) copy-start(bf16[1,128,3072]{2,1,0:T(8,128)(2,1)} %param.6) | copy-start | bytes 2359300
  7.8 119.1 %copy-start.8 = (bf16[128,1536]{1,0:T(8,128)(2,1)}, bf16[128,1536]{1,0:T(8,128)(2,1)S(1)}, u32[]{:S(2)}) copy-start(bf16[128,1536]{1,0:T(8,128)(2,1)S(1)} %get-tuple-element.54) | copy-start | bytes 1179652
  7.8 12.5 %collective-permute-start.3 = (bf16[1,128,1536]{2,1,0:T(8,128)(2,1)S(1)}, bf16[1,128,1536]{2,1,0:T(8,128)(2,1)}, u32[]{:S(2)}, u32[]{:S(2)}) collective-permute-start(bf16[1,128,1536]{2,1,0:T(8,128)(2,1)S(1)} %bitcast.50), channel_id=1, source_target_pairs={{0,4},{4,0},{1,5},{5,1},{2,6},{6,2},{3,7},{7,3},{8,12},{12,8},{9,1... | collective-permute-start | bytes 1179656 | tf_op jit(solution)/shard_map/ppermute | solution.py:194
  10.4 11.5 %collective-permute-start = (bf16[128,1536]{1,0:T(8,128)(2,1)}, bf16[128,1536]{1,0:T(8,128)(2,1)}, u32[]{:S(2)}, u32[]{:S(2)}) collective-permute-start(bf16[128,1536]{1,0:T(8,128)(2,1)} %get-tuple-element.50), channel_id=1, source_target_pairs={{0,16},{16,0},{1,17},{17,1},{2,18},{18,2},{3,19},{19,3},{4,20},{20... | collective-permute-start | bytes 1179656 | tf_op jit(solution)/shard_map/ppermute | solution.py:194
  13.3 8.7 %collective-permute-start.2 = (bf16[768,128]{1,0:T(8,128)(2,1)S(1)}, bf16[768,128]{1,0:T(8,128)(2,1)S(1)}, u32[]{:S(2)}, u32[]{:S(2)}) collective-permute-start(bf16[768,128]{1,0:T(8,128)(2,1)S(1)} %get-tuple-element.51), channel_id=1, source_target_pairs={{0,2},{2,0},{1,3},{3,1},{4,6},{6,4},{5,7},{7,5},{8,10},{10,8},{9,1... | collective-permute-start | bytes 589832 | tf_op jit(solution)/shard_map/ppermute | solution.py:194
  18.7 33.5 %copy-start.9 = (bf16[1,128,3072]{2,1,0:T(8,128)(2,1)S(1)}, bf16[1,128,3072]{2,1,0:T(8,128)(2,1)}, u32[]{:S(2)}) copy-start(bf16[1,128,3072]{2,1,0:T(8,128)(2,1)} %param.9) | copy-start | bytes 2359300
  22.6 6.3 %collective-permute-start.5 = (bf16[768,128]{1,0:T(8,128)(2,1)S(1)}, bf16[768,128]{1,0:T(8,128)(2,1)S(1)}, u32[]{:S(2)}, u32[]{:S(2)}) collective-permute-start(bf16[768,128]{1,0:T(8,128)(2,1)S(1)} %get-tuple-element.56.refs_1_), channel_id=1, source_target_pairs={{0,2},{2,0},{1,3},{3,1},{4,6},{6,4},{5,7},{7,5},{8,10},{10,8},{9,1... | collective-permute-start | bytes 589832 | tf_op jit(solution)/shard_map/ppermute | solution.py:194
  24.1 5.9 %collective-permute-start.4 = (bf16[768,128]{1,0:T(8,128)(2,1)S(1)}, bf16[768,128]{1,0:T(8,128)(2,1)S(1)}, u32[]{:S(2)}, u32[]{:S(2)}) collective-permute-start(bf16[768,128]{1,0:T(8,128)(2,1)S(1)} %shard_map.88.refs_1_), channel_id=1, source_target_pairs={{0,4},{4,0},{1,5},{5,1},{2,6},{6,2},{3,7},{7,3},{8,12},{12,8},{9,1... | collective-permute-start | bytes 589832 | tf_op jit(solution)/shard_map/ppermute | solution.py:194
  30.7 10.5 %collective-permute-start.7 = (bf16[1,128,1536]{2,1,0:T(8,128)(2,1)}, bf16[1,128,1536]{2,1,0:T(8,128)(2,1)S(1)}, u32[]{:S(2)}, u32[]{:S(2)}) collective-permute-start(bf16[1,128,1536]{2,1,0:T(8,128)(2,1)} %bitcast.8.refs_1_), channel_id=1, source_target_pairs={{0,2},{2,0},{1,3},{3,1},{4,6},{6,4},{5,7},{7,5},{8,10},{10,8},{9,1... | collective-permute-start | bytes 1179656 | tf_op jit(solution)/shard_map/ppermute | solution.py:194
  31.3 9.9 %collective-permute-start.6 = (bf16[768,128]{1,0:T(8,128)(2,1)S(1)}, bf16[768,128]{1,0:T(8,128)(2,1)S(1)}, u32[]{:S(2)}, u32[]{:S(2)}) collective-permute-start(bf16[768,128]{1,0:T(8,128)(2,1)S(1)} %get-tuple-element.58), channel_id=1, source_target_pairs={{0,8},{8,0},{1,9},{9,1},{2,10},{10,2},{3,11},{11,3},{4,12},{12,4},... | collective-permute-start | bytes 589832 | tf_op jit(solution)/shard_map/ppermute | solution.py:194
  41.8 10.4 %collective-permute-start.8 = (bf16[1,128,1536]{2,1,0:T(8,128)(2,1)}, bf16[1,128,1536]{2,1,0:T(8,128)(2,1)S(1)}, u32[]{:S(2)}, u32[]{:S(2)}) collective-permute-start(bf16[1,128,1536]{2,1,0:T(8,128)(2,1)} %bitcast.8.refs_1_), channel_id=1, source_target_pairs={{0,4},{4,0},{1,5},{5,1},{2,6},{6,2},{3,7},{7,3},{8,12},{12,8},{9,1... | collective-permute-start | bytes 1179656 | tf_op jit(solution)/shard_map/ppermute | solution.py:194
  41.9 6.0 %collective-permute-start.9 = (bf16[768,128]{1,0:T(8,128)(2,1)S(1)}, bf16[768,128]{1,0:T(8,128)(2,1)S(1)}, u32[]{:S(2)}, u32[]{:S(2)}) collective-permute-start(bf16[768,128]{1,0:T(8,128)(2,1)S(1)} %get-tuple-element.62), channel_id=1, source_target_pairs={{0,2},{2,0},{1,3},{3,1},{4,6},{6,4},{5,7},{7,5},{8,10},{10,8},{9,1... | collective-permute-start | bytes 589832 | tf_op jit(solution)/shard_map/ppermute | solution.py:194
  43.3 8.9 %collective-permute-start.10 = (bf16[768,128]{1,0:T(8,128)(2,1)S(1)}, bf16[768,128]{1,0:T(8,128)(2,1)S(1)}, u32[]{:S(2)}, u32[]{:S(2)}) collective-permute-start(bf16[768,128]{1,0:T(8,128)(2,1)S(1)} %get-tuple-element.65.refs_5_), channel_id=1, source_target_pairs={{0,1},{1,0},{2,3},{3,2},{4,5},{5,4},{6,7},{7,6},{8,9},{9,8},{10,11... | collective-permute-start | bytes 589832 | tf_op jit(solution)/shard_map/ppermute | solution.py:194
  48.5 3.7 %collective-permute-start.11 = (bf16[768,128]{1,0:T(8,128)(2,1)S(1)}, bf16[768,128]{1,0:T(8,128)(2,1)S(1)}, u32[]{:S(2)}, u32[]{:S(2)}) collective-permute-start(bf16[768,128]{1,0:T(8,128)(2,1)S(1)} %shard_map.91.refs_6_), channel_id=1, source_target_pairs={{0,1},{1,0},{2,3},{3,2},{4,5},{5,4},{6,7},{7,6},{8,9},{9,8},{10,11... | collective-permute-start | bytes 589832 | tf_op jit(solution)/shard_map/ppermute | solution.py:194
  58.3 2.5 %collective-permute-start.12 = (bf16[2,2,768,128]{3,2,1,0:T(8,128)(2,1)}, bf16[2,2,768,128]{3,2,1,0:T(8,128)(2,1)S(1)}, u32[]{:S(2)}, u32[]{:S(2)}) collective-permute-start(bf16[2,2,768,128]{3,2,1,0:T(8,128)(2,1)} %bitcast.26.refs_1_), channel_id=1, source_target_pairs={{0,1},{1,0},{2,3},{3,2},{4,5},{5,4},{6,7},{7,6},{8,9},{9,8},{10,11... | collective-permute-start | bytes 2359304 | tf_op jit(solution)/shard_map/ppermute | solution.py:194
  62.0 11.2 %collective-permute-start.14 = (bf16[1,128,1536]{2,1,0:T(8,128)(2,1)S(1)}, bf16[1,128,1536]{2,1,0:T(8,128)(2,1)S(1)}, u32[]{:S(2)}, u32[]{:S(2)}) collective-permute-start(bf16[1,128,1536]{2,1,0:T(8,128)(2,1)S(1)} %copy-done.16), channel_id=1, source_target_pairs={{0,4},{4,0},{1,5},{5,1},{2,6},{6,2},{3,7},{7,3},{8,12},{12,8},{9,1... | collective-permute-start | bytes 1179656 | tf_op jit(solution)/shard_map/ppermute | solution.py:194
  62.4 6.7 %collective-permute-start.13 = (bf16[768,128]{1,0:T(8,128)(2,1)S(1)}, bf16[768,128]{1,0:T(8,128)(2,1)S(1)}, u32[]{:S(2)}, u32[]{:S(2)}) collective-permute-start(bf16[768,128]{1,0:T(8,128)(2,1)S(1)} %get-tuple-element.70), channel_id=1, source_target_pairs={{0,2},{2,0},{1,3},{3,1},{4,6},{6,4},{5,7},{7,5},{8,10},{10,8},{9,1... | collective-permute-start | bytes 589832 | tf_op jit(solution)/shard_map/ppermute | solution.py:194
  73.2 30.1 %copy-start.20 = (bf16[1,128,1536]{2,1,0:T(8,128)(2,1)}, bf16[1,128,1536]{2,1,0:T(8,128)(2,1)S(1)}, u32[]{:S(2)}) copy-start(bf16[1,128,1536]{2,1,0:T(8,128)(2,1)S(1)} %collective-permute-done.14.refs_5_) | copy-start | bytes 1179652
  73.8 6.2 %collective-permute-start.16 = (bf16[768,128]{1,0:T(8,128)(2,1)S(1)}, bf16[768,128]{1,0:T(8,128)(2,1)S(1)}, u32[]{:S(2)}, u32[]{:S(2)}) collective-permute-start(bf16[768,128]{1,0:T(8,128)(2,1)S(1)} %get-tuple-element.73.refs_1_), channel_id=1, source_target_pairs={{0,2},{2,0},{1,3},{3,1},{4,6},{6,4},{5,7},{7,5},{8,10},{10,8},{9,1... | collective-permute-start | bytes 589832 | tf_op jit(solution)/shard_map/ppermute | solution.py:194
  75.1 5.8 %collective-permute-start.15 = (bf16[768,128]{1,0:T(8,128)(2,1)S(1)}, bf16[768,128]{1,0:T(8,128)(2,1)S(1)}, u32[]{:S(2)}, u32[]{:S(2)}) collective-permute-start(bf16[768,128]{1,0:T(8,128)(2,1)S(1)} %shard_map.95.refs_1_), channel_id=1, source_target_pairs={{0,4},{4,0},{1,5},{5,1},{2,6},{6,2},{3,7},{7,3},{8,12},{12,8},{9,1... | collective-permute-start | bytes 589832 | tf_op jit(solution)/shard_map/ppermute | solution.py:194
  81.6 10.3 %collective-permute-start.18 = (bf16[1,128,1536]{2,1,0:T(8,128)(2,1)S(1)}, bf16[1,128,1536]{2,1,0:T(8,128)(2,1)S(1)}, u32[]{:S(2)}, u32[]{:S(2)}) collective-permute-start(bf16[1,128,1536]{2,1,0:T(8,128)(2,1)S(1)} %bitcast.51), channel_id=1, source_target_pairs={{0,2},{2,0},{1,3},{3,1},{4,6},{6,4},{5,7},{7,5},{8,10},{10,8},{9,1... | collective-permute-start | bytes 1179656 | tf_op jit(solution)/shard_map/ppermute | solution.py:194
  82.5 9.5 %collective-permute-start.17 = (bf16[768,128]{1,0:T(8,128)(2,1)S(1)}, bf16[768,128]{1,0:T(8,128)(2,1)S(1)}, u32[]{:S(2)}, u32[]{:S(2)}) collective-permute-start(bf16[768,128]{1,0:T(8,128)(2,1)S(1)} %get-tuple-element.75), channel_id=1, source_target_pairs={{0,8},{8,0},{1,9},{9,1},{2,10},{10,2},{3,11},{11,3},{4,12},{12,4},... | collective-permute-start | bytes 589832 | tf_op jit(solution)/shard_map/ppermute | solution.py:194
  92.0 11.4 %copy-start.21 = (bf16[1,128,1536]{2,1,0:T(8,128)(2,1)}, bf16[1,128,1536]{2,1,0:T(8,128)(2,1)S(1)}, u32[]{:S(2)}) copy-start(bf16[1,128,1536]{2,1,0:T(8,128)(2,1)S(1)} %collective-permute-done.18.refs_6_) | copy-start | bytes 1179652
  92.6 5.8 %collective-permute-start.19 = (bf16[768,128]{1,0:T(8,128)(2,1)S(1)}, bf16[768,128]{1,0:T(8,128)(2,1)S(1)}, u32[]{:S(2)}, u32[]{:S(2)}) collective-permute-start(bf16[768,128]{1,0:T(8,128)(2,1)S(1)} %get-tuple-element.80), channel_id=1, source_target_pairs={{0,2},{2,0},{1,3},{3,1},{4,6},{6,4},{5,7},{7,5},{8,10},{10,8},{9,1... | collective-permute-start | bytes 589832 | tf_op jit(solution)/shard_map/ppermute | solution.py:194
  94.1 9.8 %collective-permute-start.22 = (bf16[1,128,1536]{2,1,0:T(8,128)(2,1)S(1)}, bf16[1,128,1536]{2,1,0:T(8,128)(2,1)S(1)}, u32[]{:S(2)}, u32[]{:S(2)}) collective-permute-start(bf16[1,128,1536]{2,1,0:T(8,128)(2,1)S(1)} %collective-permute-done.18.refs_6_), channel_id=1, source_target_pairs={{0,4},{4,0},{1,5},{5,1},{2,6},{6,2},{3,7},{7,3},{8,12},{12,8},{9,1... | collective-permute-start | bytes 1179656 | tf_op jit(solution)/shard_map/ppermute | solution.py:194
  94.1 5.1 %collective-permute-start.20 = (bf16[768,128]{1,0:T(8,128)(2,1)S(1)}, bf16[768,128]{1,0:T(8,128)(2,1)S(1)}, u32[]{:S(2)}, u32[]{:S(2)}) collective-permute-start(bf16[768,128]{1,0:T(8,128)(2,1)S(1)} %get-tuple-element.79.refs_5_), channel_id=1, source_target_pairs={{0,1},{1,0},{2,3},{3,2},{4,5},{5,4},{6,7},{7,6},{8,9},{9,8},{10,11... | collective-permute-start | bytes 589832 | tf_op jit(solution)/shard_map/ppermute | solution.py:194
  99.0 1.5 collective-permute-start.21
  122.3 5.3 %copy-start.17 = (bf16[1,128,1536]{2,1,0:T(8,128)(2,1)S(1)}, bf16[1,128,1536]{2,1,0:T(8,128)(2,1)}, u32[]{:S(2)}) copy-start(bf16[1,128,1536]{2,1,0:T(8,128)(2,1)} %copy-done.15) | copy-start | bytes 1179652
  122.3 5.7 %copy-start.19 = (bf16[1,128,1536]{2,1,0:T(8,128)(2,1)S(1)}, bf16[1,128,1536]{2,1,0:T(8,128)(2,1)}, u32[]{:S(2)}) copy-start(bf16[1,128,1536]{2,1,0:T(8,128)(2,1)} %copy-done.18) | copy-start | bytes 1179652
  122.3 18.6 %all-to-all-start = ((bf16[16,192,128]{2,1,0:T(8,128)(2,1)}), bf16[16,192,128]{2,1,0:T(8,128)(2,1)}, u32[]{:S(2)}, u32[]{:S(2)}) async-start(bf16[16,192,128]{2,1,0:T(8,128)(2,1)} %bitcast.28), calls=%async_computation | async-start | bytes 1572864 | tf_op jit(solution)/shard_map/all_to_all | solution.py:473
  126.9 1.8 %collective-permute-start.23 = (bf16[1,128,1536]{2,1,0:T(8,128)(2,1)S(1)}, bf16[1,128,1536]{2,1,0:T(8,128)(2,1)S(1)}, u32[]{:S(2)}, u32[]{:S(2)}) collective-permute-start(bf16[1,128,1536]{2,1,0:T(8,128)(2,1)S(1)} %bitcast.52), channel_id=1, source_target_pairs={{0,1},{1,0},{2,3},{3,2},{4,5},{5,4},{6,7},{7,6},{8,9},{9,8},{10,11... | collective-permute-start | bytes 1179656 | tf_op jit(solution)/shard_map/ppermute | solution.py:194
  127.1 2.6 %collective-permute-start.25 = (bf16[1,128,1536]{2,1,0:T(8,128)(2,1)}, bf16[1,128,1536]{2,1,0:T(8,128)(2,1)}, u32[]{:S(2)}, u32[]{:S(2)}) collective-permute-start(bf16[1,128,1536]{2,1,0:T(8,128)(2,1)} %collective-permute-done.3.refs_2_), channel_id=1, source_target_pairs={{0,1},{1,0},{2,3},{3,2},{4,5},{5,4},{6,7},{7,6},{8,9},{9,8},{10,11... | collective-permute-start | bytes 1179656 | tf_op jit(solution)/shard_map/ppermute | solution.py:194
  127.5 3.2 %collective-permute-start.24 = (bf16[1,128,1536]{2,1,0:T(8,128)(2,1)}, bf16[1,128,1536]{2,1,0:T(8,128)(2,1)}, u32[]{:S(2)}, u32[]{:S(2)}) collective-permute-start(bf16[1,128,1536]{2,1,0:T(8,128)(2,1)} %bitcast.8.refs_1_), channel_id=1, source_target_pairs={{0,1},{1,0},{2,3},{3,2},{4,5},{5,4},{6,7},{7,6},{8,9},{9,8},{10,11... | collective-permute-start | bytes 1179656 | tf_op jit(solution)/shard_map/ppermute | solution.py:194
  127.6 4.0 %collective-permute-start.27 = (bf16[1,128,1536]{2,1,0:T(8,128)(2,1)S(1)}, bf16[1,128,1536]{2,1,0:T(8,128)(2,1)}, u32[]{:S(2)}, u32[]{:S(2)}) collective-permute-start(bf16[1,128,1536]{2,1,0:T(8,128)(2,1)S(1)} %copy-done.17), channel_id=1, source_target_pairs={{0,1},{1,0},{2,3},{3,2},{4,5},{5,4},{6,7},{7,6},{8,9},{9,8},{10,11... | collective-permute-start | bytes 1179656 | tf_op jit(solution)/shard_map/ppermute | solution.py:194
  128.0 3.6 %collective-permute-start.26 = (bf16[1,128,1536]{2,1,0:T(8,128)(2,1)S(1)}, bf16[1,128,1536]{2,1,0:T(8,128)(2,1)}, u32[]{:S(2)}, u32[]{:S(2)}) collective-permute-start(bf16[1,128,1536]{2,1,0:T(8,128)(2,1)S(1)} %copy-done.19), channel_id=1, source_target_pairs={{0,1},{1,0},{2,3},{3,2},{4,5},{5,4},{6,7},{7,6},{8,9},{9,8},{10,11... | collective-permute-start | bytes 1179656 | tf_op jit(solution)/shard_map/ppermute | solution.py:194
  129.5 2.8 %collective-permute-start.28 = (bf16[1,128,1536]{2,1,0:T(8,128)(2,1)}, bf16[1,128,1536]{2,1,0:T(8,128)(2,1)S(1)}, u32[]{:S(2)}, u32[]{:S(2)}) collective-permute-start(bf16[1,128,1536]{2,1,0:T(8,128)(2,1)} %copy-done.20), channel_id=1, source_target_pairs={{0,1},{1,0},{2,3},{3,2},{4,5},{5,4},{6,7},{7,6},{8,9},{9,8},{10,11... | collective-permute-start | bytes 1179656 | tf_op jit(solution)/shard_map/ppermute | solution.py:194
  129.6 2.8 %collective-permute-start.29 = (bf16[1,128,1536]{2,1,0:T(8,128)(2,1)}, bf16[1,128,1536]{2,1,0:T(8,128)(2,1)}, u32[]{:S(2)}, u32[]{:S(2)}) collective-permute-start(bf16[1,128,1536]{2,1,0:T(8,128)(2,1)} %copy-done.21), channel_id=1, source_target_pairs={{0,1},{1,0},{2,3},{3,2},{4,5},{5,4},{6,7},{7,6},{8,9},{9,8},{10,11... | collective-permute-start | bytes 1179656 | tf_op jit(solution)/shard_map/ppermute | solution.py:194
  130.8 2.2 %collective-permute-start.30 = (bf16[1,128,1536]{2,1,0:T(8,128)(2,1)}, bf16[1,128,1536]{2,1,0:T(8,128)(2,1)}, u32[]{:S(2)}, u32[]{:S(2)}) collective-permute-start(bf16[1,128,1536]{2,1,0:T(8,128)(2,1)} %copy-done.22), channel_id=1, source_target_pairs={{0,1},{1,0},{2,3},{3,2},{4,5},{5,4},{6,7},{7,6},{8,9},{9,8},{10,11... | collective-permute-start | bytes 1179656 | tf_op jit(solution)/shard_map/ppermute | solution.py:194
  138.7 9.5 %copy-start.7 = (bf16[128,3072]{1,0:T(8,128)(2,1)S(1)}, bf16[128,3072]{1,0:T(8,128)(2,1)}, u32[]{:S(2)}) copy-start(bf16[128,3072]{1,0:T(8,128)(2,1)} %copy-done.5) | copy-start | bytes 2359300
  138.7 23.7 %collective-permute-start.31 = (bf16[96,1536]{1,0:T(8,128)(2,1)}, bf16[96,1536]{1,0:T(8,128)(2,1)S(1)}, u32[]{:S(2)}, u32[]{:S(2)}) collective-permute-start(bf16[96,1536]{1,0:T(8,128)(2,1)} %bitcast.61), channel_id=1, source_target_pairs={{0,8},{8,0},{1,9},{9,1},{2,10},{10,2},{3,11},{11,3},{4,12},{12,4},... | collective-permute-start | bytes 884744 | tf_op jit(solution)/shard_map/ppermute | solution.py:476
  141.0 7.2 %copy-start.11 = (bf16[3072,128]{1,0:T(8,128)(2,1)S(1)}, bf16[3072,128]{1,0:T(8,128)(2,1)}, u32[]{:S(2)}) copy-start(bf16[3072,128]{1,0:T(8,128)(2,1)} %copy-done.10) | copy-start | bytes 2359300
  141.0 7.2 %copy-start.13 = (bf16[3072,128]{1,0:T(8,128)(2,1)S(1)}, bf16[3072,128]{1,0:T(8,128)(2,1)}, u32[]{:S(2)}) copy-start(bf16[3072,128]{1,0:T(8,128)(2,1)} %copy-done.12) | copy-start | bytes 2359300
  146.7 21.2 %collective-permute-start.32 = (bf16[96,1536]{1,0:T(8,128)(2,1)}, bf16[96,1536]{1,0:T(8,128)(2,1)S(1)}, u32[]{:S(2)}, u32[]{:S(2)}) collective-permute-start(bf16[96,1536]{1,0:T(8,128)(2,1)} %bitcast.62), channel_id=1, source_target_pairs={{0,8},{8,0},{1,9},{9,1},{2,10},{10,2},{3,11},{11,3},{4,12},{12,4},... | collective-permute-start | bytes 884744 | tf_op jit(solution)/shard_map/ppermute | solution.py:476
  148.1 14.2 %copy-start.25 = (f32[96,1536]{1,0:T(8,128)S(1)}, f32[96,1536]{1,0:T(8,128)}, u32[]{:S(2)}) copy-start(f32[96,1536]{1,0:T(8,128)} %get-tuple-element.94) | copy-start | bytes 1769476
  154.1 13.8 %copy-start.26 = (f32[96,1536]{1,0:T(8,128)S(1)}, f32[96,1536]{1,0:T(8,128)}, u32[]{:S(2)}) copy-start(f32[96,1536]{1,0:T(8,128)} %get-tuple-element.95) | copy-start | bytes 1769476
  (13 other events, 25.0 us)

commit v4 on v3

--- a/solution.py
+++ b/solution.py
@@ -55,21 +55,21 @@
     local_ref[:, at] = dot(scores, v_ref[:, at], NN)
 
 
-def assemble(at, flags_ref, other_ref, quarter_refs, state_ref):
+def assemble(at, counts, flags_ref, other_ref, quarter_refs, state_ref):
     size = quarter_refs[0].shape[0]
     quarter, start = divmod(at.start, size)
     near = flags_ref[0] == quarter // 2
     same = flags_ref[1] == quarter % 2
     own, other, swapped_own, swapped_other = [ref[start : start + HEAD_DIM, :] for ref in quarter_refs]
     total = jnp.where(same, jnp.where(near, own, swapped_own), jnp.where(near, other, swapped_other))
-    total = added_if(flags_ref[2] == 1, total, other_ref[at, :])
+    total = added_if(flags_ref[counts] == 1, total, other_ref[at, :])
     state_ref[at, :] = total
     return total
 
 
-def grad_output_head(at, flags_ref, q_ref, local_ref, upstream_ref, other_ref, *refs):
+def grad_output_head(counts, at, flags_ref, q_ref, local_ref, upstream_ref, other_ref, *refs):
     *quarter_refs, grad_ref, block_ref, state_ref = refs
-    state = assemble(at, flags_ref, other_ref, quarter_refs, state_ref)
+    state = assemble(at, counts, flags_ref, other_ref, quarter_refs, state_ref)
     query = feature(q_ref[:, at])
     output = local_ref[:, at] + dot(query, state, NN)
     inverse_rms = lax.rsqrt(jnp.mean(output * output, axis=-1, keepdims=True) + EPSILON)
@@ -86,10 +86,12 @@
     key_out[:, at] = dot(grad_scores, feature(q_ref[:, at]), NN)
 
 
-def key_grad_head(at, flags_ref, k_ref, v_ref, local_ref, other_ref, *refs):
-    *quarter_refs, key_out, turned_out, state_ref = refs
-    cuts, copies, devices, halves, rows, tokens = turned_out.shape
-    state = assemble(at, flags_ref, other_ref, quarter_refs, state_ref)
+def key_grad_head(counts, at, flags_ref, k_ref, v_ref, local_ref, other_ref, *refs):
+    *quarter_refs, key_out, state_ref = refs[:6]
+    turned_out = refs[6:]
+    cuts = len(turned_out)
+    copies, devices, halves, rows, tokens = turned_out[0].shape
+    state = assemble(at, counts, flags_ref, other_ref, quarter_refs, state_ref)
     key = local_ref[:, at] + dot(v_ref[:, at], state, NT)
     key = (key * slope(k_ref[:, at])).astype(BF16)
     key_out[:, at] = key
@@ -101,7 +103,7 @@
         owner, cut = divmod(block, cuts)
         half, device = divmod(owner, devices)
         for copy in range(copies):
-            turned_out[cut, copy, device, half, row : row + size] = turned[start - at.start : start - at.start + size]
+            turned_out[cut][copy, device, half, row : row + size] = turned[start - at.start : start - at.start + size]
         start += size
 
 
@@ -224,13 +226,10 @@
 
 
 class Scan:
-    def __init__(self, state, bits, backward):
+    def __init__(self, state, bits, backward, flags):
         first, second, *self.rest = bits
         self.first, self.second = first, second
-        after = 0 if backward else 1
-        place = [lax.axis_index(bit) for bit in bits]
-        self.flags = jnp.stack([*place, *[(at == after).astype(jnp.int32) for at in place]])
-        self.counts = len(bits)
+        self.flags, self.counts = flags, (2 if backward else 1) * len(bits)
         state = state.reshape(2, 2, -1, HEAD_DIM)
         self.other = swap(state, first)
 
@@ -241,7 +240,7 @@
         self.theirs, self.mine = small(quarters, self.flags, [state, self.other], 2)
         self.arrived = swap(self.theirs, second)
 
-    def spread(self, due, meanwhile):
+    def spread(self, due, early, meanwhile, rest_early):
         counts = self.counts
         self.arrived = after(self.arrived, *due)
 
@@ -250,10 +249,12 @@
 
         (total,) = small(start, self.flags, [self.mine, self.arrived], 1)
         self.rest_arrived = swap(after(self.mine, self.arrived), self.second)
+        if rest_early:
+            early = [self.rest_arrived, *early]
         before = None
         for index, bit in enumerate(self.rest, 2):
             last = bit == self.rest[-1]
-            pieces = meanwhile(total) if last else [self.rest_arrived]
+            pieces = meanwhile(total) if last else list(early)
             arrived = after(swap(total, bit), *pieces)
 
             def first(flags, total, arrived):
@@ -284,44 +285,53 @@
         arrays = [swap(self.before, self.second), self.rest_arrived]
         (other,) = small(finish, self.flags, arrays, 1)
         quarters = [self.own, other, swap(self.own, self.first), swap(other, self.first)]
-        self.kinds = jnp.stack([self.flags[0], self.flags[1], self.flags[counts]])
         self.operands = [("whole", self.other.reshape(-1, HEAD_DIM))]
         self.operands += [("held", quarter) for quarter in quarters]
 
 
-def sides_kernel(which_ref, in_ref, own_ref, gone_ref):
+def sides_kernel(flags_ref, in_ref, own_ref, gone_ref):
     columns = own_ref.shape[1]
-
-    @pl.when(which_ref[0] == 0)
+    mine = flags_ref[flags_ref.shape[0] - 2]
+
+    @pl.when(mine == 0)
     def _():
         own_ref[...] = in_ref[:, :columns]
         gone_ref[...] = in_ref[:, columns:]
 
-    @pl.when(which_ref[0] == 1)
+    @pl.when(mine == 1)
     def _():
         own_ref[...] = in_ref[:, columns:]
         gone_ref[...] = in_ref[:, :columns]
 
 
-def sides(array, which):
+def sides(array, flags):
     rows, columns = array.shape
-    tile = rows // 4
+    tile = rows // 2
     out = jax.ShapeDtypeStruct((rows, columns // 2), array.dtype)
     return pl.pallas_call(
         sides_kernel,
         grid_spec=pltpu.PrefetchScalarGridSpec(
             num_scalar_prefetch=1,
             grid=(rows // tile,),
-            in_specs=[pl.BlockSpec((tile, columns), lambda i, which: (i, 0))],
-            out_specs=[pl.BlockSpec((tile, columns // 2), lambda i, which: (i, 0))] * 2,
+            in_specs=[pl.BlockSpec((tile, columns), lambda i, flags: (i, 0))],
+            out_specs=[pl.BlockSpec((tile, columns // 2), lambda i, flags: (i, 0))] * 2,
         ),
         out_shape=[out, out],
-        compiler_params=pltpu.CompilerParams(vmem_limit_bytes=6 * 1024 * 1024),
+        compiler_params=pltpu.CompilerParams(vmem_limit_bytes=VMEM_MIB * 1024 * 1024),
         cost_estimate=pl.CostEstimate(flops=0, bytes_accessed=4 * array.size, transcendentals=0),
-    )(jnp.reshape(which, (1,)).astype(jnp.int32), array)
-
-
-def weight_kernel(order_ref, turned_ref, *refs):
+    )(flags, array)
+
+
+def weight_kernel(sources_of, flags_ref, turned_ref, *refs):
+    numbers = flags_ref.shape[0]
+    mine, span = flags_ref[numbers - 2], flags_ref[numbers - 1]
+    order = []
+    for sequences, flips in sources_of:
+        device = 0
+        for bit, flip in enumerate(flips):
+            device += 2**bit * (1 - flags_ref[bit] if flip else flags_ref[bit])
+        pair = turned_ref.shape[0] == 16
+        order += [8 * (lax.rem(mine + at, 2) if pair else at) + device for at in sequences]
     *held, kept_ref, sent_ref, total_ref, buffer_ref, arrival = refs
     sources, _, tokens = turned_ref.shape
     others, rows, columns = sent_ref.shape
@@ -337,25 +347,24 @@
         for copy in copies[step * len(copies) // steps : (step + 1) * len(copies) // steps]:
             copy.wait()
         first = step * per_step
-        lhs = jnp.concatenate([turned_ref[order_ref[first + i]] for i in range(per_step)], axis=1)
+        lhs = jnp.concatenate([turned_ref[order[first + i]] for i in range(per_step)], axis=1)
         for start in range(0, columns, tile):
             cut = slice(start, start + tile)
             rhs = buffer_ref[first : first + per_step, :, cut].reshape(per_step * tokens, tile)
             product = dot(lhs, rhs, NN)
             total_ref[:, cut] = product if step == 0 else total_ref[:, cut] + product
-    span = order_ref[sources]
     kept_ref[...] = total_ref[pl.ds(pl.multiple_of(span * rows, 16), rows), :]
     for turn in range(others):
         target = lax.rem(span + turn + 1, others + 1)
         sent_ref[turn] = total_ref[pl.ds(pl.multiple_of(target * rows, 16), rows), :].astype(BF16)
 
 
-def weight_part(order, turned, inputs, halves):
+def weight_part(sources_of, flags, turned, inputs, halves):
     sources, rows, tokens = turned.shape
     columns = inputs[0].shape[-1]
     vmem = pl.BlockSpec(memory_space=pltpu.VMEM)
     return pl.pallas_call(
-        weight_kernel,
+        functools.partial(weight_kernel, sources_of),
         in_specs=[pl.BlockSpec(memory_space=pltpu.SMEM), vmem]
         + [pl.BlockSpec(memory_space=pl.ANY)] * len(inputs),
         out_specs=[vmem, vmem],
@@ -374,7 +383,7 @@
             bytes_accessed=sources * tokens * columns * 2 + rows * columns * 6,
             transcendentals=0,
         ),
-    )(order, turned, *inputs)
+    )(flags, turned, *inputs)
 
 
 def shards(layer_input, query_rows, key_rows, value_rows, out_grad, bits):
@@ -388,90 +397,93 @@
     cuts = 2
     rows = features // places // cuts
 
-    mine = lax.axis_index("dp")
+    place = [lax.axis_index(bit) for bit in bits]
+    mine, span = lax.axis_index("dp"), lax.axis_index(spans)
+    flags = jnp.stack(place + place + [1 - at for at in place] + [mine, span]).astype(jnp.int32)
+
+    (block_state,) = by_heads(
+        block_state_head, [("row", key), ("row", value)], [("held state", BF16)], 1, vmem=44
+    )
+    forward = Scan(block_state, bits, False, flags)
+
     if sequences == 2:
-        own, gone = sides(layer_input[0], mine)
+        own, gone = sides(after(layer_input[0], forward.mine), flags)
         own, far = own[None], swap(gone, "dp")[None]
-        own_id, far_id = mine[None], 1 - mine[None]
     else:
         wide = lax.all_to_all(layer_input[0].reshape(tokens, sequences, -1), "dp", 1, 0)
         own, far = wide[: sequences // 2], wide[sequences // 2 :]
-        own_id, far_id = jnp.split(jnp.arange(sequences), 2)
-    own_layer = swap(own, layer)
-
-    (block_state,) = by_heads(block_state_head, [("row", key), ("row", value)], [("held state", BF16)], 1)
-    forward = Scan(block_state, bits, False)
-    (output,) = by_heads(
-        local_output_head,
-        [("held", after(query, forward.mine)), ("held", key), ("held", value)],
-        [("held row", F32)],
-        2,
-    )
-    far_side = []
+
+    far_side, far_both, output = [], [], []
 
     def along_side(token):
         far_side.append(swap(after(far, token), side))
-        return far_side
-
-    forward.spread([output, far, own_layer], along_side)
+        output.extend(
+            by_heads(
+                local_output_head,
+                [("held", after(query, token)), ("held", key), ("held", value)],
+                [("held row", F32)],
+                2,
+            )
+        )
+        return far_side + output
+
+    forward.spread([], [far], along_side, True)
     forward.collect()
     far_layer = swap(after(far, forward.before), layer)
     grad_output, block_grad, state_in = by_heads(
-        grad_output_head,
-        [("held", query), ("held", output), ("held", upstream), *forward.operands],
+        functools.partial(grad_output_head, forward.counts),
+        [("held", query), ("held", output[0]), ("held", upstream), *forward.operands],
         [("held row", BF16), ("held state", BF16), ("state", BF16)],
         2,
-        after(forward.kinds, far_layer),
+        forward.flags,
     )
-    backward = Scan(block_grad, bits, True)
+    own_layer = swap(after(own, block_grad), layer)
+    backward = Scan(after(block_grad, far_layer), bits, True, flags)
+    own_side = swap(after(own, backward.mine), side)
     (key_local,) = by_heads(
         key_local_head,
         [("held", query), ("held", value), ("held", after(grad_output, backward.mine))],
         [("held row", F32)],
         2,
     )
-    far_both = swap(after(far_side[0], backward.mine), layer)
-    own_side = []
 
     def along_side_again(token):
-        own_side.append(swap(after(own, token), side))
-        return own_side
-
-    backward.spread([key_local, far_both], along_side_again)
+        far_both.append(swap(after(far_layer, token), side))
+        return far_both
+
+    backward.spread([key_local], [own_side, own_layer], along_side_again, False)
     backward.collect()
-    own_both = swap(after(own_side[0], backward.before), layer)
-    key_grad, turned, grad_in = by_heads(
-        key_grad_head,
+    own_both = swap(after(own_side, backward.before), layer)
+    key_grad, grad_in, *turned = by_heads(
+        functools.partial(key_grad_head, backward.counts),
         [("held", key), ("held", value), ("held", key_local), *backward.operands],
-        [("row", BF16), ((cuts, sequences, 8, halves, rows, tokens), BF16), ("state", BF16)],
+        [("row", BF16), ("state", BF16)] + [((sequences, 8, halves, rows, tokens), BF16)] * cuts,
         1,
-        backward.kinds,
+        after(backward.flags, own_both),
     )
-    turned = after(turned, own_both)
-    held, order = [], []
+    own_ids, far_ids = range(sequences // 2), range(sequences // 2, sequences)
+    held, sources_of = [], []
     for array, ids, layered, sided in (
-        (own, own_id, 0, 0),
-        (far, far_id, 0, 0),
-        (own_layer, own_id, 1, 0),
-        (far_layer, far_id, 1, 0),
-        (far_side[0], far_id, 0, 1),
-        (far_both, far_id, 1, 1),
-        (own_side[0], own_id, 0, 1),
-        (own_both, own_id, 1, 1),
+        (own, own_ids, 0, 0),
+        (far, far_ids, 0, 0),
+        (own_layer, own_ids, 1, 0),
+        (far_layer, far_ids, 1, 0),
+        (far_side[0], far_ids, 0, 1),
+        (far_both[0], far_ids, 1, 1),
+        (own_side, own_ids, 0, 1),
+        (own_both, own_ids, 1, 1),
     ):
         held.append(array)
-        order.append(8 * ids + 4 * (lax.axis_index(layer) ^ layered) + 2 * (lax.axis_index(side) ^ sided))
+        sources_of.append((ids, (0, sided, layered)))
     held += [swap(array, core) for array in held]
-    at = lax.axis_index(core)
-    span = lax.axis_index(spans)
-    order = jnp.concatenate([ids + at for ids in order] + [ids + 1 - at for ids in order] + [span[None]])
-    order = order.astype(jnp.int32)
-
-    sums, done = [], turned
+    sources_of += [(ids, (1, sided, layered)) for ids, (_, sided, layered) in sources_of]
+    turned[0] = after(turned[0], *held[8:])
+
+    sums, done = [], turned[0]
     for cut in range(cuts):
         part = turned[cut].reshape(sequences * 8, halves * rows, tokens)
         part = lax.all_to_all(part, ("dp", layer, side, core), 0, 0, tiled=True)
-        total, sent = weight_part(order, after(part, done), held, halves)
+        total, sent = weight_part(sources_of, flags, after(part, done), held, halves)
         for turn in range(1, halves):
             moved = lax.ppermute(sent[turn - 1], spans, [(i, (i + turn) % halves) for i in range(halves)])
             total += moved.astype(F32)

time: 170 us -> 156 us (0.918)
  waiting for transfers between devices: 68.9 us -> 56.5 us
  local copies, waits for them, and re-layouts: 8.64 us -> 4.08 us
  starting transfers between devices: 29.7 us -> 34.1 us
    ppermute x31, waiting for transfers between devices: 55.2 us -> 41.9 us  [swap(): return lax.ppermute(array, axis, [(0, 1), (1, 0)])]
    all_to_all x1, waiting for transfers between devices: 0.01 us -> 7.99 us  [shards(): part = lax.all_to_all(part, ('dp', layer, side, core), 0, 0, tiled=True)]
    ppermute x2, waiting for transfers between devices: 13.7 us -> 6.63 us  [shards(): lax.ppermute(sent[turn - 1], spans, [(i, (i + turn) % halves) for i in ra...]
    ppermute x31, starting transfers between devices: 21.4 us -> 25.9 us  [swap(): return lax.ppermute(array, axis, [(0, 1), (1, 0)])]
    unnamed x54 -> x66, local copies, waits for them, and re-layouts: 6.8 us -> 4 us
  transfers between devices with their start and end apart: 34 -> 34, of which waited for: 23 -> 19; matrix products, arithmetic and copies ran while one was open for 1% -> 0% of each run, Pallas kernels for 19% -> 24%
where the time goes in v4:
time: 156 us
  waiting for transfers between devices  56.5 us (36%)
  Pallas kernels  41.5 us (27%)
  starting transfers between devices  34.1 us (22%)
  blocking collectives  17.3 us (11%)
  local copies, waits for them, and re-layouts  4.08 us (3%)
    ppermute x31, waiting for transfers between devices, swap(): return lax.ppermute(array, axis, [(0, 1), (1, 0)])  41.9 us
    ppermute x31, starting transfers between devices, swap(): return lax.ppermute(array, axis, [(0, 1), (1, 0)])  25.9 us
    pallas_call x6, Pallas kernels, by_heads(): pl.pallas_call(body, in_specs=([] if flags is None else [pl.BlockSpec(mem...  21.4 us
    all_to_all x1, blocking collectives, shards(): part = lax.all_to_all(part, ('dp', layer, side, core), 0, 0, tiled=True)  17.3 us
    pallas_call x2, Pallas kernels, weight_part(): pl.pallas_call(functools.partial(weight_kernel, sources_of), in_specs=[pl...  11.3 us
    all_to_all x1, waiting for transfers between devices, shards(): part = lax.all_to_all(part, ('dp', layer, side, core), 0, 0, tiled=True)  7.99 us
    ppermute x2, waiting for transfers between devices, shards(): lax.ppermute(sent[turn - 1], spans, [(i, (i + turn) % halves) for i in ra...  6.63 us
    pallas_call x10, Pallas kernels, small(): pl.pallas_call(kernel, in_specs=[pl.BlockSpec(memory_space=pltpu.SMEM)] +...  6.24 us
  transfers between devices with their start and end apart: 34, of which 19 were waited for; matrix products, arithmetic and copies ran while one was open for 0% of the time, Pallas kernels for 24%

profile of v4, /device:TPU:0, one launch (start us, length us, event | category | flops | bytes accessed | tf_op | source)
XLA Modules:
  0.0 155.9 jit_solution(4997267355571556038)
XLA Ops:
  0.6 1.1 copy-done
  1.8 1.1 copy-done.2
  2.9 1.0 shard_map.84
  4.6 1.8 %collective-permute-done.refs_2_ = bf16[2,2,768,128]{3,2,1,0:T(8,128)(2,1)S(1)} collective-permute-done((bf16[2,2,768,128]{3,2,1,0:T(8,128)(2,1)S(1)}, bf16[2,2,768,128]{3,2,1,0:T(8,128)(2,1)S(1)}, u32[]{:S(2)}, u32[]{:S(2)}) %collective-permute-start) | collective-permute-done | bytes 786464 | tf_op jit(solution)/shard_map/ppermute | solution.py:196
  7.0 2.9 %collective-permute-start.1 = (bf16[768,128]{1,0:T(8,128)(2,1)S(1)}, bf16[768,128]{1,0:T(8,128)(2,1)S(1)}, u32[]{:S(2)}, u32[]{:S(2)}) collective-permute-start(bf16[768,128]{1,0:T(8,128)(2,1)S(1)} %get-tuple-element.54), channel_id=1, source_target_pairs={{0,2},{2,0},{1,3},{3,1},{4,6},{6,4},{5,7},{7,5},{8,10},{10,8},{9,1... | collective-permute-start | bytes 589832 | tf_op jit(solution)/shard_map/ppermute | solution.py:196
  10.0 2.6 %shard_map.87 = (bf16[128,1536]{1,0:T(8,128)(2,1)}, bf16[128,1536]{1,0:T(8,128)(2,1)}) custom-call(s32[14]{0:T(128)} %copy-done.12, bf16[128,3072]{1,0:T(8,128)(2,1)} %bitcast.58), custom_call_target="tpu_custom_call" | custom-call | bytes 1572864 | tf_op jit(solution)/shard_map/pallas_call | solution.py:311
  12.5 1.5 collective-permute-start.4
  14.1 1.1 collective-permute-done.1.refs_2_.refs_1_
  15.2 0.7 copy-done.13
  16.4 1.9 %collective-permute-start.2 = (bf16[768,128]{1,0:T(8,128)(2,1)S(1)}, bf16[768,128]{1,0:T(8,128)(2,1)S(1)}, u32[]{:S(2)}, u32[]{:S(2)}) collective-permute-start(bf16[768,128]{1,0:T(8,128)(2,1)S(1)} %shard_map.86.refs_1_), channel_id=1, source_target_pairs={{0,4},{4,0},{1,5},{5,1},{2,6},{6,2},{3,7},{7,3},{8,12},{12,8},{9,1... | collective-permute-start | bytes 589832 | tf_op jit(solution)/shard_map/ppermute | solution.py:196
  18.3 1.5 collective-permute-start.3
  19.8 3.1 %collective-permute-done.2.refs_2_ = bf16[768,128]{1,0:T(8,128)(2,1)S(1)} collective-permute-done((bf16[768,128]{1,0:T(8,128)(2,1)S(1)}, bf16[768,128]{1,0:T(8,128)(2,1)S(1)}, u32[]{:S(2)}, u32[]{:S(2)}) %collective-permute-start.2) | collective-permute-done | bytes 196640 | tf_op jit(solution)/shard_map/ppermute | solution.py:196
  22.9 1.2 collective-permute-done.3.refs_2_
  24.8 1.6 collective-permute-start.6
  26.4 2.6 %collective-permute-start.5 = (bf16[768,128]{1,0:T(8,128)(2,1)S(1)}, bf16[768,128]{1,0:T(8,128)(2,1)S(1)}, u32[]{:S(2)}, u32[]{:S(2)}) collective-permute-start(bf16[768,128]{1,0:T(8,128)(2,1)S(1)} %get-tuple-element.59), channel_id=1, source_target_pairs={{0,8},{8,0},{1,9},{9,1},{2,10},{10,2},{3,11},{11,3},{4,12},{12,4},... | collective-permute-start | bytes 589832 | tf_op jit(solution)/shard_map/ppermute | solution.py:196
  29.0 3.9 %shard_map.89.refs_2_ = f32[128,3072]{1,0:T(8,128)S(1)} custom-call(bf16[128,3072]{1,0:T(8,128)(2,1)S(1)} %bitcast.36, bf16[128,3072]{1,0:T(8,128)(2,1)S(1)} %bitcast.33, bf16[128,3072]{1,0:T(8,128)(2,1)S(1)} %bitcast.28), custom_call_target="tpu_custom_call" | custom-call | flops 201326592 | bytes 3145728 | tf_op jit(solution)/shard_map/pallas_call | solution.py:177
  32.9 3.3 %collective-permute-done.5.refs_2_ = bf16[768,128]{1,0:T(8,128)(2,1)S(1)} collective-permute-done((bf16[768,128]{1,0:T(8,128)(2,1)S(1)}, bf16[768,128]{1,0:T(8,128)(2,1)S(1)}, u32[]{:S(2)}, u32[]{:S(2)}) %collective-permute-start.5) | collective-permute-done | bytes 196640 | tf_op jit(solution)/shard_map/ppermute | solution.py:196
  36.8 0.9 collective-permute-start.7
  38.4 4.4 %collective-permute-done.7.refs_1_ = bf16[768,128]{1,0:T(8,128)(2,1)S(1)} collective-permute-done((bf16[768,128]{1,0:T(8,128)(2,1)S(1)}, bf16[768,128]{1,0:T(8,128)(2,1)S(1)}, u32[]{:S(2)}, u32[]{:S(2)}) %collective-permute-start.7) | collective-permute-done | bytes 196640 | tf_op jit(solution)/shard_map/ppermute | solution.py:196
  43.5 1.4 collective-permute-done.9.refs_8_
  44.9 3.4 %shard_map.92 = (bf16[128,3072]{1,0:T(8,128)(2,1)S(1)}, bf16[3072,128]{1,0:T(8,128)(2,1)S(1)}, bf16[3072,128]{1,0:T(8,128)(2,1)S(1)}) custom-call(s32[14]{0:T(128)S(1)} %copy-done.14, bf16[128,3072]{1,0:T(8,128)(2,1)S(1)} %bitcast.37, f32[128,3072]{1,0:T(8,128)S(1)} %shard_map.89.refs_2_, bf16[128,3072]{1,0:T(8,128)(2,1)S(1)} %bitcast.44, ...), custom_call_target="tpu_custom_call" | custom-call | flops 201326592 | bytes 8650752 | tf_op jit(solution)/shard_map/pallas_call | solution.py:177
  48.6 1.1 collective-permute-start.15
  49.7 1.0 collective-permute-done.11.refs_2_
  51.4 0.7 collective-permute-start.13
  52.1 1.4 collective-permute-start.12
  53.5 3.9 %shard_map.94.refs_3_ = f32[128,3072]{1,0:T(8,128)S(1)} custom-call(bf16[128,3072]{1,0:T(8,128)(2,1)S(1)} %bitcast.38, bf16[128,3072]{1,0:T(8,128)(2,1)S(1)} %bitcast.29, bf16[128,3072]{1,0:T(8,128)(2,1)S(1)} %get-tuple-element.94.refs_2_.refs_3_), custom_call_target="tpu_custom_call" | custom-call | flops 201326592 | bytes 3145728 | tf_op jit(solution)/shard_map/pallas_call | solution.py:177
  57.4 1.8 %collective-permute-done.13.refs_2_.refs_1_ = bf16[768,128]{1,0:T(8,128)(2,1)S(1)} collective-permute-done((bf16[768,128]{1,0:T(8,128)(2,1)S(1)}, bf16[768,128]{1,0:T(8,128)(2,1)S(1)}, u32[]{:S(2)}, u32[]{:S(2)}) %collective-permute-start.13) | collective-permute-done | bytes 196640 | tf_op jit(solution)/shard_map/ppermute | solution.py:196
  59.8 1.1 collective-permute-start.14
  60.9 5.9 %collective-permute-done.12.refs_6_ = bf16[1,128,1536]{2,1,0:T(8,128)(2,1)S(1)} collective-permute-done((bf16[1,128,1536]{2,1,0:T(8,128)(2,1)S(1)}, bf16[1,128,1536]{2,1,0:T(8,128)(2,1)S(1)}, u32[]{:S(2)}, u32[]{:S(2)}) %collective-permute-start.12) | collective-permute-done | bytes 393248 | tf_op jit(solution)/shard_map/ppermute | solution.py:196
  67.5 0.7 collective-permute-start.17
  68.2 2.8 %collective-permute-start.16 = (bf16[768,128]{1,0:T(8,128)(2,1)S(1)}, bf16[768,128]{1,0:T(8,128)(2,1)S(1)}, u32[]{:S(2)}, u32[]{:S(2)}) collective-permute-start(bf16[768,128]{1,0:T(8,128)(2,1)S(1)} %get-tuple-element.78), channel_id=1, source_target_pairs={{0,8},{8,0},{1,9},{9,1},{2,10},{10,2},{3,11},{11,3},{4,12},{12,4},... | collective-permute-start | bytes 589832 | tf_op jit(solution)/shard_map/ppermute | solution.py:196
  71.0 0.9 collective-permute-start.20
  72.1 7.1 %collective-permute-done.16.refs_2_ = bf16[768,128]{1,0:T(8,128)(2,1)S(1)} collective-permute-done((bf16[768,128]{1,0:T(8,128)(2,1)S(1)}, bf16[768,128]{1,0:T(8,128)(2,1)S(1)}, u32[]{:S(2)}, u32[]{:S(2)}) %collective-permute-start.16) | collective-permute-done | bytes 196640 | tf_op jit(solution)/shard_map/ppermute | solution.py:196
  80.2 1.0 collective-permute-start.19
  81.2 2.0 %collective-permute-done.20.refs_2_ = bf16[768,128]{1,0:T(8,128)(2,1)S(1)} collective-permute-done((bf16[768,128]{1,0:T(8,128)(2,1)S(1)}, bf16[768,128]{1,0:T(8,128)(2,1)S(1)}, u32[]{:S(2)}, u32[]{:S(2)}) %collective-permute-start.20) | collective-permute-done | bytes 196640 | tf_op jit(solution)/shard_map/ppermute | solution.py:196
  83.3 3.0 %collective-permute-done.19.refs_1_ = bf16[768,128]{1,0:T(8,128)(2,1)S(1)} collective-permute-done((bf16[768,128]{1,0:T(8,128)(2,1)S(1)}, bf16[768,128]{1,0:T(8,128)(2,1)S(1)}, u32[]{:S(2)}, u32[]{:S(2)}) %collective-permute-start.19) | collective-permute-done | bytes 196640 | tf_op jit(solution)/shard_map/ppermute | solution.py:196
  88.9 3.8 %collective-permute-done.18.refs_7_ = bf16[1,128,1536]{2,1,0:T(8,128)(2,1)S(1)} collective-permute-done((bf16[1,128,1536]{2,1,0:T(8,128)(2,1)S(1)}, bf16[1,128,1536]{2,1,0:T(8,128)(2,1)S(1)}, u32[]{:S(2)}, u32[]{:S(2)}) %collective-permute-start.18) | collective-permute-done | bytes 393248 | tf_op jit(solution)/shard_map/ppermute | solution.py:196
  92.8 3.3 %shard_map.99 = (bf16[128,3072]{1,0:T(8,128)(2,1)}, bf16[3072,128]{1,0:T(8,128)(2,1)S(1)}, bf16[2,8,2,96,128]{4,3,2,1,0:T(8,128)(2,1)S(1)}, bf16[2,8,2,96,128]{4,3,2,1,0:T(8,128)(2,1)}) custom-call(s32[14]{0:T(128)S(1)} %copy-done.14, bf16[128,3072]{1,0:T(8,128)(2,1)S(1)} %bitcast.34, bf16[128,3072]{1,0:T(8,128)(2,1)S(1)} %bitcast.30, ...), custom_call_target="tpu_custom_call" | custom-call | flops 100663296 | bytes 9437184 | tf_op jit(solution)/shard_map/pallas_call | solution.py:177
  96.2 0.9 copy-done.10
  97.2 17.3 %all_to_all.10.turned_ref = bf16[16,192,128]{2,1,0:T(8,128)(2,1)} all-to-all(bf16[16,192,128]{2,1,0:T(8,128)(2,1)S(1)} %bitcast.47), channel_id=1, replica_groups=mesh['dp'=2,'bit3'=2,'bit2'=2,'bit1'=2,'bit0'=2] {'dp','bit2','bit1','bi..., dimensions={0} | all-to-all | bytes 1572864 | tf_op jit(solution)/shard_map/all_to_all | solution.py:485
  114.6 4.5 %all-to-all-start = ((bf16[16,192,128]{2,1,0:T(8,128)(2,1)}), bf16[16,192,128]{2,1,0:T(8,128)(2,1)}, u32[]{:S(2)}, u32[]{:S(2)}) async-start(bf16[16,192,128]{2,1,0:T(8,128)(2,1)} %bitcast.20), calls=%async_computation | async-start | bytes 1572864 | tf_op jit(solution)/shard_map/all_to_all | solution.py:485
  119.1 5.6 %shard_map.100 = (f32[96,1536]{1,0:T(8,128)}, bf16[1,96,1536]{2,1,0:T(8,128)(2,1)}) custom-call(s32[14]{0:T(128)} %copy-done.12, bf16[16,192,128]{2,1,0:T(8,128)(2,1)} %all_to_all.10.turned_ref, bf16[1,128,1536]{2,1,0:T(8,128)(2,1)} %bitcast.48, bf16[1,128,1536]{2,1,0:T(8,128)(2,1)} %bitcast.56, bf16[1,128,1536]{2,1,0:T(8,128)(2,1)} %copy-done.19, ...), custom_call_target="tpu_custom_call" | custom-call | flops 1207959552 | bytes 8060928 | tf_op jit(solution)/shard_map/pallas_call | solution.py:366
  124.7 3.4 %collective-permute-start.31 = (bf16[96,1536]{1,0:T(8,128)(2,1)}, bf16[96,1536]{1,0:T(8,128)(2,1)S(1)}, u32[]{:S(2)}, u32[]{:S(2)}) collective-permute-start(bf16[96,1536]{1,0:T(8,128)(2,1)} %bitcast.62), channel_id=1, source_target_pairs={{0,8},{8,0},{1,9},{9,1},{2,10},{10,2},{3,11},{11,3},{4,12},{12,4},... | collective-permute-start | bytes 884744 | tf_op jit(solution)/shard_map/ppermute | solution.py:488
  128.1 8.0 %all-to-all-done.turned_ref = bf16[16,192,128]{2,1,0:T(8,128)(2,1)} async-done(((bf16[16,192,128]{2,1,0:T(8,128)(2,1)}), bf16[16,192,128]{2,1,0:T(8,128)(2,1)}, u32[]{:S(2)}, u32[]{:S(2)}) %all-to-all-start) | async-done | bytes 786464 | tf_op jit(solution)/shard_map/all_to_all | solution.py:485
  136.1 5.7 %shard_map.101 = (f32[96,1536]{1,0:T(8,128)}, bf16[1,96,1536]{2,1,0:T(8,128)(2,1)}) custom-call(s32[14]{0:T(128)} %copy-done.12, bf16[16,192,128]{2,1,0:T(8,128)(2,1)} %all-to-all-done.turned_ref, bf16[1,128,1536]{2,1,0:T(8,128)(2,1)} %bitcast.49, bf16[1,128,1536]{2,1,0:T(8,128)(2,1)} %bitcast.57, bf16[1,128,1536]{2,1,0:T(8,128)(2,1)} %copy-done.19, ...), custom_call_target="tpu_custom_call" | custom-call | flops 1207959552 | bytes 8060928 | tf_op jit(solution)/shard_map/pallas_call | solution.py:366
  142.1 5.9 %shard_map.102 = (bf16[128,3072]{1,0:T(8,128)(2,1)}, bf16[128,3072]{1,0:T(8,128)(2,1)}) custom-call(bf16[128,3072]{1,0:T(8,128)(2,1)S(1)} %bitcast.39, bf16[128,3072]{1,0:T(8,128)(2,1)S(1)} %bitcast.35, bf16[128,3072]{1,0:T(8,128)(2,1)S(1)} %bitcast.31, bf16[128,3072]{1,0:T(8,128)(2,1)S(1)} %copy-done.6, bf16[3072,128]{1,0:T(8,128)(2,1)S(1)} %copy-done.9, ...), custom_call_target="tpu_custom_call" | custom-call | flops 603979776 | bytes 6291456 | tf_op jit(solution)/shard_map/pallas_call | solution.py:177
  148.5 6.2 %collective-permute-done.32 = bf16[96,1536]{1,0:T(8,128)(2,1)S(1)} collective-permute-done((bf16[96,1536]{1,0:T(8,128)(2,1)}, bf16[96,1536]{1,0:T(8,128)(2,1)S(1)}, u32[]{:S(2)}, u32[]{:S(2)}) %collective-permute-start.32) | collective-permute-done | bytes 294944 | tf_op jit(solution)/shard_map/ppermute | solution.py:488
  154.8 1.1 maximum_multiply_fusion
  (110 shorter events, 11.3 us)
Async XLA Ops:
  3.9 2.4 %collective-permute-start = (bf16[2,2,768,128]{3,2,1,0:T(8,128)(2,1)S(1)}, bf16[2,2,768,128]{3,2,1,0:T(8,128)(2,1)S(1)}, u32[]{:S(2)}, u32[]{:S(2)}) collective-permute-start(bf16[2,2,768,128]{3,2,1,0:T(8,128)(2,1)S(1)} %bitcast.42), channel_id=1, source_target_pairs={{0,1},{1,0},{2,3},{3,2},{4,5},{5,4},{6,7},{7,6},{8,9},{9,8},{10,11... | collective-permute-start | bytes 2359304 | tf_op jit(solution)/shard_map/ppermute | solution.py:196
  6.4 22.6 %copy-start.4 = (bf16[1,128,3072]{2,1,0:T(8,128)(2,1)S(1)}, bf16[1,128,3072]{2,1,0:T(8,128)(2,1)}, u32[]{:S(2)}) copy-start(bf16[1,128,3072]{2,1,0:T(8,128)(2,1)} %param.6) | copy-start | bytes 2359300
  7.0 22.0 %copy-start.1 = (bf16[1,128,3072]{2,1,0:T(8,128)(2,1)S(1)}, bf16[1,128,3072]{2,1,0:T(8,128)(2,1)}, u32[]{:S(2)}) copy-start(bf16[1,128,3072]{2,1,0:T(8,128)(2,1)} %param.8) | copy-start | bytes 2359300
  7.0 21.9 %copy-start.3 = (bf16[1,128,3072]{2,1,0:T(8,128)(2,1)S(1)}, bf16[1,128,3072]{2,1,0:T(8,128)(2,1)}, u32[]{:S(2)}) copy-start(bf16[1,128,3072]{2,1,0:T(8,128)(2,1)} %param.7) | copy-start | bytes 2359300
  7.0 8.1 %collective-permute-start.1 = (bf16[768,128]{1,0:T(8,128)(2,1)S(1)}, bf16[768,128]{1,0:T(8,128)(2,1)S(1)}, u32[]{:S(2)}, u32[]{:S(2)}) collective-permute-start(bf16[768,128]{1,0:T(8,128)(2,1)S(1)} %get-tuple-element.54), channel_id=1, source_target_pairs={{0,2},{2,0},{1,3},{3,1},{4,6},{6,4},{5,7},{7,5},{8,10},{10,8},{9,1... | collective-permute-start | bytes 589832 | tf_op jit(solution)/shard_map/ppermute | solution.py:196
  12.5 11.6 %collective-permute-start.4 = (bf16[128,1536]{1,0:T(8,128)(2,1)}, bf16[128,1536]{1,0:T(8,128)(2,1)S(1)}, u32[]{:S(2)}, u32[]{:S(2)}) collective-permute-start(bf16[128,1536]{1,0:T(8,128)(2,1)} %get-tuple-element.57), channel_id=1, source_target_pairs={{0,16},{16,0},{1,17},{17,1},{2,18},{18,2},{3,19},{19,3},{4,20},{20... | collective-permute-start | bytes 1179656 | tf_op jit(solution)/shard_map/ppermute | solution.py:196
  16.4 6.5 %collective-permute-start.2 = (bf16[768,128]{1,0:T(8,128)(2,1)S(1)}, bf16[768,128]{1,0:T(8,128)(2,1)S(1)}, u32[]{:S(2)}, u32[]{:S(2)}) collective-permute-start(bf16[768,128]{1,0:T(8,128)(2,1)S(1)} %shard_map.86.refs_1_), channel_id=1, source_target_pairs={{0,4},{4,0},{1,5},{5,1},{2,6},{6,2},{3,7},{7,3},{8,12},{12,8},{9,1... | collective-permute-start | bytes 589832 | tf_op jit(solution)/shard_map/ppermute | solution.py:196
  18.3 5.8 %collective-permute-start.3 = (bf16[768,128]{1,0:T(8,128)(2,1)S(1)}, bf16[768,128]{1,0:T(8,128)(2,1)S(1)}, u32[]{:S(2)}, u32[]{:S(2)}) collective-permute-start(bf16[768,128]{1,0:T(8,128)(2,1)S(1)} %get-tuple-element.55.refs_1_), channel_id=1, source_target_pairs={{0,2},{2,0},{1,3},{3,1},{4,6},{6,4},{5,7},{7,5},{8,10},{10,8},{9,1... | collective-permute-start | bytes 589832 | tf_op jit(solution)/shard_map/ppermute | solution.py:196
  24.2 47.7 %copy-start.16 = (bf16[128,1536]{1,0:T(8,128)(2,1)}, bf16[128,1536]{1,0:T(8,128)(2,1)S(1)}, u32[]{:S(2)}) copy-start(bf16[128,1536]{1,0:T(8,128)(2,1)S(1)} %collective-permute-done.4) | copy-start | bytes 1179652
  24.8 11.3 %collective-permute-start.6 = (bf16[1,128,1536]{2,1,0:T(8,128)(2,1)S(1)}, bf16[1,128,1536]{2,1,0:T(8,128)(2,1)S(1)}, u32[]{:S(2)}, u32[]{:S(2)}) collective-permute-start(bf16[1,128,1536]{2,1,0:T(8,128)(2,1)S(1)} %bitcast.53), channel_id=1, source_target_pairs={{0,2},{2,0},{1,3},{3,1},{4,6},{6,4},{5,7},{7,5},{8,10},{10,8},{9,1... | collective-permute-start | bytes 1179656 | tf_op jit(solution)/shard_map/ppermute | solution.py:196
  26.4 9.7 %collective-permute-start.5 = (bf16[768,128]{1,0:T(8,128)(2,1)S(1)}, bf16[768,128]{1,0:T(8,128)(2,1)S(1)}, u32[]{:S(2)}, u32[]{:S(2)}) collective-permute-start(bf16[768,128]{1,0:T(8,128)(2,1)S(1)} %get-tuple-element.59), channel_id=1, source_target_pairs={{0,8},{8,0},{1,9},{9,1},{2,10},{10,2},{3,11},{11,3},{4,12},{12,4},... | collective-permute-start | bytes 589832 | tf_op jit(solution)/shard_map/ppermute | solution.py:196
  36.1 45.1 %copy-start.17 = (bf16[1,128,1536]{2,1,0:T(8,128)(2,1)}, bf16[1,128,1536]{2,1,0:T(8,128)(2,1)S(1)}, u32[]{:S(2)}) copy-start(bf16[1,128,1536]{2,1,0:T(8,128)(2,1)S(1)} %collective-permute-done.6.refs_4_) | copy-start | bytes 1179652
  36.8 6.0 %collective-permute-start.7 = (bf16[768,128]{1,0:T(8,128)(2,1)S(1)}, bf16[768,128]{1,0:T(8,128)(2,1)S(1)}, u32[]{:S(2)}, u32[]{:S(2)}) collective-permute-start(bf16[768,128]{1,0:T(8,128)(2,1)S(1)} %get-tuple-element.65), channel_id=1, source_target_pairs={{0,2},{2,0},{1,3},{3,1},{4,6},{6,4},{5,7},{7,5},{8,10},{10,8},{9,1... | collective-permute-start | bytes 589832 | tf_op jit(solution)/shard_map/ppermute | solution.py:196
  37.7 10.6 %collective-permute-start.10 = (bf16[1,128,1536]{2,1,0:T(8,128)(2,1)S(1)}, bf16[1,128,1536]{2,1,0:T(8,128)(2,1)S(1)}, u32[]{:S(2)}, u32[]{:S(2)}) collective-permute-start(bf16[1,128,1536]{2,1,0:T(8,128)(2,1)S(1)} %bitcast.54), channel_id=1, source_target_pairs={{0,4},{4,0},{1,5},{5,1},{2,6},{6,2},{3,7},{7,3},{8,12},{12,8},{9,1... | collective-permute-start | bytes 1179656 | tf_op jit(solution)/shard_map/ppermute | solution.py:196
  38.4 5.1 %collective-permute-start.8 = (bf16[768,128]{1,0:T(8,128)(2,1)S(1)}, bf16[768,128]{1,0:T(8,128)(2,1)S(1)}, u32[]{:S(2)}, u32[]{:S(2)}) collective-permute-start(bf16[768,128]{1,0:T(8,128)(2,1)S(1)} %get-tuple-element.64.refs_5_), channel_id=1, source_target_pairs={{0,1},{1,0},{2,3},{3,2},{4,5},{5,4},{6,7},{7,6},{8,9},{9,8},{10,11... | collective-permute-start | bytes 589832 | tf_op jit(solution)/shard_map/ppermute | solution.py:196
  43.4 1.5 collective-permute-start.9
  48.4 39.1 %copy-start.18 = (bf16[1,128,1536]{2,1,0:T(8,128)(2,1)}, bf16[1,128,1536]{2,1,0:T(8,128)(2,1)S(1)}, u32[]{:S(2)}) copy-start(bf16[1,128,1536]{2,1,0:T(8,128)(2,1)S(1)} %collective-permute-done.10.refs_3_) | copy-start | bytes 1179652
  48.4 2.4 %collective-permute-start.11 = (bf16[2,2,768,128]{3,2,1,0:T(8,128)(2,1)S(1)}, bf16[2,2,768,128]{3,2,1,0:T(8,128)(2,1)S(1)}, u32[]{:S(2)}, u32[]{:S(2)}) collective-permute-start(bf16[2,2,768,128]{3,2,1,0:T(8,128)(2,1)S(1)} %bitcast.45), channel_id=1, source_target_pairs={{0,1},{1,0},{2,3},{3,2},{4,5},{5,4},{6,7},{7,6},{8,9},{9,8},{10,11... | collective-permute-start | bytes 2359304 | tf_op jit(solution)/shard_map/ppermute | solution.py:196
  48.6 12.3 %collective-permute-start.15 = (bf16[1,128,1536]{2,1,0:T(8,128)(2,1)S(1)}, bf16[1,128,1536]{2,1,0:T(8,128)(2,1)S(1)}, u32[]{:S(2)}, u32[]{:S(2)}) collective-permute-start(bf16[1,128,1536]{2,1,0:T(8,128)(2,1)S(1)} %bitcast.50), channel_id=1, source_target_pairs={{0,4},{4,0},{1,5},{5,1},{2,6},{6,2},{3,7},{7,3},{8,12},{12,8},{9,1... | collective-permute-start | bytes 1179656 | tf_op jit(solution)/shard_map/ppermute | solution.py:196
  51.4 7.8 %collective-permute-start.13 = (bf16[768,128]{1,0:T(8,128)(2,1)S(1)}, bf16[768,128]{1,0:T(8,128)(2,1)S(1)}, u32[]{:S(2)}, u32[]{:S(2)}) collective-permute-start(bf16[768,128]{1,0:T(8,128)(2,1)S(1)} %get-tuple-element.73), channel_id=1, source_target_pairs={{0,2},{2,0},{1,3},{3,1},{4,6},{6,4},{5,7},{7,5},{8,10},{10,8},{9,1... | collective-permute-start | bytes 589832 | tf_op jit(solution)/shard_map/ppermute | solution.py:196
  52.1 14.7 %collective-permute-start.12 = (bf16[1,128,1536]{2,1,0:T(8,128)(2,1)S(1)}, bf16[1,128,1536]{2,1,0:T(8,128)(2,1)S(1)}, u32[]{:S(2)}, u32[]{:S(2)}) collective-permute-start(bf16[1,128,1536]{2,1,0:T(8,128)(2,1)S(1)} %bitcast.51), channel_id=1, source_target_pairs={{0,2},{2,0},{1,3},{3,1},{4,6},{6,4},{5,7},{7,5},{8,10},{10,8},{9,1... | collective-permute-start | bytes 1179656 | tf_op jit(solution)/shard_map/ppermute | solution.py:196
  59.8 7.0 %collective-permute-start.14 = (bf16[768,128]{1,0:T(8,128)(2,1)S(1)}, bf16[768,128]{1,0:T(8,128)(2,1)S(1)}, u32[]{:S(2)}, u32[]{:S(2)}) collective-permute-start(bf16[768,128]{1,0:T(8,128)(2,1)S(1)} %shard_map.95.refs_1_), channel_id=1, source_target_pairs={{0,4},{4,0},{1,5},{5,1},{2,6},{6,2},{3,7},{7,3},{8,12},{12,8},{9,1... | collective-permute-start | bytes 589832 | tf_op jit(solution)/shard_map/ppermute | solution.py:196
  60.9 35.2 %copy-start.19 = (bf16[1,128,1536]{2,1,0:T(8,128)(2,1)}, bf16[1,128,1536]{2,1,0:T(8,128)(2,1)S(1)}, u32[]{:S(2)}) copy-start(bf16[1,128,1536]{2,1,0:T(8,128)(2,1)S(1)} %collective-permute-done.15.refs_2_) | copy-start | bytes 1179652
  66.8 29.3 %copy-start.20 = (bf16[1,128,1536]{2,1,0:T(8,128)(2,1)}, bf16[1,128,1536]{2,1,0:T(8,128)(2,1)S(1)}, u32[]{:S(2)}) copy-start(bf16[1,128,1536]{2,1,0:T(8,128)(2,1)S(1)} %collective-permute-done.12.refs_6_) | copy-start | bytes 1179652
  67.5 12.1 %collective-permute-start.17 = (bf16[1,128,1536]{2,1,0:T(8,128)(2,1)S(1)}, bf16[1,128,1536]{2,1,0:T(8,128)(2,1)S(1)}, u32[]{:S(2)}, u32[]{:S(2)}) collective-permute-start(bf16[1,128,1536]{2,1,0:T(8,128)(2,1)S(1)} %collective-permute-done.10.refs_3_), channel_id=1, source_target_pairs={{0,2},{2,0},{1,3},{3,1},{4,6},{6,4},{5,7},{7,5},{8,10},{10,8},{9,1... | collective-permute-start | bytes 1179656 | tf_op jit(solution)/shard_map/ppermute | solution.py:196
  68.2 11.0 %collective-permute-start.16 = (bf16[768,128]{1,0:T(8,128)(2,1)S(1)}, bf16[768,128]{1,0:T(8,128)(2,1)S(1)}, u32[]{:S(2)}, u32[]{:S(2)}) collective-permute-start(bf16[768,128]{1,0:T(8,128)(2,1)S(1)} %get-tuple-element.78), channel_id=1, source_target_pairs={{0,8},{8,0},{1,9},{9,1},{2,10},{10,2},{3,11},{11,3},{4,12},{12,4},... | collective-permute-start | bytes 589832 | tf_op jit(solution)/shard_map/ppermute | solution.py:196
  71.0 15.9 %collective-permute-start.23 = (bf16[1,128,1536]{2,1,0:T(8,128)(2,1)S(1)}, bf16[1,128,1536]{2,1,0:T(8,128)(2,1)S(1)}, u32[]{:S(2)}, u32[]{:S(2)}) collective-permute-start(bf16[1,128,1536]{2,1,0:T(8,128)(2,1)S(1)} %bitcast.52), channel_id=1, source_target_pairs={{0,1},{1,0},{2,3},{3,2},{4,5},{5,4},{6,7},{7,6},{8,9},{9,8},{10,11... | collective-permute-start | bytes 1179656 | tf_op jit(solution)/shard_map/ppermute | solution.py:196
  71.0 12.3 %collective-permute-start.20 = (bf16[768,128]{1,0:T(8,128)(2,1)S(1)}, bf16[768,128]{1,0:T(8,128)(2,1)S(1)}, u32[]{:S(2)}, u32[]{:S(2)}) collective-permute-start(bf16[768,128]{1,0:T(8,128)(2,1)S(1)} %get-tuple-element.86.refs_1_), channel_id=1, source_target_pairs={{0,2},{2,0},{1,3},{3,1},{4,6},{6,4},{5,7},{7,5},{8,10},{10,8},{9,1... | collective-permute-start | bytes 589832 | tf_op jit(solution)/shard_map/ppermute | solution.py:196
  71.8 15.7 %collective-permute-start.24 = (bf16[1,128,1536]{2,1,0:T(8,128)(2,1)S(1)}, bf16[1,128,1536]{2,1,0:T(8,128)(2,1)S(1)}, u32[]{:S(2)}, u32[]{:S(2)}) collective-permute-start(bf16[1,128,1536]{2,1,0:T(8,128)(2,1)S(1)} %bitcast.55), channel_id=1, source_target_pairs={{0,1},{1,0},{2,3},{3,2},{4,5},{5,4},{6,7},{7,6},{8,9},{9,8},{10,11... | collective-permute-start | bytes 1179656 | tf_op jit(solution)/shard_map/ppermute | solution.py:196
  80.2 6.0 %collective-permute-start.19 = (bf16[768,128]{1,0:T(8,128)(2,1)S(1)}, bf16[768,128]{1,0:T(8,128)(2,1)S(1)}, u32[]{:S(2)}, u32[]{:S(2)}) collective-permute-start(bf16[768,128]{1,0:T(8,128)(2,1)S(1)} %get-tuple-element.82), channel_id=1, source_target_pairs={{0,2},{2,0},{1,3},{3,1},{4,6},{6,4},{5,7},{7,5},{8,10},{10,8},{9,1... | collective-permute-start | bytes 589832 | tf_op jit(solution)/shard_map/ppermute | solution.py:196
  81.2 6.4 %collective-permute-start.27 = (bf16[1,128,1536]{2,1,0:T(8,128)(2,1)S(1)}, bf16[1,128,1536]{2,1,0:T(8,128)(2,1)S(1)}, u32[]{:S(2)}, u32[]{:S(2)}) collective-permute-start(bf16[1,128,1536]{2,1,0:T(8,128)(2,1)S(1)} %collective-permute-done.6.refs_4_), channel_id=1, source_target_pairs={{0,1},{1,0},{2,3},{3,2},{4,5},{5,4},{6,7},{7,6},{8,9},{9,8},{10,11... | collective-permute-start | bytes 1179656 | tf_op jit(solution)/shard_map/ppermute | solution.py:196
  83.3 9.5 %collective-permute-start.18 = (bf16[1,128,1536]{2,1,0:T(8,128)(2,1)S(1)}, bf16[1,128,1536]{2,1,0:T(8,128)(2,1)S(1)}, u32[]{:S(2)}, u32[]{:S(2)}) collective-permute-start(bf16[1,128,1536]{2,1,0:T(8,128)(2,1)S(1)} %collective-permute-done.12.refs_6_), channel_id=1, source_target_pairs={{0,4},{4,0},{1,5},{5,1},{2,6},{6,2},{3,7},{7,3},{8,12},{12,8},{9,1... | collective-permute-start | bytes 1179656 | tf_op jit(solution)/shard_map/ppermute | solution.py:196
  86.3 1.8 %collective-permute-start.21 = (bf16[768,128]{1,0:T(8,128)(2,1)S(1)}, bf16[768,128]{1,0:T(8,128)(2,1)S(1)}, u32[]{:S(2)}, u32[]{:S(2)}) collective-permute-start(bf16[768,128]{1,0:T(8,128)(2,1)S(1)} %get-tuple-element.85.refs_5_), channel_id=1, source_target_pairs={{0,1},{1,0},{2,3},{3,2},{4,5},{5,4},{6,7},{7,6},{8,9},{9,8},{10,11... | collective-permute-start | bytes 589832 | tf_op jit(solution)/shard_map/ppermute | solution.py:196
  86.9 1.6 %collective-permute-start.22 = (bf16[768,128]{1,0:T(8,128)(2,1)S(1)}, bf16[768,128]{1,0:T(8,128)(2,1)S(1)}, u32[]{:S(2)}, u32[]{:S(2)}) collective-permute-start(bf16[768,128]{1,0:T(8,128)(2,1)S(1)} %shard_map.98.refs_6_), channel_id=1, source_target_pairs={{0,1},{1,0},{2,3},{3,2},{4,5},{5,4},{6,7},{7,6},{8,9},{9,8},{10,11... | collective-permute-start | bytes 589832 | tf_op jit(solution)/shard_map/ppermute | solution.py:196
  87.5 9.6 %collective-permute-start.26 = (bf16[1,128,1536]{2,1,0:T(8,128)(2,1)S(1)}, bf16[1,128,1536]{2,1,0:T(8,128)(2,1)S(1)}, u32[]{:S(2)}, u32[]{:S(2)}) collective-permute-start(bf16[1,128,1536]{2,1,0:T(8,128)(2,1)S(1)} %collective-permute-done.10.refs_3_), channel_id=1, source_target_pairs={{0,1},{1,0},{2,3},{3,2},{4,5},{5,4},{6,7},{7,6},{8,9},{9,8},{10,11... | collective-permute-start | bytes 1179656 | tf_op jit(solution)/shard_map/ppermute | solution.py:196
  87.6 9.5 %collective-permute-start.25 = (bf16[1,128,1536]{2,1,0:T(8,128)(2,1)S(1)}, bf16[1,128,1536]{2,1,0:T(8,128)(2,1)S(1)}, u32[]{:S(2)}, u32[]{:S(2)}) collective-permute-start(bf16[1,128,1536]{2,1,0:T(8,128)(2,1)S(1)} %collective-permute-done.15.refs_2_), channel_id=1, source_target_pairs={{0,1},{1,0},{2,3},{3,2},{4,5},{5,4},{6,7},{7,6},{8,9},{9,8},{10,11... | collective-permute-start | bytes 1179656 | tf_op jit(solution)/shard_map/ppermute | solution.py:196
  88.1 9.1 %collective-permute-start.29 = (bf16[1,128,1536]{2,1,0:T(8,128)(2,1)S(1)}, bf16[1,128,1536]{2,1,0:T(8,128)(2,1)S(1)}, u32[]{:S(2)}, u32[]{:S(2)}) collective-permute-start(bf16[1,128,1536]{2,1,0:T(8,128)(2,1)S(1)} %collective-permute-done.12.refs_6_), channel_id=1, source_target_pairs={{0,1},{1,0},{2,3},{3,2},{4,5},{5,4},{6,7},{7,6},{8,9},{9,8},{10,11... | collective-permute-start | bytes 1179656 | tf_op jit(solution)/shard_map/ppermute | solution.py:196
  88.6 8.6 %collective-permute-start.28 = (bf16[1,128,1536]{2,1,0:T(8,128)(2,1)S(1)}, bf16[1,128,1536]{2,1,0:T(8,128)(2,1)S(1)}, u32[]{:S(2)}, u32[]{:S(2)}) collective-permute-start(bf16[1,128,1536]{2,1,0:T(8,128)(2,1)S(1)} %collective-permute-done.17.refs_5_), channel_id=1, source_target_pairs={{0,1},{1,0},{2,3},{3,2},{4,5},{5,4},{6,7},{7,6},{8,9},{9,8},{10,11... | collective-permute-start | bytes 1179656 | tf_op jit(solution)/shard_map/ppermute | solution.py:196
  92.8 4.4 %collective-permute-start.30 = (bf16[1,128,1536]{2,1,0:T(8,128)(2,1)S(1)}, bf16[1,128,1536]{2,1,0:T(8,128)(2,1)S(1)}, u32[]{:S(2)}, u32[]{:S(2)}) collective-permute-start(bf16[1,128,1536]{2,1,0:T(8,128)(2,1)S(1)} %collective-permute-done.18.refs_7_), channel_id=1, source_target_pairs={{0,1},{1,0},{2,3},{3,2},{4,5},{5,4},{6,7},{7,6},{8,9},{9,8},{10,11... | collective-permute-start | bytes 1179656 | tf_op jit(solution)/shard_map/ppermute | solution.py:196
  97.1 17.4 %copy-start.26 = (bf16[1,128,1536]{2,1,0:T(8,128)(2,1)}, bf16[1,128,1536]{2,1,0:T(8,128)(2,1)S(1)}, u32[]{:S(2)}) copy-start(bf16[1,128,1536]{2,1,0:T(8,128)(2,1)S(1)} %collective-permute-done.26.refs_11_) | copy-start | bytes 1179652
  97.1 17.4 %copy-start.27 = (bf16[1,128,1536]{2,1,0:T(8,128)(2,1)}, bf16[1,128,1536]{2,1,0:T(8,128)(2,1)S(1)}, u32[]{:S(2)}) copy-start(bf16[1,128,1536]{2,1,0:T(8,128)(2,1)S(1)} %collective-permute-done.25.refs_10_) | copy-start | bytes 1179652
  97.2 17.4 %copy-start.28 = (bf16[1,128,1536]{2,1,0:T(8,128)(2,1)}, bf16[1,128,1536]{2,1,0:T(8,128)(2,1)S(1)}, u32[]{:S(2)}) copy-start(bf16[1,128,1536]{2,1,0:T(8,128)(2,1)S(1)} %collective-permute-done.29.refs_14_) | copy-start | bytes 1179652
  97.2 17.4 %copy-start.29 = (bf16[1,128,1536]{2,1,0:T(8,128)(2,1)}, bf16[1,128,1536]{2,1,0:T(8,128)(2,1)S(1)}, u32[]{:S(2)}) copy-start(bf16[1,128,1536]{2,1,0:T(8,128)(2,1)S(1)} %collective-permute-done.28.refs_13_) | copy-start | bytes 1179652
  97.2 17.4 %copy-start.30 = (bf16[1,128,1536]{2,1,0:T(8,128)(2,1)}, bf16[1,128,1536]{2,1,0:T(8,128)(2,1)S(1)}, u32[]{:S(2)}) copy-start(bf16[1,128,1536]{2,1,0:T(8,128)(2,1)S(1)} %collective-permute-done.30.refs_15_) | copy-start | bytes 1179652
  114.6 21.6 %all-to-all-start = ((bf16[16,192,128]{2,1,0:T(8,128)(2,1)}), bf16[16,192,128]{2,1,0:T(8,128)(2,1)}, u32[]{:S(2)}, u32[]{:S(2)}) async-start(bf16[16,192,128]{2,1,0:T(8,128)(2,1)} %bitcast.20), calls=%async_computation | async-start | bytes 1572864 | tf_op jit(solution)/shard_map/all_to_all | solution.py:485
  124.7 17.4 %copy-start.6 = (bf16[128,3072]{1,0:T(8,128)(2,1)S(1)}, bf16[128,3072]{1,0:T(8,128)(2,1)}, u32[]{:S(2)}) copy-start(bf16[128,3072]{1,0:T(8,128)(2,1)} %copy-done.5) | copy-start | bytes 2359300
  124.7 23.7 %collective-permute-start.31 = (bf16[96,1536]{1,0:T(8,128)(2,1)}, bf16[96,1536]{1,0:T(8,128)(2,1)S(1)}, u32[]{:S(2)}, u32[]{:S(2)}) collective-permute-start(bf16[96,1536]{1,0:T(8,128)(2,1)} %bitcast.62), channel_id=1, source_target_pairs={{0,8},{8,0},{1,9},{9,1},{2,10},{10,2},{3,11},{11,3},{4,12},{12,4},... | collective-permute-start | bytes 884744 | tf_op jit(solution)/shard_map/ppermute | solution.py:488
  141.9 12.9 %collective-permute-start.32 = (bf16[96,1536]{1,0:T(8,128)(2,1)}, bf16[96,1536]{1,0:T(8,128)(2,1)S(1)}, u32[]{:S(2)}, u32[]{:S(2)}) collective-permute-start(bf16[96,1536]{1,0:T(8,128)(2,1)} %bitcast.63), channel_id=1, source_target_pairs={{0,8},{8,0},{1,9},{9,1},{2,10},{10,2},{3,11},{11,3},{4,12},{12,4},... | collective-permute-start | bytes 884744 | tf_op jit(solution)/shard_map/ppermute | solution.py:488
  (19 other events, 121.6 us)

commit v5 on v4

--- a/solution.py
+++ b/solution.py
@@ -118,7 +118,7 @@
     value_out[:, at] = value.astype(BF16)
 
 
-def by_heads(head, operands, outs, matmuls, flags=None, vmem=12):
+def by_heads(head, operands, outs, matmuls, bits=None, vmem=12):
     tokens, features = operands[0][1].shape
     groups = 2 if features % (2 * HEAD_DIM) == 0 else 1
     group = features // groups
@@ -137,8 +137,7 @@
         return ref.at[:, cut] if kind == "row" else ref.at[cut, :]
 
     def body(*refs):
-        numbers = [] if flags is None else [refs[0]]
-        refs = refs[len(numbers) :]
+        numbers = [] if bits is None else [numbers_of(bits)]
         there, moved = refs[: len(kinds)], refs[-1]
         scratch = iter(refs[len(kinds) : -1])
         here = [ref if stays else next(scratch) for stays, ref in zip(held, there)]
@@ -176,7 +175,7 @@
     places = [pl.BlockSpec(memory_space=pltpu.VMEM) if stays else anywhere for stays in held]
     return pl.pallas_call(
         body,
-        in_specs=([] if flags is None else [pl.BlockSpec(memory_space=pltpu.SMEM)]) + places[:count],
+        in_specs=places[:count],
         out_specs=places[count:],
         out_shape=results,
         scratch_shapes=[
@@ -189,34 +188,40 @@
             bytes_accessed=tokens * features * 2 * len(kinds),
             transcendentals=0,
         ),
-    )(*([] if flags is None else [flags]), *[array for _, array in operands])
+    )(*[array for _, array in operands])
 
 
 def swap(array, axis):
     return lax.ppermute(array, axis, [(0, 1), (1, 0)])
 
 
+def numbers_of(bits):
+    place = [lax.axis_index(bit) for bit in bits]
+    span = sum(2**index * at for index, at in enumerate(place[3:]))
+    return place + place + [1 - at for at in place] + [lax.axis_index("dp"), span]
+
+
 def added_if(flag, a, b):
     return (a.astype(F32) + jnp.where(flag, b.astype(F32), 0.0)).astype(BF16)
 
 
-def small(body, flags, arrays, outs):
+def small(body, bits, arrays, outs):
     vmem = pl.BlockSpec(memory_space=pltpu.VMEM)
     result = jax.ShapeDtypeStruct(arrays[-1].shape[-2:], BF16)
 
     def kernel(*refs):
-        values = body(*refs[: 1 + len(arrays)])
-        for ref, value in zip(refs[1 + len(arrays) :], values):
+        values = body(numbers_of(bits), *refs[: len(arrays)])
+        for ref, value in zip(refs[len(arrays) :], values):
             ref[...] = value
 
     return pl.pallas_call(
         kernel,
-        in_specs=[pl.BlockSpec(memory_space=pltpu.SMEM)] + [vmem] * len(arrays),
+        in_specs=[vmem] * len(arrays),
         out_specs=[vmem] * outs,
         out_shape=[result] * outs,
         compiler_params=pltpu.CompilerParams(vmem_limit_bytes=4 * 1024 * 1024),
         cost_estimate=pl.CostEstimate(flops=0, bytes_accessed=1024, transcendentals=0),
-    )(flags, *arrays)
+    )(*arrays)
 
 
 def after(array, *others):
@@ -226,10 +231,10 @@
 
 
 class Scan:
-    def __init__(self, state, bits, backward, flags):
+    def __init__(self, state, bits, backward):
         first, second, *self.rest = bits
         self.first, self.second = first, second
-        self.flags, self.counts = flags, (2 if backward else 1) * len(bits)
+        self.bits, self.counts = bits, (2 if backward else 1) * len(bits)
         state = state.reshape(2, 2, -1, HEAD_DIM)
         self.other = swap(state, first)
 
@@ -237,7 +242,7 @@
             core, side = flags[0], flags[1]
             return [added_if(True, state[core, at], other[core, at]) for at in (1 - side, side)]
 
-        self.theirs, self.mine = small(quarters, self.flags, [state, self.other], 2)
+        self.theirs, self.mine = small(quarters, self.bits, [state, self.other], 2)
         self.arrived = swap(self.theirs, second)
 
     def spread(self, due, early, meanwhile, rest_early):
@@ -247,7 +252,7 @@
         def start(flags, mine, arrived):
             return [added_if(True, mine[...], arrived[...])]
 
-        (total,) = small(start, self.flags, [self.mine, self.arrived], 1)
+        (total,) = small(start, self.bits, [self.mine, self.arrived], 1)
         self.rest_arrived = swap(after(self.mine, self.arrived), self.second)
         if rest_early:
             early = [self.rest_arrived, *early]
@@ -270,11 +275,11 @@
                 return [value, added_if(flags[counts + 1] == 1, value, side[...])]
 
             if before is None:
-                before, total = small(first, self.flags, [total, arrived], 2)
+                before, total = small(first, self.bits, [total, arrived], 2)
             elif not last:
-                before, total = small(middle, self.flags, [total, arrived, before], 2)
+                before, total = small(middle, self.bits, [total, arrived, before], 2)
             else:
-                self.before, self.own = small(final, self.flags, [self.arrived, arrived, before], 2)
+                self.before, self.own = small(final, self.bits, [self.arrived, arrived, before], 2)
 
     def collect(self):
         counts = self.counts
@@ -283,15 +288,15 @@
             return [added_if(flags[counts + 1] == 1, swapped[...], rest[...])]
 
         arrays = [swap(self.before, self.second), self.rest_arrived]
-        (other,) = small(finish, self.flags, arrays, 1)
+        (other,) = small(finish, self.bits, arrays, 1)
         quarters = [self.own, other, swap(self.own, self.first), swap(other, self.first)]
         self.operands = [("whole", self.other.reshape(-1, HEAD_DIM))]
         self.operands += [("held", quarter) for quarter in quarters]
 
 
-def sides_kernel(flags_ref, in_ref, own_ref, gone_ref):
+def sides_kernel(in_ref, own_ref, gone_ref):
     columns = own_ref.shape[1]
-    mine = flags_ref[flags_ref.shape[0] - 2]
+    mine = lax.axis_index("dp")
 
     @pl.when(mine == 0)
     def _():
@@ -304,37 +309,35 @@
         gone_ref[...] = in_ref[:, :columns]
 
 
-def sides(array, flags):
+def sides(array):
     rows, columns = array.shape
     tile = rows // 2
     out = jax.ShapeDtypeStruct((rows, columns // 2), array.dtype)
     return pl.pallas_call(
         sides_kernel,
-        grid_spec=pltpu.PrefetchScalarGridSpec(
-            num_scalar_prefetch=1,
-            grid=(rows // tile,),
-            in_specs=[pl.BlockSpec((tile, columns), lambda i, flags: (i, 0))],
-            out_specs=[pl.BlockSpec((tile, columns // 2), lambda i, flags: (i, 0))] * 2,
-        ),
+        grid=(rows // tile,),
+        in_specs=[pl.BlockSpec((tile, columns), lambda i: (i, 0))],
+        out_specs=[pl.BlockSpec((tile, columns // 2), lambda i: (i, 0))] * 2,
         out_shape=[out, out],
         compiler_params=pltpu.CompilerParams(vmem_limit_bytes=VMEM_MIB * 1024 * 1024),
         cost_estimate=pl.CostEstimate(flops=0, bytes_accessed=4 * array.size, transcendentals=0),
-    )(flags, array)
-
-
-def weight_kernel(sources_of, flags_ref, turned_ref, *refs):
-    numbers = flags_ref.shape[0]
-    mine, span = flags_ref[numbers - 2], flags_ref[numbers - 1]
+    )(array)
+
+
+def weight_kernel(sources_of, bits, turned_in, *refs):
+    *numbers, mine, span = numbers_of(bits)
     order = []
     for sequences, flips in sources_of:
         device = 0
         for bit, flip in enumerate(flips):
-            device += 2**bit * (1 - flags_ref[bit] if flip else flags_ref[bit])
-        pair = turned_ref.shape[0] == 16
+            device += 2**bit * (1 - numbers[bit] if flip else numbers[bit])
+        pair = turned_in.shape[0] == 16
         order += [8 * (lax.rem(mine + at, 2) if pair else at) + device for at in sequences]
-    *held, kept_ref, sent_ref, total_ref, buffer_ref, arrival = refs
+    *held, kept_out, sent_out, total_ref, turned_ref, buffer_ref, kept_ref, sent_ref, arrival, departure = refs
     sources, _, tokens = turned_ref.shape
     others, rows, columns = sent_ref.shape
+    turning = pltpu.make_async_copy(turned_in, turned_ref, arrival.at[len(held)])
+    turning.start()
     copies, at = [], 0
     for index, ref in enumerate(held):
         count = ref.shape[0]
@@ -343,39 +346,54 @@
         at += count
     per_step, tile = 4, 512 if columns % 512 == 0 else columns
     steps = sources // per_step
+    leaving = []
+    turning.wait()
     for step in range(steps):
         for copy in copies[step * len(copies) // steps : (step + 1) * len(copies) // steps]:
             copy.wait()
         first = step * per_step
         lhs = jnp.concatenate([turned_ref[order[first + i]] for i in range(per_step)], axis=1)
-        for start in range(0, columns, tile):
+        for index, start in enumerate(range(0, columns, tile)):
             cut = slice(start, start + tile)
             rhs = buffer_ref[first : first + per_step, :, cut].reshape(per_step * tokens, tile)
             product = dot(lhs, rhs, NN)
             total_ref[:, cut] = product if step == 0 else total_ref[:, cut] + product
-    kept_ref[...] = total_ref[pl.ds(pl.multiple_of(span * rows, 16), rows), :]
-    for turn in range(others):
-        target = lax.rem(span + turn + 1, others + 1)
-        sent_ref[turn] = total_ref[pl.ds(pl.multiple_of(target * rows, 16), rows), :].astype(BF16)
-
-
-def weight_part(sources_of, flags, turned, inputs, halves):
+            if step < steps - 1:
+                continue
+            kept_ref[:, cut] = total_ref[pl.ds(pl.multiple_of(span * rows, 16), rows), cut]
+            for turn in range(others):
+                target = lax.rem(span + turn + 1, others + 1)
+                sent_ref[turn, :, cut] = total_ref[pl.ds(pl.multiple_of(target * rows, 16), rows), cut].astype(BF16)
+            there = pl.ds(start, tile)
+            leaving += [
+                pltpu.make_async_copy(kept_ref.at[:, there], kept_out.at[:, there], departure.at[0, index]),
+                pltpu.make_async_copy(sent_ref.at[:, :, there], sent_out.at[:, :, there], departure.at[1, index]),
+            ]
+            leaving[-2].start()
+            leaving[-1].start()
+    for copy in leaving:
+        copy.wait()
+
+
+def weight_part(sources_of, bits, turned, inputs, halves):
     sources, rows, tokens = turned.shape
     columns = inputs[0].shape[-1]
-    vmem = pl.BlockSpec(memory_space=pltpu.VMEM)
     return pl.pallas_call(
-        functools.partial(weight_kernel, sources_of),
-        in_specs=[pl.BlockSpec(memory_space=pltpu.SMEM), vmem]
-        + [pl.BlockSpec(memory_space=pl.ANY)] * len(inputs),
-        out_specs=[vmem, vmem],
+        functools.partial(weight_kernel, sources_of, bits),
+        in_specs=[pl.BlockSpec(memory_space=pl.ANY)] * (1 + len(inputs)),
+        out_specs=[pl.BlockSpec(memory_space=pl.ANY)] * 2,
         out_shape=[
             jax.ShapeDtypeStruct((rows // halves, columns), F32),
             jax.ShapeDtypeStruct((halves - 1, rows // halves, columns), BF16),
         ],
         scratch_shapes=[
             pltpu.VMEM((rows, columns), F32),
+            pltpu.VMEM(turned.shape, BF16),
             pltpu.VMEM((sources, tokens, columns), BF16),
-            pltpu.SemaphoreType.DMA((len(inputs),)),
+            pltpu.VMEM((rows // halves, columns), F32),
+            pltpu.VMEM((halves - 1, rows // halves, columns), BF16),
+            pltpu.SemaphoreType.DMA((len(inputs) + 1,)),
+            pltpu.SemaphoreType.DMA((2, max(columns // 512, 1))),
         ],
         compiler_params=pltpu.CompilerParams(vmem_limit_bytes=VMEM_MIB * 1024 * 1024),
         cost_estimate=pl.CostEstimate(
@@ -383,7 +401,7 @@
             bytes_accessed=sources * tokens * columns * 2 + rows * columns * 6,
             transcendentals=0,
         ),
-    )(flags, turned, *inputs)
+    )(turned, *inputs)
 
 
 def shards(layer_input, query_rows, key_rows, value_rows, out_grad, bits):
@@ -397,17 +415,13 @@
     cuts = 2
     rows = features // places // cuts
 
-    place = [lax.axis_index(bit) for bit in bits]
-    mine, span = lax.axis_index("dp"), lax.axis_index(spans)
-    flags = jnp.stack(place + place + [1 - at for at in place] + [mine, span]).astype(jnp.int32)
-
     (block_state,) = by_heads(
         block_state_head, [("row", key), ("row", value)], [("held state", BF16)], 1, vmem=44
     )
-    forward = Scan(block_state, bits, False, flags)
+    forward = Scan(block_state, bits, False)
 
     if sequences == 2:
-        own, gone = sides(after(layer_input[0], forward.mine), flags)
+        own, gone = sides(after(layer_input[0], forward.mine))
         own, far = own[None], swap(gone, "dp")[None]
     else:
         wide = lax.all_to_all(layer_input[0].reshape(tokens, sequences, -1), "dp", 1, 0)
@@ -435,10 +449,10 @@
         [("held", query), ("held", output[0]), ("held", upstream), *forward.operands],
         [("held row", BF16), ("held state", BF16), ("state", BF16)],
         2,
-        forward.flags,
+        bits,
     )
     own_layer = swap(after(own, block_grad), layer)
-    backward = Scan(after(block_grad, far_layer), bits, True, flags)
+    backward = Scan(after(block_grad, far_layer), bits, True)
     own_side = swap(after(own, backward.mine), side)
     (key_local,) = by_heads(
         key_local_head,
@@ -456,10 +470,10 @@
     own_both = swap(after(own_side, backward.before), layer)
     key_grad, grad_in, *turned = by_heads(
         functools.partial(key_grad_head, backward.counts),
-        [("held", key), ("held", value), ("held", key_local), *backward.operands],
+        [("held", after(key, own_both)), ("held", value), ("held", key_local), *backward.operands],
         [("row", BF16), ("state", BF16)] + [((sequences, 8, halves, rows, tokens), BF16)] * cuts,
         1,
-        after(backward.flags, own_both),
+        bits,
     )
     own_ids, far_ids = range(sequences // 2), range(sequences // 2, sequences)
     held, sources_of = [], []
@@ -483,7 +497,7 @@
     for cut in range(cuts):
         part = turned[cut].reshape(sequences * 8, halves * rows, tokens)
         part = lax.all_to_all(part, ("dp", layer, side, core), 0, 0, tiled=True)
-        total, sent = weight_part(sources_of, flags, after(part, done), held, halves)
+        total, sent = weight_part(sources_of, bits, after(part, done), held, halves)
         for turn in range(1, halves):
             moved = lax.ppermute(sent[turn - 1], spans, [(i, (i + turn) % halves) for i in range(halves)])
             total += moved.astype(F32)

time: 156 us -> 151 us (0.968)
  Pallas kernels: 41.5 us -> 31.9 us
  starting transfers between devices: 34.1 us -> 37.1 us
  waiting for transfers between devices: 56.5 us -> 59 us
    pallas_call x19, Pallas kernels: 41.5 us -> 31.9 us  [the longest x6 19.8 us: by_heads(): pl.pallas_call(body, in_specs=places[:count], out_specs=places[count:], o...]
    ppermute x31, starting transfers between devices: 25.9 us -> 29.1 us  [swap(): return lax.ppermute(array, axis, [(0, 1), (1, 0)])]
    all_to_all x1, waiting for transfers between devices: 7.99 us -> 9.8 us  [shards(): part = lax.all_to_all(part, ('dp', layer, side, core), 0, 0, tiled=True)]
    unnamed x66 -> x58, local copies, waits for them, and re-layouts: 4 us -> 3.25 us
  transfers between devices with their start and end apart: 34 -> 34, of which waited for: 19 -> 20; matrix products, arithmetic and copies ran while one was open for 0% -> 0% of each run, Pallas kernels for 24% -> 20%
where the time goes in v5:
time: 151 us
  waiting for transfers between devices  59 us (39%)
  starting transfers between devices  37.1 us (25%)
  Pallas kernels  31.9 us (21%)
  blocking collectives  17.2 us (11%)
  local copies, waits for them, and re-layouts  3.25 us (2%)
    ppermute x31, waiting for transfers between devices, swap(): return lax.ppermute(array, axis, [(0, 1), (1, 0)])  42 us
    ppermute x31, starting transfers between devices, swap(): return lax.ppermute(array, axis, [(0, 1), (1, 0)])  29.1 us
    pallas_call x6, Pallas kernels, by_heads(): pl.pallas_call(body, in_specs=places[:count], out_specs=places[count:], o...  19.8 us
    all_to_all x1, blocking collectives, shards(): part = lax.all_to_all(part, ('dp', layer, side, core), 0, 0, tiled=True)  17.2 us
    all_to_all x1, waiting for transfers between devices, shards(): part = lax.all_to_all(part, ('dp', layer, side, core), 0, 0, tiled=True)  9.8 us
    pallas_call x2, Pallas kernels, weight_part(): pl.pallas_call(functools.partial(weight_kernel, sources_of, bits), in_spe...  9.29 us
    ppermute x2, waiting for transfers between devices, shards(): lax.ppermute(sent[turn - 1], spans, [(i, (i + turn) % halves) for i in ra...  7.21 us
    all_to_all x1, starting transfers between devices, shards(): part = lax.all_to_all(part, ('dp', layer, side, core), 0, 0, tiled=True)  4.48 us
  transfers between devices with their start and end apart: 34, of which 20 were waited for; matrix products, arithmetic and copies ran while one was open for 0% of the time, Pallas kernels for 20%

profile of v5, /device:TPU:0, one launch (start us, length us, event | category | flops | bytes accessed | tf_op | source)
XLA Modules:
  0.0 150.7 jit_solution(6118370621402049209)
XLA Ops:
  0.6 1.1 copy-done
  1.8 1.1 copy-done.2
  2.9 1.0 shard_map.84
  4.5 1.9 %collective-permute-done.refs_1_ = bf16[2,2,768,128]{3,2,1,0:T(8,128)(2,1)S(1)} collective-permute-done((bf16[2,2,768,128]{3,2,1,0:T(8,128)(2,1)S(1)}, bf16[2,2,768,128]{3,2,1,0:T(8,128)(2,1)S(1)}, u32[]{:S(2)}, u32[]{:S(2)}) %collective-permute-start) | collective-permute-done | bytes 786464 | tf_op jit(solution)/shard_map/ppermute | solution.py:195
  6.5 2.9 %collective-permute-start.1 = (bf16[768,128]{1,0:T(8,128)(2,1)S(1)}, bf16[768,128]{1,0:T(8,128)(2,1)S(1)}, u32[]{:S(2)}, u32[]{:S(2)}) collective-permute-start(bf16[768,128]{1,0:T(8,128)(2,1)S(1)} %get-tuple-element.54), channel_id=1, source_target_pairs={{0,2},{2,0},{1,3},{3,1},{4,6},{6,4},{5,7},{7,5},{8,10},{10,8},{9,1... | collective-permute-start | bytes 589832 | tf_op jit(solution)/shard_map/ppermute | solution.py:195
  9.4 1.9 %shard_map.87 = (bf16[128,1536]{1,0:T(8,128)(2,1)}, bf16[128,1536]{1,0:T(8,128)(2,1)}) custom-call(bf16[128,3072]{1,0:T(8,128)(2,1)} %bitcast.50), custom_call_target="tpu_custom_call" | custom-call | bytes 1572864 | tf_op jit(solution)/shard_map/pallas_call | solution.py:316
  11.3 1.5 %collective-permute-start.4 = (bf16[128,1536]{1,0:T(8,128)(2,1)}, bf16[128,1536]{1,0:T(8,128)(2,1)S(1)}, u32[]{:S(2)}, u32[]{:S(2)}) collective-permute-start(bf16[128,1536]{1,0:T(8,128)(2,1)} %get-tuple-element.57), channel_id=1, source_target_pairs={{0,16},{16,0},{1,17},{17,1},{2,18},{18,2},{3,19},{19,3},{4,20},{20... | collective-permute-start | bytes 1179656 | tf_op jit(solution)/shard_map/ppermute | solution.py:195
  12.8 1.8 %collective-permute-done.1.refs_1_.refs_0_ = bf16[768,128]{1,0:T(8,128)(2,1)S(1)} collective-permute-done((bf16[768,128]{1,0:T(8,128)(2,1)S(1)}, bf16[768,128]{1,0:T(8,128)(2,1)S(1)}, u32[]{:S(2)}, u32[]{:S(2)}) %collective-permute-start.1) | collective-permute-done | bytes 196640 | tf_op jit(solution)/shard_map/ppermute | solution.py:195
  14.6 1.7 %collective-permute-start.3 = (bf16[768,128]{1,0:T(8,128)(2,1)S(1)}, bf16[768,128]{1,0:T(8,128)(2,1)S(1)}, u32[]{:S(2)}, u32[]{:S(2)}) collective-permute-start(bf16[768,128]{1,0:T(8,128)(2,1)S(1)} %get-tuple-element.55.refs_0_), channel_id=1, source_target_pairs={{0,2},{2,0},{1,3},{3,1},{4,6},{6,4},{5,7},{7,5},{8,10},{10,8},{9,1... | collective-permute-start | bytes 589832 | tf_op jit(solution)/shard_map/ppermute | solution.py:195
  16.4 1.6 %collective-permute-start.2 = (bf16[768,128]{1,0:T(8,128)(2,1)S(1)}, bf16[768,128]{1,0:T(8,128)(2,1)S(1)}, u32[]{:S(2)}, u32[]{:S(2)}) collective-permute-start(bf16[768,128]{1,0:T(8,128)(2,1)S(1)} %shard_map.86.refs_0_), channel_id=1, source_target_pairs={{0,4},{4,0},{1,5},{5,1},{2,6},{6,2},{3,7},{7,3},{8,12},{12,8},{9,1... | collective-permute-start | bytes 589832 | tf_op jit(solution)/shard_map/ppermute | solution.py:195
  18.1 3.0 %collective-permute-done.3.refs_1_ = bf16[768,128]{1,0:T(8,128)(2,1)S(1)} collective-permute-done((bf16[768,128]{1,0:T(8,128)(2,1)S(1)}, bf16[768,128]{1,0:T(8,128)(2,1)S(1)}, u32[]{:S(2)}, u32[]{:S(2)}) %collective-permute-start.3) | collective-permute-done | bytes 196640 | tf_op jit(solution)/shard_map/ppermute | solution.py:195
  21.1 1.3 collective-permute-done.2.refs_1_
  23.1 2.8 %collective-permute-start.5 = (bf16[768,128]{1,0:T(8,128)(2,1)S(1)}, bf16[768,128]{1,0:T(8,128)(2,1)S(1)}, u32[]{:S(2)}, u32[]{:S(2)}) collective-permute-start(bf16[768,128]{1,0:T(8,128)(2,1)S(1)} %get-tuple-element.59), channel_id=1, source_target_pairs={{0,8},{8,0},{1,9},{9,1},{2,10},{10,2},{3,11},{11,3},{4,12},{12,4},... | collective-permute-start | bytes 589832 | tf_op jit(solution)/shard_map/ppermute | solution.py:195
  25.9 3.9 %shard_map.89.refs_1_ = f32[128,3072]{1,0:T(8,128)S(1)} custom-call(bf16[128,3072]{1,0:T(8,128)(2,1)S(1)} %bitcast.27, bf16[128,3072]{1,0:T(8,128)(2,1)S(1)} %bitcast.24, bf16[128,3072]{1,0:T(8,128)(2,1)S(1)} %bitcast.19), custom_call_target="tpu_custom_call" | custom-call | flops 201326592 | bytes 3145728 | tf_op jit(solution)/shard_map/pallas_call | solution.py:176
  29.8 4.3 %collective-permute-done.5.refs_1_ = bf16[768,128]{1,0:T(8,128)(2,1)S(1)} collective-permute-done((bf16[768,128]{1,0:T(8,128)(2,1)S(1)}, bf16[768,128]{1,0:T(8,128)(2,1)S(1)}, u32[]{:S(2)}, u32[]{:S(2)}) %collective-permute-start.5) | collective-permute-done | bytes 196640 | tf_op jit(solution)/shard_map/ppermute | solution.py:195
  34.3 1.1 collective-permute-start.7
  35.4 0.7 collective-permute-start.10
  36.1 3.9 %collective-permute-done.7.refs_0_ = bf16[768,128]{1,0:T(8,128)(2,1)S(1)} collective-permute-done((bf16[768,128]{1,0:T(8,128)(2,1)S(1)}, bf16[768,128]{1,0:T(8,128)(2,1)S(1)}, u32[]{:S(2)}, u32[]{:S(2)}) %collective-permute-start.7) | collective-permute-done | bytes 196640 | tf_op jit(solution)/shard_map/ppermute | solution.py:195
  40.2 1.4 collective-permute-done.9.refs_7_
  41.6 2.8 %shard_map.92 = (bf16[128,3072]{1,0:T(8,128)(2,1)S(1)}, bf16[3072,128]{1,0:T(8,128)(2,1)S(1)}, bf16[3072,128]{1,0:T(8,128)(2,1)S(1)}) custom-call(bf16[128,3072]{1,0:T(8,128)(2,1)S(1)} %bitcast.28, f32[128,3072]{1,0:T(8,128)S(1)} %shard_map.89.refs_1_, bf16[128,3072]{1,0:T(8,128)(2,1)S(1)} %bitcast.35, bf16[3072,128]{1,0:T(8,128)(2,1)S(1)} %bitcast.32, ...), custom_call_target="tpu_custom_call" | custom-call | flops 201326592 | bytes 8650752 | tf_op jit(solution)/shard_map/pallas_call | solution.py:176
  44.5 0.6 collective-permute-done.10.refs_3_
  45.1 1.8 %collective-permute-start.15 = (bf16[1,128,1536]{2,1,0:T(8,128)(2,1)S(1)}, bf16[1,128,1536]{2,1,0:T(8,128)(2,1)S(1)}, u32[]{:S(2)}, u32[]{:S(2)}) collective-permute-start(bf16[1,128,1536]{2,1,0:T(8,128)(2,1)S(1)} %bitcast.42), channel_id=1, source_target_pairs={{0,4},{4,0},{1,5},{5,1},{2,6},{6,2},{3,7},{7,3},{8,12},{12,8},{9,1... | collective-permute-start | bytes 1179656 | tf_op jit(solution)/shard_map/ppermute | solution.py:195
  47.5 1.1 collective-permute-start.13
  48.6 1.0 collective-permute-start.12
  49.6 3.9 %shard_map.94.refs_2_ = f32[128,3072]{1,0:T(8,128)S(1)} custom-call(bf16[128,3072]{1,0:T(8,128)(2,1)S(1)} %bitcast.29, bf16[128,3072]{1,0:T(8,128)(2,1)S(1)} %bitcast.20, bf16[128,3072]{1,0:T(8,128)(2,1)S(1)} %get-tuple-element.94.refs_2_.refs_3_), custom_call_target="tpu_custom_call" | custom-call | flops 201326592 | bytes 3145728 | tf_op jit(solution)/shard_map/pallas_call | solution.py:176
  53.5 1.8 %collective-permute-done.13.refs_1_.refs_0_ = bf16[768,128]{1,0:T(8,128)(2,1)S(1)} collective-permute-done((bf16[768,128]{1,0:T(8,128)(2,1)S(1)}, bf16[768,128]{1,0:T(8,128)(2,1)S(1)}, u32[]{:S(2)}, u32[]{:S(2)}) %collective-permute-start.13) | collective-permute-done | bytes 196640 | tf_op jit(solution)/shard_map/ppermute | solution.py:195
  55.3 1.8 %collective-permute-start.14 = (bf16[768,128]{1,0:T(8,128)(2,1)S(1)}, bf16[768,128]{1,0:T(8,128)(2,1)S(1)}, u32[]{:S(2)}, u32[]{:S(2)}) collective-permute-start(bf16[768,128]{1,0:T(8,128)(2,1)S(1)} %shard_map.95.refs_0_), channel_id=1, source_target_pairs={{0,4},{4,0},{1,5},{5,1},{2,6},{6,2},{3,7},{7,3},{8,12},{12,8},{9,1... | collective-permute-start | bytes 589832 | tf_op jit(solution)/shard_map/ppermute | solution.py:195
  57.1 5.8 %collective-permute-done.12.refs_6_ = bf16[1,128,1536]{2,1,0:T(8,128)(2,1)S(1)} collective-permute-done((bf16[1,128,1536]{2,1,0:T(8,128)(2,1)S(1)}, bf16[1,128,1536]{2,1,0:T(8,128)(2,1)S(1)}, u32[]{:S(2)}, u32[]{:S(2)}) %collective-permute-start.12) | collective-permute-done | bytes 393248 | tf_op jit(solution)/shard_map/ppermute | solution.py:195
  63.0 1.1 collective-permute-start.17
  64.1 3.4 %collective-permute-start.16 = (bf16[768,128]{1,0:T(8,128)(2,1)S(1)}, bf16[768,128]{1,0:T(8,128)(2,1)S(1)}, u32[]{:S(2)}, u32[]{:S(2)}) collective-permute-start(bf16[768,128]{1,0:T(8,128)(2,1)S(1)} %get-tuple-element.78), channel_id=1, source_target_pairs={{0,8},{8,0},{1,9},{9,1},{2,10},{10,2},{3,11},{11,3},{4,12},{12,4},... | collective-permute-start | bytes 589832 | tf_op jit(solution)/shard_map/ppermute | solution.py:195
  67.5 1.0 collective-permute-start.20
  68.7 7.1 %collective-permute-done.16.refs_1_ = bf16[768,128]{1,0:T(8,128)(2,1)S(1)} collective-permute-done((bf16[768,128]{1,0:T(8,128)(2,1)S(1)}, bf16[768,128]{1,0:T(8,128)(2,1)S(1)}, u32[]{:S(2)}, u32[]{:S(2)}) %collective-permute-start.16) | collective-permute-done | bytes 196640 | tf_op jit(solution)/shard_map/ppermute | solution.py:195
  75.9 1.0 collective-permute-start.19
  77.0 0.9 collective-permute-done.20.refs_1_
  77.8 1.5 collective-permute-start.18
  79.3 2.5 %collective-permute-done.19.refs_0_ = bf16[768,128]{1,0:T(8,128)(2,1)S(1)} collective-permute-done((bf16[768,128]{1,0:T(8,128)(2,1)S(1)}, bf16[768,128]{1,0:T(8,128)(2,1)S(1)}, u32[]{:S(2)}, u32[]{:S(2)}) %collective-permute-start.19) | collective-permute-done | bytes 196640 | tf_op jit(solution)/shard_map/ppermute | solution.py:195
  84.0 4.5 %collective-permute-done.18.refs_7_ = bf16[1,128,1536]{2,1,0:T(8,128)(2,1)S(1)} collective-permute-done((bf16[1,128,1536]{2,1,0:T(8,128)(2,1)S(1)}, bf16[1,128,1536]{2,1,0:T(8,128)(2,1)S(1)}, u32[]{:S(2)}, u32[]{:S(2)}) %collective-permute-start.18) | collective-permute-done | bytes 393248 | tf_op jit(solution)/shard_map/ppermute | solution.py:195
  88.5 2.3 %shard_map.99 = (bf16[128,3072]{1,0:T(8,128)(2,1)}, bf16[3072,128]{1,0:T(8,128)(2,1)S(1)}, bf16[2,8,2,96,128]{4,3,2,1,0:T(8,128)(2,1)S(1)}, bf16[2,8,2,96,128]{4,3,2,1,0:T(8,128)(2,1)S(1)}) custom-call(bf16[128,3072]{1,0:T(8,128)(2,1)S(1)} %bitcast.25, bf16[128,3072]{1,0:T(8,128)(2,1)S(1)} %bitcast.21, f32[128,3072]{1,0:T(8,128)S(1)} %shard_map.94.refs_2_, ...), custom_call_target="tpu_custom_call" | custom-call | flops 100663296 | bytes 9437184 | tf_op jit(solution)/shard_map/pallas_call | solution.py:176
  90.9 0.9 copy-done.8
  91.9 17.2 %all_to_all.10.turned_in = bf16[16,192,128]{2,1,0:T(8,128)(2,1)} all-to-all(bf16[16,192,128]{2,1,0:T(8,128)(2,1)S(1)} %bitcast.39), channel_id=1, replica_groups=mesh['dp'=2,'bit3'=2,'bit2'=2,'bit1'=2,'bit0'=2] {'dp','bit2','bit1','bi..., dimensions={0} | all-to-all | bytes 1572864 | tf_op jit(solution)/shard_map/all_to_all | solution.py:499
  109.1 4.5 %all-to-all-start = ((bf16[16,192,128]{2,1,0:T(8,128)(2,1)}), bf16[16,192,128]{2,1,0:T(8,128)(2,1)}, u32[]{:S(2)}, u32[]{:S(2)}) async-start(bf16[16,192,128]{2,1,0:T(8,128)(2,1)} %bitcast.36), calls=%async_computation | async-start | bytes 1572864 | tf_op jit(solution)/shard_map/all_to_all | solution.py:499
  113.6 4.6 %shard_map.100 = (f32[96,1536]{1,0:T(8,128)}, bf16[1,96,1536]{2,1,0:T(8,128)(2,1)}) custom-call(bf16[16,192,128]{2,1,0:T(8,128)(2,1)} %all_to_all.10.turned_in, bf16[1,128,1536]{2,1,0:T(8,128)(2,1)} %bitcast.40, bf16[1,128,1536]{2,1,0:T(8,128)(2,1)} %bitcast.48, bf16[1,128,1536]{2,1,0:T(8,128)(2,1)} %copy-done.15, bf16[1,128,1536]{2,1,0:T(8,128)(2,1)} %copy-done.14, ...), custom_call_target="tpu_custom_call" | custom-call | flops 1207959552 | bytes 8060928 | tf_op jit(solution)/shard_map/pallas_call | solution.py:381
  118.2 3.5 %collective-permute-start.31 = (bf16[96,1536]{1,0:T(8,128)(2,1)}, bf16[96,1536]{1,0:T(8,128)(2,1)S(1)}, u32[]{:S(2)}, u32[]{:S(2)}) collective-permute-start(bf16[96,1536]{1,0:T(8,128)(2,1)} %bitcast.54), channel_id=1, source_target_pairs={{0,8},{8,0},{1,9},{9,1},{2,10},{10,2},{3,11},{11,3},{4,12},{12,4},... | collective-permute-start | bytes 884744 | tf_op jit(solution)/shard_map/ppermute | solution.py:502
  121.7 9.8 %all-to-all-done.turned_in = bf16[16,192,128]{2,1,0:T(8,128)(2,1)} async-done(((bf16[16,192,128]{2,1,0:T(8,128)(2,1)}), bf16[16,192,128]{2,1,0:T(8,128)(2,1)}, u32[]{:S(2)}, u32[]{:S(2)}) %all-to-all-start) | async-done | bytes 786464 | tf_op jit(solution)/shard_map/all_to_all | solution.py:499
  131.5 4.7 %shard_map.101 = (f32[96,1536]{1,0:T(8,128)}, bf16[1,96,1536]{2,1,0:T(8,128)(2,1)}) custom-call(bf16[16,192,128]{2,1,0:T(8,128)(2,1)} %all-to-all-done.turned_in, bf16[1,128,1536]{2,1,0:T(8,128)(2,1)} %bitcast.41, bf16[1,128,1536]{2,1,0:T(8,128)(2,1)} %bitcast.49, bf16[1,128,1536]{2,1,0:T(8,128)(2,1)} %copy-done.15, bf16[1,128,1536]{2,1,0:T(8,128)(2,1)} %copy-done.14, ...), custom_call_target="tpu_custom_call" | custom-call | flops 1207959552 | bytes 8060928 | tf_op jit(solution)/shard_map/pallas_call | solution.py:381
  136.3 5.9 %shard_map.102 = (bf16[128,3072]{1,0:T(8,128)(2,1)}, bf16[128,3072]{1,0:T(8,128)(2,1)}) custom-call(bf16[128,3072]{1,0:T(8,128)(2,1)S(1)} %bitcast.30, bf16[128,3072]{1,0:T(8,128)(2,1)S(1)} %bitcast.26, bf16[128,3072]{1,0:T(8,128)(2,1)S(1)} %bitcast.22, bf16[128,3072]{1,0:T(8,128)(2,1)S(1)} %get-tuple-element.94.refs_2_.refs_3_, ...), custom_call_target="tpu_custom_call" | custom-call | flops 603979776 | bytes 6291456 | tf_op jit(solution)/shard_map/pallas_call | solution.py:176
  142.3 7.2 %collective-permute-done.32 = bf16[96,1536]{1,0:T(8,128)(2,1)S(1)} collective-permute-done((bf16[96,1536]{1,0:T(8,128)(2,1)}, bf16[96,1536]{1,0:T(8,128)(2,1)S(1)}, u32[]{:S(2)}, u32[]{:S(2)}) %collective-permute-start.32) | collective-permute-done | bytes 294944 | tf_op jit(solution)/shard_map/ppermute | solution.py:502
  149.6 1.1 maximum_multiply_fusion
  (101 shorter events, 5.2 us)
Async XLA Ops:
  3.9 2.4 %collective-permute-start = (bf16[2,2,768,128]{3,2,1,0:T(8,128)(2,1)S(1)}, bf16[2,2,768,128]{3,2,1,0:T(8,128)(2,1)S(1)}, u32[]{:S(2)}, u32[]{:S(2)}) collective-permute-start(bf16[2,2,768,128]{3,2,1,0:T(8,128)(2,1)S(1)} %bitcast.33), channel_id=1, source_target_pairs={{0,1},{1,0},{2,3},{3,2},{4,5},{5,4},{6,7},{7,6},{8,9},{9,8},{10,11... | collective-permute-start | bytes 2359304 | tf_op jit(solution)/shard_map/ppermute | solution.py:195
  6.4 19.5 %copy-start.4 = (bf16[1,128,3072]{2,1,0:T(8,128)(2,1)S(1)}, bf16[1,128,3072]{2,1,0:T(8,128)(2,1)}, u32[]{:S(2)}) copy-start(bf16[1,128,3072]{2,1,0:T(8,128)(2,1)} %param.6) | copy-start | bytes 2359300
  6.5 19.4 %copy-start.1 = (bf16[1,128,3072]{2,1,0:T(8,128)(2,1)S(1)}, bf16[1,128,3072]{2,1,0:T(8,128)(2,1)}, u32[]{:S(2)}) copy-start(bf16[1,128,3072]{2,1,0:T(8,128)(2,1)} %param.8) | copy-start | bytes 2359300
  6.5 19.4 %copy-start.3 = (bf16[1,128,3072]{2,1,0:T(8,128)(2,1)S(1)}, bf16[1,128,3072]{2,1,0:T(8,128)(2,1)}, u32[]{:S(2)}) copy-start(bf16[1,128,3072]{2,1,0:T(8,128)(2,1)} %param.7) | copy-start | bytes 2359300
  6.5 8.1 %collective-permute-start.1 = (bf16[768,128]{1,0:T(8,128)(2,1)S(1)}, bf16[768,128]{1,0:T(8,128)(2,1)S(1)}, u32[]{:S(2)}, u32[]{:S(2)}) collective-permute-start(bf16[768,128]{1,0:T(8,128)(2,1)S(1)} %get-tuple-element.54), channel_id=1, source_target_pairs={{0,2},{2,0},{1,3},{3,1},{4,6},{6,4},{5,7},{7,5},{8,10},{10,8},{9,1... | collective-permute-start | bytes 589832 | tf_op jit(solution)/shard_map/ppermute | solution.py:195
  11.3 11.1 %collective-permute-start.4 = (bf16[128,1536]{1,0:T(8,128)(2,1)}, bf16[128,1536]{1,0:T(8,128)(2,1)S(1)}, u32[]{:S(2)}, u32[]{:S(2)}) collective-permute-start(bf16[128,1536]{1,0:T(8,128)(2,1)} %get-tuple-element.57), channel_id=1, source_target_pairs={{0,16},{16,0},{1,17},{17,1},{2,18},{18,2},{3,19},{19,3},{4,20},{20... | collective-permute-start | bytes 1179656 | tf_op jit(solution)/shard_map/ppermute | solution.py:195
  14.6 6.4 %collective-permute-start.3 = (bf16[768,128]{1,0:T(8,128)(2,1)S(1)}, bf16[768,128]{1,0:T(8,128)(2,1)S(1)}, u32[]{:S(2)}, u32[]{:S(2)}) collective-permute-start(bf16[768,128]{1,0:T(8,128)(2,1)S(1)} %get-tuple-element.55.refs_0_), channel_id=1, source_target_pairs={{0,2},{2,0},{1,3},{3,1},{4,6},{6,4},{5,7},{7,5},{8,10},{10,8},{9,1... | collective-permute-start | bytes 589832 | tf_op jit(solution)/shard_map/ppermute | solution.py:195
  16.4 5.9 %collective-permute-start.2 = (bf16[768,128]{1,0:T(8,128)(2,1)S(1)}, bf16[768,128]{1,0:T(8,128)(2,1)S(1)}, u32[]{:S(2)}, u32[]{:S(2)}) collective-permute-start(bf16[768,128]{1,0:T(8,128)(2,1)S(1)} %shard_map.86.refs_0_), channel_id=1, source_target_pairs={{0,4},{4,0},{1,5},{5,1},{2,6},{6,2},{3,7},{7,3},{8,12},{12,8},{9,1... | collective-permute-start | bytes 589832 | tf_op jit(solution)/shard_map/ppermute | solution.py:195
  22.4 46.0 %copy-start.12 = (bf16[128,1536]{1,0:T(8,128)(2,1)}, bf16[128,1536]{1,0:T(8,128)(2,1)S(1)}, u32[]{:S(2)}) copy-start(bf16[128,1536]{1,0:T(8,128)(2,1)S(1)} %collective-permute-done.4) | copy-start | bytes 1179652
  22.5 11.6 %collective-permute-start.6 = (bf16[1,128,1536]{2,1,0:T(8,128)(2,1)S(1)}, bf16[1,128,1536]{2,1,0:T(8,128)(2,1)S(1)}, u32[]{:S(2)}, u32[]{:S(2)}) collective-permute-start(bf16[1,128,1536]{2,1,0:T(8,128)(2,1)S(1)} %bitcast.45), channel_id=1, source_target_pairs={{0,2},{2,0},{1,3},{3,1},{4,6},{6,4},{5,7},{7,5},{8,10},{10,8},{9,1... | collective-permute-start | bytes 1179656 | tf_op jit(solution)/shard_map/ppermute | solution.py:195
  23.1 11.1 %collective-permute-start.5 = (bf16[768,128]{1,0:T(8,128)(2,1)S(1)}, bf16[768,128]{1,0:T(8,128)(2,1)S(1)}, u32[]{:S(2)}, u32[]{:S(2)}) collective-permute-start(bf16[768,128]{1,0:T(8,128)(2,1)S(1)} %get-tuple-element.59), channel_id=1, source_target_pairs={{0,8},{8,0},{1,9},{9,1},{2,10},{10,2},{3,11},{11,3},{4,12},{12,4},... | collective-permute-start | bytes 589832 | tf_op jit(solution)/shard_map/ppermute | solution.py:195
  34.2 42.8 %copy-start.13 = (bf16[1,128,1536]{2,1,0:T(8,128)(2,1)}, bf16[1,128,1536]{2,1,0:T(8,128)(2,1)S(1)}, u32[]{:S(2)}) copy-start(bf16[1,128,1536]{2,1,0:T(8,128)(2,1)S(1)} %collective-permute-done.6.refs_4_) | copy-start | bytes 1179652
  34.3 5.8 %collective-permute-start.7 = (bf16[768,128]{1,0:T(8,128)(2,1)S(1)}, bf16[768,128]{1,0:T(8,128)(2,1)S(1)}, u32[]{:S(2)}, u32[]{:S(2)}) collective-permute-start(bf16[768,128]{1,0:T(8,128)(2,1)S(1)} %get-tuple-element.65), channel_id=1, source_target_pairs={{0,2},{2,0},{1,3},{3,1},{4,6},{6,4},{5,7},{7,5},{8,10},{10,8},{9,1... | collective-permute-start | bytes 589832 | tf_op jit(solution)/shard_map/ppermute | solution.py:195
  35.4 9.7 %collective-permute-start.10 = (bf16[1,128,1536]{2,1,0:T(8,128)(2,1)S(1)}, bf16[1,128,1536]{2,1,0:T(8,128)(2,1)S(1)}, u32[]{:S(2)}, u32[]{:S(2)}) collective-permute-start(bf16[1,128,1536]{2,1,0:T(8,128)(2,1)S(1)} %bitcast.46), channel_id=1, source_target_pairs={{0,4},{4,0},{1,5},{5,1},{2,6},{6,2},{3,7},{7,3},{8,12},{12,8},{9,1... | collective-permute-start | bytes 1179656 | tf_op jit(solution)/shard_map/ppermute | solution.py:195
  36.1 4.1 %collective-permute-start.8 = (bf16[768,128]{1,0:T(8,128)(2,1)S(1)}, bf16[768,128]{1,0:T(8,128)(2,1)S(1)}, u32[]{:S(2)}, u32[]{:S(2)}) collective-permute-start(bf16[768,128]{1,0:T(8,128)(2,1)S(1)} %get-tuple-element.64.refs_4_), channel_id=1, source_target_pairs={{0,1},{1,0},{2,3},{3,2},{4,5},{5,4},{6,7},{7,6},{8,9},{9,8},{10,11... | collective-permute-start | bytes 589832 | tf_op jit(solution)/shard_map/ppermute | solution.py:195
  40.1 1.5 %collective-permute-start.9 = (bf16[768,128]{1,0:T(8,128)(2,1)S(1)}, bf16[768,128]{1,0:T(8,128)(2,1)S(1)}, u32[]{:S(2)}, u32[]{:S(2)}) collective-permute-start(bf16[768,128]{1,0:T(8,128)(2,1)S(1)} %shard_map.91.refs_5_), channel_id=1, source_target_pairs={{0,1},{1,0},{2,3},{3,2},{4,5},{5,4},{6,7},{7,6},{8,9},{9,8},{10,11... | collective-permute-start | bytes 589832 | tf_op jit(solution)/shard_map/ppermute | solution.py:195
  45.1 37.4 %copy-start.14 = (bf16[1,128,1536]{2,1,0:T(8,128)(2,1)}, bf16[1,128,1536]{2,1,0:T(8,128)(2,1)S(1)}, u32[]{:S(2)}) copy-start(bf16[1,128,1536]{2,1,0:T(8,128)(2,1)S(1)} %collective-permute-done.10.refs_3_) | copy-start | bytes 1179652
  45.1 2.3 %collective-permute-start.11 = (bf16[2,2,768,128]{3,2,1,0:T(8,128)(2,1)S(1)}, bf16[2,2,768,128]{3,2,1,0:T(8,128)(2,1)S(1)}, u32[]{:S(2)}, u32[]{:S(2)}) collective-permute-start(bf16[2,2,768,128]{3,2,1,0:T(8,128)(2,1)S(1)} %bitcast.37), channel_id=1, source_target_pairs={{0,1},{1,0},{2,3},{3,2},{4,5},{5,4},{6,7},{7,6},{8,9},{9,8},{10,11... | collective-permute-start | bytes 2359304 | tf_op jit(solution)/shard_map/ppermute | solution.py:195
  45.1 12.0 %collective-permute-start.15 = (bf16[1,128,1536]{2,1,0:T(8,128)(2,1)S(1)}, bf16[1,128,1536]{2,1,0:T(8,128)(2,1)S(1)}, u32[]{:S(2)}, u32[]{:S(2)}) collective-permute-start(bf16[1,128,1536]{2,1,0:T(8,128)(2,1)S(1)} %bitcast.42), channel_id=1, source_target_pairs={{0,4},{4,0},{1,5},{5,1},{2,6},{6,2},{3,7},{7,3},{8,12},{12,8},{9,1... | collective-permute-start | bytes 1179656 | tf_op jit(solution)/shard_map/ppermute | solution.py:195
  47.5 7.8 %collective-permute-start.13 = (bf16[768,128]{1,0:T(8,128)(2,1)S(1)}, bf16[768,128]{1,0:T(8,128)(2,1)S(1)}, u32[]{:S(2)}, u32[]{:S(2)}) collective-permute-start(bf16[768,128]{1,0:T(8,128)(2,1)S(1)} %get-tuple-element.73), channel_id=1, source_target_pairs={{0,2},{2,0},{1,3},{3,1},{4,6},{6,4},{5,7},{7,5},{8,10},{10,8},{9,1... | collective-permute-start | bytes 589832 | tf_op jit(solution)/shard_map/ppermute | solution.py:195
  48.6 14.4 %collective-permute-start.12 = (bf16[1,128,1536]{2,1,0:T(8,128)(2,1)S(1)}, bf16[1,128,1536]{2,1,0:T(8,128)(2,1)S(1)}, u32[]{:S(2)}, u32[]{:S(2)}) collective-permute-start(bf16[1,128,1536]{2,1,0:T(8,128)(2,1)S(1)} %bitcast.43), channel_id=1, source_target_pairs={{0,2},{2,0},{1,3},{3,1},{4,6},{6,4},{5,7},{7,5},{8,10},{10,8},{9,1... | collective-permute-start | bytes 1179656 | tf_op jit(solution)/shard_map/ppermute | solution.py:195
  55.3 7.6 %collective-permute-start.14 = (bf16[768,128]{1,0:T(8,128)(2,1)S(1)}, bf16[768,128]{1,0:T(8,128)(2,1)S(1)}, u32[]{:S(2)}, u32[]{:S(2)}) collective-permute-start(bf16[768,128]{1,0:T(8,128)(2,1)S(1)} %shard_map.95.refs_0_), channel_id=1, source_target_pairs={{0,4},{4,0},{1,5},{5,1},{2,6},{6,2},{3,7},{7,3},{8,12},{12,8},{9,1... | collective-permute-start | bytes 589832 | tf_op jit(solution)/shard_map/ppermute | solution.py:195
  57.1 33.8 %copy-start.15 = (bf16[1,128,1536]{2,1,0:T(8,128)(2,1)}, bf16[1,128,1536]{2,1,0:T(8,128)(2,1)S(1)}, u32[]{:S(2)}) copy-start(bf16[1,128,1536]{2,1,0:T(8,128)(2,1)S(1)} %collective-permute-done.15.refs_2_) | copy-start | bytes 1179652
  62.9 28.0 %copy-start.16 = (bf16[1,128,1536]{2,1,0:T(8,128)(2,1)}, bf16[1,128,1536]{2,1,0:T(8,128)(2,1)S(1)}, u32[]{:S(2)}) copy-start(bf16[1,128,1536]{2,1,0:T(8,128)(2,1)S(1)} %collective-permute-done.12.refs_6_) | copy-start | bytes 1179652
  63.0 12.8 %collective-permute-start.17 = (bf16[1,128,1536]{2,1,0:T(8,128)(2,1)S(1)}, bf16[1,128,1536]{2,1,0:T(8,128)(2,1)S(1)}, u32[]{:S(2)}, u32[]{:S(2)}) collective-permute-start(bf16[1,128,1536]{2,1,0:T(8,128)(2,1)S(1)} %collective-permute-done.10.refs_3_), channel_id=1, source_target_pairs={{0,2},{2,0},{1,3},{3,1},{4,6},{6,4},{5,7},{7,5},{8,10},{10,8},{9,1... | collective-permute-start | bytes 1179656 | tf_op jit(solution)/shard_map/ppermute | solution.py:195
  64.1 11.7 %collective-permute-start.16 = (bf16[768,128]{1,0:T(8,128)(2,1)S(1)}, bf16[768,128]{1,0:T(8,128)(2,1)S(1)}, u32[]{:S(2)}, u32[]{:S(2)}) collective-permute-start(bf16[768,128]{1,0:T(8,128)(2,1)S(1)} %get-tuple-element.78), channel_id=1, source_target_pairs={{0,8},{8,0},{1,9},{9,1},{2,10},{10,2},{3,11},{11,3},{4,12},{12,4},... | collective-permute-start | bytes 589832 | tf_op jit(solution)/shard_map/ppermute | solution.py:195
  67.5 14.4 %collective-permute-start.23 = (bf16[1,128,1536]{2,1,0:T(8,128)(2,1)S(1)}, bf16[1,128,1536]{2,1,0:T(8,128)(2,1)S(1)}, u32[]{:S(2)}, u32[]{:S(2)}) collective-permute-start(bf16[1,128,1536]{2,1,0:T(8,128)(2,1)S(1)} %bitcast.44), channel_id=1, source_target_pairs={{0,1},{1,0},{2,3},{3,2},{4,5},{5,4},{6,7},{7,6},{8,9},{9,8},{10,11... | collective-permute-start | bytes 1179656 | tf_op jit(solution)/shard_map/ppermute | solution.py:195
  67.5 10.4 %collective-permute-start.20 = (bf16[768,128]{1,0:T(8,128)(2,1)S(1)}, bf16[768,128]{1,0:T(8,128)(2,1)S(1)}, u32[]{:S(2)}, u32[]{:S(2)}) collective-permute-start(bf16[768,128]{1,0:T(8,128)(2,1)S(1)} %get-tuple-element.86.refs_0_), channel_id=1, source_target_pairs={{0,2},{2,0},{1,3},{3,1},{4,6},{6,4},{5,7},{7,5},{8,10},{10,8},{9,1... | collective-permute-start | bytes 589832 | tf_op jit(solution)/shard_map/ppermute | solution.py:195
  68.4 14.1 %collective-permute-start.24 = (bf16[1,128,1536]{2,1,0:T(8,128)(2,1)S(1)}, bf16[1,128,1536]{2,1,0:T(8,128)(2,1)S(1)}, u32[]{:S(2)}, u32[]{:S(2)}) collective-permute-start(bf16[1,128,1536]{2,1,0:T(8,128)(2,1)S(1)} %bitcast.47), channel_id=1, source_target_pairs={{0,1},{1,0},{2,3},{3,2},{4,5},{5,4},{6,7},{7,6},{8,9},{9,8},{10,11... | collective-permute-start | bytes 1179656 | tf_op jit(solution)/shard_map/ppermute | solution.py:195
  75.9 5.9 %collective-permute-start.19 = (bf16[768,128]{1,0:T(8,128)(2,1)S(1)}, bf16[768,128]{1,0:T(8,128)(2,1)S(1)}, u32[]{:S(2)}, u32[]{:S(2)}) collective-permute-start(bf16[768,128]{1,0:T(8,128)(2,1)S(1)} %get-tuple-element.82), channel_id=1, source_target_pairs={{0,2},{2,0},{1,3},{3,1},{4,6},{6,4},{5,7},{7,5},{8,10},{10,8},{9,1... | collective-permute-start | bytes 589832 | tf_op jit(solution)/shard_map/ppermute | solution.py:195
  77.0 5.7 %collective-permute-start.27 = (bf16[1,128,1536]{2,1,0:T(8,128)(2,1)S(1)}, bf16[1,128,1536]{2,1,0:T(8,128)(2,1)S(1)}, u32[]{:S(2)}, u32[]{:S(2)}) collective-permute-start(bf16[1,128,1536]{2,1,0:T(8,128)(2,1)S(1)} %collective-permute-done.6.refs_4_), channel_id=1, source_target_pairs={{0,1},{1,0},{2,3},{3,2},{4,5},{5,4},{6,7},{7,6},{8,9},{9,8},{10,11... | collective-permute-start | bytes 1179656 | tf_op jit(solution)/shard_map/ppermute | solution.py:195
  77.8 10.7 %collective-permute-start.18 = (bf16[1,128,1536]{2,1,0:T(8,128)(2,1)S(1)}, bf16[1,128,1536]{2,1,0:T(8,128)(2,1)S(1)}, u32[]{:S(2)}, u32[]{:S(2)}) collective-permute-start(bf16[1,128,1536]{2,1,0:T(8,128)(2,1)S(1)} %collective-permute-done.12.refs_6_), channel_id=1, source_target_pairs={{0,4},{4,0},{1,5},{5,1},{2,6},{6,2},{3,7},{7,3},{8,12},{12,8},{9,1... | collective-permute-start | bytes 1179656 | tf_op jit(solution)/shard_map/ppermute | solution.py:195
  81.8 1.4 collective-permute-start.21
  81.9 1.6 %collective-permute-start.22 = (bf16[768,128]{1,0:T(8,128)(2,1)S(1)}, bf16[768,128]{1,0:T(8,128)(2,1)S(1)}, u32[]{:S(2)}, u32[]{:S(2)}) collective-permute-start(bf16[768,128]{1,0:T(8,128)(2,1)S(1)} %shard_map.98.refs_5_), channel_id=1, source_target_pairs={{0,1},{1,0},{2,3},{3,2},{4,5},{5,4},{6,7},{7,6},{8,9},{9,8},{10,11... | collective-permute-start | bytes 589832 | tf_op jit(solution)/shard_map/ppermute | solution.py:195
  82.5 9.3 %collective-permute-start.26 = (bf16[1,128,1536]{2,1,0:T(8,128)(2,1)S(1)}, bf16[1,128,1536]{2,1,0:T(8,128)(2,1)S(1)}, u32[]{:S(2)}, u32[]{:S(2)}) collective-permute-start(bf16[1,128,1536]{2,1,0:T(8,128)(2,1)S(1)} %collective-permute-done.10.refs_3_), channel_id=1, source_target_pairs={{0,1},{1,0},{2,3},{3,2},{4,5},{5,4},{6,7},{7,6},{8,9},{9,8},{10,11... | collective-permute-start | bytes 1179656 | tf_op jit(solution)/shard_map/ppermute | solution.py:195
  82.6 9.2 %collective-permute-start.25 = (bf16[1,128,1536]{2,1,0:T(8,128)(2,1)S(1)}, bf16[1,128,1536]{2,1,0:T(8,128)(2,1)S(1)}, u32[]{:S(2)}, u32[]{:S(2)}) collective-permute-start(bf16[1,128,1536]{2,1,0:T(8,128)(2,1)S(1)} %collective-permute-done.15.refs_2_), channel_id=1, source_target_pairs={{0,1},{1,0},{2,3},{3,2},{4,5},{5,4},{6,7},{7,6},{8,9},{9,8},{10,11... | collective-permute-start | bytes 1179656 | tf_op jit(solution)/shard_map/ppermute | solution.py:195
  83.3 8.5 %collective-permute-start.29 = (bf16[1,128,1536]{2,1,0:T(8,128)(2,1)S(1)}, bf16[1,128,1536]{2,1,0:T(8,128)(2,1)S(1)}, u32[]{:S(2)}, u32[]{:S(2)}) collective-permute-start(bf16[1,128,1536]{2,1,0:T(8,128)(2,1)S(1)} %collective-permute-done.12.refs_6_), channel_id=1, source_target_pairs={{0,1},{1,0},{2,3},{3,2},{4,5},{5,4},{6,7},{7,6},{8,9},{9,8},{10,11... | collective-permute-start | bytes 1179656 | tf_op jit(solution)/shard_map/ppermute | solution.py:195
  83.6 8.3 %collective-permute-start.28 = (bf16[1,128,1536]{2,1,0:T(8,128)(2,1)S(1)}, bf16[1,128,1536]{2,1,0:T(8,128)(2,1)S(1)}, u32[]{:S(2)}, u32[]{:S(2)}) collective-permute-start(bf16[1,128,1536]{2,1,0:T(8,128)(2,1)S(1)} %collective-permute-done.17.refs_5_), channel_id=1, source_target_pairs={{0,1},{1,0},{2,3},{3,2},{4,5},{5,4},{6,7},{7,6},{8,9},{9,8},{10,11... | collective-permute-start | bytes 1179656 | tf_op jit(solution)/shard_map/ppermute | solution.py:195
  88.5 3.4 %collective-permute-start.30 = (bf16[1,128,1536]{2,1,0:T(8,128)(2,1)S(1)}, bf16[1,128,1536]{2,1,0:T(8,128)(2,1)S(1)}, u32[]{:S(2)}, u32[]{:S(2)}) collective-permute-start(bf16[1,128,1536]{2,1,0:T(8,128)(2,1)S(1)} %collective-permute-done.18.refs_7_), channel_id=1, source_target_pairs={{0,1},{1,0},{2,3},{3,2},{4,5},{5,4},{6,7},{7,6},{8,9},{9,8},{10,11... | collective-permute-start | bytes 1179656 | tf_op jit(solution)/shard_map/ppermute | solution.py:195
  91.8 17.3 %copy-start.10 = (bf16[2,8,2,96,128]{4,3,2,1,0:T(8,128)(2,1)}, bf16[2,8,2,96,128]{4,3,2,1,0:T(8,128)(2,1)S(1)}, u32[]{:S(2)}) copy-start(bf16[2,8,2,96,128]{4,3,2,1,0:T(8,128)(2,1)S(1)} %get-tuple-element.87) | copy-start | bytes 2359300
  91.8 17.3 %copy-start.22 = (bf16[1,128,1536]{2,1,0:T(8,128)(2,1)}, bf16[1,128,1536]{2,1,0:T(8,128)(2,1)S(1)}, u32[]{:S(2)}) copy-start(bf16[1,128,1536]{2,1,0:T(8,128)(2,1)S(1)} %collective-permute-done.26.refs_11_) | copy-start | bytes 1179652
  91.8 17.3 %copy-start.23 = (bf16[1,128,1536]{2,1,0:T(8,128)(2,1)}, bf16[1,128,1536]{2,1,0:T(8,128)(2,1)S(1)}, u32[]{:S(2)}) copy-start(bf16[1,128,1536]{2,1,0:T(8,128)(2,1)S(1)} %collective-permute-done.25.refs_10_) | copy-start | bytes 1179652
  91.8 17.3 %copy-start.24 = (bf16[1,128,1536]{2,1,0:T(8,128)(2,1)}, bf16[1,128,1536]{2,1,0:T(8,128)(2,1)S(1)}, u32[]{:S(2)}) copy-start(bf16[1,128,1536]{2,1,0:T(8,128)(2,1)S(1)} %collective-permute-done.29.refs_14_) | copy-start | bytes 1179652
  91.8 17.3 %copy-start.25 = (bf16[1,128,1536]{2,1,0:T(8,128)(2,1)}, bf16[1,128,1536]{2,1,0:T(8,128)(2,1)S(1)}, u32[]{:S(2)}) copy-start(bf16[1,128,1536]{2,1,0:T(8,128)(2,1)S(1)} %collective-permute-done.28.refs_13_) | copy-start | bytes 1179652
  91.9 17.3 %copy-start.26 = (bf16[1,128,1536]{2,1,0:T(8,128)(2,1)}, bf16[1,128,1536]{2,1,0:T(8,128)(2,1)S(1)}, u32[]{:S(2)}) copy-start(bf16[1,128,1536]{2,1,0:T(8,128)(2,1)S(1)} %collective-permute-done.30.refs_15_) | copy-start | bytes 1179652
  109.1 22.4 %all-to-all-start = ((bf16[16,192,128]{2,1,0:T(8,128)(2,1)}), bf16[16,192,128]{2,1,0:T(8,128)(2,1)}, u32[]{:S(2)}, u32[]{:S(2)}) async-start(bf16[16,192,128]{2,1,0:T(8,128)(2,1)} %bitcast.36), calls=%async_computation | async-start | bytes 1572864 | tf_op jit(solution)/shard_map/all_to_all | solution.py:499
  118.2 24.0 %collective-permute-start.31 = (bf16[96,1536]{1,0:T(8,128)(2,1)}, bf16[96,1536]{1,0:T(8,128)(2,1)S(1)}, u32[]{:S(2)}, u32[]{:S(2)}) collective-permute-start(bf16[96,1536]{1,0:T(8,128)(2,1)} %bitcast.54), channel_id=1, source_target_pairs={{0,8},{8,0},{1,9},{9,1},{2,10},{10,2},{3,11},{11,3},{4,12},{12,4},... | collective-permute-start | bytes 884744 | tf_op jit(solution)/shard_map/ppermute | solution.py:502
  136.2 13.3 %collective-permute-start.32 = (bf16[96,1536]{1,0:T(8,128)(2,1)}, bf16[96,1536]{1,0:T(8,128)(2,1)S(1)}, u32[]{:S(2)}, u32[]{:S(2)}) collective-permute-start(bf16[96,1536]{1,0:T(8,128)(2,1)} %bitcast.55), channel_id=1, source_target_pairs={{0,8},{8,0},{1,9},{9,1},{2,10},{10,2},{3,11},{11,3},{4,12},{12,4},... | collective-permute-start | bytes 884744 | tf_op jit(solution)/shard_map/ppermute | solution.py:502
  (15 other events, 86.2 us)

commit v6 on v5

--- a/solution.py
+++ b/solution.py
@@ -55,21 +55,20 @@
     local_ref[:, at] = dot(scores, v_ref[:, at], NN)
 
 
-def assemble(at, counts, flags_ref, other_ref, quarter_refs, state_ref):
+def assemble(at, counts, flags_ref, other_ref, quarter_refs):
     size = quarter_refs[0].shape[0]
     quarter, start = divmod(at.start, size)
     near = flags_ref[0] == quarter // 2
     same = flags_ref[1] == quarter % 2
     own, other, swapped_own, swapped_other = [ref[start : start + HEAD_DIM, :] for ref in quarter_refs]
     total = jnp.where(same, jnp.where(near, own, swapped_own), jnp.where(near, other, swapped_other))
-    total = added_if(flags_ref[counts] == 1, total, other_ref[at, :])
-    state_ref[at, :] = total
-    return total
+    return added_if(flags_ref[counts] == 1, total, other_ref[at, :])
 
 
 def grad_output_head(counts, at, flags_ref, q_ref, local_ref, upstream_ref, other_ref, *refs):
     *quarter_refs, grad_ref, block_ref, state_ref = refs
-    state = assemble(at, counts, flags_ref, other_ref, quarter_refs, state_ref)
+    state = assemble(at, counts, flags_ref, other_ref, quarter_refs)
+    state_ref[at, :] = state
     query = feature(q_ref[:, at])
     output = local_ref[:, at] + dot(query, state, NN)
     inverse_rms = lax.rsqrt(jnp.mean(output * output, axis=-1, keepdims=True) + EPSILON)
@@ -87,11 +86,11 @@
 
 
 def key_grad_head(counts, at, flags_ref, k_ref, v_ref, local_ref, other_ref, *refs):
-    *quarter_refs, key_out, state_ref = refs[:6]
-    turned_out = refs[6:]
+    *quarter_refs, key_out = refs[:5]
+    turned_out = refs[5:]
     cuts = len(turned_out)
     copies, devices, halves, rows, tokens = turned_out[0].shape
-    state = assemble(at, counts, flags_ref, other_ref, quarter_refs, state_ref)
+    state = assemble(at, counts, flags_ref, other_ref, quarter_refs)
     key = local_ref[:, at] + dot(v_ref[:, at], state, NT)
     key = (key * slope(k_ref[:, at])).astype(BF16)
     key_out[:, at] = key
@@ -107,14 +106,16 @@
         start += size
 
 
-def other_grads_head(at, q_ref, k_ref, v_ref, grad_ref, state_ref, later_ref, query_out, value_out):
+def other_grads_head(counts, at, flags_ref, q_ref, k_ref, v_ref, grad_ref, state_ref, other_ref, *refs):
+    *quarter_refs, query_out, value_out = refs
+    later = assemble(at, counts, flags_ref, other_ref, quarter_refs)
     grad = grad_ref[:, at]
     key = feature(k_ref[:, at])
     grad_scores = causal_scores(grad, v_ref[:, at])
     query = dot(grad_scores, key, NN) + dot(grad, state_ref[at, :], NT)
     query_out[:, at] = (query * slope(q_ref[:, at])).astype(BF16)
     scores = causal_scores_turned(feature(q_ref[:, at]), key)
-    value = dot(scores, grad, NN) + dot(key, later_ref[at, :], NN)
+    value = dot(scores, grad, NN) + dot(key, later, NN)
     value_out[:, at] = value.astype(BF16)
 
 
@@ -468,10 +469,10 @@
     backward.spread([key_local], [own_side, own_layer], along_side_again, False)
     backward.collect()
     own_both = swap(after(own_side, backward.before), layer)
-    key_grad, grad_in, *turned = by_heads(
+    key_grad, *turned = by_heads(
         functools.partial(key_grad_head, backward.counts),
         [("held", after(key, own_both)), ("held", value), ("held", key_local), *backward.operands],
-        [("row", BF16), ("state", BF16)] + [((sequences, 8, halves, rows, tokens), BF16)] * cuts,
+        [("row", BF16)] + [((sequences, 8, halves, rows, tokens), BF16)] * cuts,
         1,
         bits,
     )
@@ -505,17 +506,18 @@
         sums.append(total)
     weight_grad = jnp.concatenate(sums) * (sequences * places * tokens) ** (-0.5)
     query_grad, value_grad = by_heads(
-        other_grads_head,
+        functools.partial(other_grads_head, backward.counts),
         [
             ("held", query),
             ("held", key),
             ("held", value),
             ("held", after(grad_output, done)),
             ("state", state_in),
-            ("state", grad_in),
+            *backward.operands,
         ],
         [("row", BF16), ("row", BF16)],
         6,
+        bits,
     )
     return (query_grad[None], key_grad[None], value_grad[None], weight_grad)
 

time: 151 us -> 150 us (level)
    unnamed x58 -> x66, local copies, waits for them, and re-layouts: 3.25 us -> 2.4 us
  transfers between devices with their start and end apart: 34 -> 34, of which waited for: 20 -> 20; matrix products, arithmetic and copies ran while one was open for 0% -> 1% of each run, Pallas kernels for 20% -> 20%
where the time goes in v6:
time: 150 us
  waiting for transfers between devices  58.2 us (39%)
  starting transfers between devices  37.1 us (25%)
  Pallas kernels  31.5 us (21%)
  blocking collectives  17.2 us (11%)
  local copies, waits for them, and re-layouts  2.4 us (2%)
  other arithmetic  2.22 us (1%)
    ppermute x31, waiting for transfers between devices, swap(): return lax.ppermute(array, axis, [(0, 1), (1, 0)])  41.9 us
    ppermute x31, starting transfers between devices, swap(): return lax.ppermute(array, axis, [(0, 1), (1, 0)])  29.1 us
    pallas_call x6, Pallas kernels, by_heads(): pl.pallas_call(body, in_specs=places[:count], out_specs=places[count:], o...  19.4 us
    all_to_all x1, blocking collectives, shards(): part = lax.all_to_all(part, ('dp', layer, side, core), 0, 0, tiled=True)  17.2 us
    all_to_all x1, waiting for transfers between devices, shards(): part = lax.all_to_all(part, ('dp', layer, side, core), 0, 0, tiled=True)  9.88 us
    pallas_call x2, Pallas kernels, weight_part(): pl.pallas_call(functools.partial(weight_kernel, sources_of, bits), in_spe...  9.3 us
    ppermute x2, waiting for transfers between devices, shards(): lax.ppermute(sent[turn - 1], spans, [(i, (i + turn) % halves) for i in ra...  6.39 us
    all_to_all x1, starting transfers between devices, shards(): part = lax.all_to_all(part, ('dp', layer, side, core), 0, 0, tiled=True)  4.47 us
  transfers between devices with their start and end apart: 34, of which 20 were waited for; matrix products, arithmetic and copies ran while one was open for 1% of the time, Pallas kernels for 20%

profile of v6, /device:TPU:0, one launch (start us, length us, event | category | flops | bytes accessed | tf_op | source)
XLA Modules:
  0.0 149.7 jit_solution(1581193374338502490)
XLA Ops:
  0.6 1.1 copy-done
  1.8 1.1 copy-done.2
  2.9 1.0 shard_map.84
  4.5 1.9 %collective-permute-done.refs_1_ = bf16[2,2,768,128]{3,2,1,0:T(8,128)(2,1)S(1)} collective-permute-done((bf16[2,2,768,128]{3,2,1,0:T(8,128)(2,1)S(1)}, bf16[2,2,768,128]{3,2,1,0:T(8,128)(2,1)S(1)}, u32[]{:S(2)}, u32[]{:S(2)}) %collective-permute-start) | collective-permute-done | bytes 786464 | tf_op jit(solution)/shard_map/ppermute | solution.py:196
  6.5 2.9 %collective-permute-start.1 = (bf16[768,128]{1,0:T(8,128)(2,1)S(1)}, bf16[768,128]{1,0:T(8,128)(2,1)S(1)}, u32[]{:S(2)}, u32[]{:S(2)}) collective-permute-start(bf16[768,128]{1,0:T(8,128)(2,1)S(1)} %get-tuple-element.53), channel_id=1, source_target_pairs={{0,2},{2,0},{1,3},{3,1},{4,6},{6,4},{5,7},{7,5},{8,10},{10,8},{9,1... | collective-permute-start | bytes 589832 | tf_op jit(solution)/shard_map/ppermute | solution.py:196
  9.4 1.9 %shard_map.87 = (bf16[128,1536]{1,0:T(8,128)(2,1)}, bf16[128,1536]{1,0:T(8,128)(2,1)}) custom-call(bf16[128,3072]{1,0:T(8,128)(2,1)} %bitcast.51), custom_call_target="tpu_custom_call" | custom-call | bytes 1572864 | tf_op jit(solution)/shard_map/pallas_call | solution.py:317
  11.3 1.5 %collective-permute-start.4 = (bf16[128,1536]{1,0:T(8,128)(2,1)}, bf16[128,1536]{1,0:T(8,128)(2,1)S(1)}, u32[]{:S(2)}, u32[]{:S(2)}) collective-permute-start(bf16[128,1536]{1,0:T(8,128)(2,1)} %get-tuple-element.56), channel_id=1, source_target_pairs={{0,16},{16,0},{1,17},{17,1},{2,18},{18,2},{3,19},{19,3},{4,20},{20... | collective-permute-start | bytes 1179656 | tf_op jit(solution)/shard_map/ppermute | solution.py:196
  12.8 1.8 %collective-permute-done.1.refs_1_.refs_0_ = bf16[768,128]{1,0:T(8,128)(2,1)S(1)} collective-permute-done((bf16[768,128]{1,0:T(8,128)(2,1)S(1)}, bf16[768,128]{1,0:T(8,128)(2,1)S(1)}, u32[]{:S(2)}, u32[]{:S(2)}) %collective-permute-start.1) | collective-permute-done | bytes 196640 | tf_op jit(solution)/shard_map/ppermute | solution.py:196
  14.6 1.7 %collective-permute-start.3 = (bf16[768,128]{1,0:T(8,128)(2,1)S(1)}, bf16[768,128]{1,0:T(8,128)(2,1)S(1)}, u32[]{:S(2)}, u32[]{:S(2)}) collective-permute-start(bf16[768,128]{1,0:T(8,128)(2,1)S(1)} %get-tuple-element.54.refs_0_), channel_id=1, source_target_pairs={{0,2},{2,0},{1,3},{3,1},{4,6},{6,4},{5,7},{7,5},{8,10},{10,8},{9,1... | collective-permute-start | bytes 589832 | tf_op jit(solution)/shard_map/ppermute | solution.py:196
  16.4 1.6 %collective-permute-start.2 = (bf16[768,128]{1,0:T(8,128)(2,1)S(1)}, bf16[768,128]{1,0:T(8,128)(2,1)S(1)}, u32[]{:S(2)}, u32[]{:S(2)}) collective-permute-start(bf16[768,128]{1,0:T(8,128)(2,1)S(1)} %shard_map.86.refs_0_), channel_id=1, source_target_pairs={{0,4},{4,0},{1,5},{5,1},{2,6},{6,2},{3,7},{7,3},{8,12},{12,8},{9,1... | collective-permute-start | bytes 589832 | tf_op jit(solution)/shard_map/ppermute | solution.py:196
  18.1 3.0 %collective-permute-done.3.refs_1_ = bf16[768,128]{1,0:T(8,128)(2,1)S(1)} collective-permute-done((bf16[768,128]{1,0:T(8,128)(2,1)S(1)}, bf16[768,128]{1,0:T(8,128)(2,1)S(1)}, u32[]{:S(2)}, u32[]{:S(2)}) %collective-permute-start.3) | collective-permute-done | bytes 196640 | tf_op jit(solution)/shard_map/ppermute | solution.py:196
  21.1 1.3 collective-permute-done.2.refs_1_
  23.1 2.8 %collective-permute-start.5 = (bf16[768,128]{1,0:T(8,128)(2,1)S(1)}, bf16[768,128]{1,0:T(8,128)(2,1)S(1)}, u32[]{:S(2)}, u32[]{:S(2)}) collective-permute-start(bf16[768,128]{1,0:T(8,128)(2,1)S(1)} %get-tuple-element.58), channel_id=1, source_target_pairs={{0,8},{8,0},{1,9},{9,1},{2,10},{10,2},{3,11},{11,3},{4,12},{12,4},... | collective-permute-start | bytes 589832 | tf_op jit(solution)/shard_map/ppermute | solution.py:196
  25.9 3.9 %shard_map.89.refs_1_ = f32[128,3072]{1,0:T(8,128)S(1)} custom-call(bf16[128,3072]{1,0:T(8,128)(2,1)S(1)} %bitcast.27, bf16[128,3072]{1,0:T(8,128)(2,1)S(1)} %bitcast.24, bf16[128,3072]{1,0:T(8,128)(2,1)S(1)} %bitcast.19), custom_call_target="tpu_custom_call" | custom-call | flops 201326592 | bytes 3145728 | tf_op jit(solution)/shard_map/pallas_call | solution.py:177
  29.8 4.3 %collective-permute-done.5.refs_1_ = bf16[768,128]{1,0:T(8,128)(2,1)S(1)} collective-permute-done((bf16[768,128]{1,0:T(8,128)(2,1)S(1)}, bf16[768,128]{1,0:T(8,128)(2,1)S(1)}, u32[]{:S(2)}, u32[]{:S(2)}) %collective-permute-start.5) | collective-permute-done | bytes 196640 | tf_op jit(solution)/shard_map/ppermute | solution.py:196
  34.3 1.1 collective-permute-start.7
  35.4 0.7 collective-permute-start.10
  36.1 3.9 %collective-permute-done.7.refs_0_ = bf16[768,128]{1,0:T(8,128)(2,1)S(1)} collective-permute-done((bf16[768,128]{1,0:T(8,128)(2,1)S(1)}, bf16[768,128]{1,0:T(8,128)(2,1)S(1)}, u32[]{:S(2)}, u32[]{:S(2)}) %collective-permute-start.7) | collective-permute-done | bytes 196640 | tf_op jit(solution)/shard_map/ppermute | solution.py:196
  40.2 1.4 collective-permute-done.9.refs_7_
  41.6 2.8 %shard_map.92 = (bf16[128,3072]{1,0:T(8,128)(2,1)S(1)}, bf16[3072,128]{1,0:T(8,128)(2,1)S(1)}, bf16[3072,128]{1,0:T(8,128)(2,1)S(1)}) custom-call(bf16[128,3072]{1,0:T(8,128)(2,1)S(1)} %bitcast.28, f32[128,3072]{1,0:T(8,128)S(1)} %shard_map.89.refs_1_, bf16[128,3072]{1,0:T(8,128)(2,1)S(1)} %bitcast.36, bf16[3072,128]{1,0:T(8,128)(2,1)S(1)} %bitcast.33, ...), custom_call_target="tpu_custom_call" | custom-call | flops 201326592 | bytes 8650752 | tf_op jit(solution)/shard_map/pallas_call | solution.py:177
  44.5 0.6 collective-permute-done.10.refs_3_
  45.1 1.8 %collective-permute-start.15 = (bf16[1,128,1536]{2,1,0:T(8,128)(2,1)S(1)}, bf16[1,128,1536]{2,1,0:T(8,128)(2,1)S(1)}, u32[]{:S(2)}, u32[]{:S(2)}) collective-permute-start(bf16[1,128,1536]{2,1,0:T(8,128)(2,1)S(1)} %bitcast.43), channel_id=1, source_target_pairs={{0,4},{4,0},{1,5},{5,1},{2,6},{6,2},{3,7},{7,3},{8,12},{12,8},{9,1... | collective-permute-start | bytes 1179656 | tf_op jit(solution)/shard_map/ppermute | solution.py:196
  47.5 1.1 collective-permute-start.13
  48.6 1.0 collective-permute-start.12
  49.6 3.9 %shard_map.94.refs_2_ = f32[128,3072]{1,0:T(8,128)S(1)} custom-call(bf16[128,3072]{1,0:T(8,128)(2,1)S(1)} %bitcast.29, bf16[128,3072]{1,0:T(8,128)(2,1)S(1)} %bitcast.20, bf16[128,3072]{1,0:T(8,128)(2,1)S(1)} %get-tuple-element.93.refs_2_.refs_3_), custom_call_target="tpu_custom_call" | custom-call | flops 201326592 | bytes 3145728 | tf_op jit(solution)/shard_map/pallas_call | solution.py:177
  53.5 1.8 %collective-permute-done.13.refs_1_.refs_0_ = bf16[768,128]{1,0:T(8,128)(2,1)S(1)} collective-permute-done((bf16[768,128]{1,0:T(8,128)(2,1)S(1)}, bf16[768,128]{1,0:T(8,128)(2,1)S(1)}, u32[]{:S(2)}, u32[]{:S(2)}) %collective-permute-start.13) | collective-permute-done | bytes 196640 | tf_op jit(solution)/shard_map/ppermute | solution.py:196
  55.3 1.8 %collective-permute-start.14 = (bf16[768,128]{1,0:T(8,128)(2,1)S(1)}, bf16[768,128]{1,0:T(8,128)(2,1)S(1)}, u32[]{:S(2)}, u32[]{:S(2)}) collective-permute-start(bf16[768,128]{1,0:T(8,128)(2,1)S(1)} %shard_map.95.refs_0_), channel_id=1, source_target_pairs={{0,4},{4,0},{1,5},{5,1},{2,6},{6,2},{3,7},{7,3},{8,12},{12,8},{9,1... | collective-permute-start | bytes 589832 | tf_op jit(solution)/shard_map/ppermute | solution.py:196
  57.1 5.8 %collective-permute-done.12.refs_6_ = bf16[1,128,1536]{2,1,0:T(8,128)(2,1)S(1)} collective-permute-done((bf16[1,128,1536]{2,1,0:T(8,128)(2,1)S(1)}, bf16[1,128,1536]{2,1,0:T(8,128)(2,1)S(1)}, u32[]{:S(2)}, u32[]{:S(2)}) %collective-permute-start.12) | collective-permute-done | bytes 393248 | tf_op jit(solution)/shard_map/ppermute | solution.py:196
  63.0 1.1 collective-permute-start.17
  64.1 3.4 %collective-permute-start.16 = (bf16[768,128]{1,0:T(8,128)(2,1)S(1)}, bf16[768,128]{1,0:T(8,128)(2,1)S(1)}, u32[]{:S(2)}, u32[]{:S(2)}) collective-permute-start(bf16[768,128]{1,0:T(8,128)(2,1)S(1)} %get-tuple-element.77), channel_id=1, source_target_pairs={{0,8},{8,0},{1,9},{9,1},{2,10},{10,2},{3,11},{11,3},{4,12},{12,4},... | collective-permute-start | bytes 589832 | tf_op jit(solution)/shard_map/ppermute | solution.py:196
  67.5 1.0 collective-permute-start.20
  68.7 7.1 %collective-permute-done.16.refs_1_ = bf16[768,128]{1,0:T(8,128)(2,1)S(1)} collective-permute-done((bf16[768,128]{1,0:T(8,128)(2,1)S(1)}, bf16[768,128]{1,0:T(8,128)(2,1)S(1)}, u32[]{:S(2)}, u32[]{:S(2)}) %collective-permute-start.16) | collective-permute-done | bytes 196640 | tf_op jit(solution)/shard_map/ppermute | solution.py:196
  75.9 1.0 collective-permute-start.19
  77.0 0.9 collective-permute-done.20.refs_1_
  77.8 1.5 collective-permute-start.18
  79.3 2.5 %collective-permute-done.19.refs_0_ = bf16[768,128]{1,0:T(8,128)(2,1)S(1)} collective-permute-done((bf16[768,128]{1,0:T(8,128)(2,1)S(1)}, bf16[768,128]{1,0:T(8,128)(2,1)S(1)}, u32[]{:S(2)}, u32[]{:S(2)}) %collective-permute-start.19) | collective-permute-done | bytes 196640 | tf_op jit(solution)/shard_map/ppermute | solution.py:196
  84.0 4.5 %collective-permute-done.18.refs_7_ = bf16[1,128,1536]{2,1,0:T(8,128)(2,1)S(1)} collective-permute-done((bf16[1,128,1536]{2,1,0:T(8,128)(2,1)S(1)}, bf16[1,128,1536]{2,1,0:T(8,128)(2,1)S(1)}, u32[]{:S(2)}, u32[]{:S(2)}) %collective-permute-start.18) | collective-permute-done | bytes 393248 | tf_op jit(solution)/shard_map/ppermute | solution.py:196
  88.5 2.1 %shard_map.99 = (bf16[128,3072]{1,0:T(8,128)(2,1)}, bf16[2,8,2,96,128]{4,3,2,1,0:T(8,128)(2,1)S(1)}, bf16[2,8,2,96,128]{4,3,2,1,0:T(8,128)(2,1)S(1)}) custom-call(bf16[128,3072]{1,0:T(8,128)(2,1)S(1)} %bitcast.25, bf16[128,3072]{1,0:T(8,128)(2,1)S(1)} %bitcast.21, f32[128,3072]{1,0:T(8,128)S(1)} %shard_map.94.refs_2_, bf16[3072,128]{1,0:T(8,128)(2,1)S(1)} %bitcast.31, ...), custom_call_target="tpu_custom_call" | custom-call | flops 100663296 | bytes 8650752 | tf_op jit(solution)/shard_map/pallas_call | solution.py:177
  90.8 17.2 %all_to_all.10.turned_in = bf16[16,192,128]{2,1,0:T(8,128)(2,1)} all-to-all(bf16[16,192,128]{2,1,0:T(8,128)(2,1)S(1)} %bitcast.40), channel_id=1, replica_groups=mesh['dp'=2,'bit3'=2,'bit2'=2,'bit1'=2,'bit0'=2] {'dp','bit2','bit1','bi..., dimensions={0} | all-to-all | bytes 1572864 | tf_op jit(solution)/shard_map/all_to_all | solution.py:500
  108.1 4.5 %all-to-all-start = ((bf16[16,192,128]{2,1,0:T(8,128)(2,1)}), bf16[16,192,128]{2,1,0:T(8,128)(2,1)}, u32[]{:S(2)}, u32[]{:S(2)}) async-start(bf16[16,192,128]{2,1,0:T(8,128)(2,1)} %bitcast.37), calls=%async_computation | async-start | bytes 1572864 | tf_op jit(solution)/shard_map/all_to_all | solution.py:500
  112.6 4.6 %shard_map.100 = (f32[96,1536]{1,0:T(8,128)}, bf16[1,96,1536]{2,1,0:T(8,128)(2,1)}) custom-call(bf16[16,192,128]{2,1,0:T(8,128)(2,1)} %all_to_all.10.turned_in, bf16[1,128,1536]{2,1,0:T(8,128)(2,1)} %bitcast.41, bf16[1,128,1536]{2,1,0:T(8,128)(2,1)} %bitcast.49, bf16[1,128,1536]{2,1,0:T(8,128)(2,1)} %copy-done.19, bf16[1,128,1536]{2,1,0:T(8,128)(2,1)} %copy-done.18, ...), custom_call_target="tpu_custom_call" | custom-call | flops 1207959552 | bytes 8060928 | tf_op jit(solution)/shard_map/pallas_call | solution.py:382
  117.2 3.4 %collective-permute-start.31 = (bf16[96,1536]{1,0:T(8,128)(2,1)}, bf16[96,1536]{1,0:T(8,128)(2,1)}, u32[]{:S(2)}, u32[]{:S(2)}) collective-permute-start(bf16[96,1536]{1,0:T(8,128)(2,1)} %bitcast.55), channel_id=1, source_target_pairs={{0,8},{8,0},{1,9},{9,1},{2,10},{10,2},{3,11},{11,3},{4,12},{12,4},... | collective-permute-start | bytes 884744 | tf_op jit(solution)/shard_map/ppermute | solution.py:503
  120.6 9.9 %all-to-all-done.turned_in = bf16[16,192,128]{2,1,0:T(8,128)(2,1)} async-done(((bf16[16,192,128]{2,1,0:T(8,128)(2,1)}), bf16[16,192,128]{2,1,0:T(8,128)(2,1)}, u32[]{:S(2)}, u32[]{:S(2)}) %all-to-all-start) | async-done | bytes 786464 | tf_op jit(solution)/shard_map/all_to_all | solution.py:500
  130.5 4.7 %shard_map.101 = (f32[96,1536]{1,0:T(8,128)}, bf16[1,96,1536]{2,1,0:T(8,128)(2,1)}) custom-call(bf16[16,192,128]{2,1,0:T(8,128)(2,1)} %all-to-all-done.turned_in, bf16[1,128,1536]{2,1,0:T(8,128)(2,1)} %bitcast.42, bf16[1,128,1536]{2,1,0:T(8,128)(2,1)} %bitcast.50, bf16[1,128,1536]{2,1,0:T(8,128)(2,1)} %copy-done.19, bf16[1,128,1536]{2,1,0:T(8,128)(2,1)} %copy-done.18, ...), custom_call_target="tpu_custom_call" | custom-call | flops 1207959552 | bytes 8060928 | tf_op jit(solution)/shard_map/pallas_call | solution.py:382
  135.3 5.7 %shard_map.102 = (bf16[128,3072]{1,0:T(8,128)(2,1)}, bf16[128,3072]{1,0:T(8,128)(2,1)}) custom-call(bf16[128,3072]{1,0:T(8,128)(2,1)S(1)} %bitcast.30, bf16[128,3072]{1,0:T(8,128)(2,1)S(1)} %bitcast.26, bf16[128,3072]{1,0:T(8,128)(2,1)S(1)} %bitcast.22, bf16[128,3072]{1,0:T(8,128)(2,1)S(1)} %copy-done.6, bf16[3072,128]{1,0:T(8,128)(2,1)S(1)} %copy-done.14, ...), custom_call_target="tpu_custom_call" | custom-call | flops 603979776 | bytes 9437184 | tf_op jit(solution)/shard_map/pallas_call | solution.py:177
  141.1 1.1 convert_add_fusion.1
  142.2 6.4 %collective-permute-done.32 = bf16[96,1536]{1,0:T(8,128)(2,1)S(1)} collective-permute-done((bf16[96,1536]{1,0:T(8,128)(2,1)}, bf16[96,1536]{1,0:T(8,128)(2,1)S(1)}, u32[]{:S(2)}, u32[]{:S(2)}) %collective-permute-start.32) | collective-permute-done | bytes 294944 | tf_op jit(solution)/shard_map/ppermute | solution.py:503
  148.6 1.1 maximum_multiply_fusion
  (109 shorter events, 5.2 us)
Async XLA Ops:
  3.9 2.4 %collective-permute-start = (bf16[2,2,768,128]{3,2,1,0:T(8,128)(2,1)S(1)}, bf16[2,2,768,128]{3,2,1,0:T(8,128)(2,1)S(1)}, u32[]{:S(2)}, u32[]{:S(2)}) collective-permute-start(bf16[2,2,768,128]{3,2,1,0:T(8,128)(2,1)S(1)} %bitcast.34), channel_id=1, source_target_pairs={{0,1},{1,0},{2,3},{3,2},{4,5},{5,4},{6,7},{7,6},{8,9},{9,8},{10,11... | collective-permute-start | bytes 2359304 | tf_op jit(solution)/shard_map/ppermute | solution.py:196
  6.4 19.5 %copy-start.4 = (bf16[1,128,3072]{2,1,0:T(8,128)(2,1)S(1)}, bf16[1,128,3072]{2,1,0:T(8,128)(2,1)}, u32[]{:S(2)}) copy-start(bf16[1,128,3072]{2,1,0:T(8,128)(2,1)} %param.6) | copy-start | bytes 2359300
  6.5 19.4 %copy-start.1 = (bf16[1,128,3072]{2,1,0:T(8,128)(2,1)S(1)}, bf16[1,128,3072]{2,1,0:T(8,128)(2,1)}, u32[]{:S(2)}) copy-start(bf16[1,128,3072]{2,1,0:T(8,128)(2,1)} %param.8) | copy-start | bytes 2359300
  6.5 19.4 %copy-start.3 = (bf16[1,128,3072]{2,1,0:T(8,128)(2,1)S(1)}, bf16[1,128,3072]{2,1,0:T(8,128)(2,1)}, u32[]{:S(2)}) copy-start(bf16[1,128,3072]{2,1,0:T(8,128)(2,1)} %param.7) | copy-start | bytes 2359300
  6.5 8.1 %collective-permute-start.1 = (bf16[768,128]{1,0:T(8,128)(2,1)S(1)}, bf16[768,128]{1,0:T(8,128)(2,1)S(1)}, u32[]{:S(2)}, u32[]{:S(2)}) collective-permute-start(bf16[768,128]{1,0:T(8,128)(2,1)S(1)} %get-tuple-element.53), channel_id=1, source_target_pairs={{0,2},{2,0},{1,3},{3,1},{4,6},{6,4},{5,7},{7,5},{8,10},{10,8},{9,1... | collective-permute-start | bytes 589832 | tf_op jit(solution)/shard_map/ppermute | solution.py:196
  11.3 11.1 %collective-permute-start.4 = (bf16[128,1536]{1,0:T(8,128)(2,1)}, bf16[128,1536]{1,0:T(8,128)(2,1)S(1)}, u32[]{:S(2)}, u32[]{:S(2)}) collective-permute-start(bf16[128,1536]{1,0:T(8,128)(2,1)} %get-tuple-element.56), channel_id=1, source_target_pairs={{0,16},{16,0},{1,17},{17,1},{2,18},{18,2},{3,19},{19,3},{4,20},{20... | collective-permute-start | bytes 1179656 | tf_op jit(solution)/shard_map/ppermute | solution.py:196
  14.6 6.4 %collective-permute-start.3 = (bf16[768,128]{1,0:T(8,128)(2,1)S(1)}, bf16[768,128]{1,0:T(8,128)(2,1)S(1)}, u32[]{:S(2)}, u32[]{:S(2)}) collective-permute-start(bf16[768,128]{1,0:T(8,128)(2,1)S(1)} %get-tuple-element.54.refs_0_), channel_id=1, source_target_pairs={{0,2},{2,0},{1,3},{3,1},{4,6},{6,4},{5,7},{7,5},{8,10},{10,8},{9,1... | collective-permute-start | bytes 589832 | tf_op jit(solution)/shard_map/ppermute | solution.py:196
  16.4 5.9 %collective-permute-start.2 = (bf16[768,128]{1,0:T(8,128)(2,1)S(1)}, bf16[768,128]{1,0:T(8,128)(2,1)S(1)}, u32[]{:S(2)}, u32[]{:S(2)}) collective-permute-start(bf16[768,128]{1,0:T(8,128)(2,1)S(1)} %shard_map.86.refs_0_), channel_id=1, source_target_pairs={{0,4},{4,0},{1,5},{5,1},{2,6},{6,2},{3,7},{7,3},{8,12},{12,8},{9,1... | collective-permute-start | bytes 589832 | tf_op jit(solution)/shard_map/ppermute | solution.py:196
  22.4 46.0 %copy-start.16 = (bf16[128,1536]{1,0:T(8,128)(2,1)}, bf16[128,1536]{1,0:T(8,128)(2,1)S(1)}, u32[]{:S(2)}) copy-start(bf16[128,1536]{1,0:T(8,128)(2,1)S(1)} %collective-permute-done.4) | copy-start | bytes 1179652
  22.5 11.6 %collective-permute-start.6 = (bf16[1,128,1536]{2,1,0:T(8,128)(2,1)S(1)}, bf16[1,128,1536]{2,1,0:T(8,128)(2,1)S(1)}, u32[]{:S(2)}, u32[]{:S(2)}) collective-permute-start(bf16[1,128,1536]{2,1,0:T(8,128)(2,1)S(1)} %bitcast.46), channel_id=1, source_target_pairs={{0,2},{2,0},{1,3},{3,1},{4,6},{6,4},{5,7},{7,5},{8,10},{10,8},{9,1... | collective-permute-start | bytes 1179656 | tf_op jit(solution)/shard_map/ppermute | solution.py:196
  23.1 11.1 %collective-permute-start.5 = (bf16[768,128]{1,0:T(8,128)(2,1)S(1)}, bf16[768,128]{1,0:T(8,128)(2,1)S(1)}, u32[]{:S(2)}, u32[]{:S(2)}) collective-permute-start(bf16[768,128]{1,0:T(8,128)(2,1)S(1)} %get-tuple-element.58), channel_id=1, source_target_pairs={{0,8},{8,0},{1,9},{9,1},{2,10},{10,2},{3,11},{11,3},{4,12},{12,4},... | collective-permute-start | bytes 589832 | tf_op jit(solution)/shard_map/ppermute | solution.py:196
  34.2 42.8 %copy-start.17 = (bf16[1,128,1536]{2,1,0:T(8,128)(2,1)}, bf16[1,128,1536]{2,1,0:T(8,128)(2,1)S(1)}, u32[]{:S(2)}) copy-start(bf16[1,128,1536]{2,1,0:T(8,128)(2,1)S(1)} %collective-permute-done.6.refs_4_) | copy-start | bytes 1179652
  34.3 5.8 %collective-permute-start.7 = (bf16[768,128]{1,0:T(8,128)(2,1)S(1)}, bf16[768,128]{1,0:T(8,128)(2,1)S(1)}, u32[]{:S(2)}, u32[]{:S(2)}) collective-permute-start(bf16[768,128]{1,0:T(8,128)(2,1)S(1)} %get-tuple-element.64), channel_id=1, source_target_pairs={{0,2},{2,0},{1,3},{3,1},{4,6},{6,4},{5,7},{7,5},{8,10},{10,8},{9,1... | collective-permute-start | bytes 589832 | tf_op jit(solution)/shard_map/ppermute | solution.py:196
  35.4 9.7 %collective-permute-start.10 = (bf16[1,128,1536]{2,1,0:T(8,128)(2,1)S(1)}, bf16[1,128,1536]{2,1,0:T(8,128)(2,1)S(1)}, u32[]{:S(2)}, u32[]{:S(2)}) collective-permute-start(bf16[1,128,1536]{2,1,0:T(8,128)(2,1)S(1)} %bitcast.47), channel_id=1, source_target_pairs={{0,4},{4,0},{1,5},{5,1},{2,6},{6,2},{3,7},{7,3},{8,12},{12,8},{9,1... | collective-permute-start | bytes 1179656 | tf_op jit(solution)/shard_map/ppermute | solution.py:196
  36.1 4.1 %collective-permute-start.8 = (bf16[768,128]{1,0:T(8,128)(2,1)S(1)}, bf16[768,128]{1,0:T(8,128)(2,1)S(1)}, u32[]{:S(2)}, u32[]{:S(2)}) collective-permute-start(bf16[768,128]{1,0:T(8,128)(2,1)S(1)} %get-tuple-element.63.refs_4_), channel_id=1, source_target_pairs={{0,1},{1,0},{2,3},{3,2},{4,5},{5,4},{6,7},{7,6},{8,9},{9,8},{10,11... | collective-permute-start | bytes 589832 | tf_op jit(solution)/shard_map/ppermute | solution.py:196
  40.1 1.5 %collective-permute-start.9 = (bf16[768,128]{1,0:T(8,128)(2,1)S(1)}, bf16[768,128]{1,0:T(8,128)(2,1)S(1)}, u32[]{:S(2)}, u32[]{:S(2)}) collective-permute-start(bf16[768,128]{1,0:T(8,128)(2,1)S(1)} %shard_map.91.refs_5_), channel_id=1, source_target_pairs={{0,1},{1,0},{2,3},{3,2},{4,5},{5,4},{6,7},{7,6},{8,9},{9,8},{10,11... | collective-permute-start | bytes 589832 | tf_op jit(solution)/shard_map/ppermute | solution.py:196
  45.1 37.4 %copy-start.18 = (bf16[1,128,1536]{2,1,0:T(8,128)(2,1)}, bf16[1,128,1536]{2,1,0:T(8,128)(2,1)S(1)}, u32[]{:S(2)}) copy-start(bf16[1,128,1536]{2,1,0:T(8,128)(2,1)S(1)} %collective-permute-done.10.refs_3_) | copy-start | bytes 1179652
  45.1 2.3 %collective-permute-start.11 = (bf16[2,2,768,128]{3,2,1,0:T(8,128)(2,1)S(1)}, bf16[2,2,768,128]{3,2,1,0:T(8,128)(2,1)S(1)}, u32[]{:S(2)}, u32[]{:S(2)}) collective-permute-start(bf16[2,2,768,128]{3,2,1,0:T(8,128)(2,1)S(1)} %bitcast.38), channel_id=1, source_target_pairs={{0,1},{1,0},{2,3},{3,2},{4,5},{5,4},{6,7},{7,6},{8,9},{9,8},{10,11... | collective-permute-start | bytes 2359304 | tf_op jit(solution)/shard_map/ppermute | solution.py:196
  45.1 12.0 %collective-permute-start.15 = (bf16[1,128,1536]{2,1,0:T(8,128)(2,1)S(1)}, bf16[1,128,1536]{2,1,0:T(8,128)(2,1)S(1)}, u32[]{:S(2)}, u32[]{:S(2)}) collective-permute-start(bf16[1,128,1536]{2,1,0:T(8,128)(2,1)S(1)} %bitcast.43), channel_id=1, source_target_pairs={{0,4},{4,0},{1,5},{5,1},{2,6},{6,2},{3,7},{7,3},{8,12},{12,8},{9,1... | collective-permute-start | bytes 1179656 | tf_op jit(solution)/shard_map/ppermute | solution.py:196
  47.5 7.8 %collective-permute-start.13 = (bf16[768,128]{1,0:T(8,128)(2,1)S(1)}, bf16[768,128]{1,0:T(8,128)(2,1)S(1)}, u32[]{:S(2)}, u32[]{:S(2)}) collective-permute-start(bf16[768,128]{1,0:T(8,128)(2,1)S(1)} %get-tuple-element.72), channel_id=1, source_target_pairs={{0,2},{2,0},{1,3},{3,1},{4,6},{6,4},{5,7},{7,5},{8,10},{10,8},{9,1... | collective-permute-start | bytes 589832 | tf_op jit(solution)/shard_map/ppermute | solution.py:196
  48.6 14.4 %collective-permute-start.12 = (bf16[1,128,1536]{2,1,0:T(8,128)(2,1)S(1)}, bf16[1,128,1536]{2,1,0:T(8,128)(2,1)S(1)}, u32[]{:S(2)}, u32[]{:S(2)}) collective-permute-start(bf16[1,128,1536]{2,1,0:T(8,128)(2,1)S(1)} %bitcast.44), channel_id=1, source_target_pairs={{0,2},{2,0},{1,3},{3,1},{4,6},{6,4},{5,7},{7,5},{8,10},{10,8},{9,1... | collective-permute-start | bytes 1179656 | tf_op jit(solution)/shard_map/ppermute | solution.py:196
  55.3 7.6 %collective-permute-start.14 = (bf16[768,128]{1,0:T(8,128)(2,1)S(1)}, bf16[768,128]{1,0:T(8,128)(2,1)S(1)}, u32[]{:S(2)}, u32[]{:S(2)}) collective-permute-start(bf16[768,128]{1,0:T(8,128)(2,1)S(1)} %shard_map.95.refs_0_), channel_id=1, source_target_pairs={{0,4},{4,0},{1,5},{5,1},{2,6},{6,2},{3,7},{7,3},{8,12},{12,8},{9,1... | collective-permute-start | bytes 589832 | tf_op jit(solution)/shard_map/ppermute | solution.py:196
  57.1 33.5 %copy-start.19 = (bf16[1,128,1536]{2,1,0:T(8,128)(2,1)}, bf16[1,128,1536]{2,1,0:T(8,128)(2,1)S(1)}, u32[]{:S(2)}) copy-start(bf16[1,128,1536]{2,1,0:T(8,128)(2,1)S(1)} %collective-permute-done.15.refs_2_) | copy-start | bytes 1179652
  62.9 27.7 %copy-start.20 = (bf16[1,128,1536]{2,1,0:T(8,128)(2,1)}, bf16[1,128,1536]{2,1,0:T(8,128)(2,1)S(1)}, u32[]{:S(2)}) copy-start(bf16[1,128,1536]{2,1,0:T(8,128)(2,1)S(1)} %collective-permute-done.12.refs_6_) | copy-start | bytes 1179652
  63.0 12.8 %collective-permute-start.17 = (bf16[1,128,1536]{2,1,0:T(8,128)(2,1)S(1)}, bf16[1,128,1536]{2,1,0:T(8,128)(2,1)S(1)}, u32[]{:S(2)}, u32[]{:S(2)}) collective-permute-start(bf16[1,128,1536]{2,1,0:T(8,128)(2,1)S(1)} %collective-permute-done.10.refs_3_), channel_id=1, source_target_pairs={{0,2},{2,0},{1,3},{3,1},{4,6},{6,4},{5,7},{7,5},{8,10},{10,8},{9,1... | collective-permute-start | bytes 1179656 | tf_op jit(solution)/shard_map/ppermute | solution.py:196
  64.1 11.7 %collective-permute-start.16 = (bf16[768,128]{1,0:T(8,128)(2,1)S(1)}, bf16[768,128]{1,0:T(8,128)(2,1)S(1)}, u32[]{:S(2)}, u32[]{:S(2)}) collective-permute-start(bf16[768,128]{1,0:T(8,128)(2,1)S(1)} %get-tuple-element.77), channel_id=1, source_target_pairs={{0,8},{8,0},{1,9},{9,1},{2,10},{10,2},{3,11},{11,3},{4,12},{12,4},... | collective-permute-start | bytes 589832 | tf_op jit(solution)/shard_map/ppermute | solution.py:196
  67.5 14.4 %collective-permute-start.23 = (bf16[1,128,1536]{2,1,0:T(8,128)(2,1)S(1)}, bf16[1,128,1536]{2,1,0:T(8,128)(2,1)S(1)}, u32[]{:S(2)}, u32[]{:S(2)}) collective-permute-start(bf16[1,128,1536]{2,1,0:T(8,128)(2,1)S(1)} %bitcast.45), channel_id=1, source_target_pairs={{0,1},{1,0},{2,3},{3,2},{4,5},{5,4},{6,7},{7,6},{8,9},{9,8},{10,11... | collective-permute-start | bytes 1179656 | tf_op jit(solution)/shard_map/ppermute | solution.py:196
  67.5 10.4 %collective-permute-start.20 = (bf16[768,128]{1,0:T(8,128)(2,1)S(1)}, bf16[768,128]{1,0:T(8,128)(2,1)S(1)}, u32[]{:S(2)}, u32[]{:S(2)}) collective-permute-start(bf16[768,128]{1,0:T(8,128)(2,1)S(1)} %get-tuple-element.85.refs_0_), channel_id=1, source_target_pairs={{0,2},{2,0},{1,3},{3,1},{4,6},{6,4},{5,7},{7,5},{8,10},{10,8},{9,1... | collective-permute-start | bytes 589832 | tf_op jit(solution)/shard_map/ppermute | solution.py:196
  68.4 14.1 %collective-permute-start.24 = (bf16[1,128,1536]{2,1,0:T(8,128)(2,1)S(1)}, bf16[1,128,1536]{2,1,0:T(8,128)(2,1)S(1)}, u32[]{:S(2)}, u32[]{:S(2)}) collective-permute-start(bf16[1,128,1536]{2,1,0:T(8,128)(2,1)S(1)} %bitcast.48), channel_id=1, source_target_pairs={{0,1},{1,0},{2,3},{3,2},{4,5},{5,4},{6,7},{7,6},{8,9},{9,8},{10,11... | collective-permute-start | bytes 1179656 | tf_op jit(solution)/shard_map/ppermute | solution.py:196
  75.9 5.9 %collective-permute-start.19 = (bf16[768,128]{1,0:T(8,128)(2,1)S(1)}, bf16[768,128]{1,0:T(8,128)(2,1)S(1)}, u32[]{:S(2)}, u32[]{:S(2)}) collective-permute-start(bf16[768,128]{1,0:T(8,128)(2,1)S(1)} %get-tuple-element.81), channel_id=1, source_target_pairs={{0,2},{2,0},{1,3},{3,1},{4,6},{6,4},{5,7},{7,5},{8,10},{10,8},{9,1... | collective-permute-start | bytes 589832 | tf_op jit(solution)/shard_map/ppermute | solution.py:196
  77.0 5.7 %collective-permute-start.27 = (bf16[1,128,1536]{2,1,0:T(8,128)(2,1)S(1)}, bf16[1,128,1536]{2,1,0:T(8,128)(2,1)S(1)}, u32[]{:S(2)}, u32[]{:S(2)}) collective-permute-start(bf16[1,128,1536]{2,1,0:T(8,128)(2,1)S(1)} %collective-permute-done.6.refs_4_), channel_id=1, source_target_pairs={{0,1},{1,0},{2,3},{3,2},{4,5},{5,4},{6,7},{7,6},{8,9},{9,8},{10,11... | collective-permute-start | bytes 1179656 | tf_op jit(solution)/shard_map/ppermute | solution.py:196
  77.8 10.7 %collective-permute-start.18 = (bf16[1,128,1536]{2,1,0:T(8,128)(2,1)S(1)}, bf16[1,128,1536]{2,1,0:T(8,128)(2,1)S(1)}, u32[]{:S(2)}, u32[]{:S(2)}) collective-permute-start(bf16[1,128,1536]{2,1,0:T(8,128)(2,1)S(1)} %collective-permute-done.12.refs_6_), channel_id=1, source_target_pairs={{0,4},{4,0},{1,5},{5,1},{2,6},{6,2},{3,7},{7,3},{8,12},{12,8},{9,1... | collective-permute-start | bytes 1179656 | tf_op jit(solution)/shard_map/ppermute | solution.py:196
  81.8 1.4 collective-permute-start.21
  81.9 1.6 %collective-permute-start.22 = (bf16[768,128]{1,0:T(8,128)(2,1)S(1)}, bf16[768,128]{1,0:T(8,128)(2,1)S(1)}, u32[]{:S(2)}, u32[]{:S(2)}) collective-permute-start(bf16[768,128]{1,0:T(8,128)(2,1)S(1)} %shard_map.98.refs_5_.refs_7_), channel_id=1, source_target_pairs={{0,1},{1,0},{2,3},{3,2},{4,5},{5,4},{6,7},{7,6},{8,9},{9,8},{10,11... | collective-permute-start | bytes 589832 | tf_op jit(solution)/shard_map/ppermute | solution.py:196
  82.5 8.2 %collective-permute-start.26 = (bf16[1,128,1536]{2,1,0:T(8,128)(2,1)S(1)}, bf16[1,128,1536]{2,1,0:T(8,128)(2,1)S(1)}, u32[]{:S(2)}, u32[]{:S(2)}) collective-permute-start(bf16[1,128,1536]{2,1,0:T(8,128)(2,1)S(1)} %collective-permute-done.10.refs_3_), channel_id=1, source_target_pairs={{0,1},{1,0},{2,3},{3,2},{4,5},{5,4},{6,7},{7,6},{8,9},{9,8},{10,11... | collective-permute-start | bytes 1179656 | tf_op jit(solution)/shard_map/ppermute | solution.py:196
  82.6 8.1 %collective-permute-start.25 = (bf16[1,128,1536]{2,1,0:T(8,128)(2,1)S(1)}, bf16[1,128,1536]{2,1,0:T(8,128)(2,1)S(1)}, u32[]{:S(2)}, u32[]{:S(2)}) collective-permute-start(bf16[1,128,1536]{2,1,0:T(8,128)(2,1)S(1)} %collective-permute-done.15.refs_2_), channel_id=1, source_target_pairs={{0,1},{1,0},{2,3},{3,2},{4,5},{5,4},{6,7},{7,6},{8,9},{9,8},{10,11... | collective-permute-start | bytes 1179656 | tf_op jit(solution)/shard_map/ppermute | solution.py:196
  83.3 7.5 %collective-permute-start.29 = (bf16[1,128,1536]{2,1,0:T(8,128)(2,1)S(1)}, bf16[1,128,1536]{2,1,0:T(8,128)(2,1)S(1)}, u32[]{:S(2)}, u32[]{:S(2)}) collective-permute-start(bf16[1,128,1536]{2,1,0:T(8,128)(2,1)S(1)} %collective-permute-done.12.refs_6_), channel_id=1, source_target_pairs={{0,1},{1,0},{2,3},{3,2},{4,5},{5,4},{6,7},{7,6},{8,9},{9,8},{10,11... | collective-permute-start | bytes 1179656 | tf_op jit(solution)/shard_map/ppermute | solution.py:196
  83.6 7.2 %collective-permute-start.28 = (bf16[1,128,1536]{2,1,0:T(8,128)(2,1)S(1)}, bf16[1,128,1536]{2,1,0:T(8,128)(2,1)S(1)}, u32[]{:S(2)}, u32[]{:S(2)}) collective-permute-start(bf16[1,128,1536]{2,1,0:T(8,128)(2,1)S(1)} %collective-permute-done.17.refs_5_), channel_id=1, source_target_pairs={{0,1},{1,0},{2,3},{3,2},{4,5},{5,4},{6,7},{7,6},{8,9},{9,8},{10,11... | collective-permute-start | bytes 1179656 | tf_op jit(solution)/shard_map/ppermute | solution.py:196
  88.5 2.3 %collective-permute-start.30 = (bf16[1,128,1536]{2,1,0:T(8,128)(2,1)S(1)}, bf16[1,128,1536]{2,1,0:T(8,128)(2,1)S(1)}, u32[]{:S(2)}, u32[]{:S(2)}) collective-permute-start(bf16[1,128,1536]{2,1,0:T(8,128)(2,1)S(1)} %collective-permute-done.18.refs_7_), channel_id=1, source_target_pairs={{0,1},{1,0},{2,3},{3,2},{4,5},{5,4},{6,7},{7,6},{8,9},{9,8},{10,11... | collective-permute-start | bytes 1179656 | tf_op jit(solution)/shard_map/ppermute | solution.py:196
  90.7 17.3 %copy-start.12 = (bf16[2,8,2,96,128]{4,3,2,1,0:T(8,128)(2,1)}, bf16[2,8,2,96,128]{4,3,2,1,0:T(8,128)(2,1)S(1)}, u32[]{:S(2)}) copy-start(bf16[2,8,2,96,128]{4,3,2,1,0:T(8,128)(2,1)S(1)} %get-tuple-element.86) | copy-start | bytes 2359300
  90.7 17.3 %copy-start.26 = (bf16[1,128,1536]{2,1,0:T(8,128)(2,1)}, bf16[1,128,1536]{2,1,0:T(8,128)(2,1)S(1)}, u32[]{:S(2)}) copy-start(bf16[1,128,1536]{2,1,0:T(8,128)(2,1)S(1)} %collective-permute-done.26.refs_11_) | copy-start | bytes 1179652
  90.7 17.3 %copy-start.27 = (bf16[1,128,1536]{2,1,0:T(8,128)(2,1)}, bf16[1,128,1536]{2,1,0:T(8,128)(2,1)S(1)}, u32[]{:S(2)}) copy-start(bf16[1,128,1536]{2,1,0:T(8,128)(2,1)S(1)} %collective-permute-done.25.refs_10_) | copy-start | bytes 1179652
  90.8 17.3 %copy-start.28 = (bf16[1,128,1536]{2,1,0:T(8,128)(2,1)}, bf16[1,128,1536]{2,1,0:T(8,128)(2,1)S(1)}, u32[]{:S(2)}) copy-start(bf16[1,128,1536]{2,1,0:T(8,128)(2,1)S(1)} %collective-permute-done.29.refs_14_) | copy-start | bytes 1179652
  90.8 17.3 %copy-start.29 = (bf16[1,128,1536]{2,1,0:T(8,128)(2,1)}, bf16[1,128,1536]{2,1,0:T(8,128)(2,1)S(1)}, u32[]{:S(2)}) copy-start(bf16[1,128,1536]{2,1,0:T(8,128)(2,1)S(1)} %collective-permute-done.28.refs_13_) | copy-start | bytes 1179652
  90.8 17.3 %copy-start.30 = (bf16[1,128,1536]{2,1,0:T(8,128)(2,1)}, bf16[1,128,1536]{2,1,0:T(8,128)(2,1)S(1)}, u32[]{:S(2)}) copy-start(bf16[1,128,1536]{2,1,0:T(8,128)(2,1)S(1)} %collective-permute-done.30.refs_15_) | copy-start | bytes 1179652
  108.1 22.4 %all-to-all-start = ((bf16[16,192,128]{2,1,0:T(8,128)(2,1)}), bf16[16,192,128]{2,1,0:T(8,128)(2,1)}, u32[]{:S(2)}, u32[]{:S(2)}) async-start(bf16[16,192,128]{2,1,0:T(8,128)(2,1)} %bitcast.37), calls=%async_computation | async-start | bytes 1572864 | tf_op jit(solution)/shard_map/all_to_all | solution.py:500
  117.2 23.9 %collective-permute-start.31 = (bf16[96,1536]{1,0:T(8,128)(2,1)}, bf16[96,1536]{1,0:T(8,128)(2,1)}, u32[]{:S(2)}, u32[]{:S(2)}) collective-permute-start(bf16[96,1536]{1,0:T(8,128)(2,1)} %bitcast.55), channel_id=1, source_target_pairs={{0,8},{8,0},{1,9},{9,1},{2,10},{10,2},{3,11},{11,3},{4,12},{12,4},... | collective-permute-start | bytes 884744 | tf_op jit(solution)/shard_map/ppermute | solution.py:503
  135.2 13.4 %collective-permute-start.32 = (bf16[96,1536]{1,0:T(8,128)(2,1)}, bf16[96,1536]{1,0:T(8,128)(2,1)S(1)}, u32[]{:S(2)}, u32[]{:S(2)}) collective-permute-start(bf16[96,1536]{1,0:T(8,128)(2,1)} %bitcast.56), channel_id=1, source_target_pairs={{0,8},{8,0},{1,9},{9,1},{2,10},{10,2},{3,11},{11,3},{4,12},{12,4},... | collective-permute-start | bytes 884744 | tf_op jit(solution)/shard_map/ppermute | solution.py:503
  (19 other events, 118.1 us)

commit v7 on v6

--- a/solution.py
+++ b/solution.py
@@ -417,7 +417,7 @@
     rows = features // places // cuts
 
     (block_state,) = by_heads(
-        block_state_head, [("row", key), ("row", value)], [("held state", BF16)], 1, vmem=44
+        block_state_head, [("held", key), ("held", value)], [("held state", BF16)], 1
     )
     forward = Scan(block_state, bits, False)
 

time: 150 us -> 150 us (level)
  no operation moved by 1% of the time
where the time goes in v7:
time: 150 us; the launch traced here: 149 us
  waiting for transfers between devices  58.2 us (39%)
  starting transfers between devices  37 us (25%)
  Pallas kernels  31.2 us (21%)
  blocking collectives  17.2 us (11%)
  local copies, waits for them, and re-layouts  2.4 us (2%)
  other arithmetic  2.22 us (1%)
    ppermute x31, waiting for transfers between devices, swap(): return lax.ppermute(array, axis, [(0, 1), (1, 0)])  41.9 us
    ppermute x31, starting transfers between devices, swap(): return lax.ppermute(array, axis, [(0, 1), (1, 0)])  29.1 us
    pallas_call x6, Pallas kernels, by_heads(): pl.pallas_call(body, in_specs=places[:count], out_specs=places[count:], o...  19.1 us
    all_to_all x1, blocking collectives, shards(): part = lax.all_to_all(part, ('dp', layer, side, core), 0, 0, tiled=True)  17.2 us
    all_to_all x1, waiting for transfers between devices, shards(): part = lax.all_to_all(part, ('dp', layer, side, core), 0, 0, tiled=True)  9.87 us
    pallas_call x2, Pallas kernels, weight_part(): pl.pallas_call(functools.partial(weight_kernel, sources_of, bits), in_spe...  9.3 us
    ppermute x2, waiting for transfers between devices, shards(): lax.ppermute(sent[turn - 1], spans, [(i, (i + turn) % halves) for i in ra...  6.41 us
    all_to_all x1, starting transfers between devices, shards(): part = lax.all_to_all(part, ('dp', layer, side, core), 0, 0, tiled=True)  4.47 us
  transfers between devices with their start and end apart: 34, of which 20 were waited for; matrix products, arithmetic and copies ran while one was open for 1% of the time, Pallas kernels for 20%

profile of v7, /device:TPU:0, one launch (start us, length us, event | category | flops | bytes accessed | tf_op | source)
XLA Modules:
  0.0 149.5 jit_solution(7279476687737554417)
XLA Ops:
  0.6 1.1 copy-done
  1.8 1.1 copy-done.2
  2.9 0.8 shard_map.84
  4.2 1.9 %collective-permute-done.refs_1_ = bf16[2,2,768,128]{3,2,1,0:T(8,128)(2,1)S(1)} collective-permute-done((bf16[2,2,768,128]{3,2,1,0:T(8,128)(2,1)S(1)}, bf16[2,2,768,128]{3,2,1,0:T(8,128)(2,1)S(1)}, u32[]{:S(2)}, u32[]{:S(2)}) %collective-permute-start) | collective-permute-done | bytes 786464 | tf_op jit(solution)/shard_map/ppermute | solution.py:196
  6.2 2.9 %collective-permute-start.1 = (bf16[768,128]{1,0:T(8,128)(2,1)S(1)}, bf16[768,128]{1,0:T(8,128)(2,1)S(1)}, u32[]{:S(2)}, u32[]{:S(2)}) collective-permute-start(bf16[768,128]{1,0:T(8,128)(2,1)S(1)} %get-tuple-element.53), channel_id=1, source_target_pairs={{0,2},{2,0},{1,3},{3,1},{4,6},{6,4},{5,7},{7,5},{8,10},{10,8},{9,1... | collective-permute-start | bytes 589832 | tf_op jit(solution)/shard_map/ppermute | solution.py:196
  9.1 1.9 %shard_map.87 = (bf16[128,1536]{1,0:T(8,128)(2,1)}, bf16[128,1536]{1,0:T(8,128)(2,1)}) custom-call(bf16[128,3072]{1,0:T(8,128)(2,1)} %bitcast.51), custom_call_target="tpu_custom_call" | custom-call | bytes 1572864 | tf_op jit(solution)/shard_map/pallas_call | solution.py:317
  11.0 1.5 %collective-permute-start.4 = (bf16[128,1536]{1,0:T(8,128)(2,1)}, bf16[128,1536]{1,0:T(8,128)(2,1)S(1)}, u32[]{:S(2)}, u32[]{:S(2)}) collective-permute-start(bf16[128,1536]{1,0:T(8,128)(2,1)} %get-tuple-element.56), channel_id=1, source_target_pairs={{0,16},{16,0},{1,17},{17,1},{2,18},{18,2},{3,19},{19,3},{4,20},{20... | collective-permute-start | bytes 1179656 | tf_op jit(solution)/shard_map/ppermute | solution.py:196
  12.6 1.8 %collective-permute-done.1.refs_1_.refs_0_ = bf16[768,128]{1,0:T(8,128)(2,1)S(1)} collective-permute-done((bf16[768,128]{1,0:T(8,128)(2,1)S(1)}, bf16[768,128]{1,0:T(8,128)(2,1)S(1)}, u32[]{:S(2)}, u32[]{:S(2)}) %collective-permute-start.1) | collective-permute-done | bytes 196640 | tf_op jit(solution)/shard_map/ppermute | solution.py:196
  14.4 1.7 %collective-permute-start.3 = (bf16[768,128]{1,0:T(8,128)(2,1)S(1)}, bf16[768,128]{1,0:T(8,128)(2,1)S(1)}, u32[]{:S(2)}, u32[]{:S(2)}) collective-permute-start(bf16[768,128]{1,0:T(8,128)(2,1)S(1)} %get-tuple-element.54.refs_0_), channel_id=1, source_target_pairs={{0,2},{2,0},{1,3},{3,1},{4,6},{6,4},{5,7},{7,5},{8,10},{10,8},{9,1... | collective-permute-start | bytes 589832 | tf_op jit(solution)/shard_map/ppermute | solution.py:196
  16.1 1.6 %collective-permute-start.2 = (bf16[768,128]{1,0:T(8,128)(2,1)S(1)}, bf16[768,128]{1,0:T(8,128)(2,1)S(1)}, u32[]{:S(2)}, u32[]{:S(2)}) collective-permute-start(bf16[768,128]{1,0:T(8,128)(2,1)S(1)} %shard_map.86.refs_0_), channel_id=1, source_target_pairs={{0,4},{4,0},{1,5},{5,1},{2,6},{6,2},{3,7},{7,3},{8,12},{12,8},{9,1... | collective-permute-start | bytes 589832 | tf_op jit(solution)/shard_map/ppermute | solution.py:196
  17.8 3.0 %collective-permute-done.3.refs_1_ = bf16[768,128]{1,0:T(8,128)(2,1)S(1)} collective-permute-done((bf16[768,128]{1,0:T(8,128)(2,1)S(1)}, bf16[768,128]{1,0:T(8,128)(2,1)S(1)}, u32[]{:S(2)}, u32[]{:S(2)}) %collective-permute-start.3) | collective-permute-done | bytes 196640 | tf_op jit(solution)/shard_map/ppermute | solution.py:196
  20.8 1.3 collective-permute-done.2.refs_1_
  22.8 2.8 %collective-permute-start.5 = (bf16[768,128]{1,0:T(8,128)(2,1)S(1)}, bf16[768,128]{1,0:T(8,128)(2,1)S(1)}, u32[]{:S(2)}, u32[]{:S(2)}) collective-permute-start(bf16[768,128]{1,0:T(8,128)(2,1)S(1)} %get-tuple-element.58), channel_id=1, source_target_pairs={{0,8},{8,0},{1,9},{9,1},{2,10},{10,2},{3,11},{11,3},{4,12},{12,4},... | collective-permute-start | bytes 589832 | tf_op jit(solution)/shard_map/ppermute | solution.py:196
  25.6 3.9 %shard_map.89.refs_1_ = f32[128,3072]{1,0:T(8,128)S(1)} custom-call(bf16[128,3072]{1,0:T(8,128)(2,1)S(1)} %bitcast.27, bf16[128,3072]{1,0:T(8,128)(2,1)S(1)} %bitcast.24, bf16[128,3072]{1,0:T(8,128)(2,1)S(1)} %bitcast.19), custom_call_target="tpu_custom_call" | custom-call | flops 201326592 | bytes 3145728 | tf_op jit(solution)/shard_map/pallas_call | solution.py:177
  29.5 4.4 %collective-permute-done.5.refs_1_ = bf16[768,128]{1,0:T(8,128)(2,1)S(1)} collective-permute-done((bf16[768,128]{1,0:T(8,128)(2,1)S(1)}, bf16[768,128]{1,0:T(8,128)(2,1)S(1)}, u32[]{:S(2)}, u32[]{:S(2)}) %collective-permute-start.5) | collective-permute-done | bytes 196640 | tf_op jit(solution)/shard_map/ppermute | solution.py:196
  34.0 1.1 collective-permute-start.7
  35.1 0.7 collective-permute-start.10
  35.8 3.9 %collective-permute-done.7.refs_0_ = bf16[768,128]{1,0:T(8,128)(2,1)S(1)} collective-permute-done((bf16[768,128]{1,0:T(8,128)(2,1)S(1)}, bf16[768,128]{1,0:T(8,128)(2,1)S(1)}, u32[]{:S(2)}, u32[]{:S(2)}) %collective-permute-start.7) | collective-permute-done | bytes 196640 | tf_op jit(solution)/shard_map/ppermute | solution.py:196
  39.9 1.4 collective-permute-done.9.refs_7_
  41.4 2.8 %shard_map.92 = (bf16[128,3072]{1,0:T(8,128)(2,1)S(1)}, bf16[3072,128]{1,0:T(8,128)(2,1)S(1)}, bf16[3072,128]{1,0:T(8,128)(2,1)S(1)}) custom-call(bf16[128,3072]{1,0:T(8,128)(2,1)S(1)} %bitcast.28, f32[128,3072]{1,0:T(8,128)S(1)} %shard_map.89.refs_1_, bf16[128,3072]{1,0:T(8,128)(2,1)S(1)} %bitcast.36, bf16[3072,128]{1,0:T(8,128)(2,1)S(1)} %bitcast.33, ...), custom_call_target="tpu_custom_call" | custom-call | flops 201326592 | bytes 8650752 | tf_op jit(solution)/shard_map/pallas_call | solution.py:177
  44.2 0.6 collective-permute-done.10.refs_3_
  44.8 1.8 %collective-permute-start.15 = (bf16[1,128,1536]{2,1,0:T(8,128)(2,1)S(1)}, bf16[1,128,1536]{2,1,0:T(8,128)(2,1)S(1)}, u32[]{:S(2)}, u32[]{:S(2)}) collective-permute-start(bf16[1,128,1536]{2,1,0:T(8,128)(2,1)S(1)} %bitcast.43), channel_id=1, source_target_pairs={{0,4},{4,0},{1,5},{5,1},{2,6},{6,2},{3,7},{7,3},{8,12},{12,8},{9,1... | collective-permute-start | bytes 1179656 | tf_op jit(solution)/shard_map/ppermute | solution.py:196
  47.2 1.1 collective-permute-start.13
  48.3 1.0 collective-permute-start.12
  49.3 3.9 %shard_map.94.refs_2_ = f32[128,3072]{1,0:T(8,128)S(1)} custom-call(bf16[128,3072]{1,0:T(8,128)(2,1)S(1)} %bitcast.29, bf16[128,3072]{1,0:T(8,128)(2,1)S(1)} %bitcast.20, bf16[128,3072]{1,0:T(8,128)(2,1)S(1)} %get-tuple-element.93.refs_2_.refs_3_), custom_call_target="tpu_custom_call" | custom-call | flops 201326592 | bytes 3145728 | tf_op jit(solution)/shard_map/pallas_call | solution.py:177
  53.2 1.8 %collective-permute-done.13.refs_1_.refs_0_ = bf16[768,128]{1,0:T(8,128)(2,1)S(1)} collective-permute-done((bf16[768,128]{1,0:T(8,128)(2,1)S(1)}, bf16[768,128]{1,0:T(8,128)(2,1)S(1)}, u32[]{:S(2)}, u32[]{:S(2)}) %collective-permute-start.13) | collective-permute-done | bytes 196640 | tf_op jit(solution)/shard_map/ppermute | solution.py:196
  55.1 1.8 %collective-permute-start.14 = (bf16[768,128]{1,0:T(8,128)(2,1)S(1)}, bf16[768,128]{1,0:T(8,128)(2,1)S(1)}, u32[]{:S(2)}, u32[]{:S(2)}) collective-permute-start(bf16[768,128]{1,0:T(8,128)(2,1)S(1)} %shard_map.95.refs_0_), channel_id=1, source_target_pairs={{0,4},{4,0},{1,5},{5,1},{2,6},{6,2},{3,7},{7,3},{8,12},{12,8},{9,1... | collective-permute-start | bytes 589832 | tf_op jit(solution)/shard_map/ppermute | solution.py:196
  56.8 5.8 %collective-permute-done.12.refs_6_ = bf16[1,128,1536]{2,1,0:T(8,128)(2,1)S(1)} collective-permute-done((bf16[1,128,1536]{2,1,0:T(8,128)(2,1)S(1)}, bf16[1,128,1536]{2,1,0:T(8,128)(2,1)S(1)}, u32[]{:S(2)}, u32[]{:S(2)}) %collective-permute-start.12) | collective-permute-done | bytes 393248 | tf_op jit(solution)/shard_map/ppermute | solution.py:196
  62.7 1.1 collective-permute-start.17
  63.8 3.4 %collective-permute-start.16 = (bf16[768,128]{1,0:T(8,128)(2,1)S(1)}, bf16[768,128]{1,0:T(8,128)(2,1)S(1)}, u32[]{:S(2)}, u32[]{:S(2)}) collective-permute-start(bf16[768,128]{1,0:T(8,128)(2,1)S(1)} %get-tuple-element.77), channel_id=1, source_target_pairs={{0,8},{8,0},{1,9},{9,1},{2,10},{10,2},{3,11},{11,3},{4,12},{12,4},... | collective-permute-start | bytes 589832 | tf_op jit(solution)/shard_map/ppermute | solution.py:196
  67.2 1.0 collective-permute-start.20
  68.4 7.1 %collective-permute-done.16.refs_1_ = bf16[768,128]{1,0:T(8,128)(2,1)S(1)} collective-permute-done((bf16[768,128]{1,0:T(8,128)(2,1)S(1)}, bf16[768,128]{1,0:T(8,128)(2,1)S(1)}, u32[]{:S(2)}, u32[]{:S(2)}) %collective-permute-start.16) | collective-permute-done | bytes 196640 | tf_op jit(solution)/shard_map/ppermute | solution.py:196
  75.6 1.0 collective-permute-start.19
  76.7 0.9 collective-permute-done.20.refs_1_
  77.6 1.5 collective-permute-start.18
  79.0 2.5 %collective-permute-done.19.refs_0_ = bf16[768,128]{1,0:T(8,128)(2,1)S(1)} collective-permute-done((bf16[768,128]{1,0:T(8,128)(2,1)S(1)}, bf16[768,128]{1,0:T(8,128)(2,1)S(1)}, u32[]{:S(2)}, u32[]{:S(2)}) %collective-permute-start.19) | collective-permute-done | bytes 196640 | tf_op jit(solution)/shard_map/ppermute | solution.py:196
  83.7 4.5 %collective-permute-done.18.refs_7_ = bf16[1,128,1536]{2,1,0:T(8,128)(2,1)S(1)} collective-permute-done((bf16[1,128,1536]{2,1,0:T(8,128)(2,1)S(1)}, bf16[1,128,1536]{2,1,0:T(8,128)(2,1)S(1)}, u32[]{:S(2)}, u32[]{:S(2)}) %collective-permute-start.18) | collective-permute-done | bytes 393248 | tf_op jit(solution)/shard_map/ppermute | solution.py:196
  88.2 2.1 %shard_map.99 = (bf16[128,3072]{1,0:T(8,128)(2,1)}, bf16[2,8,2,96,128]{4,3,2,1,0:T(8,128)(2,1)S(1)}, bf16[2,8,2,96,128]{4,3,2,1,0:T(8,128)(2,1)S(1)}) custom-call(bf16[128,3072]{1,0:T(8,128)(2,1)S(1)} %bitcast.25, bf16[128,3072]{1,0:T(8,128)(2,1)S(1)} %bitcast.21, f32[128,3072]{1,0:T(8,128)S(1)} %shard_map.94.refs_2_, bf16[3072,128]{1,0:T(8,128)(2,1)S(1)} %bitcast.31, ...), custom_call_target="tpu_custom_call" | custom-call | flops 100663296 | bytes 8650752 | tf_op jit(solution)/shard_map/pallas_call | solution.py:177
  90.5 17.2 %all_to_all.10.turned_in = bf16[16,192,128]{2,1,0:T(8,128)(2,1)} all-to-all(bf16[16,192,128]{2,1,0:T(8,128)(2,1)S(1)} %bitcast.40), channel_id=1, replica_groups=mesh['dp'=2,'bit3'=2,'bit2'=2,'bit1'=2,'bit0'=2] {'dp','bit2','bit1','bi..., dimensions={0} | all-to-all | bytes 1572864 | tf_op jit(solution)/shard_map/all_to_all | solution.py:500
  107.8 4.5 %all-to-all-start = ((bf16[16,192,128]{2,1,0:T(8,128)(2,1)}), bf16[16,192,128]{2,1,0:T(8,128)(2,1)}, u32[]{:S(2)}, u32[]{:S(2)}) async-start(bf16[16,192,128]{2,1,0:T(8,128)(2,1)} %bitcast.37), calls=%async_computation | async-start | bytes 1572864 | tf_op jit(solution)/shard_map/all_to_all | solution.py:500
  112.3 4.6 %shard_map.100 = (f32[96,1536]{1,0:T(8,128)}, bf16[1,96,1536]{2,1,0:T(8,128)(2,1)}) custom-call(bf16[16,192,128]{2,1,0:T(8,128)(2,1)} %all_to_all.10.turned_in, bf16[1,128,1536]{2,1,0:T(8,128)(2,1)} %bitcast.41, bf16[1,128,1536]{2,1,0:T(8,128)(2,1)} %bitcast.49, bf16[1,128,1536]{2,1,0:T(8,128)(2,1)} %copy-done.19, bf16[1,128,1536]{2,1,0:T(8,128)(2,1)} %copy-done.18, ...), custom_call_target="tpu_custom_call" | custom-call | flops 1207959552 | bytes 8060928 | tf_op jit(solution)/shard_map/pallas_call | solution.py:382
  116.9 3.4 %collective-permute-start.31 = (bf16[96,1536]{1,0:T(8,128)(2,1)}, bf16[96,1536]{1,0:T(8,128)(2,1)}, u32[]{:S(2)}, u32[]{:S(2)}) collective-permute-start(bf16[96,1536]{1,0:T(8,128)(2,1)} %bitcast.55), channel_id=1, source_target_pairs={{0,8},{8,0},{1,9},{9,1},{2,10},{10,2},{3,11},{11,3},{4,12},{12,4},... | collective-permute-start | bytes 884744 | tf_op jit(solution)/shard_map/ppermute | solution.py:503
  120.3 9.9 %all-to-all-done.turned_in = bf16[16,192,128]{2,1,0:T(8,128)(2,1)} async-done(((bf16[16,192,128]{2,1,0:T(8,128)(2,1)}), bf16[16,192,128]{2,1,0:T(8,128)(2,1)}, u32[]{:S(2)}, u32[]{:S(2)}) %all-to-all-start) | async-done | bytes 786464 | tf_op jit(solution)/shard_map/all_to_all | solution.py:500
  130.2 4.7 %shard_map.101 = (f32[96,1536]{1,0:T(8,128)}, bf16[1,96,1536]{2,1,0:T(8,128)(2,1)}) custom-call(bf16[16,192,128]{2,1,0:T(8,128)(2,1)} %all-to-all-done.turned_in, bf16[1,128,1536]{2,1,0:T(8,128)(2,1)} %bitcast.42, bf16[1,128,1536]{2,1,0:T(8,128)(2,1)} %bitcast.50, bf16[1,128,1536]{2,1,0:T(8,128)(2,1)} %copy-done.19, bf16[1,128,1536]{2,1,0:T(8,128)(2,1)} %copy-done.18, ...), custom_call_target="tpu_custom_call" | custom-call | flops 1207959552 | bytes 8060928 | tf_op jit(solution)/shard_map/pallas_call | solution.py:382
  135.0 5.7 %shard_map.102 = (bf16[128,3072]{1,0:T(8,128)(2,1)}, bf16[128,3072]{1,0:T(8,128)(2,1)}) custom-call(bf16[128,3072]{1,0:T(8,128)(2,1)S(1)} %bitcast.30, bf16[128,3072]{1,0:T(8,128)(2,1)S(1)} %bitcast.26, bf16[128,3072]{1,0:T(8,128)(2,1)S(1)} %bitcast.22, bf16[128,3072]{1,0:T(8,128)(2,1)S(1)} %copy-done.6, bf16[3072,128]{1,0:T(8,128)(2,1)S(1)} %copy-done.14, ...), custom_call_target="tpu_custom_call" | custom-call | flops 603979776 | bytes 9437184 | tf_op jit(solution)/shard_map/pallas_call | solution.py:177
  140.8 1.1 convert_add_fusion.1
  141.9 6.4 %collective-permute-done.32 = bf16[96,1536]{1,0:T(8,128)(2,1)S(1)} collective-permute-done((bf16[96,1536]{1,0:T(8,128)(2,1)}, bf16[96,1536]{1,0:T(8,128)(2,1)S(1)}, u32[]{:S(2)}, u32[]{:S(2)}) %collective-permute-start.32) | collective-permute-done | bytes 294944 | tf_op jit(solution)/shard_map/ppermute | solution.py:503
  148.4 1.1 maximum_multiply_fusion
  (109 shorter events, 5.2 us)
Async XLA Ops:
  3.7 2.4 %collective-permute-start = (bf16[2,2,768,128]{3,2,1,0:T(8,128)(2,1)S(1)}, bf16[2,2,768,128]{3,2,1,0:T(8,128)(2,1)S(1)}, u32[]{:S(2)}, u32[]{:S(2)}) collective-permute-start(bf16[2,2,768,128]{3,2,1,0:T(8,128)(2,1)S(1)} %bitcast.34), channel_id=1, source_target_pairs={{0,1},{1,0},{2,3},{3,2},{4,5},{5,4},{6,7},{7,6},{8,9},{9,8},{10,11... | collective-permute-start | bytes 2359304 | tf_op jit(solution)/shard_map/ppermute | solution.py:196
  6.1 19.5 %copy-start.4 = (bf16[1,128,3072]{2,1,0:T(8,128)(2,1)S(1)}, bf16[1,128,3072]{2,1,0:T(8,128)(2,1)}, u32[]{:S(2)}) copy-start(bf16[1,128,3072]{2,1,0:T(8,128)(2,1)} %param.6) | copy-start | bytes 2359300
  6.2 19.4 %copy-start.1 = (bf16[1,128,3072]{2,1,0:T(8,128)(2,1)S(1)}, bf16[1,128,3072]{2,1,0:T(8,128)(2,1)}, u32[]{:S(2)}) copy-start(bf16[1,128,3072]{2,1,0:T(8,128)(2,1)} %param.8) | copy-start | bytes 2359300
  6.2 19.4 %copy-start.3 = (bf16[1,128,3072]{2,1,0:T(8,128)(2,1)S(1)}, bf16[1,128,3072]{2,1,0:T(8,128)(2,1)}, u32[]{:S(2)}) copy-start(bf16[1,128,3072]{2,1,0:T(8,128)(2,1)} %param.7) | copy-start | bytes 2359300
  6.2 8.1 %collective-permute-start.1 = (bf16[768,128]{1,0:T(8,128)(2,1)S(1)}, bf16[768,128]{1,0:T(8,128)(2,1)S(1)}, u32[]{:S(2)}, u32[]{:S(2)}) collective-permute-start(bf16[768,128]{1,0:T(8,128)(2,1)S(1)} %get-tuple-element.53), channel_id=1, source_target_pairs={{0,2},{2,0},{1,3},{3,1},{4,6},{6,4},{5,7},{7,5},{8,10},{10,8},{9,1... | collective-permute-start | bytes 589832 | tf_op jit(solution)/shard_map/ppermute | solution.py:196
  11.0 11.1 %collective-permute-start.4 = (bf16[128,1536]{1,0:T(8,128)(2,1)}, bf16[128,1536]{1,0:T(8,128)(2,1)S(1)}, u32[]{:S(2)}, u32[]{:S(2)}) collective-permute-start(bf16[128,1536]{1,0:T(8,128)(2,1)} %get-tuple-element.56), channel_id=1, source_target_pairs={{0,16},{16,0},{1,17},{17,1},{2,18},{18,2},{3,19},{19,3},{4,20},{20... | collective-permute-start | bytes 1179656 | tf_op jit(solution)/shard_map/ppermute | solution.py:196
  14.4 6.4 %collective-permute-start.3 = (bf16[768,128]{1,0:T(8,128)(2,1)S(1)}, bf16[768,128]{1,0:T(8,128)(2,1)S(1)}, u32[]{:S(2)}, u32[]{:S(2)}) collective-permute-start(bf16[768,128]{1,0:T(8,128)(2,1)S(1)} %get-tuple-element.54.refs_0_), channel_id=1, source_target_pairs={{0,2},{2,0},{1,3},{3,1},{4,6},{6,4},{5,7},{7,5},{8,10},{10,8},{9,1... | collective-permute-start | bytes 589832 | tf_op jit(solution)/shard_map/ppermute | solution.py:196
  16.1 5.9 %collective-permute-start.2 = (bf16[768,128]{1,0:T(8,128)(2,1)S(1)}, bf16[768,128]{1,0:T(8,128)(2,1)S(1)}, u32[]{:S(2)}, u32[]{:S(2)}) collective-permute-start(bf16[768,128]{1,0:T(8,128)(2,1)S(1)} %shard_map.86.refs_0_), channel_id=1, source_target_pairs={{0,4},{4,0},{1,5},{5,1},{2,6},{6,2},{3,7},{7,3},{8,12},{12,8},{9,1... | collective-permute-start | bytes 589832 | tf_op jit(solution)/shard_map/ppermute | solution.py:196
  22.1 46.0 %copy-start.16 = (bf16[128,1536]{1,0:T(8,128)(2,1)}, bf16[128,1536]{1,0:T(8,128)(2,1)S(1)}, u32[]{:S(2)}) copy-start(bf16[128,1536]{1,0:T(8,128)(2,1)S(1)} %collective-permute-done.4) | copy-start | bytes 1179652
  22.2 11.6 %collective-permute-start.6 = (bf16[1,128,1536]{2,1,0:T(8,128)(2,1)S(1)}, bf16[1,128,1536]{2,1,0:T(8,128)(2,1)S(1)}, u32[]{:S(2)}, u32[]{:S(2)}) collective-permute-start(bf16[1,128,1536]{2,1,0:T(8,128)(2,1)S(1)} %bitcast.46), channel_id=1, source_target_pairs={{0,2},{2,0},{1,3},{3,1},{4,6},{6,4},{5,7},{7,5},{8,10},{10,8},{9,1... | collective-permute-start | bytes 1179656 | tf_op jit(solution)/shard_map/ppermute | solution.py:196
  22.8 11.1 %collective-permute-start.5 = (bf16[768,128]{1,0:T(8,128)(2,1)S(1)}, bf16[768,128]{1,0:T(8,128)(2,1)S(1)}, u32[]{:S(2)}, u32[]{:S(2)}) collective-permute-start(bf16[768,128]{1,0:T(8,128)(2,1)S(1)} %get-tuple-element.58), channel_id=1, source_target_pairs={{0,8},{8,0},{1,9},{9,1},{2,10},{10,2},{3,11},{11,3},{4,12},{12,4},... | collective-permute-start | bytes 589832 | tf_op jit(solution)/shard_map/ppermute | solution.py:196
  33.9 42.8 %copy-start.17 = (bf16[1,128,1536]{2,1,0:T(8,128)(2,1)}, bf16[1,128,1536]{2,1,0:T(8,128)(2,1)S(1)}, u32[]{:S(2)}) copy-start(bf16[1,128,1536]{2,1,0:T(8,128)(2,1)S(1)} %collective-permute-done.6.refs_4_) | copy-start | bytes 1179652
  34.0 5.8 %collective-permute-start.7 = (bf16[768,128]{1,0:T(8,128)(2,1)S(1)}, bf16[768,128]{1,0:T(8,128)(2,1)S(1)}, u32[]{:S(2)}, u32[]{:S(2)}) collective-permute-start(bf16[768,128]{1,0:T(8,128)(2,1)S(1)} %get-tuple-element.64), channel_id=1, source_target_pairs={{0,2},{2,0},{1,3},{3,1},{4,6},{6,4},{5,7},{7,5},{8,10},{10,8},{9,1... | collective-permute-start | bytes 589832 | tf_op jit(solution)/shard_map/ppermute | solution.py:196
  35.1 9.7 %collective-permute-start.10 = (bf16[1,128,1536]{2,1,0:T(8,128)(2,1)S(1)}, bf16[1,128,1536]{2,1,0:T(8,128)(2,1)S(1)}, u32[]{:S(2)}, u32[]{:S(2)}) collective-permute-start(bf16[1,128,1536]{2,1,0:T(8,128)(2,1)S(1)} %bitcast.47), channel_id=1, source_target_pairs={{0,4},{4,0},{1,5},{5,1},{2,6},{6,2},{3,7},{7,3},{8,12},{12,8},{9,1... | collective-permute-start | bytes 1179656 | tf_op jit(solution)/shard_map/ppermute | solution.py:196
  35.8 4.1 %collective-permute-start.8 = (bf16[768,128]{1,0:T(8,128)(2,1)S(1)}, bf16[768,128]{1,0:T(8,128)(2,1)S(1)}, u32[]{:S(2)}, u32[]{:S(2)}) collective-permute-start(bf16[768,128]{1,0:T(8,128)(2,1)S(1)} %get-tuple-element.63.refs_4_), channel_id=1, source_target_pairs={{0,1},{1,0},{2,3},{3,2},{4,5},{5,4},{6,7},{7,6},{8,9},{9,8},{10,11... | collective-permute-start | bytes 589832 | tf_op jit(solution)/shard_map/ppermute | solution.py:196
  39.8 1.5 %collective-permute-start.9 = (bf16[768,128]{1,0:T(8,128)(2,1)S(1)}, bf16[768,128]{1,0:T(8,128)(2,1)S(1)}, u32[]{:S(2)}, u32[]{:S(2)}) collective-permute-start(bf16[768,128]{1,0:T(8,128)(2,1)S(1)} %shard_map.91.refs_5_), channel_id=1, source_target_pairs={{0,1},{1,0},{2,3},{3,2},{4,5},{5,4},{6,7},{7,6},{8,9},{9,8},{10,11... | collective-permute-start | bytes 589832 | tf_op jit(solution)/shard_map/ppermute | solution.py:196
  44.8 37.4 %copy-start.18 = (bf16[1,128,1536]{2,1,0:T(8,128)(2,1)}, bf16[1,128,1536]{2,1,0:T(8,128)(2,1)S(1)}, u32[]{:S(2)}) copy-start(bf16[1,128,1536]{2,1,0:T(8,128)(2,1)S(1)} %collective-permute-done.10.refs_3_) | copy-start | bytes 1179652
  44.8 2.3 %collective-permute-start.11 = (bf16[2,2,768,128]{3,2,1,0:T(8,128)(2,1)S(1)}, bf16[2,2,768,128]{3,2,1,0:T(8,128)(2,1)S(1)}, u32[]{:S(2)}, u32[]{:S(2)}) collective-permute-start(bf16[2,2,768,128]{3,2,1,0:T(8,128)(2,1)S(1)} %bitcast.38), channel_id=1, source_target_pairs={{0,1},{1,0},{2,3},{3,2},{4,5},{5,4},{6,7},{7,6},{8,9},{9,8},{10,11... | collective-permute-start | bytes 2359304 | tf_op jit(solution)/shard_map/ppermute | solution.py:196
  44.8 12.0 %collective-permute-start.15 = (bf16[1,128,1536]{2,1,0:T(8,128)(2,1)S(1)}, bf16[1,128,1536]{2,1,0:T(8,128)(2,1)S(1)}, u32[]{:S(2)}, u32[]{:S(2)}) collective-permute-start(bf16[1,128,1536]{2,1,0:T(8,128)(2,1)S(1)} %bitcast.43), channel_id=1, source_target_pairs={{0,4},{4,0},{1,5},{5,1},{2,6},{6,2},{3,7},{7,3},{8,12},{12,8},{9,1... | collective-permute-start | bytes 1179656 | tf_op jit(solution)/shard_map/ppermute | solution.py:196
  47.2 7.8 %collective-permute-start.13 = (bf16[768,128]{1,0:T(8,128)(2,1)S(1)}, bf16[768,128]{1,0:T(8,128)(2,1)S(1)}, u32[]{:S(2)}, u32[]{:S(2)}) collective-permute-start(bf16[768,128]{1,0:T(8,128)(2,1)S(1)} %get-tuple-element.72), channel_id=1, source_target_pairs={{0,2},{2,0},{1,3},{3,1},{4,6},{6,4},{5,7},{7,5},{8,10},{10,8},{9,1... | collective-permute-start | bytes 589832 | tf_op jit(solution)/shard_map/ppermute | solution.py:196
  48.3 14.4 %collective-permute-start.12 = (bf16[1,128,1536]{2,1,0:T(8,128)(2,1)S(1)}, bf16[1,128,1536]{2,1,0:T(8,128)(2,1)S(1)}, u32[]{:S(2)}, u32[]{:S(2)}) collective-permute-start(bf16[1,128,1536]{2,1,0:T(8,128)(2,1)S(1)} %bitcast.44), channel_id=1, source_target_pairs={{0,2},{2,0},{1,3},{3,1},{4,6},{6,4},{5,7},{7,5},{8,10},{10,8},{9,1... | collective-permute-start | bytes 1179656 | tf_op jit(solution)/shard_map/ppermute | solution.py:196
  55.1 7.6 %collective-permute-start.14 = (bf16[768,128]{1,0:T(8,128)(2,1)S(1)}, bf16[768,128]{1,0:T(8,128)(2,1)S(1)}, u32[]{:S(2)}, u32[]{:S(2)}) collective-permute-start(bf16[768,128]{1,0:T(8,128)(2,1)S(1)} %shard_map.95.refs_0_), channel_id=1, source_target_pairs={{0,4},{4,0},{1,5},{5,1},{2,6},{6,2},{3,7},{7,3},{8,12},{12,8},{9,1... | collective-permute-start | bytes 589832 | tf_op jit(solution)/shard_map/ppermute | solution.py:196
  56.8 33.5 %copy-start.19 = (bf16[1,128,1536]{2,1,0:T(8,128)(2,1)}, bf16[1,128,1536]{2,1,0:T(8,128)(2,1)S(1)}, u32[]{:S(2)}) copy-start(bf16[1,128,1536]{2,1,0:T(8,128)(2,1)S(1)} %collective-permute-done.15.refs_2_) | copy-start | bytes 1179652
  62.6 27.7 %copy-start.20 = (bf16[1,128,1536]{2,1,0:T(8,128)(2,1)}, bf16[1,128,1536]{2,1,0:T(8,128)(2,1)S(1)}, u32[]{:S(2)}) copy-start(bf16[1,128,1536]{2,1,0:T(8,128)(2,1)S(1)} %collective-permute-done.12.refs_6_) | copy-start | bytes 1179652
  62.7 12.8 %collective-permute-start.17 = (bf16[1,128,1536]{2,1,0:T(8,128)(2,1)S(1)}, bf16[1,128,1536]{2,1,0:T(8,128)(2,1)S(1)}, u32[]{:S(2)}, u32[]{:S(2)}) collective-permute-start(bf16[1,128,1536]{2,1,0:T(8,128)(2,1)S(1)} %collective-permute-done.10.refs_3_), channel_id=1, source_target_pairs={{0,2},{2,0},{1,3},{3,1},{4,6},{6,4},{5,7},{7,5},{8,10},{10,8},{9,1... | collective-permute-start | bytes 1179656 | tf_op jit(solution)/shard_map/ppermute | solution.py:196
  63.8 11.7 %collective-permute-start.16 = (bf16[768,128]{1,0:T(8,128)(2,1)S(1)}, bf16[768,128]{1,0:T(8,128)(2,1)S(1)}, u32[]{:S(2)}, u32[]{:S(2)}) collective-permute-start(bf16[768,128]{1,0:T(8,128)(2,1)S(1)} %get-tuple-element.77), channel_id=1, source_target_pairs={{0,8},{8,0},{1,9},{9,1},{2,10},{10,2},{3,11},{11,3},{4,12},{12,4},... | collective-permute-start | bytes 589832 | tf_op jit(solution)/shard_map/ppermute | solution.py:196
  67.2 14.4 %collective-permute-start.23 = (bf16[1,128,1536]{2,1,0:T(8,128)(2,1)S(1)}, bf16[1,128,1536]{2,1,0:T(8,128)(2,1)S(1)}, u32[]{:S(2)}, u32[]{:S(2)}) collective-permute-start(bf16[1,128,1536]{2,1,0:T(8,128)(2,1)S(1)} %bitcast.45), channel_id=1, source_target_pairs={{0,1},{1,0},{2,3},{3,2},{4,5},{5,4},{6,7},{7,6},{8,9},{9,8},{10,11... | collective-permute-start | bytes 1179656 | tf_op jit(solution)/shard_map/ppermute | solution.py:196
  67.2 10.4 %collective-permute-start.20 = (bf16[768,128]{1,0:T(8,128)(2,1)S(1)}, bf16[768,128]{1,0:T(8,128)(2,1)S(1)}, u32[]{:S(2)}, u32[]{:S(2)}) collective-permute-start(bf16[768,128]{1,0:T(8,128)(2,1)S(1)} %get-tuple-element.85.refs_0_), channel_id=1, source_target_pairs={{0,2},{2,0},{1,3},{3,1},{4,6},{6,4},{5,7},{7,5},{8,10},{10,8},{9,1... | collective-permute-start | bytes 589832 | tf_op jit(solution)/shard_map/ppermute | solution.py:196
  68.2 14.1 %collective-permute-start.24 = (bf16[1,128,1536]{2,1,0:T(8,128)(2,1)S(1)}, bf16[1,128,1536]{2,1,0:T(8,128)(2,1)S(1)}, u32[]{:S(2)}, u32[]{:S(2)}) collective-permute-start(bf16[1,128,1536]{2,1,0:T(8,128)(2,1)S(1)} %bitcast.48), channel_id=1, source_target_pairs={{0,1},{1,0},{2,3},{3,2},{4,5},{5,4},{6,7},{7,6},{8,9},{9,8},{10,11... | collective-permute-start | bytes 1179656 | tf_op jit(solution)/shard_map/ppermute | solution.py:196
  75.6 5.9 %collective-permute-start.19 = (bf16[768,128]{1,0:T(8,128)(2,1)S(1)}, bf16[768,128]{1,0:T(8,128)(2,1)S(1)}, u32[]{:S(2)}, u32[]{:S(2)}) collective-permute-start(bf16[768,128]{1,0:T(8,128)(2,1)S(1)} %get-tuple-element.81), channel_id=1, source_target_pairs={{0,2},{2,0},{1,3},{3,1},{4,6},{6,4},{5,7},{7,5},{8,10},{10,8},{9,1... | collective-permute-start | bytes 589832 | tf_op jit(solution)/shard_map/ppermute | solution.py:196
  76.7 5.7 %collective-permute-start.27 = (bf16[1,128,1536]{2,1,0:T(8,128)(2,1)S(1)}, bf16[1,128,1536]{2,1,0:T(8,128)(2,1)S(1)}, u32[]{:S(2)}, u32[]{:S(2)}) collective-permute-start(bf16[1,128,1536]{2,1,0:T(8,128)(2,1)S(1)} %collective-permute-done.6.refs_4_), channel_id=1, source_target_pairs={{0,1},{1,0},{2,3},{3,2},{4,5},{5,4},{6,7},{7,6},{8,9},{9,8},{10,11... | collective-permute-start | bytes 1179656 | tf_op jit(solution)/shard_map/ppermute | solution.py:196
  77.6 10.6 %collective-permute-start.18 = (bf16[1,128,1536]{2,1,0:T(8,128)(2,1)S(1)}, bf16[1,128,1536]{2,1,0:T(8,128)(2,1)S(1)}, u32[]{:S(2)}, u32[]{:S(2)}) collective-permute-start(bf16[1,128,1536]{2,1,0:T(8,128)(2,1)S(1)} %collective-permute-done.12.refs_6_), channel_id=1, source_target_pairs={{0,4},{4,0},{1,5},{5,1},{2,6},{6,2},{3,7},{7,3},{8,12},{12,8},{9,1... | collective-permute-start | bytes 1179656 | tf_op jit(solution)/shard_map/ppermute | solution.py:196
  81.6 1.4 collective-permute-start.21
  81.7 1.6 %collective-permute-start.22 = (bf16[768,128]{1,0:T(8,128)(2,1)S(1)}, bf16[768,128]{1,0:T(8,128)(2,1)S(1)}, u32[]{:S(2)}, u32[]{:S(2)}) collective-permute-start(bf16[768,128]{1,0:T(8,128)(2,1)S(1)} %shard_map.98.refs_5_.refs_7_), channel_id=1, source_target_pairs={{0,1},{1,0},{2,3},{3,2},{4,5},{5,4},{6,7},{7,6},{8,9},{9,8},{10,11... | collective-permute-start | bytes 589832 | tf_op jit(solution)/shard_map/ppermute | solution.py:196
  82.2 8.2 %collective-permute-start.26 = (bf16[1,128,1536]{2,1,0:T(8,128)(2,1)S(1)}, bf16[1,128,1536]{2,1,0:T(8,128)(2,1)S(1)}, u32[]{:S(2)}, u32[]{:S(2)}) collective-permute-start(bf16[1,128,1536]{2,1,0:T(8,128)(2,1)S(1)} %collective-permute-done.10.refs_3_), channel_id=1, source_target_pairs={{0,1},{1,0},{2,3},{3,2},{4,5},{5,4},{6,7},{7,6},{8,9},{9,8},{10,11... | collective-permute-start | bytes 1179656 | tf_op jit(solution)/shard_map/ppermute | solution.py:196
  82.3 8.1 %collective-permute-start.25 = (bf16[1,128,1536]{2,1,0:T(8,128)(2,1)S(1)}, bf16[1,128,1536]{2,1,0:T(8,128)(2,1)S(1)}, u32[]{:S(2)}, u32[]{:S(2)}) collective-permute-start(bf16[1,128,1536]{2,1,0:T(8,128)(2,1)S(1)} %collective-permute-done.15.refs_2_), channel_id=1, source_target_pairs={{0,1},{1,0},{2,3},{3,2},{4,5},{5,4},{6,7},{7,6},{8,9},{9,8},{10,11... | collective-permute-start | bytes 1179656 | tf_op jit(solution)/shard_map/ppermute | solution.py:196
  83.0 7.5 %collective-permute-start.29 = (bf16[1,128,1536]{2,1,0:T(8,128)(2,1)S(1)}, bf16[1,128,1536]{2,1,0:T(8,128)(2,1)S(1)}, u32[]{:S(2)}, u32[]{:S(2)}) collective-permute-start(bf16[1,128,1536]{2,1,0:T(8,128)(2,1)S(1)} %collective-permute-done.12.refs_6_), channel_id=1, source_target_pairs={{0,1},{1,0},{2,3},{3,2},{4,5},{5,4},{6,7},{7,6},{8,9},{9,8},{10,11... | collective-permute-start | bytes 1179656 | tf_op jit(solution)/shard_map/ppermute | solution.py:196
  83.3 7.2 %collective-permute-start.28 = (bf16[1,128,1536]{2,1,0:T(8,128)(2,1)S(1)}, bf16[1,128,1536]{2,1,0:T(8,128)(2,1)S(1)}, u32[]{:S(2)}, u32[]{:S(2)}) collective-permute-start(bf16[1,128,1536]{2,1,0:T(8,128)(2,1)S(1)} %collective-permute-done.17.refs_5_), channel_id=1, source_target_pairs={{0,1},{1,0},{2,3},{3,2},{4,5},{5,4},{6,7},{7,6},{8,9},{9,8},{10,11... | collective-permute-start | bytes 1179656 | tf_op jit(solution)/shard_map/ppermute | solution.py:196
  88.2 2.3 %collective-permute-start.30 = (bf16[1,128,1536]{2,1,0:T(8,128)(2,1)S(1)}, bf16[1,128,1536]{2,1,0:T(8,128)(2,1)S(1)}, u32[]{:S(2)}, u32[]{:S(2)}) collective-permute-start(bf16[1,128,1536]{2,1,0:T(8,128)(2,1)S(1)} %collective-permute-done.18.refs_7_), channel_id=1, source_target_pairs={{0,1},{1,0},{2,3},{3,2},{4,5},{5,4},{6,7},{7,6},{8,9},{9,8},{10,11... | collective-permute-start | bytes 1179656 | tf_op jit(solution)/shard_map/ppermute | solution.py:196
  90.4 17.3 %copy-start.12 = (bf16[2,8,2,96,128]{4,3,2,1,0:T(8,128)(2,1)}, bf16[2,8,2,96,128]{4,3,2,1,0:T(8,128)(2,1)S(1)}, u32[]{:S(2)}) copy-start(bf16[2,8,2,96,128]{4,3,2,1,0:T(8,128)(2,1)S(1)} %get-tuple-element.86) | copy-start | bytes 2359300
  90.4 17.3 %copy-start.26 = (bf16[1,128,1536]{2,1,0:T(8,128)(2,1)}, bf16[1,128,1536]{2,1,0:T(8,128)(2,1)S(1)}, u32[]{:S(2)}) copy-start(bf16[1,128,1536]{2,1,0:T(8,128)(2,1)S(1)} %collective-permute-done.26.refs_11_) | copy-start | bytes 1179652
  90.5 17.3 %copy-start.27 = (bf16[1,128,1536]{2,1,0:T(8,128)(2,1)}, bf16[1,128,1536]{2,1,0:T(8,128)(2,1)S(1)}, u32[]{:S(2)}) copy-start(bf16[1,128,1536]{2,1,0:T(8,128)(2,1)S(1)} %collective-permute-done.25.refs_10_) | copy-start | bytes 1179652
  90.5 17.3 %copy-start.28 = (bf16[1,128,1536]{2,1,0:T(8,128)(2,1)}, bf16[1,128,1536]{2,1,0:T(8,128)(2,1)S(1)}, u32[]{:S(2)}) copy-start(bf16[1,128,1536]{2,1,0:T(8,128)(2,1)S(1)} %collective-permute-done.29.refs_14_) | copy-start | bytes 1179652
  90.5 17.3 %copy-start.29 = (bf16[1,128,1536]{2,1,0:T(8,128)(2,1)}, bf16[1,128,1536]{2,1,0:T(8,128)(2,1)S(1)}, u32[]{:S(2)}) copy-start(bf16[1,128,1536]{2,1,0:T(8,128)(2,1)S(1)} %collective-permute-done.28.refs_13_) | copy-start | bytes 1179652
  90.5 17.3 %copy-start.30 = (bf16[1,128,1536]{2,1,0:T(8,128)(2,1)}, bf16[1,128,1536]{2,1,0:T(8,128)(2,1)S(1)}, u32[]{:S(2)}) copy-start(bf16[1,128,1536]{2,1,0:T(8,128)(2,1)S(1)} %collective-permute-done.30.refs_15_) | copy-start | bytes 1179652
  107.8 22.4 %all-to-all-start = ((bf16[16,192,128]{2,1,0:T(8,128)(2,1)}), bf16[16,192,128]{2,1,0:T(8,128)(2,1)}, u32[]{:S(2)}, u32[]{:S(2)}) async-start(bf16[16,192,128]{2,1,0:T(8,128)(2,1)} %bitcast.37), calls=%async_computation | async-start | bytes 1572864 | tf_op jit(solution)/shard_map/all_to_all | solution.py:500
  116.9 23.9 %collective-permute-start.31 = (bf16[96,1536]{1,0:T(8,128)(2,1)}, bf16[96,1536]{1,0:T(8,128)(2,1)}, u32[]{:S(2)}, u32[]{:S(2)}) collective-permute-start(bf16[96,1536]{1,0:T(8,128)(2,1)} %bitcast.55), channel_id=1, source_target_pairs={{0,8},{8,0},{1,9},{9,1},{2,10},{10,2},{3,11},{11,3},{4,12},{12,4},... | collective-permute-start | bytes 884744 | tf_op jit(solution)/shard_map/ppermute | solution.py:503
  134.9 13.4 %collective-permute-start.32 = (bf16[96,1536]{1,0:T(8,128)(2,1)}, bf16[96,1536]{1,0:T(8,128)(2,1)S(1)}, u32[]{:S(2)}, u32[]{:S(2)}) collective-permute-start(bf16[96,1536]{1,0:T(8,128)(2,1)} %bitcast.56), channel_id=1, source_target_pairs={{0,8},{8,0},{1,9},{9,1},{2,10},{10,2},{3,11},{11,3},{4,12},{12,4},... | collective-permute-start | bytes 884744 | tf_op jit(solution)/shard_map/ppermute | solution.py:503
  (19 other events, 118.1 us)

commit v8 on v7

--- a/solution.py
+++ b/solution.py
@@ -499,26 +499,27 @@
         part = turned[cut].reshape(sequences * 8, halves * rows, tokens)
         part = lax.all_to_all(part, ("dp", layer, side, core), 0, 0, tiled=True)
         total, sent = weight_part(sources_of, bits, after(part, done), held, halves)
+        if not sums:
+            query_grad, value_grad = by_heads(
+                functools.partial(other_grads_head, backward.counts),
+                [
+                    ("held", query),
+                    ("held", key),
+                    ("held", value),
+                    ("held", after(grad_output, sent)),
+                    ("state", state_in),
+                    *backward.operands,
+                ],
+                [("row", BF16), ("row", BF16)],
+                6,
+                bits,
+            )
         for turn in range(1, halves):
             moved = lax.ppermute(sent[turn - 1], spans, [(i, (i + turn) % halves) for i in range(halves)])
             total += moved.astype(F32)
-        done = sent
+        done = value_grad if not sums else sent
         sums.append(total)
     weight_grad = jnp.concatenate(sums) * (sequences * places * tokens) ** (-0.5)
-    query_grad, value_grad = by_heads(
-        functools.partial(other_grads_head, backward.counts),
-        [
-            ("held", query),
-            ("held", key),
-            ("held", value),
-            ("held", after(grad_output, done)),
-            ("state", state_in),
-            *backward.operands,
-        ],
-        [("row", BF16), ("row", BF16)],
-        6,
-        bits,
-    )
     return (query_grad[None], key_grad[None], value_grad[None], weight_grad)
 
 

time: 150 us -> 150 us (level)
    all_to_all x1, waiting for transfers between devices: 9.87 us -> 3.78 us  [shards(): part = lax.all_to_all(part, ('dp', layer, side, core), 0, 0, tiled=True)]
    ppermute x2, waiting for transfers between devices: 6.41 us -> 12.4 us  [shards(): lax.ppermute(sent[turn - 1], spans, [(i, (i + turn) % halves) for i in ra...]
where the time goes in v8:
time: 150 us; the launch traced here: 149 us
  waiting for transfers between devices  58.1 us (39%)
  starting transfers between devices  37.1 us (25%)
  Pallas kernels  31.2 us (21%)
  blocking collectives  17.2 us (11%)
  local copies, waits for them, and re-layouts  2.4 us (2%)
  other arithmetic  2.23 us (1%)
    ppermute x31, waiting for transfers between devices, swap(): return lax.ppermute(array, axis, [(0, 1), (1, 0)])  41.9 us
    ppermute x31, starting transfers between devices, swap(): return lax.ppermute(array, axis, [(0, 1), (1, 0)])  29.1 us
    pallas_call x6, Pallas kernels, by_heads(): pl.pallas_call(body, in_specs=places[:count], out_specs=places[count:], o...  19.1 us
    all_to_all x1, blocking collectives, shards(): part = lax.all_to_all(part, ('dp', layer, side, core), 0, 0, tiled=True)  17.2 us
    ppermute x2, waiting for transfers between devices, shards(): lax.ppermute(sent[turn - 1], spans, [(i, (i + turn) % halves) for i in ra...  12.4 us
    pallas_call x2, Pallas kernels, weight_part(): pl.pallas_call(functools.partial(weight_kernel, sources_of, bits), in_spe...  9.36 us
    all_to_all x1, starting transfers between devices, shards(): part = lax.all_to_all(part, ('dp', layer, side, core), 0, 0, tiled=True)  4.47 us
    all_to_all x1, waiting for transfers between devices, shards(): part = lax.all_to_all(part, ('dp', layer, side, core), 0, 0, tiled=True)  3.78 us
  transfers between devices with their start and end apart: 34, of which 20 were waited for; matrix products, arithmetic and copies ran while one was open for 1% of the time, Pallas kernels for 20%

profile of v8, /device:TPU:0, one launch (start us, length us, event | category | flops | bytes accessed | tf_op | source)
XLA Modules:
  0.0 149.4 jit_solution(15850124916155955630)
XLA Ops:
  0.6 1.1 copy-done
  1.8 1.1 copy-done.2
  2.9 0.8 shard_map.84
  4.2 1.9 %collective-permute-done.refs_1_ = bf16[2,2,768,128]{3,2,1,0:T(8,128)(2,1)S(1)} collective-permute-done((bf16[2,2,768,128]{3,2,1,0:T(8,128)(2,1)S(1)}, bf16[2,2,768,128]{3,2,1,0:T(8,128)(2,1)S(1)}, u32[]{:S(2)}, u32[]{:S(2)}) %collective-permute-start) | collective-permute-done | bytes 786464 | tf_op jit(solution)/shard_map/ppermute | solution.py:196
  6.2 2.9 %collective-permute-start.1 = (bf16[768,128]{1,0:T(8,128)(2,1)S(1)}, bf16[768,128]{1,0:T(8,128)(2,1)S(1)}, u32[]{:S(2)}, u32[]{:S(2)}) collective-permute-start(bf16[768,128]{1,0:T(8,128)(2,1)S(1)} %get-tuple-element.53), channel_id=1, source_target_pairs={{0,2},{2,0},{1,3},{3,1},{4,6},{6,4},{5,7},{7,5},{8,10},{10,8},{9,1... | collective-permute-start | bytes 589832 | tf_op jit(solution)/shard_map/ppermute | solution.py:196
  9.1 1.9 %shard_map.87 = (bf16[128,1536]{1,0:T(8,128)(2,1)}, bf16[128,1536]{1,0:T(8,128)(2,1)}) custom-call(bf16[128,3072]{1,0:T(8,128)(2,1)} %bitcast.51), custom_call_target="tpu_custom_call" | custom-call | bytes 1572864 | tf_op jit(solution)/shard_map/pallas_call | solution.py:317
  11.0 1.5 %collective-permute-start.4 = (bf16[128,1536]{1,0:T(8,128)(2,1)}, bf16[128,1536]{1,0:T(8,128)(2,1)S(1)}, u32[]{:S(2)}, u32[]{:S(2)}) collective-permute-start(bf16[128,1536]{1,0:T(8,128)(2,1)} %get-tuple-element.56), channel_id=1, source_target_pairs={{0,16},{16,0},{1,17},{17,1},{2,18},{18,2},{3,19},{19,3},{4,20},{20... | collective-permute-start | bytes 1179656 | tf_op jit(solution)/shard_map/ppermute | solution.py:196
  12.6 1.8 %collective-permute-done.1.refs_1_.refs_0_ = bf16[768,128]{1,0:T(8,128)(2,1)S(1)} collective-permute-done((bf16[768,128]{1,0:T(8,128)(2,1)S(1)}, bf16[768,128]{1,0:T(8,128)(2,1)S(1)}, u32[]{:S(2)}, u32[]{:S(2)}) %collective-permute-start.1) | collective-permute-done | bytes 196640 | tf_op jit(solution)/shard_map/ppermute | solution.py:196
  14.4 1.7 %collective-permute-start.3 = (bf16[768,128]{1,0:T(8,128)(2,1)S(1)}, bf16[768,128]{1,0:T(8,128)(2,1)S(1)}, u32[]{:S(2)}, u32[]{:S(2)}) collective-permute-start(bf16[768,128]{1,0:T(8,128)(2,1)S(1)} %get-tuple-element.54.refs_0_), channel_id=1, source_target_pairs={{0,2},{2,0},{1,3},{3,1},{4,6},{6,4},{5,7},{7,5},{8,10},{10,8},{9,1... | collective-permute-start | bytes 589832 | tf_op jit(solution)/shard_map/ppermute | solution.py:196
  16.1 1.6 %collective-permute-start.2 = (bf16[768,128]{1,0:T(8,128)(2,1)S(1)}, bf16[768,128]{1,0:T(8,128)(2,1)S(1)}, u32[]{:S(2)}, u32[]{:S(2)}) collective-permute-start(bf16[768,128]{1,0:T(8,128)(2,1)S(1)} %shard_map.86.refs_0_), channel_id=1, source_target_pairs={{0,4},{4,0},{1,5},{5,1},{2,6},{6,2},{3,7},{7,3},{8,12},{12,8},{9,1... | collective-permute-start | bytes 589832 | tf_op jit(solution)/shard_map/ppermute | solution.py:196
  17.8 3.0 %collective-permute-done.3.refs_1_ = bf16[768,128]{1,0:T(8,128)(2,1)S(1)} collective-permute-done((bf16[768,128]{1,0:T(8,128)(2,1)S(1)}, bf16[768,128]{1,0:T(8,128)(2,1)S(1)}, u32[]{:S(2)}, u32[]{:S(2)}) %collective-permute-start.3) | collective-permute-done | bytes 196640 | tf_op jit(solution)/shard_map/ppermute | solution.py:196
  20.8 1.3 collective-permute-done.2.refs_1_
  22.8 2.8 %collective-permute-start.5 = (bf16[768,128]{1,0:T(8,128)(2,1)S(1)}, bf16[768,128]{1,0:T(8,128)(2,1)S(1)}, u32[]{:S(2)}, u32[]{:S(2)}) collective-permute-start(bf16[768,128]{1,0:T(8,128)(2,1)S(1)} %get-tuple-element.58), channel_id=1, source_target_pairs={{0,8},{8,0},{1,9},{9,1},{2,10},{10,2},{3,11},{11,3},{4,12},{12,4},... | collective-permute-start | bytes 589832 | tf_op jit(solution)/shard_map/ppermute | solution.py:196
  25.6 3.9 %shard_map.89.refs_1_ = f32[128,3072]{1,0:T(8,128)S(1)} custom-call(bf16[128,3072]{1,0:T(8,128)(2,1)S(1)} %bitcast.27, bf16[128,3072]{1,0:T(8,128)(2,1)S(1)} %bitcast.24, bf16[128,3072]{1,0:T(8,128)(2,1)S(1)} %bitcast.19), custom_call_target="tpu_custom_call" | custom-call | flops 201326592 | bytes 3145728 | tf_op jit(solution)/shard_map/pallas_call | solution.py:177
  29.5 4.4 %collective-permute-done.5.refs_1_ = bf16[768,128]{1,0:T(8,128)(2,1)S(1)} collective-permute-done((bf16[768,128]{1,0:T(8,128)(2,1)S(1)}, bf16[768,128]{1,0:T(8,128)(2,1)S(1)}, u32[]{:S(2)}, u32[]{:S(2)}) %collective-permute-start.5) | collective-permute-done | bytes 196640 | tf_op jit(solution)/shard_map/ppermute | solution.py:196
  34.0 1.1 collective-permute-start.7
  35.1 0.7 collective-permute-start.10
  35.8 3.9 %collective-permute-done.7.refs_0_ = bf16[768,128]{1,0:T(8,128)(2,1)S(1)} collective-permute-done((bf16[768,128]{1,0:T(8,128)(2,1)S(1)}, bf16[768,128]{1,0:T(8,128)(2,1)S(1)}, u32[]{:S(2)}, u32[]{:S(2)}) %collective-permute-start.7) | collective-permute-done | bytes 196640 | tf_op jit(solution)/shard_map/ppermute | solution.py:196
  39.9 1.4 collective-permute-done.9.refs_7_
  41.4 2.8 %shard_map.92 = (bf16[128,3072]{1,0:T(8,128)(2,1)S(1)}, bf16[3072,128]{1,0:T(8,128)(2,1)S(1)}, bf16[3072,128]{1,0:T(8,128)(2,1)S(1)}) custom-call(bf16[128,3072]{1,0:T(8,128)(2,1)S(1)} %bitcast.28, f32[128,3072]{1,0:T(8,128)S(1)} %shard_map.89.refs_1_, bf16[128,3072]{1,0:T(8,128)(2,1)S(1)} %bitcast.36, bf16[3072,128]{1,0:T(8,128)(2,1)S(1)} %bitcast.33, ...), custom_call_target="tpu_custom_call" | custom-call | flops 201326592 | bytes 8650752 | tf_op jit(solution)/shard_map/pallas_call | solution.py:177
  44.2 0.6 collective-permute-done.10.refs_3_
  44.8 1.8 %collective-permute-start.15 = (bf16[1,128,1536]{2,1,0:T(8,128)(2,1)S(1)}, bf16[1,128,1536]{2,1,0:T(8,128)(2,1)S(1)}, u32[]{:S(2)}, u32[]{:S(2)}) collective-permute-start(bf16[1,128,1536]{2,1,0:T(8,128)(2,1)S(1)} %bitcast.43), channel_id=1, source_target_pairs={{0,4},{4,0},{1,5},{5,1},{2,6},{6,2},{3,7},{7,3},{8,12},{12,8},{9,1... | collective-permute-start | bytes 1179656 | tf_op jit(solution)/shard_map/ppermute | solution.py:196
  47.2 1.1 collective-permute-start.13
  48.3 1.0 collective-permute-start.12
  49.3 3.9 %shard_map.94.refs_2_ = f32[128,3072]{1,0:T(8,128)S(1)} custom-call(bf16[128,3072]{1,0:T(8,128)(2,1)S(1)} %bitcast.29, bf16[128,3072]{1,0:T(8,128)(2,1)S(1)} %bitcast.20, bf16[128,3072]{1,0:T(8,128)(2,1)S(1)} %get-tuple-element.90.refs_2_.refs_3_), custom_call_target="tpu_custom_call" | custom-call | flops 201326592 | bytes 3145728 | tf_op jit(solution)/shard_map/pallas_call | solution.py:177
  53.2 1.8 %collective-permute-done.13.refs_1_.refs_0_ = bf16[768,128]{1,0:T(8,128)(2,1)S(1)} collective-permute-done((bf16[768,128]{1,0:T(8,128)(2,1)S(1)}, bf16[768,128]{1,0:T(8,128)(2,1)S(1)}, u32[]{:S(2)}, u32[]{:S(2)}) %collective-permute-start.13) | collective-permute-done | bytes 196640 | tf_op jit(solution)/shard_map/ppermute | solution.py:196
  55.1 1.8 %collective-permute-start.14 = (bf16[768,128]{1,0:T(8,128)(2,1)S(1)}, bf16[768,128]{1,0:T(8,128)(2,1)S(1)}, u32[]{:S(2)}, u32[]{:S(2)}) collective-permute-start(bf16[768,128]{1,0:T(8,128)(2,1)S(1)} %shard_map.95.refs_0_), channel_id=1, source_target_pairs={{0,4},{4,0},{1,5},{5,1},{2,6},{6,2},{3,7},{7,3},{8,12},{12,8},{9,1... | collective-permute-start | bytes 589832 | tf_op jit(solution)/shard_map/ppermute | solution.py:196
  56.8 5.8 %collective-permute-done.12.refs_6_ = bf16[1,128,1536]{2,1,0:T(8,128)(2,1)S(1)} collective-permute-done((bf16[1,128,1536]{2,1,0:T(8,128)(2,1)S(1)}, bf16[1,128,1536]{2,1,0:T(8,128)(2,1)S(1)}, u32[]{:S(2)}, u32[]{:S(2)}) %collective-permute-start.12) | collective-permute-done | bytes 393248 | tf_op jit(solution)/shard_map/ppermute | solution.py:196
  62.7 1.1 collective-permute-start.17
  63.8 3.4 %collective-permute-start.16 = (bf16[768,128]{1,0:T(8,128)(2,1)S(1)}, bf16[768,128]{1,0:T(8,128)(2,1)S(1)}, u32[]{:S(2)}, u32[]{:S(2)}) collective-permute-start(bf16[768,128]{1,0:T(8,128)(2,1)S(1)} %get-tuple-element.77), channel_id=1, source_target_pairs={{0,8},{8,0},{1,9},{9,1},{2,10},{10,2},{3,11},{11,3},{4,12},{12,4},... | collective-permute-start | bytes 589832 | tf_op jit(solution)/shard_map/ppermute | solution.py:196
  67.2 1.0 collective-permute-start.20
  68.4 7.1 %collective-permute-done.16.refs_1_ = bf16[768,128]{1,0:T(8,128)(2,1)S(1)} collective-permute-done((bf16[768,128]{1,0:T(8,128)(2,1)S(1)}, bf16[768,128]{1,0:T(8,128)(2,1)S(1)}, u32[]{:S(2)}, u32[]{:S(2)}) %collective-permute-start.16) | collective-permute-done | bytes 196640 | tf_op jit(solution)/shard_map/ppermute | solution.py:196
  75.6 1.0 collective-permute-start.19
  76.7 0.9 collective-permute-done.20.refs_1_
  77.6 1.5 collective-permute-start.18
  79.0 2.5 %collective-permute-done.19.refs_0_ = bf16[768,128]{1,0:T(8,128)(2,1)S(1)} collective-permute-done((bf16[768,128]{1,0:T(8,128)(2,1)S(1)}, bf16[768,128]{1,0:T(8,128)(2,1)S(1)}, u32[]{:S(2)}, u32[]{:S(2)}) %collective-permute-start.19) | collective-permute-done | bytes 196640 | tf_op jit(solution)/shard_map/ppermute | solution.py:196
  83.7 4.5 %collective-permute-done.18.refs_7_ = bf16[1,128,1536]{2,1,0:T(8,128)(2,1)S(1)} collective-permute-done((bf16[1,128,1536]{2,1,0:T(8,128)(2,1)S(1)}, bf16[1,128,1536]{2,1,0:T(8,128)(2,1)S(1)}, u32[]{:S(2)}, u32[]{:S(2)}) %collective-permute-start.18) | collective-permute-done | bytes 393248 | tf_op jit(solution)/shard_map/ppermute | solution.py:196
  88.2 2.1 %shard_map.99 = (bf16[128,3072]{1,0:T(8,128)(2,1)}, bf16[2,8,2,96,128]{4,3,2,1,0:T(8,128)(2,1)S(1)}, bf16[2,8,2,96,128]{4,3,2,1,0:T(8,128)(2,1)S(1)}) custom-call(bf16[128,3072]{1,0:T(8,128)(2,1)S(1)} %bitcast.25, bf16[128,3072]{1,0:T(8,128)(2,1)S(1)} %bitcast.21, f32[128,3072]{1,0:T(8,128)S(1)} %shard_map.94.refs_2_, bf16[3072,128]{1,0:T(8,128)(2,1)S(1)} %bitcast.31, ...), custom_call_target="tpu_custom_call" | custom-call | flops 100663296 | bytes 8650752 | tf_op jit(solution)/shard_map/pallas_call | solution.py:177
  90.5 17.2 %all_to_all.10.turned_in = bf16[16,192,128]{2,1,0:T(8,128)(2,1)} all-to-all(bf16[16,192,128]{2,1,0:T(8,128)(2,1)S(1)} %bitcast.40), channel_id=1, replica_groups=mesh['dp'=2,'bit3'=2,'bit2'=2,'bit1'=2,'bit0'=2] {'dp','bit2','bit1','bi..., dimensions={0} | all-to-all | bytes 1572864 | tf_op jit(solution)/shard_map/all_to_all | solution.py:500
  107.8 4.5 %all-to-all-start.1 = ((bf16[16,192,128]{2,1,0:T(8,128)(2,1)}), bf16[16,192,128]{2,1,0:T(8,128)(2,1)}, u32[]{:S(2)}, u32[]{:S(2)}) async-start(bf16[16,192,128]{2,1,0:T(8,128)(2,1)} %bitcast.37), calls=%async_computation.1 | async-start | bytes 1572864 | tf_op jit(solution)/shard_map/all_to_all | solution.py:500
  112.3 4.7 %shard_map.100 = (f32[96,1536]{1,0:T(8,128)}, bf16[1,96,1536]{2,1,0:T(8,128)(2,1)}) custom-call(bf16[16,192,128]{2,1,0:T(8,128)(2,1)} %all_to_all.10.turned_in, bf16[1,128,1536]{2,1,0:T(8,128)(2,1)} %bitcast.41, bf16[1,128,1536]{2,1,0:T(8,128)(2,1)} %bitcast.49, bf16[1,128,1536]{2,1,0:T(8,128)(2,1)} %copy-done.19, bf16[1,128,1536]{2,1,0:T(8,128)(2,1)} %copy-done.18, ...), custom_call_target="tpu_custom_call" | custom-call | flops 1207959552 | bytes 8060928 | tf_op jit(solution)/shard_map/pallas_call | solution.py:382
  117.0 3.5 %collective-permute-start.31 = (bf16[96,1536]{1,0:T(8,128)(2,1)}, bf16[96,1536]{1,0:T(8,128)(2,1)}, u32[]{:S(2)}, u32[]{:S(2)}) collective-permute-start(bf16[96,1536]{1,0:T(8,128)(2,1)} %bitcast.55), channel_id=1, source_target_pairs={{0,8},{8,0},{1,9},{9,1},{2,10},{10,2},{3,11},{11,3},{4,12},{12,4},... | collective-permute-start | bytes 884744 | tf_op jit(solution)/shard_map/ppermute | solution.py:518
  120.5 5.7 %shard_map.101 = (bf16[128,3072]{1,0:T(8,128)(2,1)}, bf16[128,3072]{1,0:T(8,128)(2,1)}) custom-call(bf16[128,3072]{1,0:T(8,128)(2,1)S(1)} %bitcast.30, bf16[128,3072]{1,0:T(8,128)(2,1)S(1)} %bitcast.26, bf16[128,3072]{1,0:T(8,128)(2,1)S(1)} %bitcast.22, bf16[128,3072]{1,0:T(8,128)(2,1)S(1)} %copy-done.6, bf16[3072,128]{1,0:T(8,128)(2,1)S(1)} %copy-done.14, ...), custom_call_target="tpu_custom_call" | custom-call | flops 603979776 | bytes 9437184 | tf_op jit(solution)/shard_map/pallas_call | solution.py:177
  126.3 3.8 %all-to-all-done.1.turned_in = bf16[16,192,128]{2,1,0:T(8,128)(2,1)} async-done(((bf16[16,192,128]{2,1,0:T(8,128)(2,1)}), bf16[16,192,128]{2,1,0:T(8,128)(2,1)}, u32[]{:S(2)}, u32[]{:S(2)}) %all-to-all-start.1) | async-done | bytes 786464 | tf_op jit(solution)/shard_map/all_to_all | solution.py:500
  130.0 4.6 %shard_map.102 = (f32[96,1536]{1,0:T(8,128)}, bf16[1,96,1536]{2,1,0:T(8,128)(2,1)}) custom-call(bf16[16,192,128]{2,1,0:T(8,128)(2,1)} %all-to-all-done.1.turned_in, bf16[1,128,1536]{2,1,0:T(8,128)(2,1)} %bitcast.42, bf16[1,128,1536]{2,1,0:T(8,128)(2,1)} %bitcast.50, bf16[1,128,1536]{2,1,0:T(8,128)(2,1)} %copy-done.19, bf16[1,128,1536]{2,1,0:T(8,128)(2,1)} %copy-done.18, ...), custom_call_target="tpu_custom_call" | custom-call | flops 1207959552 | bytes 8060928 | tf_op jit(solution)/shard_map/pallas_call | solution.py:382
  134.8 1.1 convert_add_fusion.1
  135.9 12.4 %collective-permute-done.32 = bf16[96,1536]{1,0:T(8,128)(2,1)S(1)} collective-permute-done((bf16[96,1536]{1,0:T(8,128)(2,1)}, bf16[96,1536]{1,0:T(8,128)(2,1)S(1)}, u32[]{:S(2)}, u32[]{:S(2)}) %collective-permute-start.32) | collective-permute-done | bytes 294944 | tf_op jit(solution)/shard_map/ppermute | solution.py:518
  148.3 1.1 maximum_multiply_fusion
  (109 shorter events, 5.2 us)
Async XLA Ops:
  3.7 2.4 %collective-permute-start = (bf16[2,2,768,128]{3,2,1,0:T(8,128)(2,1)S(1)}, bf16[2,2,768,128]{3,2,1,0:T(8,128)(2,1)S(1)}, u32[]{:S(2)}, u32[]{:S(2)}) collective-permute-start(bf16[2,2,768,128]{3,2,1,0:T(8,128)(2,1)S(1)} %bitcast.34), channel_id=1, source_target_pairs={{0,1},{1,0},{2,3},{3,2},{4,5},{5,4},{6,7},{7,6},{8,9},{9,8},{10,11... | collective-permute-start | bytes 2359304 | tf_op jit(solution)/shard_map/ppermute | solution.py:196
  6.1 19.5 %copy-start.4 = (bf16[1,128,3072]{2,1,0:T(8,128)(2,1)S(1)}, bf16[1,128,3072]{2,1,0:T(8,128)(2,1)}, u32[]{:S(2)}) copy-start(bf16[1,128,3072]{2,1,0:T(8,128)(2,1)} %param.6) | copy-start | bytes 2359300
  6.2 19.4 %copy-start.1 = (bf16[1,128,3072]{2,1,0:T(8,128)(2,1)S(1)}, bf16[1,128,3072]{2,1,0:T(8,128)(2,1)}, u32[]{:S(2)}) copy-start(bf16[1,128,3072]{2,1,0:T(8,128)(2,1)} %param.8) | copy-start | bytes 2359300
  6.2 19.4 %copy-start.3 = (bf16[1,128,3072]{2,1,0:T(8,128)(2,1)S(1)}, bf16[1,128,3072]{2,1,0:T(8,128)(2,1)}, u32[]{:S(2)}) copy-start(bf16[1,128,3072]{2,1,0:T(8,128)(2,1)} %param.7) | copy-start | bytes 2359300
  6.2 8.1 %collective-permute-start.1 = (bf16[768,128]{1,0:T(8,128)(2,1)S(1)}, bf16[768,128]{1,0:T(8,128)(2,1)S(1)}, u32[]{:S(2)}, u32[]{:S(2)}) collective-permute-start(bf16[768,128]{1,0:T(8,128)(2,1)S(1)} %get-tuple-element.53), channel_id=1, source_target_pairs={{0,2},{2,0},{1,3},{3,1},{4,6},{6,4},{5,7},{7,5},{8,10},{10,8},{9,1... | collective-permute-start | bytes 589832 | tf_op jit(solution)/shard_map/ppermute | solution.py:196
  11.0 11.1 %collective-permute-start.4 = (bf16[128,1536]{1,0:T(8,128)(2,1)}, bf16[128,1536]{1,0:T(8,128)(2,1)S(1)}, u32[]{:S(2)}, u32[]{:S(2)}) collective-permute-start(bf16[128,1536]{1,0:T(8,128)(2,1)} %get-tuple-element.56), channel_id=1, source_target_pairs={{0,16},{16,0},{1,17},{17,1},{2,18},{18,2},{3,19},{19,3},{4,20},{20... | collective-permute-start | bytes 1179656 | tf_op jit(solution)/shard_map/ppermute | solution.py:196
  14.4 6.4 %collective-permute-start.3 = (bf16[768,128]{1,0:T(8,128)(2,1)S(1)}, bf16[768,128]{1,0:T(8,128)(2,1)S(1)}, u32[]{:S(2)}, u32[]{:S(2)}) collective-permute-start(bf16[768,128]{1,0:T(8,128)(2,1)S(1)} %get-tuple-element.54.refs_0_), channel_id=1, source_target_pairs={{0,2},{2,0},{1,3},{3,1},{4,6},{6,4},{5,7},{7,5},{8,10},{10,8},{9,1... | collective-permute-start | bytes 589832 | tf_op jit(solution)/shard_map/ppermute | solution.py:196
  16.1 5.9 %collective-permute-start.2 = (bf16[768,128]{1,0:T(8,128)(2,1)S(1)}, bf16[768,128]{1,0:T(8,128)(2,1)S(1)}, u32[]{:S(2)}, u32[]{:S(2)}) collective-permute-start(bf16[768,128]{1,0:T(8,128)(2,1)S(1)} %shard_map.86.refs_0_), channel_id=1, source_target_pairs={{0,4},{4,0},{1,5},{5,1},{2,6},{6,2},{3,7},{7,3},{8,12},{12,8},{9,1... | collective-permute-start | bytes 589832 | tf_op jit(solution)/shard_map/ppermute | solution.py:196
  22.1 46.0 %copy-start.16 = (bf16[128,1536]{1,0:T(8,128)(2,1)}, bf16[128,1536]{1,0:T(8,128)(2,1)S(1)}, u32[]{:S(2)}) copy-start(bf16[128,1536]{1,0:T(8,128)(2,1)S(1)} %collective-permute-done.4) | copy-start | bytes 1179652
  22.2 11.6 %collective-permute-start.6 = (bf16[1,128,1536]{2,1,0:T(8,128)(2,1)S(1)}, bf16[1,128,1536]{2,1,0:T(8,128)(2,1)S(1)}, u32[]{:S(2)}, u32[]{:S(2)}) collective-permute-start(bf16[1,128,1536]{2,1,0:T(8,128)(2,1)S(1)} %bitcast.46), channel_id=1, source_target_pairs={{0,2},{2,0},{1,3},{3,1},{4,6},{6,4},{5,7},{7,5},{8,10},{10,8},{9,1... | collective-permute-start | bytes 1179656 | tf_op jit(solution)/shard_map/ppermute | solution.py:196
  22.8 11.1 %collective-permute-start.5 = (bf16[768,128]{1,0:T(8,128)(2,1)S(1)}, bf16[768,128]{1,0:T(8,128)(2,1)S(1)}, u32[]{:S(2)}, u32[]{:S(2)}) collective-permute-start(bf16[768,128]{1,0:T(8,128)(2,1)S(1)} %get-tuple-element.58), channel_id=1, source_target_pairs={{0,8},{8,0},{1,9},{9,1},{2,10},{10,2},{3,11},{11,3},{4,12},{12,4},... | collective-permute-start | bytes 589832 | tf_op jit(solution)/shard_map/ppermute | solution.py:196
  33.9 42.8 %copy-start.17 = (bf16[1,128,1536]{2,1,0:T(8,128)(2,1)}, bf16[1,128,1536]{2,1,0:T(8,128)(2,1)S(1)}, u32[]{:S(2)}) copy-start(bf16[1,128,1536]{2,1,0:T(8,128)(2,1)S(1)} %collective-permute-done.6.refs_4_) | copy-start | bytes 1179652
  34.0 5.8 %collective-permute-start.7 = (bf16[768,128]{1,0:T(8,128)(2,1)S(1)}, bf16[768,128]{1,0:T(8,128)(2,1)S(1)}, u32[]{:S(2)}, u32[]{:S(2)}) collective-permute-start(bf16[768,128]{1,0:T(8,128)(2,1)S(1)} %get-tuple-element.64), channel_id=1, source_target_pairs={{0,2},{2,0},{1,3},{3,1},{4,6},{6,4},{5,7},{7,5},{8,10},{10,8},{9,1... | collective-permute-start | bytes 589832 | tf_op jit(solution)/shard_map/ppermute | solution.py:196
  35.1 9.7 %collective-permute-start.10 = (bf16[1,128,1536]{2,1,0:T(8,128)(2,1)S(1)}, bf16[1,128,1536]{2,1,0:T(8,128)(2,1)S(1)}, u32[]{:S(2)}, u32[]{:S(2)}) collective-permute-start(bf16[1,128,1536]{2,1,0:T(8,128)(2,1)S(1)} %bitcast.47), channel_id=1, source_target_pairs={{0,4},{4,0},{1,5},{5,1},{2,6},{6,2},{3,7},{7,3},{8,12},{12,8},{9,1... | collective-permute-start | bytes 1179656 | tf_op jit(solution)/shard_map/ppermute | solution.py:196
  35.8 4.1 %collective-permute-start.8 = (bf16[768,128]{1,0:T(8,128)(2,1)S(1)}, bf16[768,128]{1,0:T(8,128)(2,1)S(1)}, u32[]{:S(2)}, u32[]{:S(2)}) collective-permute-start(bf16[768,128]{1,0:T(8,128)(2,1)S(1)} %get-tuple-element.63.refs_4_), channel_id=1, source_target_pairs={{0,1},{1,0},{2,3},{3,2},{4,5},{5,4},{6,7},{7,6},{8,9},{9,8},{10,11... | collective-permute-start | bytes 589832 | tf_op jit(solution)/shard_map/ppermute | solution.py:196
  39.8 1.5 %collective-permute-start.9 = (bf16[768,128]{1,0:T(8,128)(2,1)S(1)}, bf16[768,128]{1,0:T(8,128)(2,1)S(1)}, u32[]{:S(2)}, u32[]{:S(2)}) collective-permute-start(bf16[768,128]{1,0:T(8,128)(2,1)S(1)} %shard_map.91.refs_5_), channel_id=1, source_target_pairs={{0,1},{1,0},{2,3},{3,2},{4,5},{5,4},{6,7},{7,6},{8,9},{9,8},{10,11... | collective-permute-start | bytes 589832 | tf_op jit(solution)/shard_map/ppermute | solution.py:196
  44.8 37.4 %copy-start.18 = (bf16[1,128,1536]{2,1,0:T(8,128)(2,1)}, bf16[1,128,1536]{2,1,0:T(8,128)(2,1)S(1)}, u32[]{:S(2)}) copy-start(bf16[1,128,1536]{2,1,0:T(8,128)(2,1)S(1)} %collective-permute-done.10.refs_3_) | copy-start | bytes 1179652
  44.8 2.3 %collective-permute-start.11 = (bf16[2,2,768,128]{3,2,1,0:T(8,128)(2,1)S(1)}, bf16[2,2,768,128]{3,2,1,0:T(8,128)(2,1)S(1)}, u32[]{:S(2)}, u32[]{:S(2)}) collective-permute-start(bf16[2,2,768,128]{3,2,1,0:T(8,128)(2,1)S(1)} %bitcast.38), channel_id=1, source_target_pairs={{0,1},{1,0},{2,3},{3,2},{4,5},{5,4},{6,7},{7,6},{8,9},{9,8},{10,11... | collective-permute-start | bytes 2359304 | tf_op jit(solution)/shard_map/ppermute | solution.py:196
  44.8 12.0 %collective-permute-start.15 = (bf16[1,128,1536]{2,1,0:T(8,128)(2,1)S(1)}, bf16[1,128,1536]{2,1,0:T(8,128)(2,1)S(1)}, u32[]{:S(2)}, u32[]{:S(2)}) collective-permute-start(bf16[1,128,1536]{2,1,0:T(8,128)(2,1)S(1)} %bitcast.43), channel_id=1, source_target_pairs={{0,4},{4,0},{1,5},{5,1},{2,6},{6,2},{3,7},{7,3},{8,12},{12,8},{9,1... | collective-permute-start | bytes 1179656 | tf_op jit(solution)/shard_map/ppermute | solution.py:196
  47.2 7.8 %collective-permute-start.13 = (bf16[768,128]{1,0:T(8,128)(2,1)S(1)}, bf16[768,128]{1,0:T(8,128)(2,1)S(1)}, u32[]{:S(2)}, u32[]{:S(2)}) collective-permute-start(bf16[768,128]{1,0:T(8,128)(2,1)S(1)} %get-tuple-element.72), channel_id=1, source_target_pairs={{0,2},{2,0},{1,3},{3,1},{4,6},{6,4},{5,7},{7,5},{8,10},{10,8},{9,1... | collective-permute-start | bytes 589832 | tf_op jit(solution)/shard_map/ppermute | solution.py:196
  48.3 14.4 %collective-permute-start.12 = (bf16[1,128,1536]{2,1,0:T(8,128)(2,1)S(1)}, bf16[1,128,1536]{2,1,0:T(8,128)(2,1)S(1)}, u32[]{:S(2)}, u32[]{:S(2)}) collective-permute-start(bf16[1,128,1536]{2,1,0:T(8,128)(2,1)S(1)} %bitcast.44), channel_id=1, source_target_pairs={{0,2},{2,0},{1,3},{3,1},{4,6},{6,4},{5,7},{7,5},{8,10},{10,8},{9,1... | collective-permute-start | bytes 1179656 | tf_op jit(solution)/shard_map/ppermute | solution.py:196
  55.1 7.6 %collective-permute-start.14 = (bf16[768,128]{1,0:T(8,128)(2,1)S(1)}, bf16[768,128]{1,0:T(8,128)(2,1)S(1)}, u32[]{:S(2)}, u32[]{:S(2)}) collective-permute-start(bf16[768,128]{1,0:T(8,128)(2,1)S(1)} %shard_map.95.refs_0_), channel_id=1, source_target_pairs={{0,4},{4,0},{1,5},{5,1},{2,6},{6,2},{3,7},{7,3},{8,12},{12,8},{9,1... | collective-permute-start | bytes 589832 | tf_op jit(solution)/shard_map/ppermute | solution.py:196
  56.8 33.5 %copy-start.19 = (bf16[1,128,1536]{2,1,0:T(8,128)(2,1)}, bf16[1,128,1536]{2,1,0:T(8,128)(2,1)S(1)}, u32[]{:S(2)}) copy-start(bf16[1,128,1536]{2,1,0:T(8,128)(2,1)S(1)} %collective-permute-done.15.refs_2_) | copy-start | bytes 1179652
  62.6 27.7 %copy-start.20 = (bf16[1,128,1536]{2,1,0:T(8,128)(2,1)}, bf16[1,128,1536]{2,1,0:T(8,128)(2,1)S(1)}, u32[]{:S(2)}) copy-start(bf16[1,128,1536]{2,1,0:T(8,128)(2,1)S(1)} %collective-permute-done.12.refs_6_) | copy-start | bytes 1179652
  62.7 12.8 %collective-permute-start.17 = (bf16[1,128,1536]{2,1,0:T(8,128)(2,1)S(1)}, bf16[1,128,1536]{2,1,0:T(8,128)(2,1)S(1)}, u32[]{:S(2)}, u32[]{:S(2)}) collective-permute-start(bf16[1,128,1536]{2,1,0:T(8,128)(2,1)S(1)} %collective-permute-done.10.refs_3_), channel_id=1, source_target_pairs={{0,2},{2,0},{1,3},{3,1},{4,6},{6,4},{5,7},{7,5},{8,10},{10,8},{9,1... | collective-permute-start | bytes 1179656 | tf_op jit(solution)/shard_map/ppermute | solution.py:196
  63.8 11.7 %collective-permute-start.16 = (bf16[768,128]{1,0:T(8,128)(2,1)S(1)}, bf16[768,128]{1,0:T(8,128)(2,1)S(1)}, u32[]{:S(2)}, u32[]{:S(2)}) collective-permute-start(bf16[768,128]{1,0:T(8,128)(2,1)S(1)} %get-tuple-element.77), channel_id=1, source_target_pairs={{0,8},{8,0},{1,9},{9,1},{2,10},{10,2},{3,11},{11,3},{4,12},{12,4},... | collective-permute-start | bytes 589832 | tf_op jit(solution)/shard_map/ppermute | solution.py:196
  67.2 14.4 %collective-permute-start.23 = (bf16[1,128,1536]{2,1,0:T(8,128)(2,1)S(1)}, bf16[1,128,1536]{2,1,0:T(8,128)(2,1)S(1)}, u32[]{:S(2)}, u32[]{:S(2)}) collective-permute-start(bf16[1,128,1536]{2,1,0:T(8,128)(2,1)S(1)} %bitcast.45), channel_id=1, source_target_pairs={{0,1},{1,0},{2,3},{3,2},{4,5},{5,4},{6,7},{7,6},{8,9},{9,8},{10,11... | collective-permute-start | bytes 1179656 | tf_op jit(solution)/shard_map/ppermute | solution.py:196
  67.2 10.4 %collective-permute-start.20 = (bf16[768,128]{1,0:T(8,128)(2,1)S(1)}, bf16[768,128]{1,0:T(8,128)(2,1)S(1)}, u32[]{:S(2)}, u32[]{:S(2)}) collective-permute-start(bf16[768,128]{1,0:T(8,128)(2,1)S(1)} %get-tuple-element.85.refs_0_), channel_id=1, source_target_pairs={{0,2},{2,0},{1,3},{3,1},{4,6},{6,4},{5,7},{7,5},{8,10},{10,8},{9,1... | collective-permute-start | bytes 589832 | tf_op jit(solution)/shard_map/ppermute | solution.py:196
  68.2 14.1 %collective-permute-start.24 = (bf16[1,128,1536]{2,1,0:T(8,128)(2,1)S(1)}, bf16[1,128,1536]{2,1,0:T(8,128)(2,1)S(1)}, u32[]{:S(2)}, u32[]{:S(2)}) collective-permute-start(bf16[1,128,1536]{2,1,0:T(8,128)(2,1)S(1)} %bitcast.48), channel_id=1, source_target_pairs={{0,1},{1,0},{2,3},{3,2},{4,5},{5,4},{6,7},{7,6},{8,9},{9,8},{10,11... | collective-permute-start | bytes 1179656 | tf_op jit(solution)/shard_map/ppermute | solution.py:196
  75.6 5.9 %collective-permute-start.19 = (bf16[768,128]{1,0:T(8,128)(2,1)S(1)}, bf16[768,128]{1,0:T(8,128)(2,1)S(1)}, u32[]{:S(2)}, u32[]{:S(2)}) collective-permute-start(bf16[768,128]{1,0:T(8,128)(2,1)S(1)} %get-tuple-element.81), channel_id=1, source_target_pairs={{0,2},{2,0},{1,3},{3,1},{4,6},{6,4},{5,7},{7,5},{8,10},{10,8},{9,1... | collective-permute-start | bytes 589832 | tf_op jit(solution)/shard_map/ppermute | solution.py:196
  76.7 5.7 %collective-permute-start.27 = (bf16[1,128,1536]{2,1,0:T(8,128)(2,1)S(1)}, bf16[1,128,1536]{2,1,0:T(8,128)(2,1)S(1)}, u32[]{:S(2)}, u32[]{:S(2)}) collective-permute-start(bf16[1,128,1536]{2,1,0:T(8,128)(2,1)S(1)} %collective-permute-done.6.refs_4_), channel_id=1, source_target_pairs={{0,1},{1,0},{2,3},{3,2},{4,5},{5,4},{6,7},{7,6},{8,9},{9,8},{10,11... | collective-permute-start | bytes 1179656 | tf_op jit(solution)/shard_map/ppermute | solution.py:196
  77.6 10.6 %collective-permute-start.18 = (bf16[1,128,1536]{2,1,0:T(8,128)(2,1)S(1)}, bf16[1,128,1536]{2,1,0:T(8,128)(2,1)S(1)}, u32[]{:S(2)}, u32[]{:S(2)}) collective-permute-start(bf16[1,128,1536]{2,1,0:T(8,128)(2,1)S(1)} %collective-permute-done.12.refs_6_), channel_id=1, source_target_pairs={{0,4},{4,0},{1,5},{5,1},{2,6},{6,2},{3,7},{7,3},{8,12},{12,8},{9,1... | collective-permute-start | bytes 1179656 | tf_op jit(solution)/shard_map/ppermute | solution.py:196
  81.6 1.4 collective-permute-start.21
  81.7 1.6 %collective-permute-start.22 = (bf16[768,128]{1,0:T(8,128)(2,1)S(1)}, bf16[768,128]{1,0:T(8,128)(2,1)S(1)}, u32[]{:S(2)}, u32[]{:S(2)}) collective-permute-start(bf16[768,128]{1,0:T(8,128)(2,1)S(1)} %shard_map.98.refs_5_.refs_7_), channel_id=1, source_target_pairs={{0,1},{1,0},{2,3},{3,2},{4,5},{5,4},{6,7},{7,6},{8,9},{9,8},{10,11... | collective-permute-start | bytes 589832 | tf_op jit(solution)/shard_map/ppermute | solution.py:196
  82.2 8.2 %collective-permute-start.26 = (bf16[1,128,1536]{2,1,0:T(8,128)(2,1)S(1)}, bf16[1,128,1536]{2,1,0:T(8,128)(2,1)S(1)}, u32[]{:S(2)}, u32[]{:S(2)}) collective-permute-start(bf16[1,128,1536]{2,1,0:T(8,128)(2,1)S(1)} %collective-permute-done.10.refs_3_), channel_id=1, source_target_pairs={{0,1},{1,0},{2,3},{3,2},{4,5},{5,4},{6,7},{7,6},{8,9},{9,8},{10,11... | collective-permute-start | bytes 1179656 | tf_op jit(solution)/shard_map/ppermute | solution.py:196
  82.3 8.1 %collective-permute-start.25 = (bf16[1,128,1536]{2,1,0:T(8,128)(2,1)S(1)}, bf16[1,128,1536]{2,1,0:T(8,128)(2,1)S(1)}, u32[]{:S(2)}, u32[]{:S(2)}) collective-permute-start(bf16[1,128,1536]{2,1,0:T(8,128)(2,1)S(1)} %collective-permute-done.15.refs_2_), channel_id=1, source_target_pairs={{0,1},{1,0},{2,3},{3,2},{4,5},{5,4},{6,7},{7,6},{8,9},{9,8},{10,11... | collective-permute-start | bytes 1179656 | tf_op jit(solution)/shard_map/ppermute | solution.py:196
  83.0 7.5 %collective-permute-start.29 = (bf16[1,128,1536]{2,1,0:T(8,128)(2,1)S(1)}, bf16[1,128,1536]{2,1,0:T(8,128)(2,1)S(1)}, u32[]{:S(2)}, u32[]{:S(2)}) collective-permute-start(bf16[1,128,1536]{2,1,0:T(8,128)(2,1)S(1)} %collective-permute-done.12.refs_6_), channel_id=1, source_target_pairs={{0,1},{1,0},{2,3},{3,2},{4,5},{5,4},{6,7},{7,6},{8,9},{9,8},{10,11... | collective-permute-start | bytes 1179656 | tf_op jit(solution)/shard_map/ppermute | solution.py:196
  83.3 7.2 %collective-permute-start.28 = (bf16[1,128,1536]{2,1,0:T(8,128)(2,1)S(1)}, bf16[1,128,1536]{2,1,0:T(8,128)(2,1)S(1)}, u32[]{:S(2)}, u32[]{:S(2)}) collective-permute-start(bf16[1,128,1536]{2,1,0:T(8,128)(2,1)S(1)} %collective-permute-done.17.refs_5_), channel_id=1, source_target_pairs={{0,1},{1,0},{2,3},{3,2},{4,5},{5,4},{6,7},{7,6},{8,9},{9,8},{10,11... | collective-permute-start | bytes 1179656 | tf_op jit(solution)/shard_map/ppermute | solution.py:196
  88.2 2.3 %collective-permute-start.30 = (bf16[1,128,1536]{2,1,0:T(8,128)(2,1)S(1)}, bf16[1,128,1536]{2,1,0:T(8,128)(2,1)S(1)}, u32[]{:S(2)}, u32[]{:S(2)}) collective-permute-start(bf16[1,128,1536]{2,1,0:T(8,128)(2,1)S(1)} %collective-permute-done.18.refs_7_), channel_id=1, source_target_pairs={{0,1},{1,0},{2,3},{3,2},{4,5},{5,4},{6,7},{7,6},{8,9},{9,8},{10,11... | collective-permute-start | bytes 1179656 | tf_op jit(solution)/shard_map/ppermute | solution.py:196
  90.4 17.3 %copy-start.12 = (bf16[2,8,2,96,128]{4,3,2,1,0:T(8,128)(2,1)}, bf16[2,8,2,96,128]{4,3,2,1,0:T(8,128)(2,1)S(1)}, u32[]{:S(2)}) copy-start(bf16[2,8,2,96,128]{4,3,2,1,0:T(8,128)(2,1)S(1)} %get-tuple-element.96) | copy-start | bytes 2359300
  90.4 17.3 %copy-start.26 = (bf16[1,128,1536]{2,1,0:T(8,128)(2,1)}, bf16[1,128,1536]{2,1,0:T(8,128)(2,1)S(1)}, u32[]{:S(2)}) copy-start(bf16[1,128,1536]{2,1,0:T(8,128)(2,1)S(1)} %collective-permute-done.26.refs_11_) | copy-start | bytes 1179652
  90.5 17.3 %copy-start.27 = (bf16[1,128,1536]{2,1,0:T(8,128)(2,1)}, bf16[1,128,1536]{2,1,0:T(8,128)(2,1)S(1)}, u32[]{:S(2)}) copy-start(bf16[1,128,1536]{2,1,0:T(8,128)(2,1)S(1)} %collective-permute-done.25.refs_10_) | copy-start | bytes 1179652
  90.5 17.3 %copy-start.28 = (bf16[1,128,1536]{2,1,0:T(8,128)(2,1)}, bf16[1,128,1536]{2,1,0:T(8,128)(2,1)S(1)}, u32[]{:S(2)}) copy-start(bf16[1,128,1536]{2,1,0:T(8,128)(2,1)S(1)} %collective-permute-done.29.refs_14_) | copy-start | bytes 1179652
  90.5 17.3 %copy-start.29 = (bf16[1,128,1536]{2,1,0:T(8,128)(2,1)}, bf16[1,128,1536]{2,1,0:T(8,128)(2,1)S(1)}, u32[]{:S(2)}) copy-start(bf16[1,128,1536]{2,1,0:T(8,128)(2,1)S(1)} %collective-permute-done.28.refs_13_) | copy-start | bytes 1179652
  90.5 17.3 %copy-start.30 = (bf16[1,128,1536]{2,1,0:T(8,128)(2,1)}, bf16[1,128,1536]{2,1,0:T(8,128)(2,1)S(1)}, u32[]{:S(2)}) copy-start(bf16[1,128,1536]{2,1,0:T(8,128)(2,1)S(1)} %collective-permute-done.30.refs_15_) | copy-start | bytes 1179652
  107.8 22.2 %all-to-all-start.1 = ((bf16[16,192,128]{2,1,0:T(8,128)(2,1)}), bf16[16,192,128]{2,1,0:T(8,128)(2,1)}, u32[]{:S(2)}, u32[]{:S(2)}) async-start(bf16[16,192,128]{2,1,0:T(8,128)(2,1)} %bitcast.37), calls=%async_computation.1 | async-start | bytes 1572864 | tf_op jit(solution)/shard_map/all_to_all | solution.py:500
  117.0 17.7 %collective-permute-start.31 = (bf16[96,1536]{1,0:T(8,128)(2,1)}, bf16[96,1536]{1,0:T(8,128)(2,1)}, u32[]{:S(2)}, u32[]{:S(2)}) collective-permute-start(bf16[96,1536]{1,0:T(8,128)(2,1)} %bitcast.55), channel_id=1, source_target_pairs={{0,8},{8,0},{1,9},{9,1},{2,10},{10,2},{3,11},{11,3},{4,12},{12,4},... | collective-permute-start | bytes 884744 | tf_op jit(solution)/shard_map/ppermute | solution.py:518
  134.7 13.6 %collective-permute-start.32 = (bf16[96,1536]{1,0:T(8,128)(2,1)}, bf16[96,1536]{1,0:T(8,128)(2,1)S(1)}, u32[]{:S(2)}, u32[]{:S(2)}) collective-permute-start(bf16[96,1536]{1,0:T(8,128)(2,1)} %bitcast.56), channel_id=1, source_target_pairs={{0,8},{8,0},{1,9},{9,1},{2,10},{10,2},{3,11},{11,3},{4,12},{12,4},... | collective-permute-start | bytes 884744 | tf_op jit(solution)/shard_map/ppermute | solution.py:518
  (19 other events, 136.8 us)

commit v9 on v8

--- a/solution.py
+++ b/solution.py
@@ -345,7 +345,7 @@
         copies.append(pltpu.make_async_copy(ref, buffer_ref.at[at : at + count], arrival.at[index]))
         copies[-1].start()
         at += count
-    per_step, tile = 4, 512 if columns % 512 == 0 else columns
+    per_step, tile = 4, 768 if columns % 768 == 0 else columns
     steps = sources // per_step
     leaving = []
     turning.wait()

time: 150 us -> 150 us (level)
  no operation moved by 1% of the time
where the time goes in v9:
time: 150 us
  waiting for transfers between devices  58.1 us (39%)
  starting transfers between devices  37.1 us (25%)
  Pallas kernels  31.4 us (21%)
  blocking collectives  17.2 us (11%)
  local copies, waits for them, and re-layouts  2.4 us (2%)
  other arithmetic  2.23 us (1%)
    ppermute x31, waiting for transfers between devices, swap(): return lax.ppermute(array, axis, [(0, 1), (1, 0)])  41.9 us
    ppermute x31, starting transfers between devices, swap(): return lax.ppermute(array, axis, [(0, 1), (1, 0)])  29.1 us
    pallas_call x6, Pallas kernels, by_heads(): pl.pallas_call(body, in_specs=places[:count], out_specs=places[count:], o...  19.1 us
    all_to_all x1, blocking collectives, shards(): part = lax.all_to_all(part, ('dp', layer, side, core), 0, 0, tiled=True)  17.2 us
    ppermute x2, waiting for transfers between devices, shards(): lax.ppermute(sent[turn - 1], spans, [(i, (i + turn) % halves) for i in ra...  12.6 us
    pallas_call x2, Pallas kernels, weight_part(): pl.pallas_call(functools.partial(weight_kernel, sources_of, bits), in_spe...  9.56 us
    all_to_all x1, starting transfers between devices, shards(): part = lax.all_to_all(part, ('dp', layer, side, core), 0, 0, tiled=True)  4.47 us
    all_to_all x1, waiting for transfers between devices, shards(): part = lax.all_to_all(part, ('dp', layer, side, core), 0, 0, tiled=True)  3.59 us
  transfers between devices with their start and end apart: 34, of which 20 were waited for; matrix products, arithmetic and copies ran while one was open for 1% of the time, Pallas kernels for 20%

profile of v9, /device:TPU:0, one launch (start us, length us, event | category | flops | bytes accessed | tf_op | source)
XLA Modules:
  0.0 149.6 jit_solution(15989081085710531232)
XLA Ops:
  0.6 1.1 copy-done
  1.8 1.1 copy-done.2
  2.9 0.8 shard_map.84
  4.2 1.9 %collective-permute-done.refs_1_ = bf16[2,2,768,128]{3,2,1,0:T(8,128)(2,1)S(1)} collective-permute-done((bf16[2,2,768,128]{3,2,1,0:T(8,128)(2,1)S(1)}, bf16[2,2,768,128]{3,2,1,0:T(8,128)(2,1)S(1)}, u32[]{:S(2)}, u32[]{:S(2)}) %collective-permute-start) | collective-permute-done | bytes 786464 | tf_op jit(solution)/shard_map/ppermute | solution.py:196
  6.2 2.9 %collective-permute-start.1 = (bf16[768,128]{1,0:T(8,128)(2,1)S(1)}, bf16[768,128]{1,0:T(8,128)(2,1)S(1)}, u32[]{:S(2)}, u32[]{:S(2)}) collective-permute-start(bf16[768,128]{1,0:T(8,128)(2,1)S(1)} %get-tuple-element.53), channel_id=1, source_target_pairs={{0,2},{2,0},{1,3},{3,1},{4,6},{6,4},{5,7},{7,5},{8,10},{10,8},{9,1... | collective-permute-start | bytes 589832 | tf_op jit(solution)/shard_map/ppermute | solution.py:196
  9.1 1.9 %shard_map.87 = (bf16[128,1536]{1,0:T(8,128)(2,1)}, bf16[128,1536]{1,0:T(8,128)(2,1)}) custom-call(bf16[128,3072]{1,0:T(8,128)(2,1)} %bitcast.51), custom_call_target="tpu_custom_call" | custom-call | bytes 1572864 | tf_op jit(solution)/shard_map/pallas_call | solution.py:317
  11.0 1.5 %collective-permute-start.4 = (bf16[128,1536]{1,0:T(8,128)(2,1)}, bf16[128,1536]{1,0:T(8,128)(2,1)S(1)}, u32[]{:S(2)}, u32[]{:S(2)}) collective-permute-start(bf16[128,1536]{1,0:T(8,128)(2,1)} %get-tuple-element.56), channel_id=1, source_target_pairs={{0,16},{16,0},{1,17},{17,1},{2,18},{18,2},{3,19},{19,3},{4,20},{20... | collective-permute-start | bytes 1179656 | tf_op jit(solution)/shard_map/ppermute | solution.py:196
  12.6 1.8 %collective-permute-done.1.refs_1_.refs_0_ = bf16[768,128]{1,0:T(8,128)(2,1)S(1)} collective-permute-done((bf16[768,128]{1,0:T(8,128)(2,1)S(1)}, bf16[768,128]{1,0:T(8,128)(2,1)S(1)}, u32[]{:S(2)}, u32[]{:S(2)}) %collective-permute-start.1) | collective-permute-done | bytes 196640 | tf_op jit(solution)/shard_map/ppermute | solution.py:196
  14.4 1.7 %collective-permute-start.3 = (bf16[768,128]{1,0:T(8,128)(2,1)S(1)}, bf16[768,128]{1,0:T(8,128)(2,1)S(1)}, u32[]{:S(2)}, u32[]{:S(2)}) collective-permute-start(bf16[768,128]{1,0:T(8,128)(2,1)S(1)} %get-tuple-element.54.refs_0_), channel_id=1, source_target_pairs={{0,2},{2,0},{1,3},{3,1},{4,6},{6,4},{5,7},{7,5},{8,10},{10,8},{9,1... | collective-permute-start | bytes 589832 | tf_op jit(solution)/shard_map/ppermute | solution.py:196
  16.1 1.6 %collective-permute-start.2 = (bf16[768,128]{1,0:T(8,128)(2,1)S(1)}, bf16[768,128]{1,0:T(8,128)(2,1)S(1)}, u32[]{:S(2)}, u32[]{:S(2)}) collective-permute-start(bf16[768,128]{1,0:T(8,128)(2,1)S(1)} %shard_map.86.refs_0_), channel_id=1, source_target_pairs={{0,4},{4,0},{1,5},{5,1},{2,6},{6,2},{3,7},{7,3},{8,12},{12,8},{9,1... | collective-permute-start | bytes 589832 | tf_op jit(solution)/shard_map/ppermute | solution.py:196
  17.8 3.0 %collective-permute-done.3.refs_1_ = bf16[768,128]{1,0:T(8,128)(2,1)S(1)} collective-permute-done((bf16[768,128]{1,0:T(8,128)(2,1)S(1)}, bf16[768,128]{1,0:T(8,128)(2,1)S(1)}, u32[]{:S(2)}, u32[]{:S(2)}) %collective-permute-start.3) | collective-permute-done | bytes 196640 | tf_op jit(solution)/shard_map/ppermute | solution.py:196
  20.8 1.3 collective-permute-done.2.refs_1_
  22.8 2.8 %collective-permute-start.5 = (bf16[768,128]{1,0:T(8,128)(2,1)S(1)}, bf16[768,128]{1,0:T(8,128)(2,1)S(1)}, u32[]{:S(2)}, u32[]{:S(2)}) collective-permute-start(bf16[768,128]{1,0:T(8,128)(2,1)S(1)} %get-tuple-element.58), channel_id=1, source_target_pairs={{0,8},{8,0},{1,9},{9,1},{2,10},{10,2},{3,11},{11,3},{4,12},{12,4},... | collective-permute-start | bytes 589832 | tf_op jit(solution)/shard_map/ppermute | solution.py:196
  25.6 3.9 %shard_map.89.refs_1_ = f32[128,3072]{1,0:T(8,128)S(1)} custom-call(bf16[128,3072]{1,0:T(8,128)(2,1)S(1)} %bitcast.27, bf16[128,3072]{1,0:T(8,128)(2,1)S(1)} %bitcast.24, bf16[128,3072]{1,0:T(8,128)(2,1)S(1)} %bitcast.19), custom_call_target="tpu_custom_call" | custom-call | flops 201326592 | bytes 3145728 | tf_op jit(solution)/shard_map/pallas_call | solution.py:177
  29.5 4.4 %collective-permute-done.5.refs_1_ = bf16[768,128]{1,0:T(8,128)(2,1)S(1)} collective-permute-done((bf16[768,128]{1,0:T(8,128)(2,1)S(1)}, bf16[768,128]{1,0:T(8,128)(2,1)S(1)}, u32[]{:S(2)}, u32[]{:S(2)}) %collective-permute-start.5) | collective-permute-done | bytes 196640 | tf_op jit(solution)/shard_map/ppermute | solution.py:196
  34.0 1.1 collective-permute-start.7
  35.1 0.7 collective-permute-start.10
  35.8 3.9 %collective-permute-done.7.refs_0_ = bf16[768,128]{1,0:T(8,128)(2,1)S(1)} collective-permute-done((bf16[768,128]{1,0:T(8,128)(2,1)S(1)}, bf16[768,128]{1,0:T(8,128)(2,1)S(1)}, u32[]{:S(2)}, u32[]{:S(2)}) %collective-permute-start.7) | collective-permute-done | bytes 196640 | tf_op jit(solution)/shard_map/ppermute | solution.py:196
  39.9 1.4 collective-permute-done.9.refs_7_
  41.4 2.8 %shard_map.92 = (bf16[128,3072]{1,0:T(8,128)(2,1)S(1)}, bf16[3072,128]{1,0:T(8,128)(2,1)S(1)}, bf16[3072,128]{1,0:T(8,128)(2,1)S(1)}) custom-call(bf16[128,3072]{1,0:T(8,128)(2,1)S(1)} %bitcast.28, f32[128,3072]{1,0:T(8,128)S(1)} %shard_map.89.refs_1_, bf16[128,3072]{1,0:T(8,128)(2,1)S(1)} %bitcast.36, bf16[3072,128]{1,0:T(8,128)(2,1)S(1)} %bitcast.33, ...), custom_call_target="tpu_custom_call" | custom-call | flops 201326592 | bytes 8650752 | tf_op jit(solution)/shard_map/pallas_call | solution.py:177
  44.2 0.6 collective-permute-done.10.refs_3_
  44.8 1.8 %collective-permute-start.15 = (bf16[1,128,1536]{2,1,0:T(8,128)(2,1)S(1)}, bf16[1,128,1536]{2,1,0:T(8,128)(2,1)S(1)}, u32[]{:S(2)}, u32[]{:S(2)}) collective-permute-start(bf16[1,128,1536]{2,1,0:T(8,128)(2,1)S(1)} %bitcast.43), channel_id=1, source_target_pairs={{0,4},{4,0},{1,5},{5,1},{2,6},{6,2},{3,7},{7,3},{8,12},{12,8},{9,1... | collective-permute-start | bytes 1179656 | tf_op jit(solution)/shard_map/ppermute | solution.py:196
  47.2 1.1 collective-permute-start.13
  48.3 1.0 collective-permute-start.12
  49.3 3.9 %shard_map.94.refs_2_ = f32[128,3072]{1,0:T(8,128)S(1)} custom-call(bf16[128,3072]{1,0:T(8,128)(2,1)S(1)} %bitcast.29, bf16[128,3072]{1,0:T(8,128)(2,1)S(1)} %bitcast.20, bf16[128,3072]{1,0:T(8,128)(2,1)S(1)} %get-tuple-element.90.refs_2_.refs_3_), custom_call_target="tpu_custom_call" | custom-call | flops 201326592 | bytes 3145728 | tf_op jit(solution)/shard_map/pallas_call | solution.py:177
  53.2 1.8 %collective-permute-done.13.refs_1_.refs_0_ = bf16[768,128]{1,0:T(8,128)(2,1)S(1)} collective-permute-done((bf16[768,128]{1,0:T(8,128)(2,1)S(1)}, bf16[768,128]{1,0:T(8,128)(2,1)S(1)}, u32[]{:S(2)}, u32[]{:S(2)}) %collective-permute-start.13) | collective-permute-done | bytes 196640 | tf_op jit(solution)/shard_map/ppermute | solution.py:196
  55.1 1.8 %collective-permute-start.14 = (bf16[768,128]{1,0:T(8,128)(2,1)S(1)}, bf16[768,128]{1,0:T(8,128)(2,1)S(1)}, u32[]{:S(2)}, u32[]{:S(2)}) collective-permute-start(bf16[768,128]{1,0:T(8,128)(2,1)S(1)} %shard_map.95.refs_0_), channel_id=1, source_target_pairs={{0,4},{4,0},{1,5},{5,1},{2,6},{6,2},{3,7},{7,3},{8,12},{12,8},{9,1... | collective-permute-start | bytes 589832 | tf_op jit(solution)/shard_map/ppermute | solution.py:196
  56.8 5.8 %collective-permute-done.12.refs_6_ = bf16[1,128,1536]{2,1,0:T(8,128)(2,1)S(1)} collective-permute-done((bf16[1,128,1536]{2,1,0:T(8,128)(2,1)S(1)}, bf16[1,128,1536]{2,1,0:T(8,128)(2,1)S(1)}, u32[]{:S(2)}, u32[]{:S(2)}) %collective-permute-start.12) | collective-permute-done | bytes 393248 | tf_op jit(solution)/shard_map/ppermute | solution.py:196
  62.7 1.1 collective-permute-start.17
  63.8 3.4 %collective-permute-start.16 = (bf16[768,128]{1,0:T(8,128)(2,1)S(1)}, bf16[768,128]{1,0:T(8,128)(2,1)S(1)}, u32[]{:S(2)}, u32[]{:S(2)}) collective-permute-start(bf16[768,128]{1,0:T(8,128)(2,1)S(1)} %get-tuple-element.77), channel_id=1, source_target_pairs={{0,8},{8,0},{1,9},{9,1},{2,10},{10,2},{3,11},{11,3},{4,12},{12,4},... | collective-permute-start | bytes 589832 | tf_op jit(solution)/shard_map/ppermute | solution.py:196
  67.2 1.0 collective-permute-start.20
  68.4 7.1 %collective-permute-done.16.refs_1_ = bf16[768,128]{1,0:T(8,128)(2,1)S(1)} collective-permute-done((bf16[768,128]{1,0:T(8,128)(2,1)S(1)}, bf16[768,128]{1,0:T(8,128)(2,1)S(1)}, u32[]{:S(2)}, u32[]{:S(2)}) %collective-permute-start.16) | collective-permute-done | bytes 196640 | tf_op jit(solution)/shard_map/ppermute | solution.py:196
  75.6 1.0 collective-permute-start.19
  76.7 0.9 collective-permute-done.20.refs_1_
  77.6 1.5 collective-permute-start.18
  79.0 2.5 %collective-permute-done.19.refs_0_ = bf16[768,128]{1,0:T(8,128)(2,1)S(1)} collective-permute-done((bf16[768,128]{1,0:T(8,128)(2,1)S(1)}, bf16[768,128]{1,0:T(8,128)(2,1)S(1)}, u32[]{:S(2)}, u32[]{:S(2)}) %collective-permute-start.19) | collective-permute-done | bytes 196640 | tf_op jit(solution)/shard_map/ppermute | solution.py:196
  83.7 4.5 %collective-permute-done.18.refs_7_ = bf16[1,128,1536]{2,1,0:T(8,128)(2,1)S(1)} collective-permute-done((bf16[1,128,1536]{2,1,0:T(8,128)(2,1)S(1)}, bf16[1,128,1536]{2,1,0:T(8,128)(2,1)S(1)}, u32[]{:S(2)}, u32[]{:S(2)}) %collective-permute-start.18) | collective-permute-done | bytes 393248 | tf_op jit(solution)/shard_map/ppermute | solution.py:196
  88.2 2.1 %shard_map.99 = (bf16[128,3072]{1,0:T(8,128)(2,1)}, bf16[2,8,2,96,128]{4,3,2,1,0:T(8,128)(2,1)S(1)}, bf16[2,8,2,96,128]{4,3,2,1,0:T(8,128)(2,1)S(1)}) custom-call(bf16[128,3072]{1,0:T(8,128)(2,1)S(1)} %bitcast.25, bf16[128,3072]{1,0:T(8,128)(2,1)S(1)} %bitcast.21, f32[128,3072]{1,0:T(8,128)S(1)} %shard_map.94.refs_2_, bf16[3072,128]{1,0:T(8,128)(2,1)S(1)} %bitcast.31, ...), custom_call_target="tpu_custom_call" | custom-call | flops 100663296 | bytes 8650752 | tf_op jit(solution)/shard_map/pallas_call | solution.py:177
  90.5 17.2 %all_to_all.10.turned_in = bf16[16,192,128]{2,1,0:T(8,128)(2,1)} all-to-all(bf16[16,192,128]{2,1,0:T(8,128)(2,1)S(1)} %bitcast.40), channel_id=1, replica_groups=mesh['dp'=2,'bit3'=2,'bit2'=2,'bit1'=2,'bit0'=2] {'dp','bit2','bit1','bi..., dimensions={0} | all-to-all | bytes 1572864 | tf_op jit(solution)/shard_map/all_to_all | solution.py:500
  107.8 4.5 %all-to-all-start.1 = ((bf16[16,192,128]{2,1,0:T(8,128)(2,1)}), bf16[16,192,128]{2,1,0:T(8,128)(2,1)}, u32[]{:S(2)}, u32[]{:S(2)}) async-start(bf16[16,192,128]{2,1,0:T(8,128)(2,1)} %bitcast.37), calls=%async_computation.1 | async-start | bytes 1572864 | tf_op jit(solution)/shard_map/all_to_all | solution.py:500
  112.3 4.8 %shard_map.100 = (f32[96,1536]{1,0:T(8,128)}, bf16[1,96,1536]{2,1,0:T(8,128)(2,1)}) custom-call(bf16[16,192,128]{2,1,0:T(8,128)(2,1)} %all_to_all.10.turned_in, bf16[1,128,1536]{2,1,0:T(8,128)(2,1)} %bitcast.41, bf16[1,128,1536]{2,1,0:T(8,128)(2,1)} %bitcast.49, bf16[1,128,1536]{2,1,0:T(8,128)(2,1)} %copy-done.19, bf16[1,128,1536]{2,1,0:T(8,128)(2,1)} %copy-done.18, ...), custom_call_target="tpu_custom_call" | custom-call | flops 1207959552 | bytes 8060928 | tf_op jit(solution)/shard_map/pallas_call | solution.py:382
  117.1 3.5 %collective-permute-start.31 = (bf16[96,1536]{1,0:T(8,128)(2,1)}, bf16[96,1536]{1,0:T(8,128)(2,1)}, u32[]{:S(2)}, u32[]{:S(2)}) collective-permute-start(bf16[96,1536]{1,0:T(8,128)(2,1)} %bitcast.55), channel_id=1, source_target_pairs={{0,8},{8,0},{1,9},{9,1},{2,10},{10,2},{3,11},{11,3},{4,12},{12,4},... | collective-permute-start | bytes 884744 | tf_op jit(solution)/shard_map/ppermute | solution.py:518
  120.6 5.7 %shard_map.101 = (bf16[128,3072]{1,0:T(8,128)(2,1)}, bf16[128,3072]{1,0:T(8,128)(2,1)}) custom-call(bf16[128,3072]{1,0:T(8,128)(2,1)S(1)} %bitcast.30, bf16[128,3072]{1,0:T(8,128)(2,1)S(1)} %bitcast.26, bf16[128,3072]{1,0:T(8,128)(2,1)S(1)} %bitcast.22, bf16[128,3072]{1,0:T(8,128)(2,1)S(1)} %copy-done.6, bf16[3072,128]{1,0:T(8,128)(2,1)S(1)} %copy-done.14, ...), custom_call_target="tpu_custom_call" | custom-call | flops 603979776 | bytes 9437184 | tf_op jit(solution)/shard_map/pallas_call | solution.py:177
  126.3 3.6 %all-to-all-done.1.turned_in = bf16[16,192,128]{2,1,0:T(8,128)(2,1)} async-done(((bf16[16,192,128]{2,1,0:T(8,128)(2,1)}), bf16[16,192,128]{2,1,0:T(8,128)(2,1)}, u32[]{:S(2)}, u32[]{:S(2)}) %all-to-all-start.1) | async-done | bytes 786464 | tf_op jit(solution)/shard_map/all_to_all | solution.py:500
  129.9 4.7 %shard_map.102 = (f32[96,1536]{1,0:T(8,128)}, bf16[1,96,1536]{2,1,0:T(8,128)(2,1)}) custom-call(bf16[16,192,128]{2,1,0:T(8,128)(2,1)} %all-to-all-done.1.turned_in, bf16[1,128,1536]{2,1,0:T(8,128)(2,1)} %bitcast.42, bf16[1,128,1536]{2,1,0:T(8,128)(2,1)} %bitcast.50, bf16[1,128,1536]{2,1,0:T(8,128)(2,1)} %copy-done.19, bf16[1,128,1536]{2,1,0:T(8,128)(2,1)} %copy-done.18, ...), custom_call_target="tpu_custom_call" | custom-call | flops 1207959552 | bytes 8060928 | tf_op jit(solution)/shard_map/pallas_call | solution.py:382
  134.8 1.1 convert_add_fusion.1
  135.9 12.6 %collective-permute-done.32 = bf16[96,1536]{1,0:T(8,128)(2,1)S(1)} collective-permute-done((bf16[96,1536]{1,0:T(8,128)(2,1)}, bf16[96,1536]{1,0:T(8,128)(2,1)S(1)}, u32[]{:S(2)}, u32[]{:S(2)}) %collective-permute-start.32) | collective-permute-done | bytes 294944 | tf_op jit(solution)/shard_map/ppermute | solution.py:518
  148.5 1.1 maximum_multiply_fusion
  (109 shorter events, 5.2 us)
Async XLA Ops:
  3.7 2.4 %collective-permute-start = (bf16[2,2,768,128]{3,2,1,0:T(8,128)(2,1)S(1)}, bf16[2,2,768,128]{3,2,1,0:T(8,128)(2,1)S(1)}, u32[]{:S(2)}, u32[]{:S(2)}) collective-permute-start(bf16[2,2,768,128]{3,2,1,0:T(8,128)(2,1)S(1)} %bitcast.34), channel_id=1, source_target_pairs={{0,1},{1,0},{2,3},{3,2},{4,5},{5,4},{6,7},{7,6},{8,9},{9,8},{10,11... | collective-permute-start | bytes 2359304 | tf_op jit(solution)/shard_map/ppermute | solution.py:196
  6.1 19.5 %copy-start.4 = (bf16[1,128,3072]{2,1,0:T(8,128)(2,1)S(1)}, bf16[1,128,3072]{2,1,0:T(8,128)(2,1)}, u32[]{:S(2)}) copy-start(bf16[1,128,3072]{2,1,0:T(8,128)(2,1)} %param.6) | copy-start | bytes 2359300
  6.2 19.4 %copy-start.1 = (bf16[1,128,3072]{2,1,0:T(8,128)(2,1)S(1)}, bf16[1,128,3072]{2,1,0:T(8,128)(2,1)}, u32[]{:S(2)}) copy-start(bf16[1,128,3072]{2,1,0:T(8,128)(2,1)} %param.8) | copy-start | bytes 2359300
  6.2 19.4 %copy-start.3 = (bf16[1,128,3072]{2,1,0:T(8,128)(2,1)S(1)}, bf16[1,128,3072]{2,1,0:T(8,128)(2,1)}, u32[]{:S(2)}) copy-start(bf16[1,128,3072]{2,1,0:T(8,128)(2,1)} %param.7) | copy-start | bytes 2359300
  6.2 8.1 %collective-permute-start.1 = (bf16[768,128]{1,0:T(8,128)(2,1)S(1)}, bf16[768,128]{1,0:T(8,128)(2,1)S(1)}, u32[]{:S(2)}, u32[]{:S(2)}) collective-permute-start(bf16[768,128]{1,0:T(8,128)(2,1)S(1)} %get-tuple-element.53), channel_id=1, source_target_pairs={{0,2},{2,0},{1,3},{3,1},{4,6},{6,4},{5,7},{7,5},{8,10},{10,8},{9,1... | collective-permute-start | bytes 589832 | tf_op jit(solution)/shard_map/ppermute | solution.py:196
  11.0 11.1 %collective-permute-start.4 = (bf16[128,1536]{1,0:T(8,128)(2,1)}, bf16[128,1536]{1,0:T(8,128)(2,1)S(1)}, u32[]{:S(2)}, u32[]{:S(2)}) collective-permute-start(bf16[128,1536]{1,0:T(8,128)(2,1)} %get-tuple-element.56), channel_id=1, source_target_pairs={{0,16},{16,0},{1,17},{17,1},{2,18},{18,2},{3,19},{19,3},{4,20},{20... | collective-permute-start | bytes 1179656 | tf_op jit(solution)/shard_map/ppermute | solution.py:196
  14.4 6.4 %collective-permute-start.3 = (bf16[768,128]{1,0:T(8,128)(2,1)S(1)}, bf16[768,128]{1,0:T(8,128)(2,1)S(1)}, u32[]{:S(2)}, u32[]{:S(2)}) collective-permute-start(bf16[768,128]{1,0:T(8,128)(2,1)S(1)} %get-tuple-element.54.refs_0_), channel_id=1, source_target_pairs={{0,2},{2,0},{1,3},{3,1},{4,6},{6,4},{5,7},{7,5},{8,10},{10,8},{9,1... | collective-permute-start | bytes 589832 | tf_op jit(solution)/shard_map/ppermute | solution.py:196
  16.1 5.9 %collective-permute-start.2 = (bf16[768,128]{1,0:T(8,128)(2,1)S(1)}, bf16[768,128]{1,0:T(8,128)(2,1)S(1)}, u32[]{:S(2)}, u32[]{:S(2)}) collective-permute-start(bf16[768,128]{1,0:T(8,128)(2,1)S(1)} %shard_map.86.refs_0_), channel_id=1, source_target_pairs={{0,4},{4,0},{1,5},{5,1},{2,6},{6,2},{3,7},{7,3},{8,12},{12,8},{9,1... | collective-permute-start | bytes 589832 | tf_op jit(solution)/shard_map/ppermute | solution.py:196
  22.1 46.0 %copy-start.16 = (bf16[128,1536]{1,0:T(8,128)(2,1)}, bf16[128,1536]{1,0:T(8,128)(2,1)S(1)}, u32[]{:S(2)}) copy-start(bf16[128,1536]{1,0:T(8,128)(2,1)S(1)} %collective-permute-done.4) | copy-start | bytes 1179652
  22.2 11.6 %collective-permute-start.6 = (bf16[1,128,1536]{2,1,0:T(8,128)(2,1)S(1)}, bf16[1,128,1536]{2,1,0:T(8,128)(2,1)S(1)}, u32[]{:S(2)}, u32[]{:S(2)}) collective-permute-start(bf16[1,128,1536]{2,1,0:T(8,128)(2,1)S(1)} %bitcast.46), channel_id=1, source_target_pairs={{0,2},{2,0},{1,3},{3,1},{4,6},{6,4},{5,7},{7,5},{8,10},{10,8},{9,1... | collective-permute-start | bytes 1179656 | tf_op jit(solution)/shard_map/ppermute | solution.py:196
  22.8 11.1 %collective-permute-start.5 = (bf16[768,128]{1,0:T(8,128)(2,1)S(1)}, bf16[768,128]{1,0:T(8,128)(2,1)S(1)}, u32[]{:S(2)}, u32[]{:S(2)}) collective-permute-start(bf16[768,128]{1,0:T(8,128)(2,1)S(1)} %get-tuple-element.58), channel_id=1, source_target_pairs={{0,8},{8,0},{1,9},{9,1},{2,10},{10,2},{3,11},{11,3},{4,12},{12,4},... | collective-permute-start | bytes 589832 | tf_op jit(solution)/shard_map/ppermute | solution.py:196
  33.9 42.8 %copy-start.17 = (bf16[1,128,1536]{2,1,0:T(8,128)(2,1)}, bf16[1,128,1536]{2,1,0:T(8,128)(2,1)S(1)}, u32[]{:S(2)}) copy-start(bf16[1,128,1536]{2,1,0:T(8,128)(2,1)S(1)} %collective-permute-done.6.refs_4_) | copy-start | bytes 1179652
  34.0 5.8 %collective-permute-start.7 = (bf16[768,128]{1,0:T(8,128)(2,1)S(1)}, bf16[768,128]{1,0:T(8,128)(2,1)S(1)}, u32[]{:S(2)}, u32[]{:S(2)}) collective-permute-start(bf16[768,128]{1,0:T(8,128)(2,1)S(1)} %get-tuple-element.64), channel_id=1, source_target_pairs={{0,2},{2,0},{1,3},{3,1},{4,6},{6,4},{5,7},{7,5},{8,10},{10,8},{9,1... | collective-permute-start | bytes 589832 | tf_op jit(solution)/shard_map/ppermute | solution.py:196
  35.1 9.7 %collective-permute-start.10 = (bf16[1,128,1536]{2,1,0:T(8,128)(2,1)S(1)}, bf16[1,128,1536]{2,1,0:T(8,128)(2,1)S(1)}, u32[]{:S(2)}, u32[]{:S(2)}) collective-permute-start(bf16[1,128,1536]{2,1,0:T(8,128)(2,1)S(1)} %bitcast.47), channel_id=1, source_target_pairs={{0,4},{4,0},{1,5},{5,1},{2,6},{6,2},{3,7},{7,3},{8,12},{12,8},{9,1... | collective-permute-start | bytes 1179656 | tf_op jit(solution)/shard_map/ppermute | solution.py:196
  35.8 4.1 %collective-permute-start.8 = (bf16[768,128]{1,0:T(8,128)(2,1)S(1)}, bf16[768,128]{1,0:T(8,128)(2,1)S(1)}, u32[]{:S(2)}, u32[]{:S(2)}) collective-permute-start(bf16[768,128]{1,0:T(8,128)(2,1)S(1)} %get-tuple-element.63.refs_4_), channel_id=1, source_target_pairs={{0,1},{1,0},{2,3},{3,2},{4,5},{5,4},{6,7},{7,6},{8,9},{9,8},{10,11... | collective-permute-start | bytes 589832 | tf_op jit(solution)/shard_map/ppermute | solution.py:196
  39.8 1.5 %collective-permute-start.9 = (bf16[768,128]{1,0:T(8,128)(2,1)S(1)}, bf16[768,128]{1,0:T(8,128)(2,1)S(1)}, u32[]{:S(2)}, u32[]{:S(2)}) collective-permute-start(bf16[768,128]{1,0:T(8,128)(2,1)S(1)} %shard_map.91.refs_5_), channel_id=1, source_target_pairs={{0,1},{1,0},{2,3},{3,2},{4,5},{5,4},{6,7},{7,6},{8,9},{9,8},{10,11... | collective-permute-start | bytes 589832 | tf_op jit(solution)/shard_map/ppermute | solution.py:196
  44.8 37.4 %copy-start.18 = (bf16[1,128,1536]{2,1,0:T(8,128)(2,1)}, bf16[1,128,1536]{2,1,0:T(8,128)(2,1)S(1)}, u32[]{:S(2)}) copy-start(bf16[1,128,1536]{2,1,0:T(8,128)(2,1)S(1)} %collective-permute-done.10.refs_3_) | copy-start | bytes 1179652
  44.8 2.3 %collective-permute-start.11 = (bf16[2,2,768,128]{3,2,1,0:T(8,128)(2,1)S(1)}, bf16[2,2,768,128]{3,2,1,0:T(8,128)(2,1)S(1)}, u32[]{:S(2)}, u32[]{:S(2)}) collective-permute-start(bf16[2,2,768,128]{3,2,1,0:T(8,128)(2,1)S(1)} %bitcast.38), channel_id=1, source_target_pairs={{0,1},{1,0},{2,3},{3,2},{4,5},{5,4},{6,7},{7,6},{8,9},{9,8},{10,11... | collective-permute-start | bytes 2359304 | tf_op jit(solution)/shard_map/ppermute | solution.py:196
  44.8 12.0 %collective-permute-start.15 = (bf16[1,128,1536]{2,1,0:T(8,128)(2,1)S(1)}, bf16[1,128,1536]{2,1,0:T(8,128)(2,1)S(1)}, u32[]{:S(2)}, u32[]{:S(2)}) collective-permute-start(bf16[1,128,1536]{2,1,0:T(8,128)(2,1)S(1)} %bitcast.43), channel_id=1, source_target_pairs={{0,4},{4,0},{1,5},{5,1},{2,6},{6,2},{3,7},{7,3},{8,12},{12,8},{9,1... | collective-permute-start | bytes 1179656 | tf_op jit(solution)/shard_map/ppermute | solution.py:196
  47.2 7.8 %collective-permute-start.13 = (bf16[768,128]{1,0:T(8,128)(2,1)S(1)}, bf16[768,128]{1,0:T(8,128)(2,1)S(1)}, u32[]{:S(2)}, u32[]{:S(2)}) collective-permute-start(bf16[768,128]{1,0:T(8,128)(2,1)S(1)} %get-tuple-element.72), channel_id=1, source_target_pairs={{0,2},{2,0},{1,3},{3,1},{4,6},{6,4},{5,7},{7,5},{8,10},{10,8},{9,1... | collective-permute-start | bytes 589832 | tf_op jit(solution)/shard_map/ppermute | solution.py:196
  48.3 14.4 %collective-permute-start.12 = (bf16[1,128,1536]{2,1,0:T(8,128)(2,1)S(1)}, bf16[1,128,1536]{2,1,0:T(8,128)(2,1)S(1)}, u32[]{:S(2)}, u32[]{:S(2)}) collective-permute-start(bf16[1,128,1536]{2,1,0:T(8,128)(2,1)S(1)} %bitcast.44), channel_id=1, source_target_pairs={{0,2},{2,0},{1,3},{3,1},{4,6},{6,4},{5,7},{7,5},{8,10},{10,8},{9,1... | collective-permute-start | bytes 1179656 | tf_op jit(solution)/shard_map/ppermute | solution.py:196
  55.1 7.6 %collective-permute-start.14 = (bf16[768,128]{1,0:T(8,128)(2,1)S(1)}, bf16[768,128]{1,0:T(8,128)(2,1)S(1)}, u32[]{:S(2)}, u32[]{:S(2)}) collective-permute-start(bf16[768,128]{1,0:T(8,128)(2,1)S(1)} %shard_map.95.refs_0_), channel_id=1, source_target_pairs={{0,4},{4,0},{1,5},{5,1},{2,6},{6,2},{3,7},{7,3},{8,12},{12,8},{9,1... | collective-permute-start | bytes 589832 | tf_op jit(solution)/shard_map/ppermute | solution.py:196
  56.8 33.5 %copy-start.19 = (bf16[1,128,1536]{2,1,0:T(8,128)(2,1)}, bf16[1,128,1536]{2,1,0:T(8,128)(2,1)S(1)}, u32[]{:S(2)}) copy-start(bf16[1,128,1536]{2,1,0:T(8,128)(2,1)S(1)} %collective-permute-done.15.refs_2_) | copy-start | bytes 1179652
  62.6 27.7 %copy-start.20 = (bf16[1,128,1536]{2,1,0:T(8,128)(2,1)}, bf16[1,128,1536]{2,1,0:T(8,128)(2,1)S(1)}, u32[]{:S(2)}) copy-start(bf16[1,128,1536]{2,1,0:T(8,128)(2,1)S(1)} %collective-permute-done.12.refs_6_) | copy-start | bytes 1179652
  62.7 12.8 %collective-permute-start.17 = (bf16[1,128,1536]{2,1,0:T(8,128)(2,1)S(1)}, bf16[1,128,1536]{2,1,0:T(8,128)(2,1)S(1)}, u32[]{:S(2)}, u32[]{:S(2)}) collective-permute-start(bf16[1,128,1536]{2,1,0:T(8,128)(2,1)S(1)} %collective-permute-done.10.refs_3_), channel_id=1, source_target_pairs={{0,2},{2,0},{1,3},{3,1},{4,6},{6,4},{5,7},{7,5},{8,10},{10,8},{9,1... | collective-permute-start | bytes 1179656 | tf_op jit(solution)/shard_map/ppermute | solution.py:196
  63.8 11.7 %collective-permute-start.16 = (bf16[768,128]{1,0:T(8,128)(2,1)S(1)}, bf16[768,128]{1,0:T(8,128)(2,1)S(1)}, u32[]{:S(2)}, u32[]{:S(2)}) collective-permute-start(bf16[768,128]{1,0:T(8,128)(2,1)S(1)} %get-tuple-element.77), channel_id=1, source_target_pairs={{0,8},{8,0},{1,9},{9,1},{2,10},{10,2},{3,11},{11,3},{4,12},{12,4},... | collective-permute-start | bytes 589832 | tf_op jit(solution)/shard_map/ppermute | solution.py:196
  67.2 14.4 %collective-permute-start.23 = (bf16[1,128,1536]{2,1,0:T(8,128)(2,1)S(1)}, bf16[1,128,1536]{2,1,0:T(8,128)(2,1)S(1)}, u32[]{:S(2)}, u32[]{:S(2)}) collective-permute-start(bf16[1,128,1536]{2,1,0:T(8,128)(2,1)S(1)} %bitcast.45), channel_id=1, source_target_pairs={{0,1},{1,0},{2,3},{3,2},{4,5},{5,4},{6,7},{7,6},{8,9},{9,8},{10,11... | collective-permute-start | bytes 1179656 | tf_op jit(solution)/shard_map/ppermute | solution.py:196
  67.2 10.4 %collective-permute-start.20 = (bf16[768,128]{1,0:T(8,128)(2,1)S(1)}, bf16[768,128]{1,0:T(8,128)(2,1)S(1)}, u32[]{:S(2)}, u32[]{:S(2)}) collective-permute-start(bf16[768,128]{1,0:T(8,128)(2,1)S(1)} %get-tuple-element.85.refs_0_), channel_id=1, source_target_pairs={{0,2},{2,0},{1,3},{3,1},{4,6},{6,4},{5,7},{7,5},{8,10},{10,8},{9,1... | collective-permute-start | bytes 589832 | tf_op jit(solution)/shard_map/ppermute | solution.py:196
  68.2 14.1 %collective-permute-start.24 = (bf16[1,128,1536]{2,1,0:T(8,128)(2,1)S(1)}, bf16[1,128,1536]{2,1,0:T(8,128)(2,1)S(1)}, u32[]{:S(2)}, u32[]{:S(2)}) collective-permute-start(bf16[1,128,1536]{2,1,0:T(8,128)(2,1)S(1)} %bitcast.48), channel_id=1, source_target_pairs={{0,1},{1,0},{2,3},{3,2},{4,5},{5,4},{6,7},{7,6},{8,9},{9,8},{10,11... | collective-permute-start | bytes 1179656 | tf_op jit(solution)/shard_map/ppermute | solution.py:196
  75.6 5.9 %collective-permute-start.19 = (bf16[768,128]{1,0:T(8,128)(2,1)S(1)}, bf16[768,128]{1,0:T(8,128)(2,1)S(1)}, u32[]{:S(2)}, u32[]{:S(2)}) collective-permute-start(bf16[768,128]{1,0:T(8,128)(2,1)S(1)} %get-tuple-element.81), channel_id=1, source_target_pairs={{0,2},{2,0},{1,3},{3,1},{4,6},{6,4},{5,7},{7,5},{8,10},{10,8},{9,1... | collective-permute-start | bytes 589832 | tf_op jit(solution)/shard_map/ppermute | solution.py:196
  76.7 5.7 %collective-permute-start.27 = (bf16[1,128,1536]{2,1,0:T(8,128)(2,1)S(1)}, bf16[1,128,1536]{2,1,0:T(8,128)(2,1)S(1)}, u32[]{:S(2)}, u32[]{:S(2)}) collective-permute-start(bf16[1,128,1536]{2,1,0:T(8,128)(2,1)S(1)} %collective-permute-done.6.refs_4_), channel_id=1, source_target_pairs={{0,1},{1,0},{2,3},{3,2},{4,5},{5,4},{6,7},{7,6},{8,9},{9,8},{10,11... | collective-permute-start | bytes 1179656 | tf_op jit(solution)/shard_map/ppermute | solution.py:196
  77.6 10.6 %collective-permute-start.18 = (bf16[1,128,1536]{2,1,0:T(8,128)(2,1)S(1)}, bf16[1,128,1536]{2,1,0:T(8,128)(2,1)S(1)}, u32[]{:S(2)}, u32[]{:S(2)}) collective-permute-start(bf16[1,128,1536]{2,1,0:T(8,128)(2,1)S(1)} %collective-permute-done.12.refs_6_), channel_id=1, source_target_pairs={{0,4},{4,0},{1,5},{5,1},{2,6},{6,2},{3,7},{7,3},{8,12},{12,8},{9,1... | collective-permute-start | bytes 1179656 | tf_op jit(solution)/shard_map/ppermute | solution.py:196
  81.6 1.4 collective-permute-start.21
  81.7 1.6 %collective-permute-start.22 = (bf16[768,128]{1,0:T(8,128)(2,1)S(1)}, bf16[768,128]{1,0:T(8,128)(2,1)S(1)}, u32[]{:S(2)}, u32[]{:S(2)}) collective-permute-start(bf16[768,128]{1,0:T(8,128)(2,1)S(1)} %shard_map.98.refs_5_.refs_7_), channel_id=1, source_target_pairs={{0,1},{1,0},{2,3},{3,2},{4,5},{5,4},{6,7},{7,6},{8,9},{9,8},{10,11... | collective-permute-start | bytes 589832 | tf_op jit(solution)/shard_map/ppermute | solution.py:196
  82.2 8.2 %collective-permute-start.26 = (bf16[1,128,1536]{2,1,0:T(8,128)(2,1)S(1)}, bf16[1,128,1536]{2,1,0:T(8,128)(2,1)S(1)}, u32[]{:S(2)}, u32[]{:S(2)}) collective-permute-start(bf16[1,128,1536]{2,1,0:T(8,128)(2,1)S(1)} %collective-permute-done.10.refs_3_), channel_id=1, source_target_pairs={{0,1},{1,0},{2,3},{3,2},{4,5},{5,4},{6,7},{7,6},{8,9},{9,8},{10,11... | collective-permute-start | bytes 1179656 | tf_op jit(solution)/shard_map/ppermute | solution.py:196
  82.3 8.1 %collective-permute-start.25 = (bf16[1,128,1536]{2,1,0:T(8,128)(2,1)S(1)}, bf16[1,128,1536]{2,1,0:T(8,128)(2,1)S(1)}, u32[]{:S(2)}, u32[]{:S(2)}) collective-permute-start(bf16[1,128,1536]{2,1,0:T(8,128)(2,1)S(1)} %collective-permute-done.15.refs_2_), channel_id=1, source_target_pairs={{0,1},{1,0},{2,3},{3,2},{4,5},{5,4},{6,7},{7,6},{8,9},{9,8},{10,11... | collective-permute-start | bytes 1179656 | tf_op jit(solution)/shard_map/ppermute | solution.py:196
  83.0 7.5 %collective-permute-start.29 = (bf16[1,128,1536]{2,1,0:T(8,128)(2,1)S(1)}, bf16[1,128,1536]{2,1,0:T(8,128)(2,1)S(1)}, u32[]{:S(2)}, u32[]{:S(2)}) collective-permute-start(bf16[1,128,1536]{2,1,0:T(8,128)(2,1)S(1)} %collective-permute-done.12.refs_6_), channel_id=1, source_target_pairs={{0,1},{1,0},{2,3},{3,2},{4,5},{5,4},{6,7},{7,6},{8,9},{9,8},{10,11... | collective-permute-start | bytes 1179656 | tf_op jit(solution)/shard_map/ppermute | solution.py:196
  83.3 7.2 %collective-permute-start.28 = (bf16[1,128,1536]{2,1,0:T(8,128)(2,1)S(1)}, bf16[1,128,1536]{2,1,0:T(8,128)(2,1)S(1)}, u32[]{:S(2)}, u32[]{:S(2)}) collective-permute-start(bf16[1,128,1536]{2,1,0:T(8,128)(2,1)S(1)} %collective-permute-done.17.refs_5_), channel_id=1, source_target_pairs={{0,1},{1,0},{2,3},{3,2},{4,5},{5,4},{6,7},{7,6},{8,9},{9,8},{10,11... | collective-permute-start | bytes 1179656 | tf_op jit(solution)/shard_map/ppermute | solution.py:196
  88.2 2.3 %collective-permute-start.30 = (bf16[1,128,1536]{2,1,0:T(8,128)(2,1)S(1)}, bf16[1,128,1536]{2,1,0:T(8,128)(2,1)S(1)}, u32[]{:S(2)}, u32[]{:S(2)}) collective-permute-start(bf16[1,128,1536]{2,1,0:T(8,128)(2,1)S(1)} %collective-permute-done.18.refs_7_), channel_id=1, source_target_pairs={{0,1},{1,0},{2,3},{3,2},{4,5},{5,4},{6,7},{7,6},{8,9},{9,8},{10,11... | collective-permute-start | bytes 1179656 | tf_op jit(solution)/shard_map/ppermute | solution.py:196
  90.4 17.3 %copy-start.12 = (bf16[2,8,2,96,128]{4,3,2,1,0:T(8,128)(2,1)}, bf16[2,8,2,96,128]{4,3,2,1,0:T(8,128)(2,1)S(1)}, u32[]{:S(2)}) copy-start(bf16[2,8,2,96,128]{4,3,2,1,0:T(8,128)(2,1)S(1)} %get-tuple-element.96) | copy-start | bytes 2359300
  90.4 17.3 %copy-start.26 = (bf16[1,128,1536]{2,1,0:T(8,128)(2,1)}, bf16[1,128,1536]{2,1,0:T(8,128)(2,1)S(1)}, u32[]{:S(2)}) copy-start(bf16[1,128,1536]{2,1,0:T(8,128)(2,1)S(1)} %collective-permute-done.26.refs_11_) | copy-start | bytes 1179652
  90.5 17.3 %copy-start.27 = (bf16[1,128,1536]{2,1,0:T(8,128)(2,1)}, bf16[1,128,1536]{2,1,0:T(8,128)(2,1)S(1)}, u32[]{:S(2)}) copy-start(bf16[1,128,1536]{2,1,0:T(8,128)(2,1)S(1)} %collective-permute-done.25.refs_10_) | copy-start | bytes 1179652
  90.5 17.3 %copy-start.28 = (bf16[1,128,1536]{2,1,0:T(8,128)(2,1)}, bf16[1,128,1536]{2,1,0:T(8,128)(2,1)S(1)}, u32[]{:S(2)}) copy-start(bf16[1,128,1536]{2,1,0:T(8,128)(2,1)S(1)} %collective-permute-done.29.refs_14_) | copy-start | bytes 1179652
  90.5 17.3 %copy-start.29 = (bf16[1,128,1536]{2,1,0:T(8,128)(2,1)}, bf16[1,128,1536]{2,1,0:T(8,128)(2,1)S(1)}, u32[]{:S(2)}) copy-start(bf16[1,128,1536]{2,1,0:T(8,128)(2,1)S(1)} %collective-permute-done.28.refs_13_) | copy-start | bytes 1179652
  90.5 17.3 %copy-start.30 = (bf16[1,128,1536]{2,1,0:T(8,128)(2,1)}, bf16[1,128,1536]{2,1,0:T(8,128)(2,1)S(1)}, u32[]{:S(2)}) copy-start(bf16[1,128,1536]{2,1,0:T(8,128)(2,1)S(1)} %collective-permute-done.30.refs_15_) | copy-start | bytes 1179652
  107.8 22.1 %all-to-all-start.1 = ((bf16[16,192,128]{2,1,0:T(8,128)(2,1)}), bf16[16,192,128]{2,1,0:T(8,128)(2,1)}, u32[]{:S(2)}, u32[]{:S(2)}) async-start(bf16[16,192,128]{2,1,0:T(8,128)(2,1)} %bitcast.37), calls=%async_computation.1 | async-start | bytes 1572864 | tf_op jit(solution)/shard_map/all_to_all | solution.py:500
  117.1 17.6 %collective-permute-start.31 = (bf16[96,1536]{1,0:T(8,128)(2,1)}, bf16[96,1536]{1,0:T(8,128)(2,1)}, u32[]{:S(2)}, u32[]{:S(2)}) collective-permute-start(bf16[96,1536]{1,0:T(8,128)(2,1)} %bitcast.55), channel_id=1, source_target_pairs={{0,8},{8,0},{1,9},{9,1},{2,10},{10,2},{3,11},{11,3},{4,12},{12,4},... | collective-permute-start | bytes 884744 | tf_op jit(solution)/shard_map/ppermute | solution.py:518
  134.7 13.7 %collective-permute-start.32 = (bf16[96,1536]{1,0:T(8,128)(2,1)}, bf16[96,1536]{1,0:T(8,128)(2,1)S(1)}, u32[]{:S(2)}, u32[]{:S(2)}) collective-permute-start(bf16[96,1536]{1,0:T(8,128)(2,1)} %bitcast.56), channel_id=1, source_target_pairs={{0,8},{8,0},{1,9},{9,1},{2,10},{10,2},{3,11},{11,3},{4,12},{12,4},... | collective-permute-start | bytes 884744 | tf_op jit(solution)/shard_map/ppermute | solution.py:518
  (19 other events, 137.4 us)
